TPU v7x, 32 devices: a whole 2x2x4 slice. The times are simulated.
32 devices in a mesh: member: 2 (over x), row: 16 (over z, y, core).
Axes of the slice: x: 2, y: 2, z: 4, core: 2. Of those that a mesh axis runs over, the one named last changes fastest.
Arguments:
- innovation: bfloat16 [8, 1024, 2048], P('member', 'row'), parts along dimension 0, may hold values from -6 to 6
- background: bfloat16 [8, 1024, 2048], P('member', 'row'), parts along dimension 0, may hold values from -6 to 6
- level_weight: float32 [4], replicated, may hold values from 0.25 to 4
Outputs:
- displacement: float32 [4, 1024, 2048], P('member', 'row'), parts along dimension 0
There are 2 independent parts, one for each index of `member`. A program takes and returns all parts, laid end to end along the dimension named above; an argument that names none is the same for every part. Nothing has to cross between parts.
All inputs are finite; a program needn't handle non-finite values.
Results may differ from a plain program's by a relative error of at most 0.0003.
Values may be sent and summed in bfloat16 or wider, within the bound.
No kernel may reach another device: no remote copies, remote signals or barrier semaphores. Data moves between devices by JAX's collectives and lax.ppermute only.
A program may use at most 64 MiB of HBM per device.

v0:
```python
import jax
import jax.numpy as jnp
from jax import lax
from jax.sharding import PartitionSpec as P

HALF = 64
SIGMA = 64


def padded_2(block, sides, width):
    for axis, dim in sides:
        count = lax.axis_size(axis)
        forward = [(i, i + 1) for i in range(count - 1)]
        backward = [(target, source) for source, target in forward]
        low = lax.ppermute(
            lax.slice_in_dim(block, block.shape[dim] - width, None, axis=dim), axis, forward
        )
        high = lax.ppermute(lax.slice_in_dim(block, 0, width, axis=dim), axis, backward)
        block = jnp.concatenate([low, block, high], axis=dim)
    return block


def tap_at(offset):
    grid = jnp.arange(-HALF, HALF + 1).astype(jnp.float32)
    spread = jnp.float32(SIGMA)
    total = jnp.sqrt(jnp.sum(jnp.exp(-grid * grid / (spread * spread))))
    off = offset.astype(jnp.float32)
    value = jnp.exp(-off * off / (2.0 * spread * spread)) / total
    return jnp.where(jnp.abs(offset) <= HALF, value, jnp.float32(0.0))


def band_blocks():
    inner = jnp.arange(128)[:, None]
    outer = jnp.arange(128)[None, :]
    return [tap_at(128 * shift + inner - outer) for shift in (-1, 0, 1)]


def smooth_last(values, blocks):
    lead = values.shape[:-1]
    length = values.shape[-1]
    nblocks = length // 128
    widths = [(0, 0)] * (values.ndim - 1) + [(128, 128)]
    padded = jnp.pad(values, widths).reshape(lead + (nblocks + 2, 128))
    total = jnp.zeros(lead + (nblocks, 128), jnp.float32)
    for index in range(3):
        part = padded[..., index : index + nblocks, :]
        total = total + jnp.dot(
            part, blocks[index], precision=lax.Precision.HIGHEST, preferred_element_type=jnp.float32
        )
    return total.reshape(lead + (length,))


def smooth_mid(values, blocks):
    chans, length, width = values.shape
    nblocks = length // 128
    padded = jnp.pad(values, ((0, 0), (128, 128), (0, 0))).reshape(chans, nblocks + 2, 128, width)
    total = jnp.zeros((chans, nblocks, 128, width), jnp.float32)
    for index in range(3):
        part = padded[:, index : index + nblocks]
        total = total + jnp.einsum(
            "cbix,io->cbox",
            part,
            blocks[index],
            precision=lax.Precision.HIGHEST,
            preferred_element_type=jnp.float32,
        )
    return total.reshape(chans, length, width)


def body(innovation, background, level_weight):
    blocks = band_blocks()
    rimmed = padded_2(background, (("row", 1),), 1).astype(jnp.float32)
    grad_y = 0.5 * (rimmed[:, 2:, :] - rimmed[:, :-2, :])
    padded_x = jnp.pad(rimmed[:, 1:-1, :], ((0, 0), (0, 0), (1, 1)))
    grad_x = 0.5 * (padded_x[:, :, 2:] - padded_x[:, :, :-2])
    scaled = level_weight[:, None, None] * innovation.astype(jnp.float32)
    numer_y = jnp.sum(scaled * grad_y, axis=0)
    numer_x = jnp.sum(scaled * grad_x, axis=0)
    denom = 1.0 + jnp.sum(level_weight[:, None, None] * (grad_y * grad_y + grad_x * grad_x), axis=0)
    raw = jnp.stack([numer_y / denom, numer_x / denom])
    zonal = smooth_last(raw, blocks)
    smoothed = smooth_mid(
        lax.all_to_all(zonal, "row", split_axis=2, concat_axis=1, tiled=True), blocks
    )
    return lax.all_to_all(smoothed, "row", split_axis=1, concat_axis=2, tiled=True)


def solution(mesh):
    placed = (P("member", "row", None), P("member", "row", None), P())
    return jax.shard_map(
        body, mesh=mesh, in_specs=placed, out_specs=P("member", "row", None), check_vma=False
    )
```

profile of v0, /device:TPU:11, one launch (start us, length us, event | category | flops | bytes accessed | tf_op | source)
XLA Modules:
  0.0 94.9 jit_solution(1240667817818672247)
XLA Ops:
  0.0 1.0 %fusion.82 = (bf16[4,1,2048]{2,1,0:T(2,128)(2,1)S(1)}, bf16[4,1,2048]{2,1,0:T(2,128)(2,1)S(1)}) fusion(bf16[4,64,2048]{2,1,0:T(8,128)(2,1)} %param.4), kind=kLoop, calls=%fused_computation.102 | loop fusion | bytes 65536 | tf_op jit(solution)/shard_map/slice | solution.py:16
  1.0 3.7 %collective-permute-start = (bf16[4,1,2048]{2,1,0:T(2,128)(2,1)S(1)}, bf16[4,1,2048]{2,1,0:T(2,128)(2,1)S(1)}, u32[]{:S(2)}, u32[]{:S(2)}) collective-permute-start(bf16[4,1,2048]{2,1,0:T(2,128)(2,1)S(1)} %get-tuple-element.8), channel_id=1, source_target_pairs={{0,1},{1,2},{2,3},{3,4},{4,5},{5,6},{6,7},{7,8},{8,9},{9,10},{10,1... | collective-permute-start | bytes 49160 | tf_op jit(solution)/shard_map/ppermute | solution.py:15
  4.7 1.9 %collective-permute-start.1 = (bf16[4,1,2048]{2,1,0:T(2,128)(2,1)S(1)}, bf16[4,1,2048]{2,1,0:T(2,128)(2,1)S(1)}, u32[]{:S(2)}, u32[]{:S(2)}) collective-permute-start(bf16[4,1,2048]{2,1,0:T(2,128)(2,1)S(1)} %get-tuple-element.9), channel_id=1, source_target_pairs={{1,0},{2,1},{3,2},{4,3},{5,4},{6,5},{7,6},{8,7},{9,8},{10,9},{11,1... | collective-permute-start | bytes 49160 | tf_op jit(solution)/shard_map/ppermute | solution.py:18
  6.7 0.6 fusion.63
  8.0 0.0 collective-permute-done
  8.0 2.0 %collective-permute-done.1 = bf16[4,1,2048]{2,1,0:T(2,128)(2,1)S(1)} collective-permute-done((bf16[4,1,2048]{2,1,0:T(2,128)(2,1)S(1)}, bf16[4,1,2048]{2,1,0:T(2,128)(2,1)S(1)}, u32[]{:S(2)}, u32[]{:S(2)}) %collective-permute-start.1) | collective-permute-done | bytes 16416 | tf_op jit(solution)/shard_map/ppermute | solution.py:18
  10.0 1.6 %maximum_convert_fusion = f32[4,66,2048]{2,1,0:T(8,128)S(1)} fusion(bf16[4,1,2048]{2,1,0:T(2,128)(2,1)S(1)} %collective-permute-done.1, bf16[4,64,2048]{2,1,0:T(8,128)(2,1)} %param.4, bf16[4,1,2048]{2,1,0:T(2,128)(2,1)S(1)} %collective-permute-done), kind=kLoop, calls=%fused_computation.17 | loop fusion | flops 3244032 | bytes 3244032 | tf_op jit(solution)/shard_map/convert_element_type | solution.py:72
  11.6 0.0 copy-start
  11.6 0.0 copy-start.1
  11.6 0.3 slice.54
  11.9 0.9 copy-done
  12.8 0.0 copy-done.1
  12.8 2.7 %multiply_reduce_fusion.2 = (f32[64,2048]{1,0:T(8,128)S(1)}, f32[64,2048]{1,0:T(8,128)S(1)}, f32[64,2048]{1,0:T(8,128)S(1)}) fusion(bf16[4,64,2048]{2,1,0:T(8,128)(2,1)S(1)} %copy-done, f32[4]{0:T(128)S(1)} %copy-done.1, f32[4,66,2048]{2,1,0:T(8,128)S(1)} %maximum_convert_fusion, f32[4,64,2048]{2,1,0:T(8,128)S(1)} %slice.54), kind=kLoop, calls=%fused_computation.8 | loop fusion | flops 8519680 | bytes 8912912 | tf_op jit(solution)/shard_map/reduce_sum | solution.py:77
  15.5 0.1 divide_bitcast_fusion.1
  15.6 0.1 select_maximum_fusion
  15.7 0.2 reshape.52
  15.9 1.0 %fusion.10 = f32[2,64,16,128]{3,2,1,0:T(8,128)S(1)} fusion(f32[2,64,18,128]{3,2,1,0:T(8,128)S(1)} %reshape.52, f32[]{:T(128)S(6)} %sqrt.2, s32[128]{0:T(128)S(1)} %iota_add_fusion.1), kind=kOutput, calls=%fused_computation.25 | convolution fusion | flops 402800640 | bytes 2097668 | tf_op jit(solution)/shard_map/dot_general | solution.py:47
  16.9 1.0 %convolution_add_fusion.3 = f32[2,64,16,128]{3,2,1,0:T(8,128)S(1)} fusion(f32[2,64,16,128]{3,2,1,0:T(8,128)S(1)} %fusion.10, f32[2,64,18,128]{3,2,1,0:T(8,128)S(1)} %reshape.52, f32[]{:T(128)S(6)} %sqrt.2), kind=kOutput, calls=%fused_computation.15 | convolution fusion | flops 403062784 | bytes 3145732 | tf_op jit(solution)/shard_map/dot_general | solution.py:47
  17.9 1.0 %convolution_add_fusion.2 = f32[2,64,16,128]{3,2,1,0:T(8,128)S(1)} fusion(f32[2,64,16,128]{3,2,1,0:T(8,128)S(1)} %convolution_add_fusion.3, f32[2,64,18,128]{3,2,1,0:T(8,128)S(1)} %reshape.52, s32[128]{0:T(128)S(1)} %iota_add_fusion, f32[]{:T(128)S(6)} %sqrt.2), kind=kOutput, calls=%fused_computation.14 | convolution fusion | flops 403062784 | bytes 3146244 | tf_op jit(solution)/shard_map/dot_general | solution.py:47
  18.9 1.0 %copy.30 = f32[2,64,16,128]{1,0,3,2:T(2,128)S(1)} copy(f32[2,64,16,128]{3,2,1,0:T(8,128)S(1)} %convolution_add_fusion.2) | data formatting | bytes 2097152 | tf_op jit(solution)/shard_map/reshape | solution.py:50
  20.0 2.2 %reshape.62 = f32[16,1,16384]{2,1,0:T(1,128)S(1)} reshape(f32[2048,2,64]{2,1,0:T(2,128)S(1)} %bitcast.44) | data formatting | bytes 2097152
  22.1 31.1 %all_to_all.36 = f32[16,1,16384]{2,1,0:T(1,128)S(1)} all-to-all(f32[16,1,16384]{2,1,0:T(1,128)S(1)} %reshape.62), channel_id=1, replica_groups=mesh['member'=2,'row'=16] {'row'}, dimensions={0} | all-to-all | bytes 2097152 | tf_op jit(solution)/shard_map/all_to_all | solution.py:83
  53.2 0.5 broadcast.123
  53.8 3.1 %reduce = f32[16,16384]{1,0:T(8,128)S(1)} reduce(f32[16,1,16384]{2,1,0:T(1,128)S(1)} %all_to_all.36, f32[]{:T(128)} %broadcast.123), dimensions={1}, to_apply=%all_to_all.26.reduce_sub_computation | reduce | bytes 2097156 | tf_op jit(solution)/shard_map/all_to_all | solution.py:83
  56.9 1.5 %reshape.63 = f32[2048,2,64]{2,1,0:T(2,128)S(1)} reshape(f32[16,16384]{1,0:T(8,128)S(1)} %reduce) | data formatting | bytes 2097152
  58.4 0.9 copy.18
  59.4 0.1 pad.14
  59.5 1.1 %fusion.6 = f32[128,2,8,128]{3,0,2,1:T(8,128)S(1)} fusion(f32[2,10,128,128]{3,2,1,0:T(8,128)S(1)} %bitcast.41, f32[]{:T(128)S(6)} %sqrt.2, s32[128]{0:T(128)S(1)} %iota_add_fusion.1), kind=kOutput, calls=%fused_computation.21 | convolution fusion | flops 402800640 | bytes 2097668 | tf_op jit(solution)/shard_map/cbix,io->cbox/dot_general | solution.py:60
  60.5 1.1 %convolution_add_fusion.1 = f32[128,2,8,128]{3,0,2,1:T(8,128)S(1)} fusion(f32[128,2,8,128]{3,0,2,1:T(8,128)S(1)} %fusion.6, f32[2,10,128,128]{3,2,1,0:T(8,128)S(1)} %bitcast.42, f32[]{:T(128)S(6)} %sqrt.2), kind=kOutput, calls=%fused_computation.13 | convolution fusion | flops 403062784 | bytes 3145732 | tf_op jit(solution)/shard_map/cbix,io->cbox/dot_general | solution.py:60
  61.6 1.1 %convolution_add_fusion = f32[128,2,8,128]{3,0,2,1:T(8,128)S(1)} fusion(f32[128,2,8,128]{3,0,2,1:T(8,128)S(1)} %convolution_add_fusion.1, f32[2,10,128,128]{3,2,1,0:T(8,128)S(1)} %bitcast.43, s32[128]{0:T(128)S(1)} %iota_add_fusion, f32[]{:T(128)S(6)} %sqrt.2), kind=kOutput, calls=%fused_computation.12 | convolution fusion | flops 403062784 | bytes 3146244 | tf_op jit(solution)/shard_map/cbix,io->cbox/dot_general | solution.py:60
  62.7 0.8 copy.19
  63.5 29.6 %all_to_all.37 = f32[2,1024,128]{2,0,1:T(2,128)S(1)} all-to-all(f32[2,1024,128]{2,0,1:T(2,128)S(1)} %copy.19), channel_id=1, replica_groups=mesh['member'=2,'row'=16] {'row'}, dimensions={1} | all-to-all | bytes 2097152 | tf_op jit(solution)/shard_map/all_to_all | solution.py:85
  93.2 0.6 copy.20
  93.8 1.1 %all_to_all.33 = f32[2,64,2048]{2,1,0:T(8,128)} reshape(f32[2,64,16,128]{3,2,1,0:T(8,128)S(1)} %copy.20) | data formatting | bytes 2097152 | tf_op jit(solution)/shard_map/all_to_all | solution.py:85
  (2 shorter events, 0.0 us)
Async XLA Ops:
  1.0 7.0 %collective-permute-start = (bf16[4,1,2048]{2,1,0:T(2,128)(2,1)S(1)}, bf16[4,1,2048]{2,1,0:T(2,128)(2,1)S(1)}, u32[]{:S(2)}, u32[]{:S(2)}) collective-permute-start(bf16[4,1,2048]{2,1,0:T(2,128)(2,1)S(1)} %get-tuple-element.8), channel_id=1, source_target_pairs={{0,1},{1,2},{2,3},{3,4},{4,5},{5,6},{6,7},{7,8},{8,9},{9,10},{10,1... | collective-permute-start | bytes 49160 | tf_op jit(solution)/shard_map/ppermute | solution.py:15
  4.7 5.2 %collective-permute-start.1 = (bf16[4,1,2048]{2,1,0:T(2,128)(2,1)S(1)}, bf16[4,1,2048]{2,1,0:T(2,128)(2,1)S(1)}, u32[]{:S(2)}, u32[]{:S(2)}) collective-permute-start(bf16[4,1,2048]{2,1,0:T(2,128)(2,1)S(1)} %get-tuple-element.9), channel_id=1, source_target_pairs={{1,0},{2,1},{3,2},{4,3},{5,4},{6,5},{7,6},{8,7},{9,8},{10,9},{11,1... | collective-permute-start | bytes 49160 | tf_op jit(solution)/shard_map/ppermute | solution.py:18
  11.6 1.2 %copy-start = (bf16[4,64,2048]{2,1,0:T(8,128)(2,1)S(1)}, bf16[4,64,2048]{2,1,0:T(8,128)(2,1)}, u32[]{:S(2)}) copy-start(bf16[4,64,2048]{2,1,0:T(8,128)(2,1)} %param.3) | copy-start | bytes 3145732
  11.6 1.2 %copy-start.1 = (f32[4]{0:T(128)S(1)}, f32[4]{0:T(128)}, u32[]{:S(2)}) copy-start(f32[4]{0:T(128)} %param.5) | copy-start | bytes 52
where the time goes:
time: 95.8 us; the launch traced here: 94.9 us
  blocking collectives  60.7 us (63%)
  local copies, waits for them, and re-layouts  11.2 us (12%)
  other arithmetic  8.24 us (9%)
  matrix products  6.23 us (7%)
  starting transfers between devices  5.63 us (6%)
  waiting for transfers between devices  1.97 us (2%)
    all_to_all x1, blocking collectives, body(): lax.all_to_all(zonal, 'row', split_axis=2, concat_axis=1, tiled=True)  31.1 us
    all_to_all x1, blocking collectives, body(): lax.all_to_all(smoothed, 'row', split_axis=1, concat_axis=2, tiled=True)  29.6 us
    unnamed x6, local copies, waits for them, and re-layouts  4.65 us
    ppermute x1, starting transfers between devices, padded_2(): lax.ppermute(lax.slice_in_dim(block, block.shape[dim] - width, None, axis...  3.71 us
    dot_general x3, matrix products, smooth_mid(): jnp.einsum('cbix,io->cbox', part, blocks[index], precision=lax.Precision....  3.21 us
    all_to_all x1, other arithmetic, body(): lax.all_to_all(zonal, 'row', split_axis=2, concat_axis=1, tiled=True)  3.15 us
    dot_general x3, matrix products, smooth_last(): jnp.dot(part, blocks[index], precision=lax.Precision.HIGHEST, preferred_e...  3.02 us
    reduce_sum x1, other arithmetic, body(): numer_y = jnp.sum(scaled * grad_y, axis=0)  2.69 us
  transfers between devices with their start and end apart: 2, of which 1 were waited for; matrix products, arithmetic and copies ran while one was open for 1% of the time, Pallas kernels for 0%

commit v1 on v0

v1 whole, which is shorter than its diff:
```python
import functools
import math

import jax
import jax.numpy as jnp
import numpy as np
from jax import lax
from jax.experimental import pallas as pl
from jax.experimental.pallas import tpu as pltpu
from jax.sharding import PartitionSpec as P

HALF = 64
SIGMA = 64
LANES = 128
GROUP_Y = 4
GROUP_X = 8
F32 = jnp.float32
BF16 = jnp.bfloat16
NORM = math.sqrt(sum(math.exp(-k * k / (SIGMA * SIGMA)) for k in range(-HALF, HALF + 1)))


def split(values):
    high = values.astype(BF16)
    return high, (values - high.astype(F32)).astype(BF16)


def dot(left, right):
    return jnp.dot(left, right, preferred_element_type=F32)


def iota(shape, dim):
    return lax.broadcasted_iota(jnp.int32, shape, dim)


def taps(offset):
    off = offset.astype(F32)
    value = jnp.exp(off * off * (-0.5 / (SIGMA * SIGMA))) * (1.0 / NORM)
    return jnp.where(jnp.abs(offset) <= HALF, value, 0.0)


def zonal_band():
    offset = np.arange(4 * LANES)[:, None] - LANES - np.arange(2 * LANES)[None, :]
    band = np.exp(-offset * offset / (2.0 * SIGMA * SIGMA)) / NORM
    band = np.where(np.abs(offset) <= HALF, band, 0.0).astype(np.float32)
    high = band.astype(BF16)
    return np.stack([high, (band - high.astype(np.float32)).astype(BF16)])


def windows(nblocks):
    for first in range(0, nblocks, 2):
        low, high = max(first - 1, 0), min(first + 3, nblocks)
        yield first, low, high, (low - first + 1) * LANES, (high - first + 1) * LANES


def raw_kernel(lw_ref, inno_ref, back_ref, near_ref, far_ref, raw_ref, *msg_refs):
    levels, rows, width = inno_ref.shape
    nblocks = width // LANES
    even = lax.rem(lax.axis_index("row"), 2) == 0
    row, col = iota((rows, rows), 0), iota((rows, rows), 1)
    diff_y = ((col == row + 1).astype(F32) - (col == row - 1).astype(F32)).astype(BF16)
    shape = (4 * LANES, 2 * LANES)
    off = iota(shape, 0) - LANES - iota(shape, 1)
    diff_x = ((off == 1).astype(F32) - (off == -1).astype(F32)).astype(BF16)
    at = iota((rows, 2 * LANES), 0)
    for first, low, high, top, bottom in windows(nblocks):
        here = pl.ds(first * LANES, 2 * LANES)
        numer_y = numer_x = 0.0
        denom = 1.0
        for level in range(levels):
            weight = lw_ref[level]
            near, far = near_ref[level, :, here].astype(F32), far_ref[level, :, here].astype(F32)
            above = jnp.where(even, far, near)
            below = jnp.where(even, near, far)
            grad_y = dot(diff_y, back_ref[level, :, here])
            grad_y += jnp.where(at == 0, -above, 0.0) + jnp.where(at == rows - 1, below, 0.0)
            around = back_ref[level, :, low * LANES : high * LANES]
            grad_x = dot(around, diff_x[top:bottom])
            scaled = inno_ref[level, :, here].astype(F32) * (0.5 * weight)
            numer_y += scaled * grad_y
            numer_x += scaled * grad_x
            denom += (0.25 * weight) * (grad_y * grad_y + grad_x * grad_x)
        inverse = 1.0 / denom
        for comp, numer in enumerate((numer_y, numer_x)):
            raw = numer * inverse
            for k in range(2):
                raw_ref[first + k, comp * rows : (comp + 1) * rows, :] = raw[:, k * LANES : (k + 1) * LANES]
    per = nblocks // len(msg_refs)
    both = 2 * rows
    shape = (per * LANES, per * LANES // GROUP_X)
    sum_x = (iota(shape, 0) // GROUP_X == iota(shape, 1)).astype(F32).astype(BF16)
    shape = (both // GROUP_Y, both)
    sum_y = (iota(shape, 1) // GROUP_Y == iota(shape, 0)).astype(F32).astype(BF16)
    for index, msg_ref in enumerate(msg_refs):
        total = 0.0
        for k in range(per):
            high, low = split(raw_ref[index * per + k])
            msg_ref[k * both : (k + 1) * both, :] = high
            total += dot(low, sum_x[k * LANES : (k + 1) * LANES])
        msg_ref[per * both :, :] = dot(sum_y, total.astype(BF16)).astype(BF16)


def shifted_taps(rows, shift):
    return taps(iota((rows, rows), 1) - iota((rows, rows), 0) + shift)


def near_kernel(raw_ref, near_ref, out_ref):
    nblocks, both, _ = raw_ref.shape
    rows = both // 2
    side = 1 - 2 * lax.rem(lax.axis_index("row"), 2)
    high, low = split(
        jnp.concatenate([shifted_taps(rows, 0), shifted_taps(rows, side * rows)], axis=1)
    )
    two = jnp.concatenate([high, low], axis=0)
    for first in range(0, nblocks, 2):
        for comp in range(2):
            here = pl.ds(comp * rows, rows)
            pairs = []
            for k in (first, first + 1):
                pairs.append(jnp.concatenate([raw_ref[k, here, :], near_ref[k, here, :]], axis=0))
            high_x, low_x = split(jnp.concatenate(pairs, axis=1))
            part = dot(two, high_x)
            part = part[:rows] + part[rows:] + dot(high, low_x)
            for k in range(2):
                out_ref[first + k, here, :] = part[:, k * LANES : (k + 1) * LANES]


def far_kernel(band_ref, part_ref, *refs):
    *msg_refs, out_ref, high_ref, low_ref = refs
    nblocks, both, _ = part_ref.shape
    rows = both // 2
    side = 1 - 2 * lax.rem(lax.axis_index("row"), 2)
    taps_far = shifted_taps(rows, -side * rows)
    high, low = split(taps_far)
    two = jnp.concatenate([high, low], axis=0)
    shape = (rows, rows // GROUP_Y)
    mean_y = jnp.where(iota(shape, 0) // GROUP_Y == iota(shape, 1), 1.0 / GROUP_Y, 0.0).astype(BF16)
    taps_group = dot(high, mean_y).astype(BF16)
    per = nblocks // len(msg_refs)
    shape = (per * LANES // GROUP_X, per * LANES)
    mean_x = jnp.where(iota(shape, 1) // GROUP_X == iota(shape, 0), 1.0 / GROUP_X, 0.0).astype(BF16)
    groups = rows // GROUP_Y
    for index, msg_ref in enumerate(msg_refs):
        rest = []
        for comp in range(2):
            start = per * both + comp * groups
            rest.append(dot(taps_group, msg_ref[start : start + groups, :]))
        rest = jnp.concatenate(rest, axis=0).astype(BF16)
        for first in range(0, per, 2):
            spread = dot(rest, mean_x[:, first * LANES : (first + 2) * LANES])
            for comp in range(2):
                here = pl.ds(comp * rows, rows)
                got = [
                    msg_ref[k * both + comp * rows : k * both + (comp + 1) * rows, :]
                    for k in (first, first + 1)
                ]
                part = dot(two, jnp.concatenate(got, axis=1))
                part = part[:rows] + part[rows:] + spread[comp * rows : (comp + 1) * rows]
                for k in range(2):
                    block = index * per + first + k
                    total = part_ref[block, here, :] + part[:, k * LANES : (k + 1) * LANES]
                    high_ref[block, here, :], low_ref[block, here, :] = split(total)
    for first, low_, high_, top, bottom in windows(nblocks):
        upper = jnp.concatenate([high_ref[k] for k in range(low_, high_)], axis=1)
        lower = jnp.concatenate([low_ref[k] for k in range(low_, high_)], axis=1)
        band = band_ref[0, top:bottom, :]
        result = dot(upper, band) + dot(lower, band) + dot(upper, band_ref[1, top:bottom, :])
        here = pl.ds(first * LANES, 2 * LANES)
        out_ref[0, :, here] = result[:rows]
        out_ref[1, :, here] = result[rows:]


VMEM = pl.BlockSpec(memory_space=pltpu.VMEM)
SMEM = pl.BlockSpec(memory_space=pltpu.SMEM)
PARAMS = pltpu.CompilerParams(vmem_limit_bytes=40 * 1024 * 1024)
CHUNKS = 2


def body(innovation, background, level_weight):
    levels, rows, width = innovation.shape
    if rows != HALF or width % (8 * LANES * CHUNKS):
        raise NotImplementedError("slab shape")
    nblocks = width // LANES
    both = 2 * rows
    count = lax.axis_size("row")
    chip = [(i, i ^ 1) for i in range(count) if i ^ 1 < count]
    away = [(i, j) for i in range(count) for j in [((i + 1) ^ 1) - 1] if 0 <= j < count]
    even = lax.rem(lax.axis_index("row"), 2) == 0
    first, last = background[:, :1], background[:, rows - 1 :]
    edge_near = lax.ppermute(jnp.where(even, last, first), "row", chip)
    edge_far = lax.ppermute(jnp.where(even, first, last), "row", away)
    per = nblocks // CHUNKS
    msg = jax.ShapeDtypeStruct((per * both + both // GROUP_Y * per * LANES // GROUP_X // LANES, LANES), BF16)
    blocks = jax.ShapeDtypeStruct((nblocks, both, LANES), F32)
    raw, *msgs = pl.pallas_call(
        raw_kernel,
        out_shape=[blocks] + [msg] * CHUNKS,
        in_specs=[SMEM] + [VMEM] * 4,
        out_specs=[VMEM] * (1 + CHUNKS),
        compiler_params=PARAMS,
    )(level_weight, innovation, background, edge_near, edge_far)
    msgs = [lax.ppermute(m, "row", away) for m in msgs]
    raw_near = lax.ppermute(raw, "row", chip)
    part = pl.pallas_call(
        near_kernel,
        out_shape=blocks,
        in_specs=[VMEM] * 2,
        out_specs=VMEM,
        compiler_params=PARAMS,
        cost_estimate=pl.CostEstimate(flops=10**9, bytes_accessed=3 * 2**20, transcendentals=0),
    )(raw, raw_near)
    return pl.pallas_call(
        far_kernel,
        out_shape=jax.ShapeDtypeStruct((2, rows, width), F32),
        in_specs=[VMEM] * (2 + CHUNKS),
        out_specs=VMEM,
        scratch_shapes=[pltpu.VMEM((nblocks, both, LANES), BF16)] * 2,
        compiler_params=PARAMS,
    )(jnp.asarray(zonal_band()), part, *msgs)


def solution(mesh):
    placed = (P("member", "row", None), P("member", "row", None), P())
    return jax.shard_map(
        body, mesh=mesh, in_specs=placed, out_specs=P("member", "row", None), check_vma=False
    )
```

time: 95.8 us -> 32.5 us (0.34)
  blocking collectives: 60.7 us -> 0 us
  waiting for transfers between devices: 1.97 us -> 11.6 us
  local copies, waits for them, and re-layouts: 11.2 us -> 2.46 us
  other arithmetic: 8.24 us -> 1.04 us
  matrix products: 6.23 us -> 0 us
  Pallas kernels: 0 us -> 6.11 us
  starting transfers between devices: 5.63 us -> 11 us
    all_to_all x2 -> x0, blocking collectives: 60.7 us -> none  [the longest x1 31.1 us: body(): lax.all_to_all(zonal, 'row', split_axis=2, concat_axis=1, tiled=True)]
    ppermute x2 -> x5, waiting for transfers between devices: 1.97 us -> 11.6 us  [the longest x2 10.1 us: body(): msgs = [lax.ppermute(m, 'row', away) for m in msgs]]
    dot_general x6 -> x0, matrix products: 6.23 us -> none  [the longest x3 3.21 us: smooth_mid(): jnp.einsum('cbix,io->cbox', part, blocks[index], precision=lax.Precision....]
    pallas_call x0 -> x3, Pallas kernels: none -> 6.11 us  [the longest x1 2.74 us: body(): pl.pallas_call(raw_kernel, out_shape=[blocks] + [msg] * CHUNKS, in_specs=...]
    ppermute x2 -> x5, starting transfers between devices: 5.63 us -> 11 us  [the longest x2 5.68 us: body(): msgs = [lax.ppermute(m, 'row', away) for m in msgs]]
    reduce_sum x2 -> x0, other arithmetic: 3.3 us -> none  [the longest x1 2.69 us: body(): numer_y = jnp.sum(scaled * grad_y, axis=0)]
    all_to_all x4 -> x0, local copies, waits for them, and re-layouts: 3.18 us -> none  [the longest x2 1.74 us: body(): lax.all_to_all(smoothed, 'row', split_axis=1, concat_axis=2, tiled=True)]
    all_to_all x1 -> x0, other arithmetic: 3.15 us -> none  [body(): lax.all_to_all(zonal, 'row', split_axis=2, concat_axis=1, tiled=True)]
  transfers between devices with their start and end apart: 2 -> 5, of which waited for: 1 -> 3; matrix products, arithmetic and copies ran while one was open for 1% -> 0% of each run, Pallas kernels for 0% -> 2%
where the time goes in v1:
time: 32.5 us; the launch traced here: 32.3 us
  waiting for transfers between devices  11.6 us (36%)
  starting transfers between devices  11 us (34%)
  Pallas kernels  6.11 us (19%)
  local copies, waits for them, and re-layouts  2.46 us (8%)
  other arithmetic  1.04 us (3%)
    ppermute x2, waiting for transfers between devices, body(): msgs = [lax.ppermute(m, 'row', away) for m in msgs]  10.1 us
    ppermute x2, starting transfers between devices, body(): msgs = [lax.ppermute(m, 'row', away) for m in msgs]  5.68 us
    ppermute x1, starting transfers between devices, body(): edge_far = lax.ppermute(jnp.where(even, first, last), 'row', away)  3.71 us
    pallas_call x1, Pallas kernels, body(): pl.pallas_call(raw_kernel, out_shape=[blocks] + [msg] * CHUNKS, in_specs=...  2.74 us
    pallas_call x1, Pallas kernels, body(): pl.pallas_call(far_kernel, out_shape=jax.ShapeDtypeStruct((2, rows, width...  2.73 us
    unnamed x8, local copies, waits for them, and re-layouts  2.46 us
    ppermute x1, starting transfers between devices, body(): raw_near = lax.ppermute(raw, 'row', chip)  1.52 us
    ppermute x1, waiting for transfers between devices, body(): edge_far = lax.ppermute(jnp.where(even, first, last), 'row', away)  1.5 us
  transfers between devices with their start and end apart: 5, of which 3 were waited for; matrix products, arithmetic and copies ran while one was open for 0% of the time, Pallas kernels for 2%

profile of v1, /device:TPU:11, one launch (start us, length us, event | category | flops | bytes accessed | tf_op | source)
XLA Modules:
  0.0 32.3 jit_solution(16932028065998593926)
XLA Ops:
  0.0 1.0 %broadcast_select_fusion = (bf16[4,1,2048]{2,1,0:T(2,128)(2,1)S(1)}, bf16[4,1,2048]{2,1,0:T(2,128)(2,1)S(1)}) fusion(pred[]{:T(512)S(6)} %eq.3, bf16[4,64,2048]{2,1,0:T(8,128)(2,1)} %back_ref.1), kind=kLoop, calls=%fused_computation | loop fusion | flops 16384 | bytes 65537 | tf_op jit(solution)/shard_map/jit(_where)/select_n | solution.py:190
  1.0 0.0 copy-start.3
  1.1 3.7 %collective-permute-start.1 = (bf16[4,1,2048]{2,1,0:T(2,128)(2,1)S(1)}, bf16[4,1,2048]{2,1,0:T(2,128)(2,1)S(1)}, u32[]{:S(2)}, u32[]{:S(2)}) collective-permute-start(bf16[4,1,2048]{2,1,0:T(2,128)(2,1)S(1)} %get-tuple-element.11), channel_id=1, source_target_pairs={{1,2},{2,1},{3,4},{4,3},{5,6},{6,5},{7,8},{8,7},{9,10},{10,9},{11,... | collective-permute-start | bytes 49160 | tf_op jit(solution)/shard_map/ppermute | solution.py:190
  4.8 0.1 collective-permute-start
  4.9 1.5 %collective-permute-done.1.far_ref = bf16[4,1,2048]{2,1,0:T(2,128)(2,1)S(1)} collective-permute-done((bf16[4,1,2048]{2,1,0:T(2,128)(2,1)S(1)}, bf16[4,1,2048]{2,1,0:T(2,128)(2,1)S(1)}, u32[]{:S(2)}, u32[]{:S(2)}) %collective-permute-start.1) | collective-permute-done | bytes 16416 | tf_op jit(solution)/shard_map/ppermute | solution.py:190
  6.4 0.0 collective-permute-done.near_ref
  6.4 0.0 copy-done.3
  6.4 0.0 copy-start
  6.4 1.2 %copy-done = bf16[4,64,2048]{2,1,0:T(8,128)(2,1)S(1)} copy-done((bf16[4,64,2048]{2,1,0:T(8,128)(2,1)S(1)}, bf16[4,64,2048]{2,1,0:T(8,128)(2,1)}, u32[]{:S(2)}) %copy-start) | copy-done | bytes 1048600
  7.6 0.0 copy-start.1
  7.6 1.2 %copy-done.1 = bf16[4,64,2048]{2,1,0:T(8,128)(2,1)S(1)} copy-done((bf16[4,64,2048]{2,1,0:T(8,128)(2,1)S(1)}, bf16[4,64,2048]{2,1,0:T(8,128)(2,1)}, u32[]{:S(2)}) %copy-start.1) | copy-done | bytes 1048600
  8.8 2.7 %shard_map.46 = (f32[16,128,128]{2,1,0:T(8,128)S(1)}, bf16[1056,128]{1,0:T(8,128)(2,1)S(1)}, bf16[1056,128]{1,0:T(8,128)(2,1)S(1)}) custom-call(f32[4]{0:T(128)S(1)} %copy-done.3, bf16[4,64,2048]{2,1,0:T(8,128)(2,1)S(1)} %copy-done.1, bf16[4,64,2048]{2,1,0:T(8,128)(2,1)S(1)} %copy-done, bf16[4,1,2048]{2,1,0:T(2,128)(2,1)S(1)} %collective-permute-done.near_ref, ...), custom_call_target="tpu_custom_call" | custom-call | tf_op jit(solution)/shard_map/pallas_call | solution.py:194
  11.6 1.5 %collective-permute-start.2 = (f32[16,128,128]{2,1,0:T(8,128)S(1)}, f32[16,128,128]{2,1,0:T(8,128)S(1)}, u32[]{:S(2)}, u32[]{:S(2)}) collective-permute-start(f32[16,128,128]{2,1,0:T(8,128)S(1)} %get-tuple-element.8.raw_ref), channel_id=1, source_target_pairs={{0,1},{1,0},{2,3},{3,2},{4,5},{5,4},{6,7},{7,6},{8,9},{9,8},{10,11... | collective-permute-start | bytes 3145736 | tf_op jit(solution)/shard_map/ppermute | solution.py:202
  13.1 2.9 %collective-permute-start.3 = (bf16[1056,128]{1,0:T(8,128)(2,1)S(1)}, bf16[1056,128]{1,0:T(8,128)(2,1)S(1)}, u32[]{:S(2)}, u32[]{:S(2)}) collective-permute-start(bf16[1056,128]{1,0:T(8,128)(2,1)S(1)} %get-tuple-element.9), channel_id=1, source_target_pairs={{1,2},{2,1},{3,4},{4,3},{5,6},{6,5},{7,8},{8,7},{9,10},{10,9},{11,... | collective-permute-start | bytes 811016 | tf_op jit(solution)/shard_map/ppermute | solution.py:201
  15.9 0.0 copy-start.2
  16.0 2.8 %collective-permute-start.4 = (bf16[1056,128]{1,0:T(8,128)(2,1)S(1)}, bf16[1056,128]{1,0:T(8,128)(2,1)S(1)}, u32[]{:S(2)}, u32[]{:S(2)}) collective-permute-start(bf16[1056,128]{1,0:T(8,128)(2,1)S(1)} %get-tuple-element.10), channel_id=1, source_target_pairs={{1,2},{2,1},{3,4},{4,3},{5,6},{6,5},{7,8},{8,7},{9,10},{10,9},{11,... | collective-permute-start | bytes 811016 | tf_op jit(solution)/shard_map/ppermute | solution.py:201
  18.8 0.0 collective-permute-done.2.near_ref
  18.8 0.6 %shard_map.47.part_ref = f32[16,128,128]{2,1,0:T(8,128)S(1)} custom-call(f32[16,128,128]{2,1,0:T(8,128)S(1)} %get-tuple-element.8.raw_ref, f32[16,128,128]{2,1,0:T(8,128)S(1)} %collective-permute-done.2.near_ref), custom_call_target="tpu_custom_call" | custom-call | flops 1000000000 | bytes 3145728 | tf_op jit(solution)/shard_map/pallas_call | solution.py:203
  19.4 7.2 %collective-permute-done.3.refs_0_ = bf16[1056,128]{1,0:T(8,128)(2,1)S(1)} collective-permute-done((bf16[1056,128]{1,0:T(8,128)(2,1)S(1)}, bf16[1056,128]{1,0:T(8,128)(2,1)S(1)}, u32[]{:S(2)}, u32[]{:S(2)}) %collective-permute-start.3) | collective-permute-done | bytes 270368 | tf_op jit(solution)/shard_map/ppermute | solution.py:201
  26.6 2.9 %collective-permute-done.4.refs_1_ = bf16[1056,128]{1,0:T(8,128)(2,1)S(1)} collective-permute-done((bf16[1056,128]{1,0:T(8,128)(2,1)S(1)}, bf16[1056,128]{1,0:T(8,128)(2,1)S(1)}, u32[]{:S(2)}, u32[]{:S(2)}) %collective-permute-start.4) | collective-permute-done | bytes 270368 | tf_op jit(solution)/shard_map/ppermute | solution.py:201
  29.5 0.0 copy-done.2
  29.5 2.7 %shard_map.48 = f32[2,64,2048]{2,1,0:T(8,128)} custom-call(bf16[2,512,256]{2,1,0:T(8,128)(2,1)S(1)} %copy-done.2, f32[16,128,128]{2,1,0:T(8,128)S(1)} %shard_map.47.part_ref, bf16[1056,128]{1,0:T(8,128)(2,1)S(1)} %collective-permute-done.3.refs_0_, bf16[1056,128]{1,0:T(8,128)(2,1)S(1)} %collective-permute-done.4.refs_1_), custom_call_target="tpu_custom_call" | custom-call | tf_op jit(solution)/shard_map/pallas_call | solution.py:211
Async XLA Ops:
  1.0 5.3 %copy-start.3 = (f32[4]{0:T(128)S(1)}, f32[4]{0:T(128)}, u32[]{:S(2)}) copy-start(f32[4]{0:T(128)} %lw_ref.1) | copy-start | bytes 52
  1.1 5.3 %collective-permute-start.1 = (bf16[4,1,2048]{2,1,0:T(2,128)(2,1)S(1)}, bf16[4,1,2048]{2,1,0:T(2,128)(2,1)S(1)}, u32[]{:S(2)}, u32[]{:S(2)}) collective-permute-start(bf16[4,1,2048]{2,1,0:T(2,128)(2,1)S(1)} %get-tuple-element.11), channel_id=1, source_target_pairs={{1,2},{2,1},{3,4},{4,3},{5,6},{6,5},{7,8},{8,7},{9,10},{10,9},{11,... | collective-permute-start | bytes 49160 | tf_op jit(solution)/shard_map/ppermute | solution.py:190
  4.8 1.6 %collective-permute-start = (bf16[4,1,2048]{2,1,0:T(2,128)(2,1)S(1)}, bf16[4,1,2048]{2,1,0:T(2,128)(2,1)S(1)}, u32[]{:S(2)}, u32[]{:S(2)}) collective-permute-start(bf16[4,1,2048]{2,1,0:T(2,128)(2,1)S(1)} %get-tuple-element.12), channel_id=1, source_target_pairs={{0,1},{1,0},{2,3},{3,2},{4,5},{5,4},{6,7},{7,6},{8,9},{9,8},{10,11... | collective-permute-start | bytes 49160 | tf_op jit(solution)/shard_map/ppermute | solution.py:189
  6.4 1.2 %copy-start = (bf16[4,64,2048]{2,1,0:T(8,128)(2,1)S(1)}, bf16[4,64,2048]{2,1,0:T(8,128)(2,1)}, u32[]{:S(2)}) copy-start(bf16[4,64,2048]{2,1,0:T(8,128)(2,1)} %back_ref.1) | copy-start | bytes 3145732
  7.6 1.2 %copy-start.1 = (bf16[4,64,2048]{2,1,0:T(8,128)(2,1)S(1)}, bf16[4,64,2048]{2,1,0:T(8,128)(2,1)}, u32[]{:S(2)}) copy-start(bf16[4,64,2048]{2,1,0:T(8,128)(2,1)} %inno_ref.1) | copy-start | bytes 3145732
  11.6 7.2 %collective-permute-start.2 = (f32[16,128,128]{2,1,0:T(8,128)S(1)}, f32[16,128,128]{2,1,0:T(8,128)S(1)}, u32[]{:S(2)}, u32[]{:S(2)}) collective-permute-start(f32[16,128,128]{2,1,0:T(8,128)S(1)} %get-tuple-element.8.raw_ref), channel_id=1, source_target_pairs={{0,1},{1,0},{2,3},{3,2},{4,5},{5,4},{6,7},{7,6},{8,9},{9,8},{10,11... | collective-permute-start | bytes 3145736 | tf_op jit(solution)/shard_map/ppermute | solution.py:202
  13.1 13.6 %collective-permute-start.3 = (bf16[1056,128]{1,0:T(8,128)(2,1)S(1)}, bf16[1056,128]{1,0:T(8,128)(2,1)S(1)}, u32[]{:S(2)}, u32[]{:S(2)}) collective-permute-start(bf16[1056,128]{1,0:T(8,128)(2,1)S(1)} %get-tuple-element.9), channel_id=1, source_target_pairs={{1,2},{2,1},{3,4},{4,3},{5,6},{6,5},{7,8},{8,7},{9,10},{10,9},{11,... | collective-permute-start | bytes 811016 | tf_op jit(solution)/shard_map/ppermute | solution.py:201
  15.9 13.6 %copy-start.2 = (bf16[2,512,256]{2,1,0:T(8,128)(2,1)S(1)}, bf16[2,512,256]{2,1,0:T(8,128)(2,1)}, u32[]{:S(2)}) copy-start(bf16[2,512,256]{2,1,0:T(8,128)(2,1)} %constant.12.clone.band_ref) | copy-start | bytes 1572868
  16.0 13.6 %collective-permute-start.4 = (bf16[1056,128]{1,0:T(8,128)(2,1)S(1)}, bf16[1056,128]{1,0:T(8,128)(2,1)S(1)}, u32[]{:S(2)}, u32[]{:S(2)}) collective-permute-start(bf16[1056,128]{1,0:T(8,128)(2,1)S(1)} %get-tuple-element.10), channel_id=1, source_target_pairs={{1,2},{2,1},{3,4},{4,3},{5,6},{6,5},{7,8},{8,7},{9,10},{10,9},{11,... | collective-permute-start | bytes 811016 | tf_op jit(solution)/shard_map/ppermute | solution.py:201

commit v2 on v1

v2 whole, which is shorter than its diff:
```python
import math

import jax
import jax.numpy as jnp
import numpy as np
from jax import lax
from jax.experimental import pallas as pl
from jax.experimental.pallas import tpu as pltpu
from jax.sharding import PartitionSpec as P

HALF = 64
SIGMA = 64
LANES = 128
GROUP_Y = 4
GROUP_X = 8
SPAN = LANES * GROUP_X
TILE = 16
QUARTERS = 4
F32 = jnp.float32
BF16 = jnp.bfloat16
NORM = math.sqrt(sum(math.exp(-k * k / (SIGMA * SIGMA)) for k in range(-HALF, HALF + 1)))

VMEM = pl.BlockSpec(memory_space=pltpu.VMEM)
SMEM = pl.BlockSpec(memory_space=pltpu.SMEM)
ANY = pl.BlockSpec(memory_space=pl.ANY)
PARAMS = pltpu.CompilerParams(vmem_limit_bytes=40 * 1024 * 1024)


def split(values):
    high = values.astype(BF16)
    return high, (values - high.astype(F32)).astype(BF16)


def dot(left, right):
    return jnp.dot(left, right, preferred_element_type=F32)


def iota(shape, dim):
    return lax.broadcasted_iota(jnp.int32, shape, dim)


def one_hot(mask, value=1.0):
    return jnp.where(mask, value, 0.0).astype(BF16)


def taps(offset):
    off = offset.astype(F32)
    value = jnp.exp(off * off * (-0.5 / (SIGMA * SIGMA))) * (1.0 / NORM)
    return jnp.where(jnp.abs(offset) <= HALF, value, 0.0)


def zonal_band():
    offset = np.arange(4 * LANES)[:, None] - LANES - np.arange(2 * LANES)[None, :]
    band = np.exp(-offset * offset / (2.0 * SIGMA * SIGMA)) / NORM
    band = np.where(np.abs(offset) <= HALF, band, 0.0).astype(np.float32)
    high = band.astype(BF16)
    return np.stack([high, (band - high.astype(np.float32)).astype(BF16)])


def window(first, nblocks):
    low, high = max(first - 1, 0), min(first + 3, nblocks)
    return low, high, (low - first + 1) * LANES, (high - first + 1) * LANES


def parity():
    return lax.rem(lax.axis_index("row"), 2)


def message_rows(rows, nblocks, with_edge):
    spans = -(-nblocks * LANES // SPAN)
    return nblocks * rows + spans * (rows // GROUP_Y) + (nblocks * TILE if with_edge else 0)


def raw_half(upper, lw_ref, inno_hbm, back_hbm, inno_buf, back_buf, sems, raw_ref, msgs, cut, edge, extra):
    levels, half, width = inno_buf.shape
    rows, deep = 2 * half, half + TILE
    nblocks = width // LANES
    start = jnp.where(upper, 0, half)
    from_row = jnp.where(upper, 0, rows - deep)
    part = width // QUARTERS
    copies = []
    for q in range(QUARTERS):
        cols = pl.ds(q * part, part)
        copies.append(
            [
                pltpu.make_async_copy(
                    back_hbm.at[:, pl.ds(pl.multiple_of(from_row, TILE), deep), cols],
                    back_buf.at[:, :, cols],
                    sems.at[0, q],
                ),
                pltpu.make_async_copy(
                    inno_hbm.at[:, pl.ds(pl.multiple_of(start, TILE), half), cols],
                    inno_buf.at[:, :, cols],
                    sems.at[1, q],
                ),
            ]
        )
    for pair in copies:
        for copy in pair:
            copy.start()
    off = iota((half, deep), 1) - iota((half, deep), 0) + jnp.where(upper, 0, half - deep)
    diff_y = (jnp.where(off == 1, 1.0, 0.0) - jnp.where(off == -1, 1.0, 0.0)).astype(BF16)
    off = iota((4 * LANES, 2 * LANES), 0) - LANES - iota((4 * LANES, 2 * LANES), 1)
    diff_x = (jnp.where(off == 1, 1.0, 0.0) - jnp.where(off == -1, 1.0, 0.0)).astype(BF16)
    shape = (SPAN, LANES)
    sum_x = one_hot(iota(shape, 0) // GROUP_X == iota(shape, 1))
    shape = (rows // GROUP_Y, rows)
    sum_y = one_hot(iota(shape, 1) // GROUP_Y == iota(shape, 0))
    keep = iota((half, 2 * LANES), 0) != cut
    inner = half // TILE * TILE - (deep - half)
    waited = 0
    block = 0
    for msg_ref, per, with_edge in msgs:
        base = per * rows
        spans = -(-per * LANES // SPAN)
        total = None
        for k in range(0, per, 2):
            first = block + k
            low, high, top, bottom = window(first, nblocks)
            while waited * part < high * LANES:
                for copy in copies[waited]:
                    copy.wait()
                waited += 1
            here = pl.ds(first * LANES, 2 * LANES)
            around = back_buf[:, :, low * LANES : high * LANES]
            around = jnp.where(upper, around[:, :half], around[:, deep - half :])
            grad_xs = dot(around.reshape(levels * half, -1), diff_x[top:bottom])
            numer_y = numer_x = 0.0
            denom = 1.0
            for level in range(levels):
                weight = lw_ref[level]
                grad_y = dot(diff_y, back_buf[level, :, here])
                if extra is not None:
                    grad_y += extra(level, here)
                grad_x = grad_xs[level * half : (level + 1) * half]
                scaled = inno_buf[level, :, here].astype(F32) * (0.5 * weight)
                numer_y += scaled * grad_y
                numer_x += scaled * grad_x
                denom += (0.25 * weight) * (grad_y * grad_y + grad_x * grad_x)
            inverse = 1.0 / denom
            lows = []
            for comp, numer in enumerate((numer_y, numer_x)):
                raw = jnp.where(keep, numer * inverse, 0.0) if with_edge else numer * inverse
                upto, rest = split(raw)
                lows.append(rest)
                for j in range(2):
                    cols = slice(j * LANES, (j + 1) * LANES)
                    raw_ref[first + j, pl.ds(pl.multiple_of(comp * rows + start, 8), half), :] = raw[:, cols]
                    msg_ref[pl.ds((k + j) * rows + comp * half, half), :] = upto[:, cols]
            place = k * LANES % SPAN
            part_sum = dot(jnp.concatenate(lows, axis=0), sum_x[place : place + 2 * LANES])
            total = part_sum if place == 0 else total + part_sum
            if place + 2 * LANES == SPAN or k + 2 == per:
                at = base + k * LANES // SPAN * (rows // GROUP_Y)
                msg_ref[pl.ds(at, rows // GROUP_Y), :] = dot(sum_y, total.astype(BF16)).astype(BF16)
            if with_edge:
                tile = edge(here)
                for j in range(2):
                    at = base + spans * (rows // GROUP_Y) + (k + j) * TILE
                    msg_ref[pl.ds(at, TILE), :] = tile[:, j * LANES : (j + 1) * LANES]
        block += per


def outer_kernel(lw_ref, inno_hbm, back_hbm, raw_ref, msg_ref, inno_buf, back_buf, sems):
    levels, half, width = inno_buf.shape
    deep = half + TILE
    par = parity()
    upper = par == 0
    shape = (TILE, levels * TILE)
    kind, level = iota(shape, 0) // levels, iota(shape, 0) % levels
    at = iota(shape, 1) - level * TILE
    outermost = jnp.where(upper, 0, TILE - 1)
    next_row = jnp.where(upper, 1, TILE - 2)
    of_back = one_hot(((kind == 0) & (at == outermost)) | ((kind == 1) & (at == next_row)))
    of_inno = one_hot((kind == 2) & (at == outermost))

    def edge(here):
        back = jnp.where(upper, back_buf[:, :TILE, here], back_buf[:, deep - TILE :, here])
        inno = jnp.where(upper, inno_buf[:, :TILE, here], inno_buf[:, half - TILE :, here])
        tile = dot(of_back, back.reshape(levels * TILE, -1)) + dot(of_inno, inno.reshape(levels * TILE, -1))
        return tile.astype(BF16)

    cut = jnp.where(upper, 0, half - 1)
    msgs = [(msg_ref, width // LANES, True)]
    raw_half(upper, lw_ref, inno_hbm, back_hbm, inno_buf, back_buf, sems, raw_ref, msgs, cut, edge, None)


def edge_kernel(back_hbm, raw_hbm, out_ref, buf, sem):
    levels, _, _ = buf.shape
    rows = back_hbm.shape[1]
    upper = parity() == 1
    at = pl.multiple_of(jnp.where(upper, 0, rows - TILE), TILE)
    copy = pltpu.make_async_copy(back_hbm.at[:, pl.ds(at, TILE), :], buf, sem)
    copy.start()
    shape = (TILE, levels * TILE)
    row = jnp.where(upper, 0, TILE - 1)
    pick = one_hot(iota(shape, 1) == iota(shape, 0) * TILE + row)
    copy.wait()
    out_ref[...] = dot(pick, buf[...].reshape(levels * TILE, -1)).astype(BF16)


def inner_kernel(lw_ref, inno_hbm, back_hbm, row_ref, raw_in, raw_ref, *refs):
    *msg_refs, inno_buf, back_buf, sems = refs
    levels, half, width = inno_buf.shape
    upper = parity() == 1
    at = iota((half, 2 * LANES), 0) == jnp.where(upper, 0, half - 1)
    sign = jnp.where(upper, -1.0, 1.0)

    def extra(level, here):
        return jnp.where(at, row_ref[level : level + 1, here].astype(F32) * sign, 0.0)

    msgs = [(ref, ref.shape[0] // (2 * half), False) for ref in msg_refs]
    raw_half(upper, lw_ref, inno_hbm, back_hbm, inno_buf, back_buf, sems, raw_ref, msgs, -1, None, extra)


def far_row_kernel(lw_ref, own_ref, got_ref, raw_in, raw_ref, far_ref):
    nblocks, both, _ = raw_ref.shape
    rows = both // 2
    levels = lw_ref.shape[0]
    base = own_ref.shape[0] - nblocks * TILE
    sign = jnp.where(parity() == 0, -1.0, 1.0)
    own = jnp.concatenate([own_ref[pl.ds(base + k * TILE, TILE), :] for k in range(nblocks)], axis=1)
    got = jnp.concatenate([got_ref[pl.ds(base + k * TILE, TILE), :] for k in range(nblocks)], axis=1)
    own, got = own.astype(F32), got.astype(F32)
    lane = iota((levels, nblocks * LANES), 1)

    def raw_row(mine, beyond, sign):
        here = mine[:levels]
        grad_y = (beyond[:levels] - mine[levels : 2 * levels]) * sign
        left = jnp.where(lane == 0, 0.0, pltpu.roll(here, 1, 1))
        right = jnp.where(lane == nblocks * LANES - 1, 0.0, pltpu.roll(here, nblocks * LANES - 1, 1))
        grad_x = right - left
        inno = mine[2 * levels : 3 * levels]
        numer_y = numer_x = 0.0
        denom = 1.0
        for level in range(levels):
            weight = lw_ref[level]
            one = slice(level, level + 1)
            scaled = inno[one] * (0.5 * weight)
            numer_y += scaled * grad_y[one]
            numer_x += scaled * grad_x[one]
            denom += (0.25 * weight) * (grad_y[one] * grad_y[one] + grad_x[one] * grad_x[one])
        return numer_y / denom, numer_x / denom

    first = parity() == 0
    for comp, row in enumerate(raw_row(own, got, sign)):
        for k in range(nblocks):
            for y, here in ((0, first), (rows - 1, jnp.logical_not(first))):
                at = pl.ds(comp * rows + y, 1)
                raw_ref[k, at, :] = jnp.where(here, row[:, k * LANES : (k + 1) * LANES], raw_ref[k, at, :])
    for comp, row in enumerate(raw_row(got, own, -sign)):
        far_ref[comp : comp + 1, :] = row


def far_taps(rows, part):
    side = 2 * parity() - 1
    half = rows // 2
    start = jnp.where(part == 0, jnp.where(side < 0, half, 0), jnp.where(side < 0, 0, half))
    return taps(iota((rows, half), 1) + start - iota((rows, half), 0) + side * rows)


def spread_rest(values, msg_ref, nblocks):
    rows = values.shape[0]
    half = rows // 2
    shape = (half, half // GROUP_Y)
    mean_y = one_hot(iota(shape, 0) // GROUP_Y == iota(shape, 1), 1.0 / GROUP_Y)
    group_taps = dot(values.astype(BF16), mean_y).astype(BF16)
    spans = -(-nblocks * LANES // SPAN)
    found = []
    for span in range(spans):
        at = nblocks * rows + span * (rows // GROUP_Y)
        tile = msg_ref[pl.ds(at, rows // GROUP_Y), :]
        groups = half // GROUP_Y
        found.append(jnp.concatenate([dot(group_taps, tile[:groups]), dot(group_taps, tile[groups:])], axis=0).astype(BF16))
    return found


def mean_over_x():
    shape = (LANES, SPAN)
    return one_hot(iota(shape, 1) // GROUP_X == iota(shape, 0), 1.0 / GROUP_X)


def far_part(two, rest, mean_x, msg_ref, k, rows):
    half = rows // 2
    place = k * LANES % SPAN
    spread = dot(rest[k * LANES // SPAN], mean_x[:, place : place + 2 * LANES])
    parts = []
    for comp in range(2):
        got = [msg_ref[pl.ds((k + j) * rows + comp * half, half), :] for j in range(2)]
        part = dot(two, jnp.concatenate(got, axis=1))
        parts.append(part[:rows] + part[rows:] + spread[comp * rows : (comp + 1) * rows])
    return parts


def near_kernel(raw_ref, near_ref, far_ref, msg_ref, out_ref):
    nblocks, both, _ = raw_ref.shape
    rows = both // 2
    par = parity()
    side = 1 - 2 * par
    offset = iota((rows, rows), 1) - iota((rows, rows), 0)
    high, low = split(jnp.concatenate([taps(offset), taps(offset + side * rows)], axis=1))
    two = jnp.concatenate([high, low], axis=0)
    values = far_taps(rows, 0)
    two_far = jnp.concatenate(split(values), axis=0)
    rest = spread_rest(values, msg_ref, nblocks)
    mean_x = mean_over_x()
    column = iota((rows, 2 * LANES), 0)
    edge_taps = taps(jnp.where(par == 0, -1, rows) - column)
    for first in range(0, nblocks, 2):
        added = far_part(two_far, rest, mean_x, msg_ref, first, rows)
        for comp in range(2):
            here = pl.ds(comp * rows, rows)
            pairs = []
            for k in (first, first + 1):
                pairs.append(jnp.concatenate([raw_ref[k, here, :], near_ref[k, here, :]], axis=0))
            high_x, low_x = split(jnp.concatenate(pairs, axis=1))
            part = dot(two, high_x)
            part = part[:rows] + part[rows:] + dot(high, low_x) + added[comp]
            part += edge_taps * far_ref[comp : comp + 1, pl.ds(first * LANES, 2 * LANES)]
            for j in range(2):
                out_ref[first + j, here, :] = part[:, j * LANES : (j + 1) * LANES]


def finish(band_ref, part_ref, msg_ref, total_ref, out_hbm, high_ref, low_ref, buf, sem, begin, per, firsts):
    nblocks, both, _ = part_ref.shape
    rows = both // 2
    values = far_taps(rows, 1)
    two = jnp.concatenate(split(values), axis=0)
    rest = spread_rest(values, msg_ref, per)
    mean_x = mean_over_x()
    for k in range(begin - 3 if begin else 0, begin):
        high_ref[k], low_ref[k] = split(part_ref[k])
    copies = []
    ready = begin
    for first in firsts:
        low, high, top, bottom = window(first, nblocks)
        while ready < high:
            added = far_part(two, rest, mean_x, msg_ref, ready - begin, rows)
            for comp in range(2):
                here = pl.ds(comp * rows, rows)
                for j in range(2):
                    total = part_ref[ready + j, here, :] + added[comp][:, j * LANES : (j + 1) * LANES]
                    if total_ref is not None and ready + j >= begin + per - 3:
                        total_ref[ready + j, here, :] = total
                    high_ref[ready + j, here, :], low_ref[ready + j, here, :] = split(total)
            ready += 2
        upper = jnp.concatenate([high_ref[k] for k in range(low, high)], axis=1)
        lower = jnp.concatenate([low_ref[k] for k in range(low, high)], axis=1)
        band = band_ref[0, top:bottom, :]
        result = dot(upper, band) + dot(lower, band) + dot(upper, band_ref[1, top:bottom, :])
        here = pl.ds(first * LANES, 2 * LANES)
        buf[0, :, here] = result[:rows]
        buf[1, :, here] = result[rows:]
        copy = pltpu.make_async_copy(buf.at[:, :, here], out_hbm.at[:, :, here], sem.at[first // 2])
        copy.start()
        copies.append(copy)
    for copy in copies:
        copy.wait()


def first_kernel(band_ref, part_ref, msg_ref, out_hbm, total_ref, high_ref, low_ref, buf, sem):
    per = msg_ref.shape[0] // part_ref.shape[1] * 2
    per = blocks_of(msg_ref.shape[0], part_ref.shape[1] // 2)
    firsts = range(0, per - 2, 2)
    finish(band_ref, part_ref, msg_ref, total_ref, out_hbm, high_ref, low_ref, buf, sem, 0, per, firsts)


def last_kernel(band_ref, part_ref, msg_ref, out_in, out_hbm, high_ref, low_ref, buf, sem):
    nblocks = part_ref.shape[0]
    per = blocks_of(msg_ref.shape[0], part_ref.shape[1] // 2)
    begin = nblocks - per
    firsts = range(begin - 2, nblocks, 2)
    finish(band_ref, part_ref, msg_ref, None, out_hbm, high_ref, low_ref, buf, sem, begin, per, firsts)


def blocks_of(size, rows):
    return next(k for k in range(2, size, 2) if message_rows(rows, k, False) == size)


def body(innovation, background, level_weight):
    levels, rows, width = innovation.shape
    if rows != HALF or width % (4 * SPAN // 2) or 3 * levels > TILE:
        raise NotImplementedError("slab shape")
    nblocks = width // LANES
    both, half = 2 * rows, rows // 2
    count = lax.axis_size("row")
    chip = [(i, i ^ 1) for i in range(count) if i ^ 1 < count]
    away = [(i, j) for i in range(count) for j in [((i + 1) ^ 1) - 1] if 0 <= j < count]
    blocks = jax.ShapeDtypeStruct((nblocks, both, LANES), F32)
    per = nblocks * 5 // 16 * 2
    pers = [per, nblocks - per]

    def message(nblocks, with_edge):
        return jax.ShapeDtypeStruct((message_rows(rows, nblocks, with_edge), LANES), BF16)

    scratch = [
        pltpu.VMEM((levels, half, width), BF16),
        pltpu.VMEM((levels, half + TILE, width), BF16),
        pltpu.SemaphoreType.DMA((2, QUARTERS)),
    ]
    raw, outer = pl.pallas_call(
        outer_kernel,
        out_shape=[blocks, message(nblocks, True)],
        in_specs=[SMEM, ANY, ANY],
        out_specs=[VMEM, VMEM],
        scratch_shapes=scratch,
        compiler_params=PARAMS,
        name="outer_half",
    )(level_weight, innovation, background)
    outer_got = lax.ppermute(outer, "row", away)
    edge = pl.pallas_call(
        edge_kernel,
        out_shape=jax.ShapeDtypeStruct((TILE, width), BF16),
        in_specs=[ANY, ANY],
        out_specs=VMEM,
        scratch_shapes=[pltpu.VMEM((levels, TILE, width), BF16), pltpu.SemaphoreType.DMA],
        compiler_params=PARAMS,
        name="edge_row",
    )(background, raw)
    edge = lax.ppermute(edge, "row", chip)
    raw, *msgs = pl.pallas_call(
        inner_kernel,
        out_shape=[blocks] + [message(k, False) for k in pers],
        in_specs=[SMEM, ANY, ANY, VMEM, VMEM],
        out_specs=[VMEM] * 3,
        scratch_shapes=scratch,
        input_output_aliases={4: 0},
        compiler_params=PARAMS,
        name="inner_half",
    )(level_weight, innovation, background, edge, raw)
    msgs = [lax.ppermute(m, "row", away) for m in msgs]
    raw, far = pl.pallas_call(
        far_row_kernel,
        out_shape=[blocks, jax.ShapeDtypeStruct((8, width), F32)],
        in_specs=[SMEM] + [VMEM] * 3,
        out_specs=[VMEM] * 2,
        input_output_aliases={3: 0},
        compiler_params=PARAMS,
        name="far_row",
    )(level_weight, outer, outer_got, raw)
    near = lax.ppermute(raw, "row", chip)
    part = pl.pallas_call(
        near_kernel,
        out_shape=blocks,
        in_specs=[VMEM] * 4,
        out_specs=VMEM,
        compiler_params=PARAMS,
        name="near_part",
    )(raw, near, far, outer_got)
    band = jnp.asarray(zonal_band())
    scratch = [
        pltpu.VMEM((nblocks, both, LANES), BF16),
        pltpu.VMEM((nblocks, both, LANES), BF16),
        pltpu.VMEM((2, rows, width), F32),
        pltpu.SemaphoreType.DMA((nblocks // 2,)),
    ]
    result = jax.ShapeDtypeStruct((2, rows, width), F32)
    out, part = pl.pallas_call(
        first_kernel,
        out_shape=[result, blocks],
        in_specs=[VMEM] * 3,
        out_specs=[ANY, VMEM],
        scratch_shapes=scratch,
        input_output_aliases={1: 1},
        compiler_params=PARAMS,
        name="first_columns",
    )(band, part, msgs[0])
    return pl.pallas_call(
        last_kernel,
        out_shape=result,
        in_specs=[VMEM] * 3 + [ANY],
        out_specs=ANY,
        scratch_shapes=scratch,
        input_output_aliases={3: 0},
        compiler_params=PARAMS,
        name="last_columns",
    )(band, part, msgs[1], out)


def solution(mesh):
    placed = (P("member", "row", None), P("member", "row", None), P())
    return jax.shard_map(
        body, mesh=mesh, in_specs=placed, out_specs=P("member", "row", None), check_vma=False
    )
```

time: 32.5 us -> 32.2 us (level)
  Pallas kernels: 6.11 us -> 12.7 us
  waiting for transfers between devices: 11.6 us -> 6.72 us
  starting transfers between devices: 11 us -> 9.41 us
  other arithmetic: 1.04 us -> 0 us
  local copies, waits for them, and re-layouts: 2.46 us -> 3.11 us
    ppermute x2, waiting for transfers between devices: 10.1 us -> 1.88 us  [body(): msgs = [lax.ppermute(m, 'row', away) for m in msgs]]
    pallas_call x3 -> x7, Pallas kernels: 6.11 us -> 12.7 us  [the longest x1 3.28 us: body(): pl.pallas_call(inner_kernel, out_shape=[blocks] + [message(k, False) for...]
    ppermute x3, waiting for transfers between devices: 1.51 us -> 4.84 us  [the longest x1 3.6 us: body(): outer_got = lax.ppermute(outer, 'row', away)]
    ppermute x3, starting transfers between devices: 5.3 us -> 3.85 us  [the longest x1 3.71 us: body(): outer_got = lax.ppermute(outer, 'row', away)]
    select_n x1 -> x0, other arithmetic: 1.04 us -> none  [body(): edge_far = lax.ppermute(jnp.where(even, first, last), 'row', away)]
    unnamed x8 -> x10, local copies, waits for them, and re-layouts: 2.46 us -> 3.11 us
  transfers between devices with their start and end apart: 5 -> 5, of which waited for: 3 -> 4; matrix products, arithmetic and copies ran while one was open for 0% -> 0% of each run, Pallas kernels for 2% -> 21%
where the time goes in v2:
time: 32.2 us; the launch traced here: 32 us
  Pallas kernels  12.7 us (39%)
  starting transfers between devices  9.41 us (29%)
  waiting for transfers between devices  6.72 us (21%)
  local copies, waits for them, and re-layouts  3.11 us (10%)
    ppermute x2, starting transfers between devices, body(): msgs = [lax.ppermute(m, 'row', away) for m in msgs]  5.56 us
    ppermute x1, starting transfers between devices, body(): outer_got = lax.ppermute(outer, 'row', away)  3.71 us
    ppermute x1, waiting for transfers between devices, body(): outer_got = lax.ppermute(outer, 'row', away)  3.6 us
    pallas_call x1, Pallas kernels, body(): pl.pallas_call(inner_kernel, out_shape=[blocks] + [message(k, False) for...  3.28 us
    pallas_call x1, Pallas kernels, body(): pl.pallas_call(outer_kernel, out_shape=[blocks, message(nblocks, True)],...  3.19 us
    unnamed x10, local copies, waits for them, and re-layouts  3.11 us
    pallas_call x1, Pallas kernels, body(): pl.pallas_call(first_kernel, out_shape=[result, blocks], in_specs=[VMEM]...  2.03 us
    pallas_call x1, Pallas kernels, body(): pl.pallas_call(last_kernel, out_shape=result, in_specs=[VMEM] * 3 + [ANY]...  1.9 us
  transfers between devices with their start and end apart: 5, of which 4 were waited for; matrix products, arithmetic and copies ran while one was open for 0% of the time, Pallas kernels for 21%

profile of v2, /device:TPU:11, one launch (start us, length us, event | category | flops | bytes accessed | tf_op | source)
XLA Modules:
  0.0 32.0 jit_solution(11013033934158088643)
XLA Ops:
  0.0 0.0 copy-start
  0.0 1.2 %copy-done = bf16[4,64,2048]{2,1,0:T(8,128)(2,1)S(1)} copy-done((bf16[4,64,2048]{2,1,0:T(8,128)(2,1)S(1)}, bf16[4,64,2048]{2,1,0:T(8,128)(2,1)}, u32[]{:S(2)}) %copy-start) | copy-done | bytes 1048600
  1.2 0.0 copy-start.2
  1.2 1.2 %copy-done.2 = bf16[4,64,2048]{2,1,0:T(8,128)(2,1)S(1)} copy-done((bf16[4,64,2048]{2,1,0:T(8,128)(2,1)S(1)}, bf16[4,64,2048]{2,1,0:T(8,128)(2,1)}, u32[]{:S(2)}) %copy-start.2) | copy-done | bytes 1048600
  2.5 0.0 copy-start.4
  2.5 0.7 %copy-done.4 = f32[4]{0:T(128)S(1)} copy-done((f32[4]{0:T(128)S(1)}, f32[4]{0:T(128)}, u32[]{:S(2)}) %copy-start.4) | copy-done | bytes 40
  3.1 0.0 copy-start.1
  3.1 3.2 %outer_half.1 = (f32[16,128,128]{2,1,0:T(8,128)S(1)}, bf16[1312,128]{1,0:T(8,128)(2,1)S(1)}) custom-call(f32[4]{0:T(128)S(1)} %copy-done.4, bf16[4,64,2048]{2,1,0:T(8,128)(2,1)S(1)} %copy-done.2, bf16[4,64,2048]{2,1,0:T(8,128)(2,1)S(1)} %copy-done), custom_call_target="tpu_custom_call" | custom-call | tf_op jit(solution)/shard_map/outer_half/pallas_call | solution.py:401
  6.3 3.7 %collective-permute-start = (bf16[1312,128]{1,0:T(8,128)(2,1)S(1)}, bf16[1312,128]{1,0:T(8,128)(2,1)S(1)}, u32[]{:S(2)}, u32[]{:S(2)}) collective-permute-start(bf16[1312,128]{1,0:T(8,128)(2,1)S(1)} %get-tuple-element.14.own_ref), channel_id=1, source_target_pairs={{1,2},{2,1},{3,4},{4,3},{5,6},{6,5},{7,8},{8,7},{9,10},{10,9},{11,... | collective-permute-start | bytes 1007624 | tf_op jit(solution)/shard_map/ppermute | solution.py:410
  10.0 0.0 copy-done.1
  10.0 0.2 edge_row.1
  10.2 0.1 collective-permute-start.1
  10.3 1.2 %collective-permute-done.1.row_ref = bf16[16,2048]{1,0:T(8,128)(2,1)S(1)} collective-permute-done((bf16[16,2048]{1,0:T(8,128)(2,1)S(1)}, bf16[16,2048]{1,0:T(8,128)(2,1)S(1)}, u32[]{:S(2)}, u32[]{:S(2)}) %collective-permute-start.1) | collective-permute-done | bytes 65568 | tf_op jit(solution)/shard_map/ppermute | solution.py:420
  11.6 3.3 %inner_half.1 = (f32[16,128,128]{2,1,0:T(8,128)S(1)}, bf16[672,128]{1,0:T(8,128)(2,1)S(1)}, bf16[400,128]{1,0:T(8,128)(2,1)S(1)}) custom-call(f32[4]{0:T(128)S(1)} %copy-done.4, bf16[4,64,2048]{2,1,0:T(8,128)(2,1)S(1)} %copy-done.2, bf16[4,64,2048]{2,1,0:T(8,128)(2,1)S(1)} %copy-done.1, ...), custom_call_target="tpu_custom_call", output_to_operand_aliasing={{0}: (4, {})} | custom-call | tf_op jit(solution)/shard_map/inner_half/pallas_call | solution.py:421
  14.9 3.6 %collective-permute-done.got_ref.msg_ref = bf16[1312,128]{1,0:T(8,128)(2,1)S(1)} collective-permute-done((bf16[1312,128]{1,0:T(8,128)(2,1)S(1)}, bf16[1312,128]{1,0:T(8,128)(2,1)S(1)}, u32[]{:S(2)}, u32[]{:S(2)}) %collective-permute-start) | collective-permute-done | bytes 335904 | tf_op jit(solution)/shard_map/ppermute | solution.py:410
  18.5 0.8 %far_row.1 = (f32[16,128,128]{2,1,0:T(8,128)S(1)}, f32[8,2048]{1,0:T(8,128)S(1)}) custom-call(f32[4]{0:T(128)S(1)} %copy-done.4, bf16[1312,128]{1,0:T(8,128)(2,1)S(1)} %get-tuple-element.14.own_ref, bf16[1312,128]{1,0:T(8,128)(2,1)S(1)} %collective-permute-done.got_ref.msg_ref, ...), custom_call_target="tpu_custom_call", output_to_operand_aliasing={{0}: (3, {})} | custom-call | tf_op jit(solution)/shard_map/far_row/pallas_call | solution.py:432
  19.3 0.1 collective-permute-start.2
  19.3 3.6 %collective-permute-start.3 = (bf16[672,128]{1,0:T(8,128)(2,1)S(1)}, bf16[672,128]{1,0:T(8,128)(2,1)S(1)}, u32[]{:S(2)}, u32[]{:S(2)}) collective-permute-start(bf16[672,128]{1,0:T(8,128)(2,1)S(1)} %get-tuple-element.19), channel_id=1, source_target_pairs={{1,2},{2,1},{3,4},{4,3},{5,6},{6,5},{7,8},{8,7},{9,10},{10,9},{11,... | collective-permute-start | bytes 516104 | tf_op jit(solution)/shard_map/ppermute | solution.py:431
  23.0 1.9 %collective-permute-start.4 = (bf16[400,128]{1,0:T(8,128)(2,1)S(1)}, bf16[400,128]{1,0:T(8,128)(2,1)S(1)}, u32[]{:S(2)}, u32[]{:S(2)}) collective-permute-start(bf16[400,128]{1,0:T(8,128)(2,1)S(1)} %get-tuple-element.21), channel_id=1, source_target_pairs={{1,2},{2,1},{3,4},{4,3},{5,6},{6,5},{7,8},{8,7},{9,10},{10,9},{11,... | collective-permute-start | bytes 307208 | tf_op jit(solution)/shard_map/ppermute | solution.py:431
  24.9 0.0 collective-permute-done.2.near_ref
  24.9 0.0 copy-start.3
  24.9 1.2 %near_part.1.part_ref = f32[16,128,128]{2,1,0:T(8,128)S(1)} custom-call(f32[16,128,128]{2,1,0:T(8,128)S(1)} %get-tuple-element.17.raw_ref, f32[16,128,128]{2,1,0:T(8,128)S(1)} %collective-permute-done.2.near_ref, f32[8,2048]{1,0:T(8,128)S(1)} %get-tuple-element.18.far_ref, bf16[1312,128]{1,0:T(8,128)(2,1)S(1)} %collective-permute-done.got_ref.msg_ref), custom_call_target="tpu_custom_call" | custom-call | tf_op jit(solution)/shard_map/near_part/pallas_call | solution.py:442
  26.2 1.7 %collective-permute-done.3.msg_ref = bf16[672,128]{1,0:T(8,128)(2,1)S(1)} collective-permute-done((bf16[672,128]{1,0:T(8,128)(2,1)S(1)}, bf16[672,128]{1,0:T(8,128)(2,1)S(1)}, u32[]{:S(2)}, u32[]{:S(2)}) %collective-permute-start.3) | collective-permute-done | bytes 172064 | tf_op jit(solution)/shard_map/ppermute | solution.py:431
  27.9 0.0 copy-done.3
  27.9 2.0 %first_columns.1 = (f32[2,64,2048]{2,1,0:T(8,128)}, f32[16,128,128]{2,1,0:T(8,128)S(1)}) custom-call(bf16[2,512,256]{2,1,0:T(8,128)(2,1)S(1)} %copy-done.3, f32[16,128,128]{2,1,0:T(8,128)S(1)} %near_part.1.part_ref, bf16[672,128]{1,0:T(8,128)(2,1)S(1)} %collective-permute-done.3.msg_ref), custom_call_target="tpu_custom_call", output_to_operand_aliasing={{1}: (1, {})} | custom-call | tf_op jit(solution)/shard_map/first_columns/pallas_call | solution.py:458
  30.0 0.2 collective-permute-done.4.msg_ref
  30.1 1.9 %last_columns.1 = f32[2,64,2048]{2,1,0:T(8,128)} custom-call(bf16[2,512,256]{2,1,0:T(8,128)(2,1)S(1)} %copy-done.3, f32[16,128,128]{2,1,0:T(8,128)S(1)} %get-tuple-element.20.part_ref, bf16[400,128]{1,0:T(8,128)(2,1)S(1)} %collective-permute-done.4.msg_ref, f32[2,64,2048]{2,1,0:T(8,128)} %get-tuple-element.22.out_in), custom_call_target="tpu_custom_call", output_to_operand_aliasing={{}: (3, {})} | custom-call | tf_op jit(solution)/shard_map/last_columns/pallas_call | solution.py:468
Async XLA Ops:
  0.0 1.2 %copy-start = (bf16[4,64,2048]{2,1,0:T(8,128)(2,1)S(1)}, bf16[4,64,2048]{2,1,0:T(8,128)(2,1)}, u32[]{:S(2)}) copy-start(bf16[4,64,2048]{2,1,0:T(8,128)(2,1)} %back_hbm.5) | copy-start | bytes 3145732
  1.2 1.2 %copy-start.2 = (bf16[4,64,2048]{2,1,0:T(8,128)(2,1)S(1)}, bf16[4,64,2048]{2,1,0:T(8,128)(2,1)}, u32[]{:S(2)}) copy-start(bf16[4,64,2048]{2,1,0:T(8,128)(2,1)} %inno_hbm.3) | copy-start | bytes 3145732
  2.5 0.7 %copy-start.4 = (f32[4]{0:T(128)S(1)}, f32[4]{0:T(128)}, u32[]{:S(2)}) copy-start(f32[4]{0:T(128)} %lw_ref.5) | copy-start | bytes 52
  3.1 6.9 %copy-start.1 = (bf16[4,64,2048]{2,1,0:T(8,128)(2,1)S(1)}, bf16[4,64,2048]{2,1,0:T(8,128)(2,1)}, u32[]{:S(2)}) copy-start(bf16[4,64,2048]{2,1,0:T(8,128)(2,1)} %back_hbm.5) | copy-start | bytes 3145732
  6.3 12.1 %collective-permute-start = (bf16[1312,128]{1,0:T(8,128)(2,1)S(1)}, bf16[1312,128]{1,0:T(8,128)(2,1)S(1)}, u32[]{:S(2)}, u32[]{:S(2)}) collective-permute-start(bf16[1312,128]{1,0:T(8,128)(2,1)S(1)} %get-tuple-element.14.own_ref), channel_id=1, source_target_pairs={{1,2},{2,1},{3,4},{4,3},{5,6},{6,5},{7,8},{8,7},{9,10},{10,9},{11,... | collective-permute-start | bytes 1007624 | tf_op jit(solution)/shard_map/ppermute | solution.py:410
  10.2 1.3 %collective-permute-start.1 = (bf16[16,2048]{1,0:T(8,128)(2,1)S(1)}, bf16[16,2048]{1,0:T(8,128)(2,1)S(1)}, u32[]{:S(2)}, u32[]{:S(2)}) collective-permute-start(bf16[16,2048]{1,0:T(8,128)(2,1)S(1)} %edge_row.1), channel_id=1, source_target_pairs={{0,1},{1,0},{2,3},{3,2},{4,5},{5,4},{6,7},{7,6},{8,9},{9,8},{10,11... | collective-permute-start | bytes 196616 | tf_op jit(solution)/shard_map/ppermute | solution.py:420
  19.3 5.7 %collective-permute-start.2 = (f32[16,128,128]{2,1,0:T(8,128)S(1)}, f32[16,128,128]{2,1,0:T(8,128)S(1)}, u32[]{:S(2)}, u32[]{:S(2)}) collective-permute-start(f32[16,128,128]{2,1,0:T(8,128)S(1)} %get-tuple-element.17.raw_ref), channel_id=1, source_target_pairs={{0,1},{1,0},{2,3},{3,2},{4,5},{5,4},{6,7},{7,6},{8,9},{9,8},{10,11... | collective-permute-start | bytes 3145736 | tf_op jit(solution)/shard_map/ppermute | solution.py:441
  19.3 8.6 %collective-permute-start.3 = (bf16[672,128]{1,0:T(8,128)(2,1)S(1)}, bf16[672,128]{1,0:T(8,128)(2,1)S(1)}, u32[]{:S(2)}, u32[]{:S(2)}) collective-permute-start(bf16[672,128]{1,0:T(8,128)(2,1)S(1)} %get-tuple-element.19), channel_id=1, source_target_pairs={{1,2},{2,1},{3,4},{4,3},{5,6},{6,5},{7,8},{8,7},{9,10},{10,9},{11,... | collective-permute-start | bytes 516104 | tf_op jit(solution)/shard_map/ppermute | solution.py:431
  23.0 7.1 %collective-permute-start.4 = (bf16[400,128]{1,0:T(8,128)(2,1)S(1)}, bf16[400,128]{1,0:T(8,128)(2,1)S(1)}, u32[]{:S(2)}, u32[]{:S(2)}) collective-permute-start(bf16[400,128]{1,0:T(8,128)(2,1)S(1)} %get-tuple-element.21), channel_id=1, source_target_pairs={{1,2},{2,1},{3,4},{4,3},{5,6},{6,5},{7,8},{8,7},{9,10},{10,9},{11,... | collective-permute-start | bytes 307208 | tf_op jit(solution)/shard_map/ppermute | solution.py:431
  24.9 3.0 %copy-start.3 = (bf16[2,512,256]{2,1,0:T(8,128)(2,1)S(1)}, bf16[2,512,256]{2,1,0:T(8,128)(2,1)}, u32[]{:S(2)}) copy-start(bf16[2,512,256]{2,1,0:T(8,128)(2,1)} %constant.2.clone.band_ref) | copy-start | bytes 1572868

commit v3 on v2

--- a/solution.py
+++ b/solution.py
@@ -16,13 +16,14 @@
 SPAN = LANES * GROUP_X
 TILE = 16
 QUARTERS = 4
+PIECES = 4
 F32 = jnp.float32
 BF16 = jnp.bfloat16
 NORM = math.sqrt(sum(math.exp(-k * k / (SIGMA * SIGMA)) for k in range(-HALF, HALF + 1)))
 
 VMEM = pl.BlockSpec(memory_space=pltpu.VMEM)
 SMEM = pl.BlockSpec(memory_space=pltpu.SMEM)
-ANY = pl.BlockSpec(memory_space=pl.ANY)
+HBM = pl.BlockSpec(memory_space=pltpu.HBM)
 PARAMS = pltpu.CompilerParams(vmem_limit_bytes=40 * 1024 * 1024)
 
 
@@ -71,7 +72,12 @@
     return nblocks * rows + spans * (rows // GROUP_Y) + (nblocks * TILE if with_edge else 0)
 
 
-def raw_half(upper, lw_ref, inno_hbm, back_hbm, inno_buf, back_buf, sems, raw_ref, msgs, cut, edge, extra):
+def block_of(refs, k):
+    per = refs[0].shape[0]
+    return refs[k // per].at[k % per]
+
+
+def raw_half(upper, lw_hbm, inno_hbm, back_hbm, lw_ref, inno_buf, back_buf, sems, lw_sem, raw_refs, msgs, cut, edge, extra):
     levels, half, width = inno_buf.shape
     rows, deep = 2 * half, half + TILE
     nblocks = width // LANES
@@ -95,6 +101,8 @@
                 ),
             ]
         )
+    weights = pltpu.make_async_copy(lw_hbm, lw_ref, lw_sem)
+    weights.start()
     for pair in copies:
         for copy in pair:
             copy.start()
@@ -107,7 +115,7 @@
     shape = (rows // GROUP_Y, rows)
     sum_y = one_hot(iota(shape, 1) // GROUP_Y == iota(shape, 0))
     keep = iota((half, 2 * LANES), 0) != cut
-    inner = half // TILE * TILE - (deep - half)
+    weights.wait()
     waited = 0
     block = 0
     for msg_ref, per, with_edge in msgs:
@@ -122,8 +130,8 @@
                     copy.wait()
                 waited += 1
             here = pl.ds(first * LANES, 2 * LANES)
-            around = back_buf[:, :, low * LANES : high * LANES]
-            around = jnp.where(upper, around[:, :half], around[:, deep - half :])
+            skip = pl.multiple_of(jnp.where(upper, 0, deep - half), TILE)
+            around = back_buf[:, pl.ds(skip, half), low * LANES : high * LANES]
             grad_xs = dot(around.reshape(levels * half, -1), diff_x[top:bottom])
             numer_y = numer_x = 0.0
             denom = 1.0
@@ -145,7 +153,8 @@
                 lows.append(rest)
                 for j in range(2):
                     cols = slice(j * LANES, (j + 1) * LANES)
-                    raw_ref[first + j, pl.ds(pl.multiple_of(comp * rows + start, 8), half), :] = raw[:, cols]
+                    at = pl.ds(pl.multiple_of(comp * rows + start, 8), half)
+                    block_of(raw_refs, first + j)[at, :] = raw[:, cols]
                     msg_ref[pl.ds((k + j) * rows + comp * half, half), :] = upto[:, cols]
             place = k * LANES % SPAN
             part_sum = dot(jnp.concatenate(lows, axis=0), sum_x[place : place + 2 * LANES])
@@ -161,7 +170,8 @@
         block += per
 
 
-def outer_kernel(lw_ref, inno_hbm, back_hbm, raw_ref, msg_ref, inno_buf, back_buf, sems):
+def outer_kernel(lw_hbm, inno_hbm, back_hbm, *refs):
+    *raw_refs, msg_ref, lw_ref, inno_buf, back_buf, sems, lw_sem = refs
     levels, half, width = inno_buf.shape
     deep = half + TILE
     par = parity()
@@ -175,14 +185,14 @@
     of_inno = one_hot((kind == 2) & (at == outermost))
 
     def edge(here):
-        back = jnp.where(upper, back_buf[:, :TILE, here], back_buf[:, deep - TILE :, here])
-        inno = jnp.where(upper, inno_buf[:, :TILE, here], inno_buf[:, half - TILE :, here])
+        back = back_buf[:, pl.ds(pl.multiple_of(jnp.where(upper, 0, deep - TILE), TILE), TILE), here]
+        inno = inno_buf[:, pl.ds(pl.multiple_of(jnp.where(upper, 0, half - TILE), TILE), TILE), here]
         tile = dot(of_back, back.reshape(levels * TILE, -1)) + dot(of_inno, inno.reshape(levels * TILE, -1))
         return tile.astype(BF16)
 
     cut = jnp.where(upper, 0, half - 1)
     msgs = [(msg_ref, width // LANES, True)]
-    raw_half(upper, lw_ref, inno_hbm, back_hbm, inno_buf, back_buf, sems, raw_ref, msgs, cut, edge, None)
+    raw_half(upper, lw_hbm, inno_hbm, back_hbm, lw_ref, inno_buf, back_buf, sems, lw_sem, raw_refs, msgs, cut, edge, None)
 
 
 def edge_kernel(back_hbm, raw_hbm, out_ref, buf, sem):
@@ -199,8 +209,9 @@
     out_ref[...] = dot(pick, buf[...].reshape(levels * TILE, -1)).astype(BF16)
 
 
-def inner_kernel(lw_ref, inno_hbm, back_hbm, row_ref, raw_in, raw_ref, *refs):
-    *msg_refs, inno_buf, back_buf, sems = refs
+def inner_kernel(lw_hbm, inno_hbm, back_hbm, row_ref, *refs):
+    raw_refs = refs[PIECES : 2 * PIECES]
+    *msg_refs, lw_ref, inno_buf, back_buf, sems, lw_sem = refs[2 * PIECES :]
     levels, half, width = inno_buf.shape
     upper = parity() == 1
     at = iota((half, 2 * LANES), 0) == jnp.where(upper, 0, half - 1)
@@ -210,12 +221,11 @@
         return jnp.where(at, row_ref[level : level + 1, here].astype(F32) * sign, 0.0)
 
     msgs = [(ref, ref.shape[0] // (2 * half), False) for ref in msg_refs]
-    raw_half(upper, lw_ref, inno_hbm, back_hbm, inno_buf, back_buf, sems, raw_ref, msgs, -1, None, extra)
-
-
-def far_row_kernel(lw_ref, own_ref, got_ref, raw_in, raw_ref, far_ref):
-    nblocks, both, _ = raw_ref.shape
-    rows = both // 2
+    raw_half(upper, lw_hbm, inno_hbm, back_hbm, lw_ref, inno_buf, back_buf, sems, lw_sem, raw_refs, msgs, -1, None, extra)
+
+
+def far_row_kernel(lw_ref, own_ref, got_ref, out_ref):
+    nblocks = out_ref.shape[1] // LANES
     levels = lw_ref.shape[0]
     base = own_ref.shape[0] - nblocks * TILE
     sign = jnp.where(parity() == 0, -1.0, 1.0)
@@ -242,14 +252,9 @@
             denom += (0.25 * weight) * (grad_y[one] * grad_y[one] + grad_x[one] * grad_x[one])
         return numer_y / denom, numer_x / denom
 
-    first = parity() == 0
-    for comp, row in enumerate(raw_row(own, got, sign)):
-        for k in range(nblocks):
-            for y, here in ((0, first), (rows - 1, jnp.logical_not(first))):
-                at = pl.ds(comp * rows + y, 1)
-                raw_ref[k, at, :] = jnp.where(here, row[:, k * LANES : (k + 1) * LANES], raw_ref[k, at, :])
-    for comp, row in enumerate(raw_row(got, own, -sign)):
-        far_ref[comp : comp + 1, :] = row
+    rows = (*raw_row(own, got, sign), *raw_row(got, own, -sign))
+    for index, row in enumerate(rows):
+        out_ref[index : index + 1, :] = row
 
 
 def far_taps(rows, part):
@@ -292,8 +297,10 @@
     return parts
 
 
-def near_kernel(raw_ref, near_ref, far_ref, msg_ref, out_ref):
-    nblocks, both, _ = raw_ref.shape
+def near_kernel(*refs):
+    raw_refs, near_refs = refs[:PIECES], refs[PIECES : 2 * PIECES]
+    edges_ref, msg_ref, out_ref = refs[2 * PIECES :]
+    nblocks, both, _ = out_ref.shape
     rows = both // 2
     par = parity()
     side = 1 - 2 * par
@@ -305,6 +312,7 @@
     rest = spread_rest(values, msg_ref, nblocks)
     mean_x = mean_over_x()
     column = iota((rows, 2 * LANES), 0)
+    own_taps = taps(jnp.where(par == 0, 0, rows - 1) - column)
     edge_taps = taps(jnp.where(par == 0, -1, rows) - column)
     for first in range(0, nblocks, 2):
         added = far_part(two_far, rest, mean_x, msg_ref, first, rows)
@@ -312,22 +320,26 @@
             here = pl.ds(comp * rows, rows)
             pairs = []
             for k in (first, first + 1):
-                pairs.append(jnp.concatenate([raw_ref[k, here, :], near_ref[k, here, :]], axis=0))
+                pairs.append(jnp.concatenate([block_of(raw_refs, k)[here, :], block_of(near_refs, k)[here, :]], axis=0))
             high_x, low_x = split(jnp.concatenate(pairs, axis=1))
             part = dot(two, high_x)
             part = part[:rows] + part[rows:] + dot(high, low_x) + added[comp]
-            part += edge_taps * far_ref[comp : comp + 1, pl.ds(first * LANES, 2 * LANES)]
+            cols = pl.ds(first * LANES, 2 * LANES)
+            part += own_taps * edges_ref[comp : comp + 1, cols] + edge_taps * edges_ref[2 + comp : 3 + comp, cols]
             for j in range(2):
                 out_ref[first + j, here, :] = part[:, j * LANES : (j + 1) * LANES]
 
 
-def finish(band_ref, part_ref, msg_ref, total_ref, out_hbm, high_ref, low_ref, buf, sem, begin, per, firsts):
+def finish(band_ref, part_ref, edges_ref, msg_ref, total_ref, out_hbm, high_ref, low_ref, buf, sem, begin, per, firsts):
     nblocks, both, _ = part_ref.shape
     rows = both // 2
     values = far_taps(rows, 1)
     two = jnp.concatenate(split(values), axis=0)
     rest = spread_rest(values, msg_ref, per)
     mean_x = mean_over_x()
+    side = 1 - 2 * parity()
+    edge = jnp.where(side > 0, 2 * rows - 1, -rows)
+    edge_taps = taps(edge - iota((rows, LANES), 0))
     for k in range(begin - 3 if begin else 0, begin):
         high_ref[k], low_ref[k] = split(part_ref[k])
     copies = []
@@ -340,6 +352,7 @@
                 here = pl.ds(comp * rows, rows)
                 for j in range(2):
                     total = part_ref[ready + j, here, :] + added[comp][:, j * LANES : (j + 1) * LANES]
+                    total += edge_taps * edges_ref[comp : comp + 1, pl.ds((ready + j) * LANES, LANES)]
                     if total_ref is not None and ready + j >= begin + per - 3:
                         total_ref[ready + j, here, :] = total
                     high_ref[ready + j, here, :], low_ref[ready + j, here, :] = split(total)
@@ -358,19 +371,18 @@
         copy.wait()
 
 
-def first_kernel(band_ref, part_ref, msg_ref, out_hbm, total_ref, high_ref, low_ref, buf, sem):
-    per = msg_ref.shape[0] // part_ref.shape[1] * 2
+def first_kernel(band_ref, part_ref, edges_ref, msg_ref, out_hbm, total_ref, high_ref, low_ref, buf, sem):
     per = blocks_of(msg_ref.shape[0], part_ref.shape[1] // 2)
     firsts = range(0, per - 2, 2)
-    finish(band_ref, part_ref, msg_ref, total_ref, out_hbm, high_ref, low_ref, buf, sem, 0, per, firsts)
-
-
-def last_kernel(band_ref, part_ref, msg_ref, out_in, out_hbm, high_ref, low_ref, buf, sem):
+    finish(band_ref, part_ref, edges_ref, msg_ref, total_ref, out_hbm, high_ref, low_ref, buf, sem, 0, per, firsts)
+
+
+def last_kernel(band_ref, part_ref, edges_ref, msg_ref, out_in, out_hbm, high_ref, low_ref, buf, sem):
     nblocks = part_ref.shape[0]
     per = blocks_of(msg_ref.shape[0], part_ref.shape[1] // 2)
     begin = nblocks - per
     firsts = range(begin - 2, nblocks, 2)
-    finish(band_ref, part_ref, msg_ref, None, out_hbm, high_ref, low_ref, buf, sem, begin, per, firsts)
+    finish(band_ref, part_ref, edges_ref, msg_ref, None, out_hbm, high_ref, low_ref, buf, sem, begin, per, firsts)
 
 
 def blocks_of(size, rows):
@@ -386,6 +398,9 @@
     count = lax.axis_size("row")
     chip = [(i, i ^ 1) for i in range(count) if i ^ 1 < count]
     away = [(i, j) for i in range(count) for j in [((i + 1) ^ 1) - 1] if 0 <= j < count]
+    innovation = pltpu.with_memory_space_constraint(innovation, pltpu.HBM)
+    background = pltpu.with_memory_space_constraint(background, pltpu.HBM)
+    level_weight = pltpu.with_memory_space_constraint(level_weight, pltpu.HBM)
     blocks = jax.ShapeDtypeStruct((nblocks, both, LANES), F32)
     per = nblocks * 5 // 16 * 2
     pers = [per, nblocks - per]
@@ -394,15 +409,18 @@
         return jax.ShapeDtypeStruct((message_rows(rows, nblocks, with_edge), LANES), BF16)
 
     scratch = [
+        pltpu.SMEM((levels,), F32),
         pltpu.VMEM((levels, half, width), BF16),
         pltpu.VMEM((levels, half + TILE, width), BF16),
         pltpu.SemaphoreType.DMA((2, QUARTERS)),
+        pltpu.SemaphoreType.DMA,
     ]
-    raw, outer = pl.pallas_call(
+    piece = jax.ShapeDtypeStruct((nblocks // PIECES, both, LANES), F32)
+    *raws, outer = pl.pallas_call(
         outer_kernel,
-        out_shape=[blocks, message(nblocks, True)],
-        in_specs=[SMEM, ANY, ANY],
-        out_specs=[VMEM, VMEM],
+        out_shape=[piece] * PIECES + [message(nblocks, True)],
+        in_specs=[HBM] * 3,
+        out_specs=[VMEM] * (PIECES + 1),
         scratch_shapes=scratch,
         compiler_params=PARAMS,
         name="outer_half",
@@ -411,42 +429,43 @@
     edge = pl.pallas_call(
         edge_kernel,
         out_shape=jax.ShapeDtypeStruct((TILE, width), BF16),
-        in_specs=[ANY, ANY],
+        in_specs=[HBM, HBM],
         out_specs=VMEM,
         scratch_shapes=[pltpu.VMEM((levels, TILE, width), BF16), pltpu.SemaphoreType.DMA],
         compiler_params=PARAMS,
         name="edge_row",
-    )(background, raw)
+    )(background, raws[0])
     edge = lax.ppermute(edge, "row", chip)
-    raw, *msgs = pl.pallas_call(
+    found = pl.pallas_call(
         inner_kernel,
-        out_shape=[blocks] + [message(k, False) for k in pers],
-        in_specs=[SMEM, ANY, ANY, VMEM, VMEM],
-        out_specs=[VMEM] * 3,
+        out_shape=[piece] * PIECES + [message(k, False) for k in pers],
+        in_specs=[HBM] * 3 + [VMEM] * (PIECES + 1),
+        out_specs=[VMEM] * (PIECES + 2),
         scratch_shapes=scratch,
-        input_output_aliases={4: 0},
+        input_output_aliases={4 + k: k for k in range(PIECES)},
         compiler_params=PARAMS,
         name="inner_half",
-    )(level_weight, innovation, background, edge, raw)
-    msgs = [lax.ppermute(m, "row", away) for m in msgs]
-    raw, far = pl.pallas_call(
+    )(level_weight, innovation, background, edge, *raws)
+    raws = found[:PIECES]
+    msgs = [lax.ppermute(m, "row", away) for m in found[PIECES:]]
+    nears = [lax.ppermute(r, "row", chip) for r in raws]
+    edges = pl.pallas_call(
         far_row_kernel,
-        out_shape=[blocks, jax.ShapeDtypeStruct((8, width), F32)],
-        in_specs=[SMEM] + [VMEM] * 3,
-        out_specs=[VMEM] * 2,
-        input_output_aliases={3: 0},
-        compiler_params=PARAMS,
-        name="far_row",
-    )(level_weight, outer, outer_got, raw)
-    near = lax.ppermute(raw, "row", chip)
+        out_shape=jax.ShapeDtypeStruct((4, width), F32),
+        in_specs=[SMEM] + [VMEM] * 2,
+        out_specs=VMEM,
+        compiler_params=PARAMS,
+        name="outermost_rows",
+    )(level_weight, outer, outer_got)
+    edges_near = lax.ppermute(edges, "row", chip)
     part = pl.pallas_call(
         near_kernel,
         out_shape=blocks,
-        in_specs=[VMEM] * 4,
+        in_specs=[VMEM] * (2 * PIECES + 2),
         out_specs=VMEM,
         compiler_params=PARAMS,
         name="near_part",
-    )(raw, near, far, outer_got)
+    )(*raws, *nears, edges, outer_got)
     band = jnp.asarray(zonal_band())
     scratch = [
         pltpu.VMEM((nblocks, both, LANES), BF16),
@@ -458,23 +477,23 @@
     out, part = pl.pallas_call(
         first_kernel,
         out_shape=[result, blocks],
-        in_specs=[VMEM] * 3,
-        out_specs=[ANY, VMEM],
+        in_specs=[VMEM] * 4,
+        out_specs=[HBM, VMEM],
         scratch_shapes=scratch,
         input_output_aliases={1: 1},
         compiler_params=PARAMS,
         name="first_columns",
-    )(band, part, msgs[0])
+    )(band, part, edges_near, msgs[0])
     return pl.pallas_call(
         last_kernel,
         out_shape=result,
-        in_specs=[VMEM] * 3 + [ANY],
-        out_specs=ANY,
+        in_specs=[VMEM] * 4 + [HBM],
+        out_specs=HBM,
         scratch_shapes=scratch,
-        input_output_aliases={3: 0},
+        input_output_aliases={4: 0},
         compiler_params=PARAMS,
         name="last_columns",
-    )(band, part, msgs[1], out)
+    )(band, part, edges_near, msgs[1], out)
 
 
 def solution(mesh):

time: 32.2 us -> 28.2 us (0.88)
  the two profiles are of different devices: /device:TPU:11 before, /device:TPU:0 now
where the time goes in v3:
time: 28.2 us; the launch traced here: 27.9 us
  Pallas kernels  14.1 us (50%)
  starting transfers between devices  12.9 us (46%)
  waiting for transfers between devices  0.81 us (3%)
    ppermute x1, starting transfers between devices, body(): edges_near = lax.ppermute(edges, 'row', chip)  6.06 us
    ppermute x4, starting transfers between devices, body(): nears = [lax.ppermute(r, 'row', chip) for r in raws]  4.33 us
    pallas_call x1, Pallas kernels, body(): pl.pallas_call(inner_kernel, out_shape=[piece] * PIECES + [message(k, Fal...  3.47 us
    pallas_call x1, Pallas kernels, body(): pl.pallas_call(outer_kernel, out_shape=[piece] * PIECES + [message(nblock...  3.37 us
    pallas_call x1, Pallas kernels, body(): pl.pallas_call(first_kernel, out_shape=[result, blocks], in_specs=[VMEM]...  2.04 us
    pallas_call x1, Pallas kernels, body(): pl.pallas_call(last_kernel, out_shape=result, in_specs=[VMEM] * 4 + [HBM]...  1.93 us
    ppermute x2, starting transfers between devices, body(): msgs = [lax.ppermute(m, 'row', away) for m in found[PIECES:]]  1.33 us
    pallas_call x1, Pallas kernels, body(): pl.pallas_call(near_kernel, out_shape=blocks, in_specs=[VMEM] * (2 * PIEC...  1.23 us
  transfers between devices with their start and end apart: 9, of which 2 were waited for; matrix products, arithmetic and copies ran while one was open for 0% of the time, Pallas kernels for 27%

profile of v3, /device:TPU:0, one launch (start us, length us, event | category | flops | bytes accessed | tf_op | source)
XLA Modules:
  0.0 27.9 jit_solution(8856586057611030835)
XLA Ops:
  0.0 3.4 %outer_half.1 = (f32[4,128,128]{2,1,0:T(8,128)S(1)}, f32[4,128,128]{2,1,0:T(8,128)S(1)}, f32[4,128,128]{2,1,0:T(8,128)S(1)}, f32[4,128,128]{2,1,0:T(8,128)S(1)}, bf16[1312,128]{1,0:T(8,128)(2,1)S(1)}) custom-call(f32[4]{0:T(128)} %lw_ref.1, bf16[4,64,2048]{2,1,0:T(8,128)(2,1)} %inno_hbm.3, bf16[4,64,2048]{2,1,0:T(8,128)(2,1)} %back_hbm.5), custom_call_target="tpu_custom_call" | custom-call | tf_op jit(solution)/shard_map/outer_half/pallas_call | solution.py:419
  3.4 1.1 %edge_row.1 = bf16[16,2048]{1,0:T(8,128)(2,1)S(1)} custom-call(bf16[4,64,2048]{2,1,0:T(8,128)(2,1)} %back_hbm.5, f32[4,128,128]{2,1,0:T(8,128)S(1)} %get-tuple-element.18.raw_hbm.refs_0_), custom_call_target="tpu_custom_call" | custom-call | tf_op jit(solution)/shard_map/edge_row/pallas_call | solution.py:429
  4.5 0.5 %collective-permute-start = (bf16[16,2048]{1,0:T(8,128)(2,1)S(1)}, bf16[16,2048]{1,0:T(8,128)(2,1)S(1)}, u32[]{:S(2)}, u32[]{:S(2)}) collective-permute-start(bf16[16,2048]{1,0:T(8,128)(2,1)S(1)} %edge_row.1), channel_id=1, source_target_pairs={{0,1},{1,0},{2,3},{3,2},{4,5},{5,4},{6,7},{7,6},{8,9},{9,8},{10,11... | collective-permute-start | bytes 196616 | tf_op jit(solution)/shard_map/ppermute | solution.py:438
  5.0 0.7 %collective-permute-start.5 = (bf16[1312,128]{1,0:T(8,128)(2,1)S(1)}, bf16[1312,128]{1,0:T(8,128)(2,1)S(1)}, u32[]{:S(2)}, u32[]{:S(2)}) collective-permute-start(bf16[1312,128]{1,0:T(8,128)(2,1)S(1)} %get-tuple-element.26.own_ref), channel_id=1, source_target_pairs={{1,2},{2,1},{3,4},{4,3},{5,6},{6,5},{7,8},{8,7},{9,10},{10,9},{11,... | collective-permute-start | bytes 1007624 | tf_op jit(solution)/shard_map/ppermute | solution.py:428
  5.7 0.2 collective-permute-done.row_ref
  5.9 3.5 %inner_half.1 = (f32[4,128,128]{2,1,0:T(8,128)S(1)}, f32[4,128,128]{2,1,0:T(8,128)S(1)}, f32[4,128,128]{2,1,0:T(8,128)S(1)}, f32[4,128,128]{2,1,0:T(8,128)S(1)},...) custom-call(f32[4]{0:T(128)} %lw_ref.1, ...), custom_call_target="tpu_custom_call", output_to_operand_aliasing={{0}: (4, {}), {1}: (5, {}), {2}: (6, {}), {3}: (7, {})} | custom-call | tf_op jit(solution)/shard_map/inner_half/pallas_call | solution.py:439
  9.4 3.7 %collective-permute-start.1 = (f32[4,128,128]{2,1,0:T(8,128)S(1)}, f32[4,128,128]{2,1,0:T(8,128)S(1)}, u32[]{:S(2)}, u32[]{:S(2)}) collective-permute-start(f32[4,128,128]{2,1,0:T(8,128)S(1)} %get-tuple-element.22.refs_0_), channel_id=1, source_target_pairs={{0,1},{1,0},{2,3},{3,2},{4,5},{5,4},{6,7},{7,6},{8,9},{9,8},{10,11... | collective-permute-start | bytes 786440 | tf_op jit(solution)/shard_map/ppermute | solution.py:451
  13.2 0.1 collective-permute-start.2
  13.2 0.4 %collective-permute-start.3 = (f32[4,128,128]{2,1,0:T(8,128)S(1)}, f32[4,128,128]{2,1,0:T(8,128)S(1)}, u32[]{:S(2)}, u32[]{:S(2)}) collective-permute-start(f32[4,128,128]{2,1,0:T(8,128)S(1)} %get-tuple-element.24.refs_2_), channel_id=1, source_target_pairs={{0,1},{1,0},{2,3},{3,2},{4,5},{5,4},{6,7},{7,6},{8,9},{9,8},{10,11... | collective-permute-start | bytes 786440 | tf_op jit(solution)/shard_map/ppermute | solution.py:451
  13.7 0.1 collective-permute-start.4
  13.7 0.6 %collective-permute-done.1.refs_4_ = f32[4,128,128]{2,1,0:T(8,128)S(1)} collective-permute-done((f32[4,128,128]{2,1,0:T(8,128)S(1)}, f32[4,128,128]{2,1,0:T(8,128)S(1)}, u32[]{:S(2)}, u32[]{:S(2)}) %collective-permute-start.1) | collective-permute-done | bytes 262176 | tf_op jit(solution)/shard_map/ppermute | solution.py:451
  14.3 0.7 %collective-permute-start.7 = (bf16[672,128]{1,0:T(8,128)(2,1)S(1)}, bf16[672,128]{1,0:T(8,128)(2,1)S(1)}, u32[]{:S(2)}, u32[]{:S(2)}) collective-permute-start(bf16[672,128]{1,0:T(8,128)(2,1)S(1)} %get-tuple-element.27), channel_id=1, source_target_pairs={{1,2},{2,1},{3,4},{4,3},{5,6},{6,5},{7,8},{8,7},{9,10},{10,9},{11,... | collective-permute-start | bytes 516104 | tf_op jit(solution)/shard_map/ppermute | solution.py:450
  15.0 0.0 collective-permute-done.5.got_ref.refs_9_
  15.0 0.7 %collective-permute-start.8 = (bf16[400,128]{1,0:T(8,128)(2,1)S(1)}, bf16[400,128]{1,0:T(8,128)(2,1)S(1)}, u32[]{:S(2)}, u32[]{:S(2)}) collective-permute-start(bf16[400,128]{1,0:T(8,128)(2,1)S(1)} %get-tuple-element.29), channel_id=1, source_target_pairs={{1,2},{2,1},{3,4},{4,3},{5,6},{6,5},{7,8},{8,7},{9,10},{10,9},{11,... | collective-permute-start | bytes 307208 | tf_op jit(solution)/shard_map/ppermute | solution.py:450
  15.7 0.9 %outermost_rows.1.refs_8_ = f32[4,2048]{1,0:T(4,128)S(1)} custom-call(f32[4]{0:T(128)} %lw_ref.1, bf16[1312,128]{1,0:T(8,128)(2,1)S(1)} %get-tuple-element.26.own_ref, bf16[1312,128]{1,0:T(8,128)(2,1)S(1)} %collective-permute-done.5.got_ref.refs_9_), custom_call_target="tpu_custom_call" | custom-call | tf_op jit(solution)/shard_map/outermost_rows/pallas_call | solution.py:452
  16.6 0.0 copy-start
  16.6 0.0 collective-permute-done.2.refs_5_
  16.6 6.1 %collective-permute-start.6 = (f32[4,2048]{1,0:T(4,128)S(1)}, f32[4,2048]{1,0:T(4,128)S(1)}, u32[]{:S(2)}, u32[]{:S(2)}) collective-permute-start(f32[4,2048]{1,0:T(4,128)S(1)} %outermost_rows.1.refs_8_), channel_id=1, source_target_pairs={{0,1},{1,0},{2,3},{3,2},{4,5},{5,4},{6,7},{7,6},{8,9},{9,8},{10,11... | collective-permute-start | bytes 98312 | tf_op jit(solution)/shard_map/ppermute | solution.py:460
  22.7 0.0 collective-permute-done.3.refs_6_
  22.7 0.0 collective-permute-done.4.refs_7_
  22.7 1.2 %near_part.1.part_ref = f32[16,128,128]{2,1,0:T(8,128)S(1)} custom-call(f32[4,128,128]{2,1,0:T(8,128)S(1)} %get-tuple-element.22.refs_0_, f32[4,128,128]{2,1,0:T(8,128)S(1)} %get-tuple-element.23.refs_1_, f32[4,128,128]{2,1,0:T(8,128)S(1)} %get-tuple-element.24.refs_2_, f32[4,128,128]{2,1,0:T(8,128)S(1)} %get-tuple-element.25.refs_3_, ...), custom_call_target="tpu_custom_call" | custom-call | tf_op jit(solution)/shard_map/near_part/pallas_call | solution.py:461
  23.9 0.0 collective-permute-done.7.msg_ref
  23.9 0.0 collective-permute-done.6.edges_ref
  23.9 0.0 copy-done
  24.0 2.0 %first_columns.1 = (f32[2,64,2048]{2,1,0:T(8,128)}, f32[16,128,128]{2,1,0:T(8,128)S(1)}) custom-call(bf16[2,512,256]{2,1,0:T(8,128)(2,1)S(1)} %copy-done, f32[16,128,128]{2,1,0:T(8,128)S(1)} %near_part.1.part_ref, f32[4,2048]{1,0:T(4,128)S(1)} %collective-permute-done.6.edges_ref, ...), custom_call_target="tpu_custom_call", output_to_operand_aliasing={{1}: (1, {})} | custom-call | tf_op jit(solution)/shard_map/first_columns/pallas_call | solution.py:477
  26.0 0.0 collective-permute-done.8.msg_ref
  26.0 1.9 %last_columns.1 = f32[2,64,2048]{2,1,0:T(8,128)} custom-call(bf16[2,512,256]{2,1,0:T(8,128)(2,1)S(1)} %copy-done, f32[16,128,128]{2,1,0:T(8,128)S(1)} %get-tuple-element.28.part_ref, f32[4,2048]{1,0:T(4,128)S(1)} %collective-permute-done.6.edges_ref, bf16[400,128]{1,0:T(8,128)(2,1)S(1)} %collective-permute-done.8.msg_ref, ...), custom_call_target="tpu_custom_call", output_to_operand_aliasing={{}: (4, {})} | custom-call | tf_op jit(solution)/shard_map/last_columns/pallas_call | solution.py:487
Async XLA Ops:
  4.5 1.4 %collective-permute-start = (bf16[16,2048]{1,0:T(8,128)(2,1)S(1)}, bf16[16,2048]{1,0:T(8,128)(2,1)S(1)}, u32[]{:S(2)}, u32[]{:S(2)}) collective-permute-start(bf16[16,2048]{1,0:T(8,128)(2,1)S(1)} %edge_row.1), channel_id=1, source_target_pairs={{0,1},{1,0},{2,3},{3,2},{4,5},{5,4},{6,7},{7,6},{8,9},{9,8},{10,11... | collective-permute-start | bytes 196616 | tf_op jit(solution)/shard_map/ppermute | solution.py:438
  5.0 10.0 %collective-permute-start.5 = (bf16[1312,128]{1,0:T(8,128)(2,1)S(1)}, bf16[1312,128]{1,0:T(8,128)(2,1)S(1)}, u32[]{:S(2)}, u32[]{:S(2)}) collective-permute-start(bf16[1312,128]{1,0:T(8,128)(2,1)S(1)} %get-tuple-element.26.own_ref), channel_id=1, source_target_pairs={{1,2},{2,1},{3,4},{4,3},{5,6},{6,5},{7,8},{8,7},{9,10},{10,9},{11,... | collective-permute-start | bytes 1007624 | tf_op jit(solution)/shard_map/ppermute | solution.py:428
  9.4 4.9 %collective-permute-start.1 = (f32[4,128,128]{2,1,0:T(8,128)S(1)}, f32[4,128,128]{2,1,0:T(8,128)S(1)}, u32[]{:S(2)}, u32[]{:S(2)}) collective-permute-start(f32[4,128,128]{2,1,0:T(8,128)S(1)} %get-tuple-element.22.refs_0_), channel_id=1, source_target_pairs={{0,1},{1,0},{2,3},{3,2},{4,5},{5,4},{6,7},{7,6},{8,9},{9,8},{10,11... | collective-permute-start | bytes 786440 | tf_op jit(solution)/shard_map/ppermute | solution.py:451
  13.2 3.5 %collective-permute-start.2 = (f32[4,128,128]{2,1,0:T(8,128)S(1)}, f32[4,128,128]{2,1,0:T(8,128)S(1)}, u32[]{:S(2)}, u32[]{:S(2)}) collective-permute-start(f32[4,128,128]{2,1,0:T(8,128)S(1)} %get-tuple-element.23.refs_1_), channel_id=1, source_target_pairs={{0,1},{1,0},{2,3},{3,2},{4,5},{5,4},{6,7},{7,6},{8,9},{9,8},{10,11... | collective-permute-start | bytes 786440 | tf_op jit(solution)/shard_map/ppermute | solution.py:451
  13.2 9.4 %collective-permute-start.3 = (f32[4,128,128]{2,1,0:T(8,128)S(1)}, f32[4,128,128]{2,1,0:T(8,128)S(1)}, u32[]{:S(2)}, u32[]{:S(2)}) collective-permute-start(f32[4,128,128]{2,1,0:T(8,128)S(1)} %get-tuple-element.24.refs_2_), channel_id=1, source_target_pairs={{0,1},{1,0},{2,3},{3,2},{4,5},{5,4},{6,7},{7,6},{8,9},{9,8},{10,11... | collective-permute-start | bytes 786440 | tf_op jit(solution)/shard_map/ppermute | solution.py:451
  13.7 9.0 %collective-permute-start.4 = (f32[4,128,128]{2,1,0:T(8,128)S(1)}, f32[4,128,128]{2,1,0:T(8,128)S(1)}, u32[]{:S(2)}, u32[]{:S(2)}) collective-permute-start(f32[4,128,128]{2,1,0:T(8,128)S(1)} %get-tuple-element.25.refs_3_), channel_id=1, source_target_pairs={{0,1},{1,0},{2,3},{3,2},{4,5},{5,4},{6,7},{7,6},{8,9},{9,8},{10,11... | collective-permute-start | bytes 786440 | tf_op jit(solution)/shard_map/ppermute | solution.py:451
  14.3 9.6 %collective-permute-start.7 = (bf16[672,128]{1,0:T(8,128)(2,1)S(1)}, bf16[672,128]{1,0:T(8,128)(2,1)S(1)}, u32[]{:S(2)}, u32[]{:S(2)}) collective-permute-start(bf16[672,128]{1,0:T(8,128)(2,1)S(1)} %get-tuple-element.27), channel_id=1, source_target_pairs={{1,2},{2,1},{3,4},{4,3},{5,6},{6,5},{7,8},{8,7},{9,10},{10,9},{11,... | collective-permute-start | bytes 516104 | tf_op jit(solution)/shard_map/ppermute | solution.py:450
  15.0 11.0 %collective-permute-start.8 = (bf16[400,128]{1,0:T(8,128)(2,1)S(1)}, bf16[400,128]{1,0:T(8,128)(2,1)S(1)}, u32[]{:S(2)}, u32[]{:S(2)}) collective-permute-start(bf16[400,128]{1,0:T(8,128)(2,1)S(1)} %get-tuple-element.29), channel_id=1, source_target_pairs={{1,2},{2,1},{3,4},{4,3},{5,6},{6,5},{7,8},{8,7},{9,10},{10,9},{11,... | collective-permute-start | bytes 307208 | tf_op jit(solution)/shard_map/ppermute | solution.py:450
  16.6 7.3 %copy-start = (bf16[2,512,256]{2,1,0:T(8,128)(2,1)S(1)}, bf16[2,512,256]{2,1,0:T(8,128)(2,1)}, u32[]{:S(2)}) copy-start(bf16[2,512,256]{2,1,0:T(8,128)(2,1)} %constant.2.clone.band_ref) | copy-start | bytes 1572868
  16.6 7.3 %collective-permute-start.6 = (f32[4,2048]{1,0:T(4,128)S(1)}, f32[4,2048]{1,0:T(4,128)S(1)}, u32[]{:S(2)}, u32[]{:S(2)}) collective-permute-start(f32[4,2048]{1,0:T(4,128)S(1)} %outermost_rows.1.refs_8_), channel_id=1, source_target_pairs={{0,1},{1,0},{2,3},{3,2},{4,5},{5,4},{6,7},{7,6},{8,9},{9,8},{10,11... | collective-permute-start | bytes 98312 | tf_op jit(solution)/shard_map/ppermute | solution.py:460

commit v4 on v0

v4 whole, which is shorter than its diff:
```python
import math

import jax
import jax.numpy as jnp
import numpy as np
from jax import lax
from jax.experimental import pallas as pl
from jax.experimental.pallas import tpu as pltpu
from jax.sharding import PartitionSpec as P

HALF = 64
SIGMA = 64
LANES = 128
TILE = 16
SHIFT_Y, SHIFT_X, SHIFT_Z = 2, 3, 4
SPAN = LANES << SHIFT_X
PACK = 4
QUARTERS = 4
PIECES = 4
F32 = jnp.float32
BF16 = jnp.bfloat16
NORM = math.sqrt(sum(math.exp(-k * k / (SIGMA * SIGMA)) for k in range(-HALF, HALF + 1)))

VMEM = pl.BlockSpec(memory_space=pltpu.VMEM)
SMEM = pl.BlockSpec(memory_space=pltpu.SMEM)
HBM = pl.BlockSpec(memory_space=pltpu.HBM)
PARAMS = pltpu.CompilerParams(vmem_limit_bytes=40 * 1024 * 1024)


def split(values):
    high = values.astype(BF16)
    return high, (values - high.astype(F32)).astype(BF16)


def dot(left, right):
    return jnp.dot(left, right, preferred_element_type=F32)


def iota(shape, dim):
    return lax.broadcasted_iota(jnp.int32, shape, dim)


def one_hot(mask, value=1.0):
    return jnp.where(mask, value, 0.0).astype(BF16)


def difference(off):
    return (jnp.where(off == 1, 1.0, 0.0) - jnp.where(off == -1, 1.0, 0.0)).astype(BF16)


def taps(offset):
    off = offset.astype(F32)
    value = jnp.exp(off * off * (-0.5 / (SIGMA * SIGMA))) * (1.0 / NORM)
    return jnp.where(jnp.abs(offset) <= HALF, value, 0.0)


def zonal_band():
    offset = np.arange(4 * LANES)[:, None] - LANES - np.arange(2 * LANES)[None, :]
    band = np.exp(-offset * offset / (2.0 * SIGMA * SIGMA)) / NORM
    band = np.where(np.abs(offset) <= HALF, band, 0.0).astype(np.float32)
    high = band.astype(BF16)
    return np.stack([high, (band - high.astype(np.float32)).astype(BF16)])


def window(first, nblocks):
    low, high = max(first - 1, 0), min(first + 3, nblocks)
    return low, high, (low - first + 1) * LANES, (high - first + 1) * LANES


def smooth_x(band_ref, high_ref, low_ref, first, nblocks):
    low, high, top, bottom = window(first, nblocks)
    upper = jnp.concatenate([high_ref[k] for k in range(low, high)], axis=1)
    lower = jnp.concatenate([low_ref[k] for k in range(low, high)], axis=1)
    band = band_ref[0, top:bottom, :]
    return dot(upper, band) + dot(lower, band) + dot(upper, band_ref[1, top:bottom, :])


def parity():
    return lax.rem(lax.axis_index("row"), 2)


def block_of(refs, k):
    per = refs[0].shape[0]
    return refs[k // per].at[k % per]


def tile_at(row):
    return pl.ds(pl.multiple_of(row, TILE), TILE)


def raw_pair(first, lw_ref, inno, back, diff_y, diff_x, extra):
    levels, half, width = inno.shape
    upper, back_ref, at = back
    here = pl.ds(first * LANES, 2 * LANES)
    low, high, top, bottom = window(first, width // LANES)
    deep = pl.ds(pl.multiple_of(at, TILE), half + TILE)
    exact = pl.ds(pl.multiple_of(at + jnp.where(upper, 0, TILE), TILE), half)
    around = back_ref[:, exact, low * LANES : high * LANES]
    grad_xs = dot(around.reshape(levels * half, -1), diff_x[top:bottom])
    numer_y = numer_x = 0.0
    denom = 1.0
    for level in range(levels):
        weight = lw_ref[level]
        grad_y = dot(diff_y, back_ref[level, deep, here])
        if extra is not None:
            grad_y += extra(level, here)
        grad_x = grad_xs[level * half : (level + 1) * half]
        scaled = inno[level, :, here].astype(F32) * (0.5 * weight)
        numer_y += scaled * grad_y
        numer_x += scaled * grad_x
        denom += (0.25 * weight) * (grad_y * grad_y + grad_x * grad_x)
    inverse = 1.0 / denom
    return numer_y * inverse, numer_x * inverse


def differences(upper, half):
    deep = half + TILE
    diff_y = difference(iota((half, deep), 1) - iota((half, deep), 0) - jnp.where(upper, 0, TILE))
    shape = (4 * LANES, 2 * LANES)
    return diff_y, difference(iota(shape, 0) - LANES - iota(shape, 1))


def outer_kernel(lw_hbm, inno_hbm, back_hbm, *refs):
    *raw_refs, msg_ref, row_ref, lw_ref, inno_buf, back_buf, low_ref, row_buf, sems, lw_sem, row_sem = refs
    levels, half, width = inno_buf.shape
    rows, deep = 2 * half, half + TILE
    nblocks = width // LANES
    upper = parity() == 0
    start = jnp.where(upper, 0, half)
    copies = []
    part = width // QUARTERS
    back_rows = pl.ds(pl.multiple_of(jnp.where(upper, 0, rows - deep), TILE), deep)
    inno_rows = pl.ds(pl.multiple_of(start, TILE), half)
    for q in range(QUARTERS):
        cols = pl.ds(q * part, part)
        copies.append(
            [
                pltpu.make_async_copy(back_hbm.at[:, back_rows, cols], back_buf.at[:, :, cols], sems.at[0, q]),
                pltpu.make_async_copy(inno_hbm.at[:, inno_rows, cols], inno_buf.at[:, :, cols], sems.at[1, q]),
            ]
        )
    weights = pltpu.make_async_copy(lw_hbm, lw_ref, lw_sem)
    near = pltpu.make_async_copy(back_hbm.at[:, tile_at(jnp.where(upper, rows - TILE, 0)), :], row_buf, row_sem)
    weights.start()
    for pair in copies:
        for copy in pair:
            copy.start()
    near.start()
    diff_y, diff_x = differences(upper, half)
    keep = iota((half, 2 * LANES), 0) != jnp.where(upper, 0, half - 1)
    weights.wait()
    waited = 0
    for first in range(0, nblocks, 2):
        while waited * part < window(first, nblocks)[1] * LANES:
            for copy in copies[waited]:
                copy.wait()
            waited += 1
        pair = raw_pair(first, lw_ref, inno_buf, (upper, back_buf, 0), diff_y, diff_x, None)
        for comp, raw in enumerate(pair):
            raw = jnp.where(keep, raw, 0.0)
            high, low = split(raw)
            low_ref[comp * half : (comp + 1) * half, first * LANES : (first + 2) * LANES] = low
            for j in range(2):
                cols = slice(j * LANES, (j + 1) * LANES)
                at = pl.ds(pl.multiple_of(comp * rows + start, 8), half)
                block_of(raw_refs, first + j)[at, :] = raw[:, cols]
                msg_ref[pl.ds((first + j) * rows + comp * half, half), :] = high[:, cols]
    shape = (SPAN, LANES)
    sum_x = one_hot(iota(shape, 0) >> SHIFT_X == iota(shape, 1))
    groups = rows >> SHIFT_Y
    shape = (groups, rows)
    sum_y = one_hot(iota(shape, 1) >> SHIFT_Y == iota(shape, 0))
    at = nblocks * rows
    for span in range(0, width, SPAN):
        total = dot(low_ref[:, span : span + SPAN], sum_x)
        msg_ref[pl.ds(at, groups), :] = dot(sum_y, total.astype(BF16)).astype(BF16)
        at += groups
    kinds = 3 * levels
    shape = (PACK * kinds, PACK * levels * TILE)
    row, col = iota(shape, 0), iota(shape, 1)
    want = row - (col >> 6) * kinds
    level = (col >> 4) & (levels - 1)
    place = col & (TILE - 1)
    outermost = place == jnp.where(upper, 0, TILE - 1)
    next_row = place == jnp.where(upper, 1, TILE - 2)
    of_back = one_hot(((want == level) & outermost) | ((want == levels + level) & next_row))
    of_inno = one_hot((want == 2 * levels + level) & outermost)
    back_at = tile_at(jnp.where(upper, 0, deep - TILE))
    inno_at = tile_at(jnp.where(upper, 0, half - TILE))
    for first in range(0, nblocks, PACK):
        back, inno = [], []
        for k in range(first, first + PACK):
            here = pl.ds(k * LANES, LANES)
            back.append(back_buf[:, back_at, here].reshape(levels * TILE, LANES))
            inno.append(inno_buf[:, inno_at, here].reshape(levels * TILE, LANES))
        tile = dot(of_back, jnp.concatenate(back, axis=0)) + dot(of_inno, jnp.concatenate(inno, axis=0))
        msg_ref[pl.ds(at, PACK * kinds), :] = tile.astype(BF16)
        at += PACK * kinds
    near.wait()
    shape = (TILE, levels * TILE)
    pick = one_hot(iota(shape, 1) == iota(shape, 0) * TILE + jnp.where(upper, TILE - 1, 0))
    row_ref[...] = dot(pick, row_buf[...].reshape(levels * TILE, -1)).astype(BF16)


def outer_rows(rows, nblocks, levels):
    return nblocks * rows + (nblocks * LANES // SPAN) * (rows >> SHIFT_Y) + nblocks * 3 * levels


def inner_kernel(lw_ref, inno_ref, back_ref, row_ref, band_ref, *refs):
    raw_refs = refs[PIECES : 2 * PIECES]
    msg_ref, high_ref, low_ref = refs[2 * PIECES :]
    levels, rows, width = inno_ref.shape
    half = rows // 2
    nblocks = width // LANES
    upper = parity() == 1
    start = jnp.where(upper, 0, half)
    diff_y, diff_x = differences(upper, half)
    at = iota((half, 2 * LANES), 0) == jnp.where(upper, 0, half - 1)
    sign = jnp.where(upper, -1.0, 1.0)

    def extra(level, here):
        return jnp.where(at, row_ref[level : level + 1, here].astype(F32) * sign, 0.0)

    inno = inno_ref.at[:, pl.ds(pl.multiple_of(start, TILE), half), :]
    back = (upper, back_ref, jnp.where(upper, 0, half - TILE))
    for first in range(0, nblocks, 2):
        pair = raw_pair(first, lw_ref, inno, back, diff_y, diff_x, extra)
        for comp, raw in enumerate(pair):
            high, low = split(raw)
            for j in range(2):
                cols = slice(j * LANES, (j + 1) * LANES)
                here = pl.ds(pl.multiple_of(comp * rows + start, 8), half)
                block_of(raw_refs, first + j)[here, :] = raw[:, cols]
                here = pl.ds(comp * half, half)
                high_ref[first + j, here, :], low_ref[first + j, here, :] = high[:, cols], low[:, cols]
    groups = rows >> SHIFT_Z
    shape = (2 * groups, rows)
    sum_y = one_hot(iota(shape, 1) >> SHIFT_Z == iota(shape, 0))
    sums = []
    for first in range(0, nblocks, 2):
        high, low = split(smooth_x(band_ref, high_ref, low_ref, first, nblocks))
        sums.append(dot(sum_y, low)[:groups])
        for j in range(2):
            msg_ref[pl.ds((first + j) * rows, rows), :] = high[:, j * LANES : (j + 1) * LANES]
    per = TILE // (2 * groups)
    for first in range(0, len(sums), per):
        parts = [s[:, j * LANES : (j + 1) * LANES] for j in range(2) for s in sums[first : first + per]]
        at = nblocks * rows + first // per * TILE
        msg_ref[pl.ds(at, TILE), :] = jnp.concatenate(parts, axis=0).astype(BF16)


def inner_rows(rows, nblocks):
    return nblocks * rows + nblocks * (rows >> SHIFT_Z)


def outermost_kernel(lw_ref, own_ref, got_ref, out_ref):
    nblocks = out_ref.shape[1] // LANES
    levels = lw_ref.shape[0]
    kinds = 3 * levels
    base = own_ref.shape[0] - nblocks * kinds

    def unpacked(ref):
        packs = [ref[pl.ds(base + k * kinds, PACK * kinds), :].astype(F32) for k in range(0, nblocks, PACK)]
        return [
            jnp.concatenate(
                [p[j * kinds + kind * levels : j * kinds + (kind + 1) * levels] for p in packs for j in range(PACK)], axis=1
            )
            for kind in range(3)
        ]

    own, got = unpacked(own_ref), unpacked(got_ref)
    here = jnp.concatenate([own[0], got[0]], axis=0)
    beyond = jnp.concatenate([got[0], own[0]], axis=0)
    before = jnp.concatenate([own[1], got[1]], axis=0)
    inno = jnp.concatenate([own[2], got[2]], axis=0)
    shape = here.shape
    first_core = parity() == 0
    grad_y = jnp.where((iota(shape, 0) < levels) == first_core, before - beyond, beyond - before)
    lane = iota(shape, 1)
    left = jnp.where(lane == 0, 0.0, pltpu.roll(here, 1, 1))
    right = jnp.where(lane == shape[1] - 1, 0.0, pltpu.roll(here, shape[1] - 1, 1))
    grad_x = right - left
    row = iota((2 * levels, 1), 0)
    weight = jnp.zeros((2 * levels, 1), F32)
    for level in range(levels):
        weight = jnp.where(row % levels == level, lw_ref[level], weight)
    scaled = inno * (0.5 * weight)

    def total(values):
        return [sum(values[k : k + 1] for k in range(f, f + levels)) for f in (0, levels)]

    numer_y, numer_x = total(scaled * grad_y), total(scaled * grad_x)
    denom = total((0.25 * weight) * (grad_y * grad_y + grad_x * grad_x))
    for k in range(2):
        inverse = 1.0 / (1.0 + denom[k])
        out_ref[2 * k : 2 * k + 1, :] = numer_y[k] * inverse
        out_ref[2 * k + 1 : 2 * k + 2, :] = numer_x[k] * inverse


def far_taps(rows, towards):
    side = 2 * parity() - 1
    half = rows // 2
    start = jnp.where((side < 0) == towards, half, 0)
    return taps(iota((rows, half), 1) + start - iota((rows, half), 0) + side * rows)


def near_kernel(*refs):
    raw_refs, near_refs = refs[:PIECES], refs[PIECES : 2 * PIECES]
    edges_ref, near_edges_ref, msg_ref, band_ref, out_ref, high_ref, low_ref = refs[2 * PIECES :]
    _, rows, width = out_ref.shape
    nblocks = width // LANES
    half = rows // 2
    par = parity()
    side = 1 - 2 * par
    offset = iota((rows, rows), 1) - iota((rows, rows), 0)
    near_high, near_low = split(jnp.concatenate([taps(offset), taps(offset + side * rows)], axis=1))
    near_two = jnp.concatenate([near_high, near_low], axis=0)
    far_high, far_low = split(far_taps(rows, True))
    far_two = jnp.concatenate([far_high, far_low], axis=0)
    groups = half >> SHIFT_Y
    shape = (half, groups)
    mean_y = one_hot(iota(shape, 0) >> SHIFT_Y == iota(shape, 1), 1.0 / (1 << SHIFT_Y))
    group_taps = dot(far_high, mean_y).astype(BF16)
    shape = (LANES, SPAN)
    mean_x = one_hot(iota(shape, 1) >> SHIFT_X == iota(shape, 0), 1.0 / (1 << SHIFT_X))
    rest = []
    for span in range(width // SPAN):
        tile = msg_ref[pl.ds(nblocks * rows + span * 2 * groups, 2 * groups), :]
        rest.append(jnp.concatenate([dot(group_taps, tile[:groups]), dot(group_taps, tile[groups:])], axis=0).astype(BF16))
    column = iota((rows, 2 * LANES), 0)
    own_taps = taps(jnp.where(par == 0, 0, rows - 1) - column)
    far_edge_taps = taps(jnp.where(par == 0, -1, rows) - column)
    near_edge_taps = taps(jnp.where(par == 0, 2 * rows - 1, -rows) - column)
    done = 0
    for first in range(0, nblocks, 2):
        while done < min(first + 3, nblocks):
            cols = pl.ds(done * LANES, 2 * LANES)
            place = done * LANES % SPAN
            spread = dot(rest[done * LANES // SPAN], mean_x[:, place : place + 2 * LANES])
            for comp in range(2):
                here = pl.ds(comp * rows, rows)
                pairs, got = [], []
                for k in (done, done + 1):
                    pairs.append(jnp.concatenate([block_of(raw_refs, k)[here, :], block_of(near_refs, k)[here, :]], axis=0))
                    got.append(msg_ref[pl.ds(k * rows + comp * half, half), :])
                high, low = split(jnp.concatenate(pairs, axis=1))
                part = dot(near_two, high) + dot(far_two, jnp.concatenate(got, axis=1))
                part = part[:rows] + part[rows:] + dot(near_high, low) + spread[comp * rows : (comp + 1) * rows]
                part += own_taps * edges_ref[comp : comp + 1, cols]
                part += far_edge_taps * edges_ref[2 + comp : 3 + comp, cols]
                part += near_edge_taps * near_edges_ref[comp : comp + 1, cols]
                high, low = split(part)
                for j in range(2):
                    cut = slice(j * LANES, (j + 1) * LANES)
                    high_ref[done + j, here, :], low_ref[done + j, here, :] = high[:, cut], low[:, cut]
            done += 2
        result = smooth_x(band_ref, high_ref, low_ref, first, nblocks)
        here = pl.ds(first * LANES, 2 * LANES)
        out_ref[0, :, here] = result[:rows]
        out_ref[1, :, here] = result[rows:]


def last_kernel(part_ref, msg_ref, out_hbm, buf, sem):
    _, rows, width = part_ref.shape
    nblocks = width // LANES
    half = rows // 2
    high, low = split(far_taps(rows, False))
    two = jnp.concatenate([high, low], axis=0)
    groups = rows >> SHIFT_Z
    per = TILE // (2 * groups)
    shape = (rows, groups)
    mean_y = one_hot(iota((half, groups), 0) >> SHIFT_Z == iota((half, groups), 1), 1.0 / (1 << SHIFT_Z))
    mean_other = one_hot((iota((half, groups), 0) >> SHIFT_Z) + groups // 2 == iota((half, groups), 1), 1.0 / (1 << SHIFT_Z))
    group_taps = jnp.concatenate([dot(high, mean_y), dot(high, mean_other)], axis=0).astype(BF16)
    copies = []
    for index, first in enumerate(range(0, nblocks, 2)):
        here = pl.ds(first * LANES, 2 * LANES)
        tile = msg_ref[pl.ds(nblocks * rows + index // per * TILE, TILE), :].astype(F32)
        slot = index % per
        sums = [tile[(j * per + slot) * groups : (j * per + slot + 1) * groups] for j in range(2)]
        rest = dot(group_taps, jnp.concatenate(sums, axis=1).astype(BF16))
        for comp in range(2):
            got = [msg_ref[pl.ds((first + j) * rows + comp * half, half), :] for j in range(2)]
            part = dot(two, jnp.concatenate(got, axis=1))
            part = part[:rows] + part[rows:] + rest[comp * rows : (comp + 1) * rows]
            buf[comp, :, here] = part_ref[comp, :, here] + part
        copy = pltpu.make_async_copy(buf.at[:, :, here], out_hbm.at[:, :, here], sem.at[index])
        copy.start()
        copies.append(copy)
    for copy in copies:
        copy.wait()


def body(innovation, background, level_weight):
    levels, rows, width = innovation.shape
    if rows != HALF or width % SPAN or levels != 4:
        raise NotImplementedError("slab shape")
    nblocks = width // LANES
    both, half = 2 * rows, rows // 2
    count = lax.axis_size("row")
    chip = [(i, i ^ 1) for i in range(count) if i ^ 1 < count]
    away = [(i, j) for i in range(count) for j in [((i + 1) ^ 1) - 1] if 0 <= j < count]
    hbm = [pltpu.with_memory_space_constraint(x, pltpu.HBM) for x in (level_weight, innovation, background)]
    band = jnp.asarray(zonal_band())
    piece = jax.ShapeDtypeStruct((nblocks // PIECES, both, LANES), F32)
    result = jax.ShapeDtypeStruct((2, rows, width), F32)
    *raws, outer, row = pl.pallas_call(
        outer_kernel,
        out_shape=[piece] * PIECES
        + [
            jax.ShapeDtypeStruct((outer_rows(rows, nblocks, levels), LANES), BF16),
            jax.ShapeDtypeStruct((TILE, width), BF16),
        ],
        in_specs=[HBM] * 3,
        out_specs=[VMEM] * (PIECES + 2),
        scratch_shapes=[
            pltpu.SMEM((levels,), F32),
            pltpu.VMEM((levels, half, width), BF16),
            pltpu.VMEM((levels, half + TILE, width), BF16),
            pltpu.VMEM((rows, width), BF16),
            pltpu.VMEM((levels, TILE, width), BF16),
            pltpu.SemaphoreType.DMA((2, QUARTERS)),
            pltpu.SemaphoreType.DMA,
            pltpu.SemaphoreType.DMA,
        ],
        compiler_params=PARAMS,
        name="outer_half",
    )(*hbm)
    outer_got = lax.ppermute(outer, "row", away)
    row = lax.ppermute(row, "row", chip)
    *raws, inner = pl.pallas_call(
        inner_kernel,
        out_shape=[piece] * PIECES + [jax.ShapeDtypeStruct((inner_rows(rows, nblocks), LANES), BF16)],
        in_specs=[SMEM] + [VMEM] * (4 + PIECES),
        out_specs=[VMEM] * (PIECES + 1),
        scratch_shapes=[pltpu.VMEM((nblocks, rows, LANES), BF16)] * 2,
        input_output_aliases={5 + k: k for k in range(PIECES)},
        compiler_params=PARAMS,
        name="inner_half",
    )(level_weight, innovation, background, row, band, *raws)
    inner_got = lax.ppermute(inner, "row", away)
    nears = [lax.ppermute(r, "row", chip) for r in raws]
    edges = pl.pallas_call(
        outermost_kernel,
        out_shape=jax.ShapeDtypeStruct((4, width), F32),
        in_specs=[SMEM] + [VMEM] * 2,
        out_specs=VMEM,
        compiler_params=PARAMS,
        name="outermost_rows",
    )(level_weight, outer, outer_got)
    near_edges = lax.ppermute(edges, "row", chip)
    part = pl.pallas_call(
        near_kernel,
        out_shape=result,
        in_specs=[VMEM] * (2 * PIECES + 4),
        out_specs=VMEM,
        scratch_shapes=[pltpu.VMEM((nblocks, both, LANES), BF16)] * 2,
        compiler_params=PARAMS,
        name="near_part",
    )(*raws, *nears, edges, near_edges, outer_got, band)
    return pl.pallas_call(
        last_kernel,
        out_shape=result,
        in_specs=[VMEM] * 2,
        out_specs=HBM,
        scratch_shapes=[pltpu.VMEM((2, rows, width), F32), pltpu.SemaphoreType.DMA((nblocks // 2,))],
        compiler_params=PARAMS,
        name="last_part",
    )(part, inner_got)


def solution(mesh):
    placed = (P("member", "row", None), P("member", "row", None), P())
    return jax.shard_map(
        body, mesh=mesh, in_specs=placed, out_specs=P("member", "row", None), check_vma=False
    )
```

time: 95.8 us -> 26.3 us (0.27)
  blocking collectives: 60.7 us -> 0 us
  Pallas kernels: 0 us -> 11.2 us
  local copies, waits for them, and re-layouts: 11.2 us -> 1.7 us
  other arithmetic: 8.24 us -> 0 us
  matrix products: 6.23 us -> 0 us
  starting transfers between devices: 5.63 us -> 8.47 us
  waiting for transfers between devices: 1.97 us -> 4.59 us
    all_to_all x2 -> x0, blocking collectives: 60.7 us -> none  [the longest x1 31.1 us: body(): lax.all_to_all(zonal, 'row', split_axis=2, concat_axis=1, tiled=True)]
    pallas_call x0 -> x5, Pallas kernels: none -> 11.2 us  [the longest x1 3.75 us: body(): pl.pallas_call(inner_kernel, out_shape=[piece] * PIECES + [jax.ShapeDtype...]
    dot_general x6 -> x0, matrix products: 6.23 us -> none  [the longest x3 3.21 us: smooth_mid(): jnp.einsum('cbix,io->cbox', part, blocks[index], precision=lax.Precision....]
    reduce_sum x2 -> x0, other arithmetic: 3.3 us -> none  [the longest x1 2.69 us: body(): numer_y = jnp.sum(scaled * grad_y, axis=0)]
    all_to_all x4 -> x0, local copies, waits for them, and re-layouts: 3.18 us -> none  [the longest x2 1.74 us: body(): lax.all_to_all(smoothed, 'row', split_axis=1, concat_axis=2, tiled=True)]
    all_to_all x1 -> x0, other arithmetic: 3.15 us -> none  [body(): lax.all_to_all(zonal, 'row', split_axis=2, concat_axis=1, tiled=True)]
    unnamed x6 -> x10, local copies, waits for them, and re-layouts: 4.65 us -> 1.7 us
    ppermute x2 -> x8, starting transfers between devices: 5.63 us -> 8.47 us  [the longest x1 3.71 us: body(): outer_got = lax.ppermute(outer, 'row', away)]
  transfers between devices with their start and end apart: 2 -> 8, of which waited for: 1 -> 5; matrix products, arithmetic and copies ran while one was open for 1% -> 0% of each run, Pallas kernels for 0% -> 26%
where the time goes in v4:
time: 26.3 us; the launch traced here: 26 us
  Pallas kernels  11.2 us (43%)
  starting transfers between devices  8.47 us (32%)
  waiting for transfers between devices  4.59 us (17%)
  local copies, waits for them, and re-layouts  1.7 us (6%)
    pallas_call x1, Pallas kernels, body(): pl.pallas_call(inner_kernel, out_shape=[piece] * PIECES + [jax.ShapeDtype...  3.75 us
    ppermute x1, starting transfers between devices, body(): outer_got = lax.ppermute(outer, 'row', away)  3.71 us
    ppermute x1, starting transfers between devices, body(): inner_got = lax.ppermute(inner, 'row', away)  3.37 us
    pallas_call x1, Pallas kernels, body(): pl.pallas_call(outer_kernel, out_shape=[piece] * PIECES + [jax.ShapeDtype...  3.04 us
    ppermute x1, waiting for transfers between devices, body(): inner_got = lax.ppermute(inner, 'row', away)  2.48 us
    pallas_call x1, Pallas kernels, body(): pl.pallas_call(near_kernel, out_shape=result, in_specs=[VMEM] * (2 * PIEC...  2.23 us
    unnamed x10, local copies, waits for them, and re-layouts  1.7 us
    pallas_call x1, Pallas kernels, body(): pl.pallas_call(last_kernel, out_shape=result, in_specs=[VMEM] * 2, out_sp...  1.46 us
  transfers between devices with their start and end apart: 8, of which 5 were waited for; matrix products, arithmetic and copies ran while one was open for 0% of the time, Pallas kernels for 26%

profile of v4, /device:TPU:11, one launch (start us, length us, event | category | flops | bytes accessed | tf_op | source)
XLA Modules:
  0.0 26.0 jit_solution(2627679717498643675)
XLA Ops:
  0.0 0.0 copy-start.1
  0.0 0.0 copy-start
  0.0 3.0 %outer_half.1 = (f32[4,128,128]{2,1,0:T(8,128)S(1)}, f32[4,128,128]{2,1,0:T(8,128)S(1)}, f32[4,128,128]{2,1,0:T(8,128)S(1)}, f32[4,128,128]{2,1,0:T(8,128)S(1)},...) custom-call(f32[4]{0:T(128)} %lw_ref.3, bf16[4,64,2048]{2,1,0:T(8,128)(2,1)} %inno_ref.1, ...), custom_call_target="tpu_custom_call" | custom-call | tf_op jit(solution)/shard_map/outer_half/pallas_call | solution.py:407
  3.0 3.7 %collective-permute-start.5 = (bf16[1248,128]{1,0:T(8,128)(2,1)S(1)}, bf16[1248,128]{1,0:T(8,128)(2,1)S(1)}, u32[]{:S(2)}, u32[]{:S(2)}) collective-permute-start(bf16[1248,128]{1,0:T(8,128)(2,1)S(1)} %get-tuple-element.25.own_ref), channel_id=1, source_target_pairs={{1,2},{2,1},{3,4},{4,3},{5,6},{6,5},{7,8},{8,7},{9,10},{10,9},{11,... | collective-permute-start | bytes 958472 | tf_op jit(solution)/shard_map/ppermute | solution.py:429
  6.8 0.1 collective-permute-start
  6.8 1.2 %collective-permute-done.row_ref = bf16[16,2048]{1,0:T(8,128)(2,1)S(1)} collective-permute-done((bf16[16,2048]{1,0:T(8,128)(2,1)S(1)}, bf16[16,2048]{1,0:T(8,128)(2,1)S(1)}, u32[]{:S(2)}, u32[]{:S(2)}) %collective-permute-start) | collective-permute-done | bytes 65568 | tf_op jit(solution)/shard_map/ppermute | solution.py:430
  8.1 0.0 copy-start.4
  8.1 0.0 copy-done.1
  8.1 0.0 copy-done
  8.1 0.6 %copy-done.4 = f32[4]{0:T(128)S(1)} copy-done((f32[4]{0:T(128)S(1)}, f32[4]{0:T(128)}, u32[]{:S(2)}) %copy-start.4) | copy-done | bytes 40
  8.7 0.0 copy-start.2
  8.7 1.0 %copy-done.2 = bf16[2,512,256]{2,1,0:T(8,128)(2,1)S(1)} copy-done((bf16[2,512,256]{2,1,0:T(8,128)(2,1)S(1)}, bf16[2,512,256]{2,1,0:T(8,128)(2,1)}, u32[]{:S(2)}) %copy-start.2) | copy-done | bytes 524312
  9.8 3.8 %inner_half.1 = (f32[4,128,128]{2,1,0:T(8,128)S(1)}, f32[4,128,128]{2,1,0:T(8,128)S(1)}, f32[4,128,128]{2,1,0:T(8,128)S(1)}, f32[4,128,128]{2,1,0:T(8,128)S(1)}, bf16[1088,128]{1,0:T(8,128)(2,1)S(1)}) custom-call(f32[4]{0:T(128)S(1)} %copy-done.4, ...), custom_call_target="tpu_custom_call", output_to_operand_aliasing={{0}: (5, {}), {1}: (6, {}), {2}: (7, {}), {3}: (8, {})} | custom-call | tf_op jit(solution)/shard_map/inner_half/pallas_call | solution.py:431
  13.5 0.0 copy-start.3
  13.5 0.2 collective-permute-start.1
  13.7 3.4 %collective-permute-start.7 = (bf16[1088,128]{1,0:T(8,128)(2,1)S(1)}, bf16[1088,128]{1,0:T(8,128)(2,1)S(1)}, u32[]{:S(2)}, u32[]{:S(2)}) collective-permute-start(bf16[1088,128]{1,0:T(8,128)(2,1)S(1)} %get-tuple-element.26), channel_id=1, source_target_pairs={{1,2},{2,1},{3,4},{4,3},{5,6},{6,5},{7,8},{8,7},{9,10},{10,9},{11,... | collective-permute-start | bytes 835592 | tf_op jit(solution)/shard_map/ppermute | solution.py:441
  17.1 0.1 collective-permute-start.2
  17.2 0.5 %collective-permute-start.3 = (f32[4,128,128]{2,1,0:T(8,128)S(1)}, f32[4,128,128]{2,1,0:T(8,128)S(1)}, u32[]{:S(2)}, u32[]{:S(2)}) collective-permute-start(f32[4,128,128]{2,1,0:T(8,128)S(1)} %get-tuple-element.23.refs_2_), channel_id=1, source_target_pairs={{0,1},{1,0},{2,3},{3,2},{4,5},{5,4},{6,7},{7,6},{8,9},{9,8},{10,11... | collective-permute-start | bytes 786440 | tf_op jit(solution)/shard_map/ppermute | solution.py:442
  17.7 0.0 collective-permute-done.5.got_ref.refs_10_
  17.7 0.1 collective-permute-start.4
  17.7 0.7 %outermost_rows.1.refs_8_ = f32[4,2048]{1,0:T(4,128)S(1)} custom-call(f32[4]{0:T(128)S(1)} %copy-done.4, bf16[1248,128]{1,0:T(8,128)(2,1)S(1)} %get-tuple-element.25.own_ref, bf16[1248,128]{1,0:T(8,128)(2,1)S(1)} %collective-permute-done.5.got_ref.refs_10_), custom_call_target="tpu_custom_call" | custom-call | tf_op jit(solution)/shard_map/outermost_rows/pallas_call | solution.py:443
  18.4 0.0 collective-permute-done.1.refs_4_
  18.5 0.5 %collective-permute-start.6 = (f32[4,2048]{1,0:T(4,128)S(1)}, f32[4,2048]{1,0:T(4,128)S(1)}, u32[]{:S(2)}, u32[]{:S(2)}) collective-permute-start(f32[4,2048]{1,0:T(4,128)S(1)} %outermost_rows.1.refs_8_), channel_id=1, source_target_pairs={{0,1},{1,0},{2,3},{3,2},{4,5},{5,4},{6,7},{7,6},{8,9},{9,8},{10,11... | collective-permute-start | bytes 98312 | tf_op jit(solution)/shard_map/ppermute | solution.py:451
  19.0 0.0 collective-permute-done.2.refs_5_
  19.0 0.1 collective-permute-done.3.refs_6_
  19.1 0.4 %collective-permute-done.4.refs_7_ = f32[4,128,128]{2,1,0:T(8,128)S(1)} collective-permute-done((f32[4,128,128]{2,1,0:T(8,128)S(1)}, f32[4,128,128]{2,1,0:T(8,128)S(1)}, u32[]{:S(2)}, u32[]{:S(2)}) %collective-permute-start.4) | collective-permute-done | bytes 262176 | tf_op jit(solution)/shard_map/ppermute | solution.py:442
  19.4 0.4 %collective-permute-done.6.refs_9_ = f32[4,2048]{1,0:T(4,128)S(1)} collective-permute-done((f32[4,2048]{1,0:T(4,128)S(1)}, f32[4,2048]{1,0:T(4,128)S(1)}, u32[]{:S(2)}, u32[]{:S(2)}) %collective-permute-start.6) | collective-permute-done | bytes 32800 | tf_op jit(solution)/shard_map/ppermute | solution.py:451
  19.8 0.0 copy-done.3
  19.8 2.2 %near_part.1.part_ref = f32[2,64,2048]{2,1,0:T(8,128)S(1)} custom-call(f32[4,128,128]{2,1,0:T(8,128)S(1)} %get-tuple-element.21.refs_0_, f32[4,128,128]{2,1,0:T(8,128)S(1)} %get-tuple-element.22.refs_1_, f32[4,128,128]{2,1,0:T(8,128)S(1)} %get-tuple-element.23.refs_2_, f32[4,128,128]{2,1,0:T(8,128)S(1)} %get-tuple-element.24.refs_3_, ...), custom_call_target="tpu_custom_call" | custom-call | tf_op jit(solution)/shard_map/near_part/pallas_call | solution.py:452
  22.1 2.5 %collective-permute-done.7.msg_ref = bf16[1088,128]{1,0:T(8,128)(2,1)S(1)} collective-permute-done((bf16[1088,128]{1,0:T(8,128)(2,1)S(1)}, bf16[1088,128]{1,0:T(8,128)(2,1)S(1)}, u32[]{:S(2)}, u32[]{:S(2)}) %collective-permute-start.7) | collective-permute-done | bytes 278560 | tf_op jit(solution)/shard_map/ppermute | solution.py:441
  24.5 1.5 %last_part.1 = f32[2,64,2048]{2,1,0:T(8,128)} custom-call(f32[2,64,2048]{2,1,0:T(8,128)S(1)} %near_part.1.part_ref, bf16[1088,128]{1,0:T(8,128)(2,1)S(1)} %collective-permute-done.7.msg_ref), custom_call_target="tpu_custom_call" | custom-call | tf_op jit(solution)/shard_map/last_part/pallas_call | solution.py:461
Async XLA Ops:
  0.0 8.1 %copy-start.1 = (bf16[4,64,2048]{2,1,0:T(8,128)(2,1)S(1)}, bf16[4,64,2048]{2,1,0:T(8,128)(2,1)}, u32[]{:S(2)}) copy-start(bf16[4,64,2048]{2,1,0:T(8,128)(2,1)} %back_ref.1) | copy-start | bytes 3145732
  0.0 8.1 %copy-start = (bf16[4,64,2048]{2,1,0:T(8,128)(2,1)S(1)}, bf16[4,64,2048]{2,1,0:T(8,128)(2,1)}, u32[]{:S(2)}) copy-start(bf16[4,64,2048]{2,1,0:T(8,128)(2,1)} %inno_ref.1) | copy-start | bytes 3145732
  3.0 14.6 %collective-permute-start.5 = (bf16[1248,128]{1,0:T(8,128)(2,1)S(1)}, bf16[1248,128]{1,0:T(8,128)(2,1)S(1)}, u32[]{:S(2)}, u32[]{:S(2)}) collective-permute-start(bf16[1248,128]{1,0:T(8,128)(2,1)S(1)} %get-tuple-element.25.own_ref), channel_id=1, source_target_pairs={{1,2},{2,1},{3,4},{4,3},{5,6},{6,5},{7,8},{8,7},{9,10},{10,9},{11,... | collective-permute-start | bytes 958472 | tf_op jit(solution)/shard_map/ppermute | solution.py:429
  6.8 1.3 %collective-permute-start = (bf16[16,2048]{1,0:T(8,128)(2,1)S(1)}, bf16[16,2048]{1,0:T(8,128)(2,1)S(1)}, u32[]{:S(2)}, u32[]{:S(2)}) collective-permute-start(bf16[16,2048]{1,0:T(8,128)(2,1)S(1)} %get-tuple-element.16), channel_id=1, source_target_pairs={{0,1},{1,0},{2,3},{3,2},{4,5},{5,4},{6,7},{7,6},{8,9},{9,8},{10,11... | collective-permute-start | bytes 196616 | tf_op jit(solution)/shard_map/ppermute | solution.py:430
  8.1 0.7 %copy-start.4 = (f32[4]{0:T(128)S(1)}, f32[4]{0:T(128)}, u32[]{:S(2)}) copy-start(f32[4]{0:T(128)} %lw_ref.3) | copy-start | bytes 52
  8.7 1.0 %copy-start.2 = (bf16[2,512,256]{2,1,0:T(8,128)(2,1)S(1)}, bf16[2,512,256]{2,1,0:T(8,128)(2,1)}, u32[]{:S(2)}) copy-start(bf16[2,512,256]{2,1,0:T(8,128)(2,1)} %constant.2.clone.band_ref.refs_11_) | copy-start | bytes 1572868
  13.5 6.3 %copy-start.3 = (bf16[2,512,256]{2,1,0:T(8,128)(2,1)S(1)}, bf16[2,512,256]{2,1,0:T(8,128)(2,1)}, u32[]{:S(2)}) copy-start(bf16[2,512,256]{2,1,0:T(8,128)(2,1)} %constant.2.clone.band_ref.refs_11_) | copy-start | bytes 1572868
  13.5 4.9 %collective-permute-start.1 = (f32[4,128,128]{2,1,0:T(8,128)S(1)}, f32[4,128,128]{2,1,0:T(8,128)S(1)}, u32[]{:S(2)}, u32[]{:S(2)}) collective-permute-start(f32[4,128,128]{2,1,0:T(8,128)S(1)} %get-tuple-element.21.refs_0_), channel_id=1, source_target_pairs={{0,1},{1,0},{2,3},{3,2},{4,5},{5,4},{6,7},{7,6},{8,9},{9,8},{10,11... | collective-permute-start | bytes 786440 | tf_op jit(solution)/shard_map/ppermute | solution.py:442
  13.7 10.8 %collective-permute-start.7 = (bf16[1088,128]{1,0:T(8,128)(2,1)S(1)}, bf16[1088,128]{1,0:T(8,128)(2,1)S(1)}, u32[]{:S(2)}, u32[]{:S(2)}) collective-permute-start(bf16[1088,128]{1,0:T(8,128)(2,1)S(1)} %get-tuple-element.26), channel_id=1, source_target_pairs={{1,2},{2,1},{3,4},{4,3},{5,6},{6,5},{7,8},{8,7},{9,10},{10,9},{11,... | collective-permute-start | bytes 835592 | tf_op jit(solution)/shard_map/ppermute | solution.py:441
  17.1 1.9 %collective-permute-start.2 = (f32[4,128,128]{2,1,0:T(8,128)S(1)}, f32[4,128,128]{2,1,0:T(8,128)S(1)}, u32[]{:S(2)}, u32[]{:S(2)}) collective-permute-start(f32[4,128,128]{2,1,0:T(8,128)S(1)} %get-tuple-element.22.refs_1_), channel_id=1, source_target_pairs={{0,1},{1,0},{2,3},{3,2},{4,5},{5,4},{6,7},{7,6},{8,9},{9,8},{10,11... | collective-permute-start | bytes 786440 | tf_op jit(solution)/shard_map/ppermute | solution.py:442
  17.2 1.9 %collective-permute-start.3 = (f32[4,128,128]{2,1,0:T(8,128)S(1)}, f32[4,128,128]{2,1,0:T(8,128)S(1)}, u32[]{:S(2)}, u32[]{:S(2)}) collective-permute-start(f32[4,128,128]{2,1,0:T(8,128)S(1)} %get-tuple-element.23.refs_2_), channel_id=1, source_target_pairs={{0,1},{1,0},{2,3},{3,2},{4,5},{5,4},{6,7},{7,6},{8,9},{9,8},{10,11... | collective-permute-start | bytes 786440 | tf_op jit(solution)/shard_map/ppermute | solution.py:442
  17.7 1.8 %collective-permute-start.4 = (f32[4,128,128]{2,1,0:T(8,128)S(1)}, f32[4,128,128]{2,1,0:T(8,128)S(1)}, u32[]{:S(2)}, u32[]{:S(2)}) collective-permute-start(f32[4,128,128]{2,1,0:T(8,128)S(1)} %get-tuple-element.24.refs_3_), channel_id=1, source_target_pairs={{0,1},{1,0},{2,3},{3,2},{4,5},{5,4},{6,7},{7,6},{8,9},{9,8},{10,11... | collective-permute-start | bytes 786440 | tf_op jit(solution)/shard_map/ppermute | solution.py:442
  18.5 1.4 %collective-permute-start.6 = (f32[4,2048]{1,0:T(4,128)S(1)}, f32[4,2048]{1,0:T(4,128)S(1)}, u32[]{:S(2)}, u32[]{:S(2)}) collective-permute-start(f32[4,2048]{1,0:T(4,128)S(1)} %outermost_rows.1.refs_8_), channel_id=1, source_target_pairs={{0,1},{1,0},{2,3},{3,2},{4,5},{5,4},{6,7},{7,6},{8,9},{9,8},{10,11... | collective-permute-start | bytes 98312 | tf_op jit(solution)/shard_map/ppermute | solution.py:451

commit v5 on v4

v5 whole, which is shorter than its diff:
```python
import math

import jax
import jax.numpy as jnp
import numpy as np
from jax import lax
from jax.experimental import pallas as pl
from jax.experimental.pallas import tpu as pltpu
from jax.sharding import PartitionSpec as P

HALF = 64
SIGMA = 64
LANES = 128
TILE = 16
SHIFT_Y, SHIFT_X, SHIFT_Z = 2, 3, 4
SPAN = LANES << SHIFT_X
PACK = 4
QUARTERS = 4
PIECES = 4
F32 = jnp.float32
BF16 = jnp.bfloat16
NORM = math.sqrt(sum(math.exp(-k * k / (SIGMA * SIGMA)) for k in range(-HALF, HALF + 1)))

VMEM = pl.BlockSpec(memory_space=pltpu.VMEM)
HBM = pl.BlockSpec(memory_space=pltpu.HBM)
PARAMS = pltpu.CompilerParams(vmem_limit_bytes=40 * 1024 * 1024)


def split(values):
    high = values.astype(BF16)
    return high, (values - high.astype(F32)).astype(BF16)


def dot(left, right):
    return jnp.dot(left, right, preferred_element_type=F32)


def iota(shape, dim):
    return lax.broadcasted_iota(jnp.int32, shape, dim)


def one_hot(mask, value=1.0):
    return jnp.where(mask, value, 0.0).astype(BF16)


def difference(off):
    return (jnp.where(off == 1, 1.0, 0.0) - jnp.where(off == -1, 1.0, 0.0)).astype(BF16)


def taps(offset):
    off = offset.astype(F32)
    value = jnp.exp(off * off * (-0.5 / (SIGMA * SIGMA))) * (1.0 / NORM)
    return jnp.where(jnp.abs(offset) <= HALF, value, 0.0)


def zonal_band():
    offset = np.arange(4 * LANES)[:, None] - LANES - np.arange(2 * LANES)[None, :]
    band = np.exp(-offset * offset / (2.0 * SIGMA * SIGMA)) / NORM
    band = np.where(np.abs(offset) <= HALF, band, 0.0).astype(np.float32)
    high = band.astype(BF16)
    return np.stack([high, (band - high.astype(np.float32)).astype(BF16)])


def window(first, nblocks):
    low, high = max(first - 1, 0), min(first + 3, nblocks)
    return low, high, (low - first + 1) * LANES, (high - first + 1) * LANES


def smooth_x(band_ref, load, first, nblocks):
    low, high, top, bottom = window(first, nblocks)
    both = jnp.concatenate([load(k) for k in range(low, high)], axis=1)
    rows = both.shape[0] // 2
    found = dot(both, band_ref[0, top:bottom, :])
    return found[:rows] + found[rows:] + dot(both[:rows], band_ref[1, top:bottom, :])


def parity():
    return lax.rem(lax.axis_index("row"), 2)


def block_of(refs, k):
    per = refs[0].shape[0]
    return refs[k // per].at[k % per]


def tile_at(row):
    return pl.ds(pl.multiple_of(row, TILE), TILE)


def half_of(ref, comp_rows, start, part):
    half = comp_rows // 2
    return [ref[part, pl.ds(pl.multiple_of(comp * comp_rows + start, TILE), half), :] for comp in range(2)]


def raw_pair(first, weight, inno_ref, back_ref, upper, diff_y, diff_x, extra, raw_refs):
    levels, rows, width = inno_ref.shape
    half = rows // 2
    start = pl.multiple_of(jnp.where(upper, 0, half), TILE)
    exact = pl.ds(start, half)
    deep = pl.ds(pl.multiple_of(jnp.where(upper, 0, half - TILE), TILE), half + TILE)
    here = pl.ds(first * LANES, 2 * LANES)
    low, high, top, bottom = window(first, width // LANES)
    around = back_ref[:, exact, low * LANES : high * LANES]
    grad_xs = dot(around.reshape(levels * half, -1), diff_x[top:bottom])
    numer_y = numer_x = 0.0
    denom = 1.0
    for level in range(levels):
        grad_y = dot(diff_y, back_ref[level, deep, here])
        if extra is not None:
            grad_y += extra(level, here)
        grad_x = grad_xs[level * half : (level + 1) * half]
        scaled = inno_ref[level, exact, here].astype(F32) * (0.5 * weight(level))
        numer_y += scaled * grad_y
        numer_x += scaled * grad_x
        denom += (0.25 * weight(level)) * (grad_y * grad_y + grad_x * grad_x)
    inverse = 1.0 / denom
    found = []
    for comp, numer in enumerate((numer_y, numer_x)):
        raw = numer * inverse
        if extra is None:
            raw = jnp.where(iota(raw.shape, 0) == jnp.where(upper, 0, half - 1), 0.0, raw)
        found.append(split(raw))
        at = pl.ds(pl.multiple_of(comp * rows + start, TILE), half)
        for part, values in enumerate(found[-1]):
            for j in range(2):
                block_of(raw_refs, first + j)[part, at, :] = values[:, j * LANES : (j + 1) * LANES]
    return found


def differences(upper, half):
    deep = half + TILE
    diff_y = difference(iota((half, deep), 1) - iota((half, deep), 0) - jnp.where(upper, 0, TILE))
    shape = (4 * LANES, 2 * LANES)
    return diff_y, difference(iota(shape, 0) - LANES - iota(shape, 1))


def outer_kernel(lw_hbm, inno_hbm, back_hbm, *refs):
    *raw_refs, msg_ref, row_ref, inno_ref, back_ref, weight_ref, lw_ref, sum_ref, sems, rest_sems, lw_sem = refs
    levels, rows, width = inno_ref.shape
    half = rows // 2
    deep = half + TILE
    nblocks = width // LANES
    upper = parity() == 0
    start = jnp.where(upper, 0, half)
    part = width // QUARTERS

    def bring(sem, which, at, size, cols):
        index = (slice(None), pl.ds(pl.multiple_of(at, TILE), size), cols)
        source, target = ((inno_hbm, inno_ref), (back_hbm, back_ref))[which]
        return pltpu.make_async_copy(source.at[index], target.at[index], sem)

    weights = pltpu.make_async_copy(lw_hbm, lw_ref, lw_sem)
    copies = []
    for q in range(QUARTERS):
        cols = pl.ds(q * part, part)
        copies.append(
            [
                bring(sems.at[1, q], 1, jnp.where(upper, 0, rows - deep), deep, cols),
                bring(sems.at[0, q], 0, start, half, cols),
            ]
        )
    others = [
        bring(rest_sems.at[1], 1, jnp.where(upper, deep, 0), rows - deep, pl.ds(0, width)),
        bring(rest_sems.at[0], 0, half - start, half, pl.ds(0, width)),
    ]
    weights.start()
    for copy in sum(copies, []) + others:
        copy.start()
    diff_y, diff_x = differences(upper, half)
    sum_ref[...] = one_hot(iota(sum_ref.shape, 0) >> SHIFT_X == iota(sum_ref.shape, 1))
    groups = rows >> SHIFT_Y
    shape = (groups, rows)
    sum_y = one_hot(iota(shape, 1) >> SHIFT_Y == iota(shape, 0))
    weights.wait()
    waited = 0
    at = nblocks * rows
    for first in range(0, nblocks, 2):
        while waited * part < window(first, nblocks)[1] * LANES:
            for copy in copies[waited]:
                copy.wait()
            waited += 1
        found = raw_pair(first, lambda k: lw_ref[k], inno_ref, back_ref, upper, diff_y, diff_x, None, raw_refs)
        for comp, (high, _) in enumerate(found):
            for j in range(2):
                msg_ref[pl.ds((first + j) * rows + comp * half, half), :] = high[:, j * LANES : (j + 1) * LANES]
        if (first + 2) * LANES % SPAN == 0:
            blocks = range(first + 2 - SPAN // LANES, first + 2)
            lows = [jnp.concatenate(half_of(block_of(raw_refs, k), rows, start, 1), axis=0) for k in blocks]
            total = dot(jnp.concatenate(lows, axis=1), sum_ref[...])
            msg_ref[pl.ds(at, groups), :] = dot(sum_y, total.astype(BF16)).astype(BF16)
            at += groups
    kinds = 3 * levels
    shape = (PACK * kinds, PACK * levels * TILE)
    row, col = iota(shape, 0), iota(shape, 1)
    want = row - (col >> 6) * kinds
    level = (col >> 4) & (levels - 1)
    place = col & (TILE - 1)
    outermost = place == jnp.where(upper, 0, TILE - 1)
    next_row = place == jnp.where(upper, 1, TILE - 2)
    of_back = one_hot(((want == level) & outermost) | ((want == levels + level) & next_row))
    of_inno = one_hot((want == 2 * levels + level) & outermost)
    edge_at = tile_at(jnp.where(upper, 0, rows - TILE))
    for first in range(0, nblocks, PACK):
        back, inno = [], []
        for k in range(first, first + PACK):
            here = pl.ds(k * LANES, LANES)
            back.append(back_ref[:, edge_at, here].reshape(levels * TILE, LANES))
            inno.append(inno_ref[:, edge_at, here].reshape(levels * TILE, LANES))
        tile = dot(of_back, jnp.concatenate(back, axis=0)) + dot(of_inno, jnp.concatenate(inno, axis=0))
        msg_ref[pl.ds(at, PACK * kinds), :] = tile.astype(BF16)
        at += PACK * kinds
    for level in range(2 * levels):
        weight_ref[level : level + 1, :] = jnp.full((1, weight_ref.shape[1]), lw_ref[level % levels])
    for copy in others:
        copy.wait()
    shape = (TILE, levels * TILE)
    pick = one_hot(iota(shape, 1) == iota(shape, 0) * TILE + jnp.where(upper, TILE - 1, 0))
    near_rows = back_ref[:, tile_at(jnp.where(upper, rows - TILE, 0)), :]
    row_ref[...] = dot(pick, near_rows.reshape(levels * TILE, -1)).astype(BF16)


def outer_rows(rows, nblocks, levels):
    return nblocks * rows + (nblocks * LANES // SPAN) * (rows >> SHIFT_Y) + nblocks * 3 * levels


def inner_kernel(weight_ref, inno_ref, back_ref, row_ref, band_ref, *refs):
    raw_refs = refs[PIECES : 2 * PIECES]
    msg_ref = refs[2 * PIECES]
    _, rows, width = inno_ref.shape
    half = rows // 2
    nblocks = width // LANES
    upper = parity() == 1
    start = jnp.where(upper, 0, half)
    diff_y, diff_x = differences(upper, half)
    at = iota((half, 2 * LANES), 0) == jnp.where(upper, 0, half - 1)
    sign = jnp.where(upper, -1.0, 1.0)

    def extra(level, here):
        return jnp.where(at, row_ref[level : level + 1, here].astype(F32) * sign, 0.0)

    def weight(level):
        return weight_ref[level : level + 1, :]

    def load(k):
        block = block_of(raw_refs, k)
        return jnp.concatenate(half_of(block, rows, start, 0) + half_of(block, rows, start, 1), axis=0)

    groups = rows >> SHIFT_Z
    shape = (2 * groups, rows)
    sum_y = one_hot(iota(shape, 1) >> SHIFT_Z == iota(shape, 0))
    sums = []
    per = TILE // (2 * groups)
    done = 0
    for first in range(0, nblocks, 2):
        while done < min(first + 3, nblocks):
            raw_pair(done, weight, inno_ref, back_ref, upper, diff_y, diff_x, extra, raw_refs)
            done += 2
        high, low = split(smooth_x(band_ref, load, first, nblocks))
        sums.append(dot(sum_y, low)[:groups])
        for j in range(2):
            msg_ref[pl.ds((first + j) * rows, rows), :] = high[:, j * LANES : (j + 1) * LANES]
        if len(sums) == per:
            parts = [x[:, j * LANES : (j + 1) * LANES] for j in range(2) for x in sums]
            tile = nblocks * rows + first // (2 * per) * TILE
            msg_ref[pl.ds(tile, TILE), :] = jnp.concatenate(parts, axis=0).astype(BF16)
            sums = []


def inner_rows(rows, nblocks):
    return nblocks * rows + nblocks * (rows >> SHIFT_Z)


def outermost_kernel(weight_ref, own_ref, got_ref, out_ref):
    nblocks = out_ref.shape[1] // LANES
    levels = weight_ref.shape[0] // 2
    kinds = 3 * levels
    base = own_ref.shape[0] - nblocks * kinds

    def unpacked(ref):
        packs = [ref[pl.ds(base + k * kinds, PACK * kinds), :].astype(F32) for k in range(0, nblocks, PACK)]
        return [
            jnp.concatenate(
                [p[j * kinds + kind * levels : j * kinds + (kind + 1) * levels] for p in packs for j in range(PACK)], axis=1
            )
            for kind in range(3)
        ]

    own, got = unpacked(own_ref), unpacked(got_ref)
    here = jnp.concatenate([own[0], got[0]], axis=0)
    beyond = jnp.concatenate([got[0], own[0]], axis=0)
    before = jnp.concatenate([own[1], got[1]], axis=0)
    inno = jnp.concatenate([own[2], got[2]], axis=0)
    shape = here.shape
    first_core = parity() == 0
    grad_y = jnp.where((iota(shape, 0) < levels) == first_core, before - beyond, beyond - before)
    lane = iota(shape, 1)
    left = jnp.where(lane == 0, 0.0, pltpu.roll(here, 1, 1))
    right = jnp.where(lane == shape[1] - 1, 0.0, pltpu.roll(here, shape[1] - 1, 1))
    grad_x = right - left
    weight = jnp.concatenate([weight_ref[:, :LANES]] * nblocks, axis=1)
    scaled = inno * (0.5 * weight)

    def total(values):
        return [sum(values[k : k + 1] for k in range(f, f + levels)) for f in (0, levels)]

    numer_y, numer_x = total(scaled * grad_y), total(scaled * grad_x)
    denom = total((0.25 * weight) * (grad_y * grad_y + grad_x * grad_x))
    found = []
    for k in range(2):
        inverse = 1.0 / (1.0 + denom[k])
        found += [numer_y[k] * inverse, numer_x[k] * inverse]
    high, low = split(jnp.concatenate(found, axis=0))
    none = jnp.zeros((TILE - 8, shape[1]), F32)
    out_ref[...] = jnp.concatenate([high.astype(F32), low.astype(F32), none], axis=0).astype(BF16)


def far_taps(rows, towards):
    side = 2 * parity() - 1
    half = rows // 2
    start = jnp.where((side < 0) == towards, half, 0)
    return taps(iota((rows, half), 1) + start - iota((rows, half), 0) + side * rows)


def near_kernel(*refs):
    raw_refs, near_refs = refs[:PIECES], refs[PIECES : 2 * PIECES]
    edges_ref, near_edges_ref, msg_ref, band_ref, out_ref, total_ref = refs[2 * PIECES :]
    _, rows, width = out_ref.shape
    nblocks = width // LANES
    half = rows // 2
    par = parity()
    side = 1 - 2 * par
    offset = iota((rows, rows), 1) - iota((rows, rows), 0)
    near_taps = jnp.concatenate([taps(offset), taps(offset + side * rows)], axis=1)
    near_high = near_taps.astype(BF16)
    toward = far_taps(rows, True)
    shape = (rows, TILE)
    kind = iota(shape, 1)
    own_at = jnp.where(par == 0, 0, rows - 1)
    far_at = jnp.where(par == 0, -1, rows)
    near_at = jnp.where(par == 0, 2 * rows - 1, -rows)
    own_edges = taps(jnp.where(kind & 2 == 0, own_at, far_at) - iota(shape, 0))
    near_edges = jnp.where(kind & 2 == 0, taps(near_at - iota(shape, 0)), 0.0)
    stacked = []
    for comp in range(2):
        here = (kind < 8) & (kind & 1 == comp)
        all_taps = [near_taps, toward, jnp.where(here, own_edges, 0.0), jnp.where(here, near_edges, 0.0)]
        stacked.append(jnp.concatenate(split(jnp.concatenate(all_taps, axis=1)), axis=0))
    groups = half >> SHIFT_Y
    shape = (half, groups)
    mean_y = one_hot(iota(shape, 0) >> SHIFT_Y == iota(shape, 1), 1.0 / (1 << SHIFT_Y))
    group_taps = dot(toward.astype(BF16), mean_y).astype(BF16)
    shape = (LANES, SPAN)
    mean_x = one_hot(iota(shape, 1) >> SHIFT_X == iota(shape, 0), 1.0 / (1 << SHIFT_X))
    rest = []
    for span in range(width // SPAN):
        tile = msg_ref[pl.ds(nblocks * rows + span * 2 * groups, 2 * groups), :]
        rest.append(jnp.concatenate([dot(group_taps, tile[:groups]), dot(group_taps, tile[groups:])], axis=0).astype(BF16))
    done = 0
    for first in range(0, nblocks, 2):
        while done < min(first + 3, nblocks):
            cols = pl.ds(done * LANES, 2 * LANES)
            place = done * LANES % SPAN
            spread = dot(rest[done * LANES // SPAN], mean_x[:, place : place + 2 * LANES])
            for comp in range(2):
                here = pl.ds(comp * rows, rows)
                highs, lows = [], []
                for k in (done, done + 1):
                    both = (block_of(raw_refs, k), block_of(near_refs, k))
                    got = msg_ref[pl.ds(k * rows + comp * half, half), :]
                    highs.append(jnp.concatenate([ref[0, here, :] for ref in both] + [got], axis=0))
                    lows.append(jnp.concatenate([ref[1, here, :] for ref in both], axis=0))
                edges = [edges_ref[:, cols], near_edges_ref[:, cols]]
                part = dot(stacked[comp], jnp.concatenate([jnp.concatenate(highs, axis=1)] + edges, axis=0))
                part = part[:rows] + part[rows:] + dot(near_high, jnp.concatenate(lows, axis=1))
                high, low = split(part + spread[comp * rows : (comp + 1) * rows])
                for j in range(2):
                    cut = slice(j * LANES, (j + 1) * LANES)
                    total_ref[done + j, pl.ds(comp * rows, rows), :] = high[:, cut]
                    total_ref[done + j, pl.ds((2 + comp) * rows, rows), :] = low[:, cut]
            done += 2
        result = smooth_x(band_ref, lambda k: total_ref[k], first, nblocks)
        here = pl.ds(first * LANES, 2 * LANES)
        out_ref[0, :, here] = result[:rows]
        out_ref[1, :, here] = result[rows:]


def last_kernel(part_ref, msg_ref, out_hbm, buf, sem):
    _, rows, width = part_ref.shape
    nblocks = width // LANES
    half = rows // 2
    high, low = split(far_taps(rows, False))
    two = jnp.concatenate([high, low], axis=0)
    groups = rows >> SHIFT_Z
    per = TILE // (2 * groups)
    shape = (rows, groups)
    mean_y = one_hot(iota((half, groups), 0) >> SHIFT_Z == iota((half, groups), 1), 1.0 / (1 << SHIFT_Z))
    mean_other = one_hot((iota((half, groups), 0) >> SHIFT_Z) + groups // 2 == iota((half, groups), 1), 1.0 / (1 << SHIFT_Z))
    group_taps = jnp.concatenate([dot(high, mean_y), dot(high, mean_other)], axis=0).astype(BF16)
    copies = []
    for index, first in enumerate(range(0, nblocks, 2)):
        here = pl.ds(first * LANES, 2 * LANES)
        tile = msg_ref[pl.ds(nblocks * rows + index // per * TILE, TILE), :].astype(F32)
        slot = index % per
        sums = [tile[(j * per + slot) * groups : (j * per + slot + 1) * groups] for j in range(2)]
        rest = dot(group_taps, jnp.concatenate(sums, axis=1).astype(BF16))
        for comp in range(2):
            got = [msg_ref[pl.ds((first + j) * rows + comp * half, half), :] for j in range(2)]
            part = dot(two, jnp.concatenate(got, axis=1))
            part = part[:rows] + part[rows:] + rest[comp * rows : (comp + 1) * rows]
            buf[comp, :, here] = part_ref[comp, :, here] + part
        copy = pltpu.make_async_copy(buf.at[:, :, here], out_hbm.at[:, :, here], sem.at[index])
        copy.start()
        copies.append(copy)
    for copy in copies:
        copy.wait()


def body(innovation, background, level_weight):
    levels, rows, width = innovation.shape
    if rows != HALF or width % SPAN or levels != 4:
        raise NotImplementedError("slab shape")
    nblocks = width // LANES
    both, half = 2 * rows, rows // 2
    count = lax.axis_size("row")
    chip = [(i, i ^ 1) for i in range(count) if i ^ 1 < count]
    away = [(i, j) for i in range(count) for j in [((i + 1) ^ 1) - 1] if 0 <= j < count]
    hbm = [pltpu.with_memory_space_constraint(x, pltpu.HBM) for x in (level_weight, innovation, background)]
    band = jnp.asarray(zonal_band())
    piece = jax.ShapeDtypeStruct((nblocks // PIECES, 2, both, LANES), BF16)
    result = jax.ShapeDtypeStruct((2, rows, width), F32)
    *raws, outer, row, inno, back, weight = pl.pallas_call(
        outer_kernel,
        out_shape=[piece] * PIECES
        + [
            jax.ShapeDtypeStruct((outer_rows(rows, nblocks, levels), LANES), BF16),
            jax.ShapeDtypeStruct((TILE, width), BF16),
            jax.ShapeDtypeStruct(innovation.shape, BF16),
            jax.ShapeDtypeStruct(background.shape, BF16),
            jax.ShapeDtypeStruct((2 * levels, 2 * LANES), F32),
        ],
        in_specs=[HBM] * 3,
        out_specs=[VMEM] * (PIECES + 5),
        scratch_shapes=[
            pltpu.SMEM((levels,), F32),
            pltpu.VMEM((SPAN, LANES), BF16),
            pltpu.SemaphoreType.DMA((2, QUARTERS)),
            pltpu.SemaphoreType.DMA((2,)),
            pltpu.SemaphoreType.DMA,
        ],
        compiler_params=PARAMS,
        name="outer_half",
    )(*hbm)
    outer_got = lax.ppermute(outer, "row", away)
    row = lax.ppermute(row, "row", chip)
    *raws, inner = pl.pallas_call(
        inner_kernel,
        out_shape=[piece] * PIECES + [jax.ShapeDtypeStruct((inner_rows(rows, nblocks), LANES), BF16)],
        in_specs=[VMEM] * (5 + PIECES),
        out_specs=[VMEM] * (PIECES + 1),
        input_output_aliases={5 + k: k for k in range(PIECES)},
        compiler_params=PARAMS,
        name="inner_half",
    )(weight, inno, back, row, band, *raws)
    inner_got = lax.ppermute(inner, "row", away)
    nears = [lax.ppermute(r, "row", chip) for r in raws]
    edges = pl.pallas_call(
        outermost_kernel,
        out_shape=jax.ShapeDtypeStruct((TILE, width), BF16),
        in_specs=[VMEM] * 3,
        out_specs=VMEM,
        compiler_params=PARAMS,
        name="outermost_rows",
    )(weight, outer, outer_got)
    near_edges = lax.ppermute(edges, "row", chip)
    part = pl.pallas_call(
        near_kernel,
        out_shape=result,
        in_specs=[VMEM] * (2 * PIECES + 4),
        out_specs=VMEM,
        scratch_shapes=[pltpu.VMEM((nblocks, 2 * both, LANES), BF16)],
        compiler_params=PARAMS,
        name="near_part",
    )(*raws, *nears, edges, near_edges, outer_got, band)
    return pl.pallas_call(
        last_kernel,
        out_shape=result,
        in_specs=[VMEM] * 2,
        out_specs=HBM,
        scratch_shapes=[pltpu.VMEM((2, rows, width), F32), pltpu.SemaphoreType.DMA((nblocks // 2,))],
        compiler_params=PARAMS,
        name="last_part",
    )(part, inner_got)


def solution(mesh):
    placed = (P("member", "row", None), P("member", "row", None), P())
    return jax.shard_map(
        body, mesh=mesh, in_specs=placed, out_specs=P("member", "row", None), check_vma=False
    )
```

time: 26.3 us -> 24.5 us (0.932)
  local copies, waits for them, and re-layouts: 1.7 us -> 0.01 us
  waiting for transfers between devices: 4.59 us -> 5.16 us
  Pallas kernels: 11.2 us -> 10.7 us
    unnamed x10 -> x2, local copies, waits for them, and re-layouts: 1.7 us -> 0.01 us
    pallas_call x1, Pallas kernels: 0.7 us -> 0.18 us  [body(): pl.pallas_call(outermost_kernel, out_shape=jax.ShapeDtypeStruct((TILE, wi...]
    ppermute x4, waiting for transfers between devices: 0.48 us -> 1 us  [body(): nears = [lax.ppermute(r, 'row', chip) for r in raws]]
    ppermute x1, waiting for transfers between devices: 2.48 us -> 2.82 us  [body(): inner_got = lax.ppermute(inner, 'row', away)]
    ppermute x1, waiting for transfers between devices: 0.38 us -> 0.09 us  [body(): near_edges = lax.ppermute(edges, 'row', chip)]
  transfers between devices with their start and end apart: 8 -> 8, of which waited for: 5 -> 6; matrix products, arithmetic and copies ran while one was open for 0% -> 0% of each run, Pallas kernels for 26% -> 25%
where the time goes in v5:
time: 24.5 us; the launch traced here: 24.4 us
  Pallas kernels  10.7 us (44%)
  starting transfers between devices  8.46 us (35%)
  waiting for transfers between devices  5.16 us (21%)
    pallas_call x1, Pallas kernels, body(): pl.pallas_call(inner_kernel, out_shape=[piece] * PIECES + [jax.ShapeDtype...  3.73 us
    ppermute x1, starting transfers between devices, body(): outer_got = lax.ppermute(outer, 'row', away)  3.7 us
    ppermute x1, starting transfers between devices, body(): inner_got = lax.ppermute(inner, 'row', away)  3.39 us
    pallas_call x1, Pallas kernels, body(): pl.pallas_call(outer_kernel, out_shape=[piece] * PIECES + [jax.ShapeDtype...  3.15 us
    ppermute x1, waiting for transfers between devices, body(): inner_got = lax.ppermute(inner, 'row', away)  2.82 us
    pallas_call x1, Pallas kernels, body(): pl.pallas_call(near_kernel, out_shape=result, in_specs=[VMEM] * (2 * PIEC...  2.16 us
    pallas_call x1, Pallas kernels, body(): pl.pallas_call(last_kernel, out_shape=result, in_specs=[VMEM] * 2, out_sp...  1.45 us
    ppermute x1, waiting for transfers between devices, body(): row = lax.ppermute(row, 'row', chip)  1.24 us
  transfers between devices with their start and end apart: 8, of which 6 were waited for; matrix products, arithmetic and copies ran while one was open for 0% of the time, Pallas kernels for 25%

profile of v5, /device:TPU:11, one launch (start us, length us, event | category | flops | bytes accessed | tf_op | source)
XLA Modules:
  0.0 24.4 jit_solution(1133194338376674411)
XLA Ops:
  0.0 0.0 copy-start
  0.0 3.1 %outer_half.1 = (bf16[4,2,128,128]{3,2,1,0:T(8,128)(2,1)S(1)}, bf16[4,2,128,128]{3,2,1,0:T(8,128)(2,1)S(1)}, bf16[4,2,128,128]{3,2,1,0:T(8,128)(2,1)S(1)}, bf16[...) custom-call(f32[4]{0:T(128)} %lw_hbm.1, ...), custom_call_target="tpu_custom_call" | custom-call | tf_op jit(solution)/shard_map/outer_half/pallas_call | solution.py:431
  3.2 3.7 %collective-permute-start.5 = (bf16[1248,128]{1,0:T(8,128)(2,1)S(1)}, bf16[1248,128]{1,0:T(8,128)(2,1)S(1)}, u32[]{:S(2)}, u32[]{:S(2)}) collective-permute-start(bf16[1248,128]{1,0:T(8,128)(2,1)S(1)} %get-tuple-element.31.own_ref), channel_id=1, source_target_pairs={{1,2},{2,1},{3,4},{4,3},{5,6},{6,5},{7,8},{8,7},{9,10},{10,9},{11,... | collective-permute-start | bytes 958472 | tf_op jit(solution)/shard_map/ppermute | solution.py:453
  6.9 0.1 collective-permute-start
  6.9 1.2 %collective-permute-done.row_ref = bf16[16,2048]{1,0:T(8,128)(2,1)S(1)} collective-permute-done((bf16[16,2048]{1,0:T(8,128)(2,1)S(1)}, bf16[16,2048]{1,0:T(8,128)(2,1)S(1)}, u32[]{:S(2)}, u32[]{:S(2)}) %collective-permute-start) | collective-permute-done | bytes 65568 | tf_op jit(solution)/shard_map/ppermute | solution.py:454
  8.2 0.0 copy-done
  8.2 3.7 %inner_half.1 = (bf16[4,2,128,128]{3,2,1,0:T(8,128)(2,1)S(1)}, bf16[4,2,128,128]{3,2,1,0:T(8,128)(2,1)S(1)}, bf16[4,2,128,128]{3,2,1,0:T(8,128)(2,1)S(1)}, bf16[...) custom-call(f32[8,256]{1,0:T(8,128)S(1)} %get-tuple-element.19.weigh, ...), custom_call_target="tpu_custom_call", output_to_operand_aliasing={{0}: (5, {}), {1}: (6, {}), {2}: (7, {}), {3}: (8, {})} | custom-call | tf_op jit(solution)/shard_map/inner_half/pallas_call | solution.py:455
  11.9 0.1 collective-permute-start.1
  12.1 3.4 %collective-permute-start.7 = (bf16[1088,128]{1,0:T(8,128)(2,1)S(1)}, bf16[1088,128]{1,0:T(8,128)(2,1)S(1)}, u32[]{:S(2)}, u32[]{:S(2)}) collective-permute-start(bf16[1088,128]{1,0:T(8,128)(2,1)S(1)} %get-tuple-element.32), channel_id=1, source_target_pairs={{1,2},{2,1},{3,4},{4,3},{5,6},{6,5},{7,8},{8,7},{9,10},{10,9},{11,... | collective-permute-start | bytes 835592 | tf_op jit(solution)/shard_map/ppermute | solution.py:464
  15.5 0.1 collective-permute-start.2
  15.6 0.5 %collective-permute-start.3 = (bf16[4,2,128,128]{3,2,1,0:T(8,128)(2,1)S(1)}, bf16[4,2,128,128]{3,2,1,0:T(8,128)(2,1)S(1)}, u32[]{:S(2)}, u32[]{:S(2)}) collective-permute-start(bf16[4,2,128,128]{3,2,1,0:T(8,128)(2,1)S(1)} %get-tuple-element.29.refs_2_), channel_id=1, source_target_pairs={{0,1},{1,0},{2,3},{3,2},{4,5},{5,4},{6,7},{7,6},{8,9},{9,8},{10,11... | collective-permute-start | bytes 786440 | tf_op jit(solution)/shard_map/ppermute | solution.py:465
  16.0 0.0 collective-permute-done.5.got_ref.refs_10_
  16.0 0.1 collective-permute-start.4
  16.1 0.2 outermost_rows.1.refs_8_
  16.3 0.0 collective-permute-done.1.refs_4_
  16.3 0.5 %collective-permute-start.6 = (bf16[16,2048]{1,0:T(8,128)(2,1)S(1)}, bf16[16,2048]{1,0:T(8,128)(2,1)S(1)}, u32[]{:S(2)}, u32[]{:S(2)}) collective-permute-start(bf16[16,2048]{1,0:T(8,128)(2,1)S(1)} %outermost_rows.1.refs_8_), channel_id=1, source_target_pairs={{0,1},{1,0},{2,3},{3,2},{4,5},{5,4},{6,7},{7,6},{8,9},{9,8},{10,11... | collective-permute-start | bytes 196616 | tf_op jit(solution)/shard_map/ppermute | solution.py:474
  16.8 0.2 %collective-permute-done.2.refs_5_ = bf16[4,2,128,128]{3,2,1,0:T(8,128)(2,1)S(1)} collective-permute-done((bf16[4,2,128,128]{3,2,1,0:T(8,128)(2,1)S(1)}, bf16[4,2,128,128]{3,2,1,0:T(8,128)(2,1)S(1)}, u32[]{:S(2)}, u32[]{:S(2)}) %collective-permute-start.2) | collective-permute-done | bytes 262176 | tf_op jit(solution)/shard_map/ppermute | solution.py:465
  17.1 0.4 %collective-permute-done.3.refs_6_ = bf16[4,2,128,128]{3,2,1,0:T(8,128)(2,1)S(1)} collective-permute-done((bf16[4,2,128,128]{3,2,1,0:T(8,128)(2,1)S(1)}, bf16[4,2,128,128]{3,2,1,0:T(8,128)(2,1)S(1)}, u32[]{:S(2)}, u32[]{:S(2)}) %collective-permute-start.3) | collective-permute-done | bytes 262176 | tf_op jit(solution)/shard_map/ppermute | solution.py:465
  17.4 0.4 %collective-permute-done.4.refs_7_ = bf16[4,2,128,128]{3,2,1,0:T(8,128)(2,1)S(1)} collective-permute-done((bf16[4,2,128,128]{3,2,1,0:T(8,128)(2,1)S(1)}, bf16[4,2,128,128]{3,2,1,0:T(8,128)(2,1)S(1)}, u32[]{:S(2)}, u32[]{:S(2)}) %collective-permute-start.4) | collective-permute-done | bytes 262176 | tf_op jit(solution)/shard_map/ppermute | solution.py:465
  17.8 0.1 collective-permute-done.6.refs_9_
  17.9 2.2 %near_part.1.part_ref = f32[2,64,2048]{2,1,0:T(8,128)S(1)} custom-call(bf16[4,2,128,128]{3,2,1,0:T(8,128)(2,1)S(1)} %get-tuple-element.27.refs_0_, bf16[4,2,128,128]{3,2,1,0:T(8,128)(2,1)S(1)} %get-tuple-element.28.refs_1_, bf16[4,2,128,128]{3,2,1,0:T(8,128)(2,1)S(1)} %get-tuple-element.29.refs_2_, bf16[4,2,128,128]{3,2,1,0:T(8,128)(2,1)S(1)} %get-tuple-element.30.refs_3_, ...), custom_call_target="tpu_custom_call" | custom-call | tf_op jit(solution)/shard_map/near_part/pallas_call | solution.py:475
  20.1 2.8 %collective-permute-done.7.msg_ref = bf16[1088,128]{1,0:T(8,128)(2,1)S(1)} collective-permute-done((bf16[1088,128]{1,0:T(8,128)(2,1)S(1)}, bf16[1088,128]{1,0:T(8,128)(2,1)S(1)}, u32[]{:S(2)}, u32[]{:S(2)}) %collective-permute-start.7) | collective-permute-done | bytes 278560 | tf_op jit(solution)/shard_map/ppermute | solution.py:464
  22.9 1.4 %last_part.1 = f32[2,64,2048]{2,1,0:T(8,128)} custom-call(f32[2,64,2048]{2,1,0:T(8,128)S(1)} %near_part.1.part_ref, bf16[1088,128]{1,0:T(8,128)(2,1)S(1)} %collective-permute-done.7.msg_ref), custom_call_target="tpu_custom_call" | custom-call | tf_op jit(solution)/shard_map/last_part/pallas_call | solution.py:484
Async XLA Ops:
  0.0 8.2 %copy-start = (bf16[2,512,256]{2,1,0:T(8,128)(2,1)S(1)}, bf16[2,512,256]{2,1,0:T(8,128)(2,1)}, u32[]{:S(2)}) copy-start(bf16[2,512,256]{2,1,0:T(8,128)(2,1)} %constant.2.clone.band_ref.refs_11_) | copy-start | bytes 1572868
  3.2 12.9 %collective-permute-start.5 = (bf16[1248,128]{1,0:T(8,128)(2,1)S(1)}, bf16[1248,128]{1,0:T(8,128)(2,1)S(1)}, u32[]{:S(2)}, u32[]{:S(2)}) collective-permute-start(bf16[1248,128]{1,0:T(8,128)(2,1)S(1)} %get-tuple-element.31.own_ref), channel_id=1, source_target_pairs={{1,2},{2,1},{3,4},{4,3},{5,6},{6,5},{7,8},{8,7},{9,10},{10,9},{11,... | collective-permute-start | bytes 958472 | tf_op jit(solution)/shard_map/ppermute | solution.py:453
  6.9 1.3 %collective-permute-start = (bf16[16,2048]{1,0:T(8,128)(2,1)S(1)}, bf16[16,2048]{1,0:T(8,128)(2,1)S(1)}, u32[]{:S(2)}, u32[]{:S(2)}) collective-permute-start(bf16[16,2048]{1,0:T(8,128)(2,1)S(1)} %get-tuple-element.22), channel_id=1, source_target_pairs={{0,1},{1,0},{2,3},{3,2},{4,5},{5,4},{6,7},{7,6},{8,9},{9,8},{10,11... | collective-permute-start | bytes 196616 | tf_op jit(solution)/shard_map/ppermute | solution.py:454
  11.9 4.4 %collective-permute-start.1 = (bf16[4,2,128,128]{3,2,1,0:T(8,128)(2,1)S(1)}, bf16[4,2,128,128]{3,2,1,0:T(8,128)(2,1)S(1)}, u32[]{:S(2)}, u32[]{:S(2)}) collective-permute-start(bf16[4,2,128,128]{3,2,1,0:T(8,128)(2,1)S(1)} %get-tuple-element.27.refs_0_), channel_id=1, source_target_pairs={{0,1},{1,0},{2,3},{3,2},{4,5},{5,4},{6,7},{7,6},{8,9},{9,8},{10,11... | collective-permute-start | bytes 786440 | tf_op jit(solution)/shard_map/ppermute | solution.py:465
  12.1 10.8 %collective-permute-start.7 = (bf16[1088,128]{1,0:T(8,128)(2,1)S(1)}, bf16[1088,128]{1,0:T(8,128)(2,1)S(1)}, u32[]{:S(2)}, u32[]{:S(2)}) collective-permute-start(bf16[1088,128]{1,0:T(8,128)(2,1)S(1)} %get-tuple-element.32), channel_id=1, source_target_pairs={{1,2},{2,1},{3,4},{4,3},{5,6},{6,5},{7,8},{8,7},{9,10},{10,9},{11,... | collective-permute-start | bytes 835592 | tf_op jit(solution)/shard_map/ppermute | solution.py:464
  15.5 1.6 %collective-permute-start.2 = (bf16[4,2,128,128]{3,2,1,0:T(8,128)(2,1)S(1)}, bf16[4,2,128,128]{3,2,1,0:T(8,128)(2,1)S(1)}, u32[]{:S(2)}, u32[]{:S(2)}) collective-permute-start(bf16[4,2,128,128]{3,2,1,0:T(8,128)(2,1)S(1)} %get-tuple-element.28.refs_1_), channel_id=1, source_target_pairs={{0,1},{1,0},{2,3},{3,2},{4,5},{5,4},{6,7},{7,6},{8,9},{9,8},{10,11... | collective-permute-start | bytes 786440 | tf_op jit(solution)/shard_map/ppermute | solution.py:465
  15.6 1.9 %collective-permute-start.3 = (bf16[4,2,128,128]{3,2,1,0:T(8,128)(2,1)S(1)}, bf16[4,2,128,128]{3,2,1,0:T(8,128)(2,1)S(1)}, u32[]{:S(2)}, u32[]{:S(2)}) collective-permute-start(bf16[4,2,128,128]{3,2,1,0:T(8,128)(2,1)S(1)} %get-tuple-element.29.refs_2_), channel_id=1, source_target_pairs={{0,1},{1,0},{2,3},{3,2},{4,5},{5,4},{6,7},{7,6},{8,9},{9,8},{10,11... | collective-permute-start | bytes 786440 | tf_op jit(solution)/shard_map/ppermute | solution.py:465
  16.0 1.8 %collective-permute-start.4 = (bf16[4,2,128,128]{3,2,1,0:T(8,128)(2,1)S(1)}, bf16[4,2,128,128]{3,2,1,0:T(8,128)(2,1)S(1)}, u32[]{:S(2)}, u32[]{:S(2)}) collective-permute-start(bf16[4,2,128,128]{3,2,1,0:T(8,128)(2,1)S(1)} %get-tuple-element.30.refs_3_), channel_id=1, source_target_pairs={{0,1},{1,0},{2,3},{3,2},{4,5},{5,4},{6,7},{7,6},{8,9},{9,8},{10,11... | collective-permute-start | bytes 786440 | tf_op jit(solution)/shard_map/ppermute | solution.py:465
  16.3 1.6 %collective-permute-start.6 = (bf16[16,2048]{1,0:T(8,128)(2,1)S(1)}, bf16[16,2048]{1,0:T(8,128)(2,1)S(1)}, u32[]{:S(2)}, u32[]{:S(2)}) collective-permute-start(bf16[16,2048]{1,0:T(8,128)(2,1)S(1)} %outermost_rows.1.refs_8_), channel_id=1, source_target_pairs={{0,1},{1,0},{2,3},{3,2},{4,5},{5,4},{6,7},{7,6},{8,9},{9,8},{10,11... | collective-permute-start | bytes 196616 | tf_op jit(solution)/shard_map/ppermute | solution.py:474

commit v6 on v5

--- a/solution.py
+++ b/solution.py
@@ -183,12 +183,14 @@
         for comp, (high, _) in enumerate(found):
             for j in range(2):
                 msg_ref[pl.ds((first + j) * rows + comp * half, half), :] = high[:, j * LANES : (j + 1) * LANES]
-        if (first + 2) * LANES % SPAN == 0:
-            blocks = range(first + 2 - SPAN // LANES, first + 2)
-            lows = [jnp.concatenate(half_of(block_of(raw_refs, k), rows, start, 1), axis=0) for k in blocks]
-            total = dot(jnp.concatenate(lows, axis=1), sum_ref[...])
-            msg_ref[pl.ds(at, groups), :] = dot(sum_y, total.astype(BF16)).astype(BF16)
-            at += groups
+    totals = []
+    for span in range(0, nblocks, SPAN // LANES):
+        blocks = range(span, span + SPAN // LANES)
+        lows = [jnp.concatenate(half_of(block_of(raw_refs, k), rows, start, 1), axis=0) for k in blocks]
+        totals.append(dot(jnp.concatenate(lows, axis=1), sum_ref[...]))
+    for total in totals:
+        msg_ref[pl.ds(at, groups), :] = dot(sum_y, total.astype(BF16)).astype(BF16)
+        at += groups
     kinds = 3 * levels
     shape = (PACK * kinds, PACK * levels * TILE)
     row, col = iota(shape, 0), iota(shape, 1)
@@ -225,7 +227,7 @@
 
 def inner_kernel(weight_ref, inno_ref, back_ref, row_ref, band_ref, *refs):
     raw_refs = refs[PIECES : 2 * PIECES]
-    msg_ref = refs[2 * PIECES]
+    msg_ref, rest_ref = refs[2 * PIECES :]
     _, rows, width = inno_ref.shape
     half = rows // 2
     nblocks = width // LANES
@@ -248,22 +250,18 @@
     groups = rows >> SHIFT_Z
     shape = (2 * groups, rows)
     sum_y = one_hot(iota(shape, 1) >> SHIFT_Z == iota(shape, 0))
-    sums = []
-    per = TILE // (2 * groups)
-    done = 0
     for first in range(0, nblocks, 2):
-        while done < min(first + 3, nblocks):
-            raw_pair(done, weight, inno_ref, back_ref, upper, diff_y, diff_x, extra, raw_refs)
-            done += 2
+        raw_pair(first, weight, inno_ref, back_ref, upper, diff_y, diff_x, extra, raw_refs)
+    for first in range(0, nblocks, 2):
         high, low = split(smooth_x(band_ref, load, first, nblocks))
-        sums.append(dot(sum_y, low)[:groups])
+        rest_ref[:, first * LANES : (first + 2) * LANES] = low
         for j in range(2):
             msg_ref[pl.ds((first + j) * rows, rows), :] = high[:, j * LANES : (j + 1) * LANES]
-        if len(sums) == per:
-            parts = [x[:, j * LANES : (j + 1) * LANES] for j in range(2) for x in sums]
-            tile = nblocks * rows + first // (2 * per) * TILE
-            msg_ref[pl.ds(tile, TILE), :] = jnp.concatenate(parts, axis=0).astype(BF16)
-            sums = []
+    sums = dot(sum_y, rest_ref[...])
+    per = TILE // groups
+    for first in range(0, nblocks, per):
+        parts = [sums[:groups, k * LANES : (k + 1) * LANES] for k in range(first, first + per)]
+        msg_ref[pl.ds(nblocks * rows + first // per * TILE, TILE), :] = jnp.concatenate(parts, axis=0).astype(BF16)
 
 
 def inner_rows(rows, nblocks):
@@ -355,29 +353,27 @@
     for span in range(width // SPAN):
         tile = msg_ref[pl.ds(nblocks * rows + span * 2 * groups, 2 * groups), :]
         rest.append(jnp.concatenate([dot(group_taps, tile[:groups]), dot(group_taps, tile[groups:])], axis=0).astype(BF16))
-    done = 0
     for first in range(0, nblocks, 2):
-        while done < min(first + 3, nblocks):
-            cols = pl.ds(done * LANES, 2 * LANES)
-            place = done * LANES % SPAN
-            spread = dot(rest[done * LANES // SPAN], mean_x[:, place : place + 2 * LANES])
-            for comp in range(2):
-                here = pl.ds(comp * rows, rows)
-                highs, lows = [], []
-                for k in (done, done + 1):
-                    both = (block_of(raw_refs, k), block_of(near_refs, k))
-                    got = msg_ref[pl.ds(k * rows + comp * half, half), :]
-                    highs.append(jnp.concatenate([ref[0, here, :] for ref in both] + [got], axis=0))
-                    lows.append(jnp.concatenate([ref[1, here, :] for ref in both], axis=0))
-                edges = [edges_ref[:, cols], near_edges_ref[:, cols]]
-                part = dot(stacked[comp], jnp.concatenate([jnp.concatenate(highs, axis=1)] + edges, axis=0))
-                part = part[:rows] + part[rows:] + dot(near_high, jnp.concatenate(lows, axis=1))
-                high, low = split(part + spread[comp * rows : (comp + 1) * rows])
-                for j in range(2):
-                    cut = slice(j * LANES, (j + 1) * LANES)
-                    total_ref[done + j, pl.ds(comp * rows, rows), :] = high[:, cut]
-                    total_ref[done + j, pl.ds((2 + comp) * rows, rows), :] = low[:, cut]
-            done += 2
+        cols = pl.ds(first * LANES, 2 * LANES)
+        place = first * LANES % SPAN
+        spread = dot(rest[first * LANES // SPAN], mean_x[:, place : place + 2 * LANES])
+        edges = [edges_ref[:, cols], near_edges_ref[:, cols]]
+        for comp in range(2):
+            here = pl.ds(comp * rows, rows)
+            highs, lows = [], []
+            for k in (first, first + 1):
+                both = (block_of(raw_refs, k), block_of(near_refs, k))
+                got = msg_ref[pl.ds(k * rows + comp * half, half), :]
+                highs.append(jnp.concatenate([ref[0, here, :] for ref in both] + [got], axis=0))
+                lows.append(jnp.concatenate([ref[1, here, :] for ref in both], axis=0))
+            part = dot(stacked[comp], jnp.concatenate([jnp.concatenate(highs, axis=1)] + edges, axis=0))
+            part = part[:rows] + part[rows:] + dot(near_high, jnp.concatenate(lows, axis=1))
+            high, low = split(part + spread[comp * rows : (comp + 1) * rows])
+            for j in range(2):
+                cut = slice(j * LANES, (j + 1) * LANES)
+                total_ref[first + j, pl.ds(comp * rows, rows), :] = high[:, cut]
+                total_ref[first + j, pl.ds((2 + comp) * rows, rows), :] = low[:, cut]
+    for first in range(0, nblocks, 2):
         result = smooth_x(band_ref, lambda k: total_ref[k], first, nblocks)
         here = pl.ds(first * LANES, 2 * LANES)
         out_ref[0, :, here] = result[:rows]
@@ -391,17 +387,15 @@
     high, low = split(far_taps(rows, False))
     two = jnp.concatenate([high, low], axis=0)
     groups = rows >> SHIFT_Z
-    per = TILE // (2 * groups)
-    shape = (rows, groups)
+    per = TILE // groups
     mean_y = one_hot(iota((half, groups), 0) >> SHIFT_Z == iota((half, groups), 1), 1.0 / (1 << SHIFT_Z))
     mean_other = one_hot((iota((half, groups), 0) >> SHIFT_Z) + groups // 2 == iota((half, groups), 1), 1.0 / (1 << SHIFT_Z))
     group_taps = jnp.concatenate([dot(high, mean_y), dot(high, mean_other)], axis=0).astype(BF16)
     copies = []
     for index, first in enumerate(range(0, nblocks, 2)):
         here = pl.ds(first * LANES, 2 * LANES)
-        tile = msg_ref[pl.ds(nblocks * rows + index // per * TILE, TILE), :].astype(F32)
-        slot = index % per
-        sums = [tile[(j * per + slot) * groups : (j * per + slot + 1) * groups] for j in range(2)]
+        tile = msg_ref[pl.ds(nblocks * rows + first // per * TILE, TILE), :].astype(F32)
+        sums = [tile[k % per * groups : (k % per + 1) * groups] for k in (first, first + 1)]
         rest = dot(group_taps, jnp.concatenate(sums, axis=1).astype(BF16))
         for comp in range(2):
             got = [msg_ref[pl.ds((first + j) * rows + comp * half, half), :] for j in range(2)]
@@ -457,6 +451,7 @@
         out_shape=[piece] * PIECES + [jax.ShapeDtypeStruct((inner_rows(rows, nblocks), LANES), BF16)],
         in_specs=[VMEM] * (5 + PIECES),
         out_specs=[VMEM] * (PIECES + 1),
+        scratch_shapes=[pltpu.VMEM((rows, width), BF16)],
         input_output_aliases={5 + k: k for k in range(PIECES)},
         compiler_params=PARAMS,
         name="inner_half",

time: 24.5 us -> 22.4 us (0.914)
  Pallas kernels: 10.7 us -> 7.98 us
  waiting for transfers between devices: 5.16 us -> 5.62 us
    pallas_call x1, Pallas kernels: 3.73 us -> 1.52 us  [body(): pl.pallas_call(inner_kernel, out_shape=[piece] * PIECES + [jax.ShapeDtype...]
    ppermute x1, waiting for transfers between devices: 0.01 us -> 1.11 us  [body(): outer_got = lax.ppermute(outer, 'row', away)]
    ppermute x1, waiting for transfers between devices: 2.82 us -> 2.37 us  [body(): inner_got = lax.ppermute(inner, 'row', away)]
    pallas_call x1, Pallas kernels: 2.16 us -> 1.91 us  [body(): pl.pallas_call(near_kernel, out_shape=result, in_specs=[VMEM] * (2 * PIEC...]
  transfers between devices with their start and end apart: 8 -> 8, of which waited for: 6 -> 5; matrix products, arithmetic and copies ran while one was open for 0% -> 0% of each run, Pallas kernels for 25% -> 16%
where the time goes in v6:
time: 22.4 us; the launch traced here: 22.1 us
  starting transfers between devices  8.47 us (38%)
  Pallas kernels  7.98 us (36%)
  waiting for transfers between devices  5.62 us (25%)
    ppermute x1, starting transfers between devices, body(): outer_got = lax.ppermute(outer, 'row', away)  3.7 us
    ppermute x1, starting transfers between devices, body(): inner_got = lax.ppermute(inner, 'row', away)  3.39 us
    pallas_call x1, Pallas kernels, body(): pl.pallas_call(outer_kernel, out_shape=[piece] * PIECES + [jax.ShapeDtype...  2.9 us
    ppermute x1, waiting for transfers between devices, body(): inner_got = lax.ppermute(inner, 'row', away)  2.37 us
    pallas_call x1, Pallas kernels, body(): pl.pallas_call(near_kernel, out_shape=result, in_specs=[VMEM] * (2 * PIEC...  1.91 us
    pallas_call x1, Pallas kernels, body(): pl.pallas_call(inner_kernel, out_shape=[piece] * PIECES + [jax.ShapeDtype...  1.52 us
    pallas_call x1, Pallas kernels, body(): pl.pallas_call(last_kernel, out_shape=result, in_specs=[VMEM] * 2, out_sp...  1.46 us
    ppermute x1, waiting for transfers between devices, body(): row = lax.ppermute(row, 'row', chip)  1.24 us
  transfers between devices with their start and end apart: 8, of which 5 were waited for; matrix products, arithmetic and copies ran while one was open for 0% of the time, Pallas kernels for 16%

profile of v6, /device:TPU:11, one launch (start us, length us, event | category | flops | bytes accessed | tf_op | source)
XLA Modules:
  0.0 22.1 jit_solution(13575064116532068143)
XLA Ops:
  0.0 0.0 copy-start
  0.0 2.9 %outer_half.1 = (bf16[4,2,128,128]{3,2,1,0:T(8,128)(2,1)S(1)}, bf16[4,2,128,128]{3,2,1,0:T(8,128)(2,1)S(1)}, bf16[4,2,128,128]{3,2,1,0:T(8,128)(2,1)S(1)}, bf16[...) custom-call(f32[4]{0:T(128)} %lw_hbm.1, ...), custom_call_target="tpu_custom_call" | custom-call | tf_op jit(solution)/shard_map/outer_half/pallas_call | solution.py:425
  2.9 3.7 %collective-permute-start.5 = (bf16[1248,128]{1,0:T(8,128)(2,1)S(1)}, bf16[1248,128]{1,0:T(8,128)(2,1)S(1)}, u32[]{:S(2)}, u32[]{:S(2)}) collective-permute-start(bf16[1248,128]{1,0:T(8,128)(2,1)S(1)} %get-tuple-element.31.own_ref), channel_id=1, source_target_pairs={{1,2},{2,1},{3,4},{4,3},{5,6},{6,5},{7,8},{8,7},{9,10},{10,9},{11,... | collective-permute-start | bytes 958472 | tf_op jit(solution)/shard_map/ppermute | solution.py:447
  6.6 0.1 collective-permute-start
  6.7 1.2 %collective-permute-done.row_ref = bf16[16,2048]{1,0:T(8,128)(2,1)S(1)} collective-permute-done((bf16[16,2048]{1,0:T(8,128)(2,1)S(1)}, bf16[16,2048]{1,0:T(8,128)(2,1)S(1)}, u32[]{:S(2)}, u32[]{:S(2)}) %collective-permute-start) | collective-permute-done | bytes 65568 | tf_op jit(solution)/shard_map/ppermute | solution.py:448
  7.9 0.0 copy-done
  7.9 1.5 %inner_half.1 = (bf16[4,2,128,128]{3,2,1,0:T(8,128)(2,1)S(1)}, bf16[4,2,128,128]{3,2,1,0:T(8,128)(2,1)S(1)}, bf16[4,2,128,128]{3,2,1,0:T(8,128)(2,1)S(1)}, bf16[...) custom-call(f32[8,256]{1,0:T(8,128)S(1)} %get-tuple-element.19.weigh, ...), custom_call_target="tpu_custom_call", output_to_operand_aliasing={{0}: (5, {}), {1}: (6, {}), {2}: (7, {}), {3}: (8, {})} | custom-call | tf_op jit(solution)/shard_map/inner_half/pallas_call | solution.py:449
  9.5 0.1 collective-permute-start.1
  9.6 3.4 %collective-permute-start.7 = (bf16[1088,128]{1,0:T(8,128)(2,1)S(1)}, bf16[1088,128]{1,0:T(8,128)(2,1)S(1)}, u32[]{:S(2)}, u32[]{:S(2)}) collective-permute-start(bf16[1088,128]{1,0:T(8,128)(2,1)S(1)} %get-tuple-element.32), channel_id=1, source_target_pairs={{1,2},{2,1},{3,4},{4,3},{5,6},{6,5},{7,8},{8,7},{9,10},{10,9},{11,... | collective-permute-start | bytes 835592 | tf_op jit(solution)/shard_map/ppermute | solution.py:459
  13.0 0.1 collective-permute-start.2
  13.1 0.5 %collective-permute-start.3 = (bf16[4,2,128,128]{3,2,1,0:T(8,128)(2,1)S(1)}, bf16[4,2,128,128]{3,2,1,0:T(8,128)(2,1)S(1)}, u32[]{:S(2)}, u32[]{:S(2)}) collective-permute-start(bf16[4,2,128,128]{3,2,1,0:T(8,128)(2,1)S(1)} %get-tuple-element.29.refs_2_), channel_id=1, source_target_pairs={{0,1},{1,0},{2,3},{3,2},{4,5},{5,4},{6,7},{7,6},{8,9},{9,8},{10,11... | collective-permute-start | bytes 786440 | tf_op jit(solution)/shard_map/ppermute | solution.py:460
  13.6 1.1 %collective-permute-done.5.got_ref.refs_10_ = bf16[1248,128]{1,0:T(8,128)(2,1)S(1)} collective-permute-done((bf16[1248,128]{1,0:T(8,128)(2,1)S(1)}, bf16[1248,128]{1,0:T(8,128)(2,1)S(1)}, u32[]{:S(2)}, u32[]{:S(2)}) %collective-permute-start.5) | collective-permute-done | bytes 319520 | tf_op jit(solution)/shard_map/ppermute | solution.py:447
  14.7 0.0 collective-permute-start.4
  14.7 0.2 outermost_rows.1.refs_8_
  14.9 0.0 collective-permute-done.1.refs_4_
  14.9 0.6 %collective-permute-start.6 = (bf16[16,2048]{1,0:T(8,128)(2,1)S(1)}, bf16[16,2048]{1,0:T(8,128)(2,1)S(1)}, u32[]{:S(2)}, u32[]{:S(2)}) collective-permute-start(bf16[16,2048]{1,0:T(8,128)(2,1)S(1)} %outermost_rows.1.refs_8_), channel_id=1, source_target_pairs={{0,1},{1,0},{2,3},{3,2},{4,5},{5,4},{6,7},{7,6},{8,9},{9,8},{10,11... | collective-permute-start | bytes 196616 | tf_op jit(solution)/shard_map/ppermute | solution.py:469
  15.5 0.0 collective-permute-done.2.refs_5_
  15.5 0.0 collective-permute-done.3.refs_6_
  15.5 0.8 %collective-permute-done.4.refs_7_ = bf16[4,2,128,128]{3,2,1,0:T(8,128)(2,1)S(1)} collective-permute-done((bf16[4,2,128,128]{3,2,1,0:T(8,128)(2,1)S(1)}, bf16[4,2,128,128]{3,2,1,0:T(8,128)(2,1)S(1)}, u32[]{:S(2)}, u32[]{:S(2)}) %collective-permute-start.4) | collective-permute-done | bytes 262176 | tf_op jit(solution)/shard_map/ppermute | solution.py:460
  16.2 0.1 collective-permute-done.6.refs_9_
  16.4 1.9 %near_part.1.part_ref = f32[2,64,2048]{2,1,0:T(8,128)S(1)} custom-call(bf16[4,2,128,128]{3,2,1,0:T(8,128)(2,1)S(1)} %get-tuple-element.27.refs_0_, bf16[4,2,128,128]{3,2,1,0:T(8,128)(2,1)S(1)} %get-tuple-element.28.refs_1_, bf16[4,2,128,128]{3,2,1,0:T(8,128)(2,1)S(1)} %get-tuple-element.29.refs_2_, bf16[4,2,128,128]{3,2,1,0:T(8,128)(2,1)S(1)} %get-tuple-element.30.refs_3_, ...), custom_call_target="tpu_custom_call" | custom-call | tf_op jit(solution)/shard_map/near_part/pallas_call | solution.py:470
  18.3 2.4 %collective-permute-done.7.msg_ref = bf16[1088,128]{1,0:T(8,128)(2,1)S(1)} collective-permute-done((bf16[1088,128]{1,0:T(8,128)(2,1)S(1)}, bf16[1088,128]{1,0:T(8,128)(2,1)S(1)}, u32[]{:S(2)}, u32[]{:S(2)}) %collective-permute-start.7) | collective-permute-done | bytes 278560 | tf_op jit(solution)/shard_map/ppermute | solution.py:459
  20.7 1.5 %last_part.1 = f32[2,64,2048]{2,1,0:T(8,128)} custom-call(f32[2,64,2048]{2,1,0:T(8,128)S(1)} %near_part.1.part_ref, bf16[1088,128]{1,0:T(8,128)(2,1)S(1)} %collective-permute-done.7.msg_ref), custom_call_target="tpu_custom_call" | custom-call | tf_op jit(solution)/shard_map/last_part/pallas_call | solution.py:479
Async XLA Ops:
  0.0 7.9 %copy-start = (bf16[2,512,256]{2,1,0:T(8,128)(2,1)S(1)}, bf16[2,512,256]{2,1,0:T(8,128)(2,1)}, u32[]{:S(2)}) copy-start(bf16[2,512,256]{2,1,0:T(8,128)(2,1)} %constant.2.clone.band_ref.refs_11_) | copy-start | bytes 1572868
  2.9 11.8 %collective-permute-start.5 = (bf16[1248,128]{1,0:T(8,128)(2,1)S(1)}, bf16[1248,128]{1,0:T(8,128)(2,1)S(1)}, u32[]{:S(2)}, u32[]{:S(2)}) collective-permute-start(bf16[1248,128]{1,0:T(8,128)(2,1)S(1)} %get-tuple-element.31.own_ref), channel_id=1, source_target_pairs={{1,2},{2,1},{3,4},{4,3},{5,6},{6,5},{7,8},{8,7},{9,10},{10,9},{11,... | collective-permute-start | bytes 958472 | tf_op jit(solution)/shard_map/ppermute | solution.py:447
  6.6 1.3 %collective-permute-start = (bf16[16,2048]{1,0:T(8,128)(2,1)S(1)}, bf16[16,2048]{1,0:T(8,128)(2,1)S(1)}, u32[]{:S(2)}, u32[]{:S(2)}) collective-permute-start(bf16[16,2048]{1,0:T(8,128)(2,1)S(1)} %get-tuple-element.22), channel_id=1, source_target_pairs={{0,1},{1,0},{2,3},{3,2},{4,5},{5,4},{6,7},{7,6},{8,9},{9,8},{10,11... | collective-permute-start | bytes 196616 | tf_op jit(solution)/shard_map/ppermute | solution.py:448
  9.5 5.4 %collective-permute-start.1 = (bf16[4,2,128,128]{3,2,1,0:T(8,128)(2,1)S(1)}, bf16[4,2,128,128]{3,2,1,0:T(8,128)(2,1)S(1)}, u32[]{:S(2)}, u32[]{:S(2)}) collective-permute-start(bf16[4,2,128,128]{3,2,1,0:T(8,128)(2,1)S(1)} %get-tuple-element.27.refs_0_), channel_id=1, source_target_pairs={{0,1},{1,0},{2,3},{3,2},{4,5},{5,4},{6,7},{7,6},{8,9},{9,8},{10,11... | collective-permute-start | bytes 786440 | tf_op jit(solution)/shard_map/ppermute | solution.py:460
  9.6 11.1 %collective-permute-start.7 = (bf16[1088,128]{1,0:T(8,128)(2,1)S(1)}, bf16[1088,128]{1,0:T(8,128)(2,1)S(1)}, u32[]{:S(2)}, u32[]{:S(2)}) collective-permute-start(bf16[1088,128]{1,0:T(8,128)(2,1)S(1)} %get-tuple-element.32), channel_id=1, source_target_pairs={{1,2},{2,1},{3,4},{4,3},{5,6},{6,5},{7,8},{8,7},{9,10},{10,9},{11,... | collective-permute-start | bytes 835592 | tf_op jit(solution)/shard_map/ppermute | solution.py:459
  13.0 2.5 %collective-permute-start.2 = (bf16[4,2,128,128]{3,2,1,0:T(8,128)(2,1)S(1)}, bf16[4,2,128,128]{3,2,1,0:T(8,128)(2,1)S(1)}, u32[]{:S(2)}, u32[]{:S(2)}) collective-permute-start(bf16[4,2,128,128]{3,2,1,0:T(8,128)(2,1)S(1)} %get-tuple-element.28.refs_1_), channel_id=1, source_target_pairs={{0,1},{1,0},{2,3},{3,2},{4,5},{5,4},{6,7},{7,6},{8,9},{9,8},{10,11... | collective-permute-start | bytes 786440 | tf_op jit(solution)/shard_map/ppermute | solution.py:460
  13.1 2.4 %collective-permute-start.3 = (bf16[4,2,128,128]{3,2,1,0:T(8,128)(2,1)S(1)}, bf16[4,2,128,128]{3,2,1,0:T(8,128)(2,1)S(1)}, u32[]{:S(2)}, u32[]{:S(2)}) collective-permute-start(bf16[4,2,128,128]{3,2,1,0:T(8,128)(2,1)S(1)} %get-tuple-element.29.refs_2_), channel_id=1, source_target_pairs={{0,1},{1,0},{2,3},{3,2},{4,5},{5,4},{6,7},{7,6},{8,9},{9,8},{10,11... | collective-permute-start | bytes 786440 | tf_op jit(solution)/shard_map/ppermute | solution.py:460
  14.7 1.5 %collective-permute-start.4 = (bf16[4,2,128,128]{3,2,1,0:T(8,128)(2,1)S(1)}, bf16[4,2,128,128]{3,2,1,0:T(8,128)(2,1)S(1)}, u32[]{:S(2)}, u32[]{:S(2)}) collective-permute-start(bf16[4,2,128,128]{3,2,1,0:T(8,128)(2,1)S(1)} %get-tuple-element.30.refs_3_), channel_id=1, source_target_pairs={{0,1},{1,0},{2,3},{3,2},{4,5},{5,4},{6,7},{7,6},{8,9},{9,8},{10,11... | collective-permute-start | bytes 786440 | tf_op jit(solution)/shard_map/ppermute | solution.py:460
  14.9 1.5 %collective-permute-start.6 = (bf16[16,2048]{1,0:T(8,128)(2,1)S(1)}, bf16[16,2048]{1,0:T(8,128)(2,1)S(1)}, u32[]{:S(2)}, u32[]{:S(2)}) collective-permute-start(bf16[16,2048]{1,0:T(8,128)(2,1)S(1)} %outermost_rows.1.refs_8_), channel_id=1, source_target_pairs={{0,1},{1,0},{2,3},{3,2},{4,5},{5,4},{6,7},{7,6},{8,9},{9,8},{10,11... | collective-permute-start | bytes 196616 | tf_op jit(solution)/shard_map/ppermute | solution.py:469

commit v7 on v6

--- a/solution.py
+++ b/solution.py
@@ -15,7 +15,7 @@
 SHIFT_Y, SHIFT_X, SHIFT_Z = 2, 3, 4
 SPAN = LANES << SHIFT_X
 PACK = 4
-QUARTERS = 4
+CUTS = (0, 8, 16)
 PIECES = 4
 F32 = jnp.float32
 BF16 = jnp.bfloat16
@@ -114,11 +114,11 @@
         numer_x += scaled * grad_x
         denom += (0.25 * weight(level)) * (grad_y * grad_y + grad_x * grad_x)
     inverse = 1.0 / denom
+    if extra is None:
+        inverse = jnp.where(iota(inverse.shape, 0) == jnp.where(upper, 0, half - 1), 0.0, inverse)
     found = []
     for comp, numer in enumerate((numer_y, numer_x)):
         raw = numer * inverse
-        if extra is None:
-            raw = jnp.where(iota(raw.shape, 0) == jnp.where(upper, 0, half - 1), 0.0, raw)
         found.append(split(raw))
         at = pl.ds(pl.multiple_of(comp * rows + start, TILE), half)
         for part, values in enumerate(found[-1]):
@@ -142,7 +142,7 @@
     nblocks = width // LANES
     upper = parity() == 0
     start = jnp.where(upper, 0, half)
-    part = width // QUARTERS
+    cuts = [cut * nblocks // CUTS[-1] * LANES for cut in CUTS]
 
     def bring(sem, which, at, size, cols):
         index = (slice(None), pl.ds(pl.multiple_of(at, TILE), size), cols)
@@ -151,20 +151,18 @@
 
     weights = pltpu.make_async_copy(lw_hbm, lw_ref, lw_sem)
     copies = []
-    for q in range(QUARTERS):
-        cols = pl.ds(q * part, part)
+    for q, cut in enumerate(cuts[:-1]):
+        cols = pl.ds(cut, cuts[q + 1] - cut)
         copies.append(
             [
                 bring(sems.at[1, q], 1, jnp.where(upper, 0, rows - deep), deep, cols),
                 bring(sems.at[0, q], 0, start, half, cols),
             ]
         )
-    others = [
-        bring(rest_sems.at[1], 1, jnp.where(upper, deep, 0), rows - deep, pl.ds(0, width)),
-        bring(rest_sems.at[0], 0, half - start, half, pl.ds(0, width)),
-    ]
+    copies[-1].append(bring(rest_sems.at[1], 1, jnp.where(upper, deep, 0), rows - deep, pl.ds(0, width)))
+    other = bring(rest_sems.at[0], 0, half - start, half, pl.ds(0, width))
     weights.start()
-    for copy in sum(copies, []) + others:
+    for copy in sum(copies, []) + [other]:
         copy.start()
     diff_y, diff_x = differences(upper, half)
     sum_ref[...] = one_hot(iota(sum_ref.shape, 0) >> SHIFT_X == iota(sum_ref.shape, 1))
@@ -175,7 +173,7 @@
     waited = 0
     at = nblocks * rows
     for first in range(0, nblocks, 2):
-        while waited * part < window(first, nblocks)[1] * LANES:
+        while cuts[waited] < window(first, nblocks)[1] * LANES:
             for copy in copies[waited]:
                 copy.wait()
             waited += 1
@@ -213,12 +211,11 @@
         at += PACK * kinds
     for level in range(2 * levels):
         weight_ref[level : level + 1, :] = jnp.full((1, weight_ref.shape[1]), lw_ref[level % levels])
-    for copy in others:
-        copy.wait()
     shape = (TILE, levels * TILE)
     pick = one_hot(iota(shape, 1) == iota(shape, 0) * TILE + jnp.where(upper, TILE - 1, 0))
     near_rows = back_ref[:, tile_at(jnp.where(upper, rows - TILE, 0)), :]
     row_ref[...] = dot(pick, near_rows.reshape(levels * TILE, -1)).astype(BF16)
+    other.wait()
 
 
 def outer_rows(rows, nblocks, levels):
@@ -259,9 +256,11 @@
             msg_ref[pl.ds((first + j) * rows, rows), :] = high[:, j * LANES : (j + 1) * LANES]
     sums = dot(sum_y, rest_ref[...])
     per = TILE // groups
-    for first in range(0, nblocks, per):
-        parts = [sums[:groups, k * LANES : (k + 1) * LANES] for k in range(first, first + per)]
-        msg_ref[pl.ds(nblocks * rows + first // per * TILE, TILE), :] = jnp.concatenate(parts, axis=0).astype(BF16)
+    for first in range(0, nblocks, 2 * per):
+        for j in range(2):
+            parts = [sums[:groups, k * LANES : (k + 1) * LANES] for k in range(first + j, first + 2 * per, 2)]
+            tile = nblocks * rows + (first // per + j) * TILE
+            msg_ref[pl.ds(tile, TILE), :] = jnp.concatenate(parts, axis=0).astype(BF16)
 
 
 def inner_rows(rows, nblocks):
@@ -321,7 +320,7 @@
 
 def near_kernel(*refs):
     raw_refs, near_refs = refs[:PIECES], refs[PIECES : 2 * PIECES]
-    edges_ref, near_edges_ref, msg_ref, band_ref, out_ref, total_ref = refs[2 * PIECES :]
+    edges_ref, near_edges_ref, msg_ref, band_ref, out_ref, taps_ref, total_ref = refs[2 * PIECES :]
     _, rows, width = out_ref.shape
     nblocks = width // LANES
     half = rows // 2
@@ -378,29 +377,41 @@
         here = pl.ds(first * LANES, 2 * LANES)
         out_ref[0, :, here] = result[:rows]
         out_ref[1, :, here] = result[rows:]
-
-
-def last_kernel(part_ref, msg_ref, out_hbm, buf, sem):
+    for index, matrix in enumerate(last_taps(rows)):
+        taps_ref[index] = matrix
+
+
+def last_taps(rows):
+    half = rows // 2
+    away = far_taps(rows, False)
+    high, low = split(away)
+    groups = rows >> SHIFT_Z
+    shape = (half, TILE)
+    found = []
+    for place in range(TILE // groups):
+        for comp in range(2):
+            of_group = (iota(shape, 0) >> SHIFT_Z) + place * groups + comp * (groups // 2) == iota(shape, 1)
+            mean = dot(high, one_hot(of_group, 1.0 / (1 << SHIFT_Z))).astype(BF16)
+            found.append(jnp.concatenate([high, low, mean], axis=1))
+    return found
+
+
+def last_kernel(taps_ref, part_ref, msg_ref, out_hbm, buf, sem):
     _, rows, width = part_ref.shape
     nblocks = width // LANES
     half = rows // 2
-    high, low = split(far_taps(rows, False))
-    two = jnp.concatenate([high, low], axis=0)
-    groups = rows >> SHIFT_Z
-    per = TILE // groups
-    mean_y = one_hot(iota((half, groups), 0) >> SHIFT_Z == iota((half, groups), 1), 1.0 / (1 << SHIFT_Z))
-    mean_other = one_hot((iota((half, groups), 0) >> SHIFT_Z) + groups // 2 == iota((half, groups), 1), 1.0 / (1 << SHIFT_Z))
-    group_taps = jnp.concatenate([dot(high, mean_y), dot(high, mean_other)], axis=0).astype(BF16)
+    places = TILE // (rows >> SHIFT_Z)
     copies = []
     for index, first in enumerate(range(0, nblocks, 2)):
         here = pl.ds(first * LANES, 2 * LANES)
-        tile = msg_ref[pl.ds(nblocks * rows + first // per * TILE, TILE), :].astype(F32)
-        sums = [tile[k % per * groups : (k % per + 1) * groups] for k in (first, first + 1)]
-        rest = dot(group_taps, jnp.concatenate(sums, axis=1).astype(BF16))
+        tiles = [
+            msg_ref[pl.ds(nblocks * rows + (2 * (index // places) + j) * TILE, TILE), :] for j in range(2)
+        ]
+        sums = jnp.concatenate(tiles, axis=1)
         for comp in range(2):
             got = [msg_ref[pl.ds((first + j) * rows + comp * half, half), :] for j in range(2)]
-            part = dot(two, jnp.concatenate(got, axis=1))
-            part = part[:rows] + part[rows:] + rest[comp * rows : (comp + 1) * rows]
+            got = jnp.concatenate(got, axis=1)
+            part = dot(taps_ref[index % places * 2 + comp], jnp.concatenate([got, got, sums], axis=0))
             buf[comp, :, here] = part_ref[comp, :, here] + part
         copy = pltpu.make_async_copy(buf.at[:, :, here], out_hbm.at[:, :, here], sem.at[index])
         copy.start()
@@ -437,7 +448,7 @@
         scratch_shapes=[
             pltpu.SMEM((levels,), F32),
             pltpu.VMEM((SPAN, LANES), BF16),
-            pltpu.SemaphoreType.DMA((2, QUARTERS)),
+            pltpu.SemaphoreType.DMA((2, len(CUTS) - 1)),
             pltpu.SemaphoreType.DMA((2,)),
             pltpu.SemaphoreType.DMA,
         ],
@@ -467,11 +478,11 @@
         name="outermost_rows",
     )(weight, outer, outer_got)
     near_edges = lax.ppermute(edges, "row", chip)
-    part = pl.pallas_call(
+    part, last = pl.pallas_call(
         near_kernel,
-        out_shape=result,
+        out_shape=[result, jax.ShapeDtypeStruct((2 * TILE // (rows >> SHIFT_Z), rows, rows + TILE), BF16)],
         in_specs=[VMEM] * (2 * PIECES + 4),
-        out_specs=VMEM,
+        out_specs=[VMEM] * 2,
         scratch_shapes=[pltpu.VMEM((nblocks, 2 * both, LANES), BF16)],
         compiler_params=PARAMS,
         name="near_part",
@@ -479,12 +490,12 @@
     return pl.pallas_call(
         last_kernel,
         out_shape=result,
-        in_specs=[VMEM] * 2,
+        in_specs=[VMEM] * 3,
         out_specs=HBM,
         scratch_shapes=[pltpu.VMEM((2, rows, width), F32), pltpu.SemaphoreType.DMA((nblocks // 2,))],
         compiler_params=PARAMS,
         name="last_part",
-    )(part, inner_got)
+    )(last, part, inner_got)
 
 
 def solution(mesh):

time: 22.4 us -> 21.7 us (0.969)
  Pallas kernels: 7.98 us -> 7.38 us
    pallas_call x1, Pallas kernels: 2.9 us -> 2.46 us  [body(): pl.pallas_call(outer_kernel, out_shape=[piece] * PIECES + [jax.ShapeDtype...]
  transfers between devices with their start and end apart: 8 -> 8, of which waited for: 5 -> 5; matrix products, arithmetic and copies ran while one was open for 0% -> 0% of each run, Pallas kernels for 16% -> 17%
where the time goes in v7:
time: 21.7 us; the launch traced here: 21.4 us
  starting transfers between devices  8.46 us (39%)
  Pallas kernels  7.38 us (34%)
  waiting for transfers between devices  5.51 us (25%)
    ppermute x1, starting transfers between devices, body(): outer_got = lax.ppermute(outer, 'row', away)  3.7 us
    ppermute x1, starting transfers between devices, body(): inner_got = lax.ppermute(inner, 'row', away)  3.39 us
    pallas_call x1, Pallas kernels, body(): pl.pallas_call(outer_kernel, out_shape=[piece] * PIECES + [jax.ShapeDtype...  2.46 us
    ppermute x1, waiting for transfers between devices, body(): inner_got = lax.ppermute(inner, 'row', away)  2.28 us
    pallas_call x1, Pallas kernels, body(): pl.pallas_call(near_kernel, out_shape=[result, jax.ShapeDtypeStruct((2 *...  2.01 us
    pallas_call x1, Pallas kernels, body(): pl.pallas_call(inner_kernel, out_shape=[piece] * PIECES + [jax.ShapeDtype...  1.54 us
    ppermute x1, waiting for transfers between devices, body(): row = lax.ppermute(row, 'row', chip)  1.24 us
    pallas_call x1, Pallas kernels, body(): pl.pallas_call(last_kernel, out_shape=result, in_specs=[VMEM] * 3, out_sp...  1.19 us
  transfers between devices with their start and end apart: 8, of which 5 were waited for; matrix products, arithmetic and copies ran while one was open for 0% of the time, Pallas kernels for 17%

profile of v7, /device:TPU:11, one launch (start us, length us, event | category | flops | bytes accessed | tf_op | source)
XLA Modules:
  0.0 21.4 jit_solution(15052701073927378339)
XLA Ops:
  0.0 0.0 copy-start
  0.0 2.5 %outer_half.1 = (bf16[4,2,128,128]{3,2,1,0:T(8,128)(2,1)S(1)}, bf16[4,2,128,128]{3,2,1,0:T(8,128)(2,1)S(1)}, bf16[4,2,128,128]{3,2,1,0:T(8,128)(2,1)S(1)}, bf16[...) custom-call(f32[4]{0:T(128)} %lw_hbm.1, ...), custom_call_target="tpu_custom_call" | custom-call | tf_op jit(solution)/shard_map/outer_half/pallas_call | solution.py:436
  2.5 3.7 %collective-permute-start.5 = (bf16[1248,128]{1,0:T(8,128)(2,1)S(1)}, bf16[1248,128]{1,0:T(8,128)(2,1)S(1)}, u32[]{:S(2)}, u32[]{:S(2)}) collective-permute-start(bf16[1248,128]{1,0:T(8,128)(2,1)S(1)} %get-tuple-element.33.own_ref), channel_id=1, source_target_pairs={{1,2},{2,1},{3,4},{4,3},{5,6},{6,5},{7,8},{8,7},{9,10},{10,9},{11,... | collective-permute-start | bytes 958472 | tf_op jit(solution)/shard_map/ppermute | solution.py:458
  6.2 0.1 collective-permute-start
  6.3 1.2 %collective-permute-done.row_ref = bf16[16,2048]{1,0:T(8,128)(2,1)S(1)} collective-permute-done((bf16[16,2048]{1,0:T(8,128)(2,1)S(1)}, bf16[16,2048]{1,0:T(8,128)(2,1)S(1)}, u32[]{:S(2)}, u32[]{:S(2)}) %collective-permute-start) | collective-permute-done | bytes 65568 | tf_op jit(solution)/shard_map/ppermute | solution.py:459
  7.5 0.0 copy-done
  7.5 1.5 %inner_half.1 = (bf16[4,2,128,128]{3,2,1,0:T(8,128)(2,1)S(1)}, bf16[4,2,128,128]{3,2,1,0:T(8,128)(2,1)S(1)}, bf16[4,2,128,128]{3,2,1,0:T(8,128)(2,1)S(1)}, bf16[...) custom-call(f32[8,256]{1,0:T(8,128)S(1)} %get-tuple-element.21.weigh, ...), custom_call_target="tpu_custom_call", output_to_operand_aliasing={{0}: (5, {}), {1}: (6, {}), {2}: (7, {}), {3}: (8, {})} | custom-call | tf_op jit(solution)/shard_map/inner_half/pallas_call | solution.py:460
  9.0 0.1 collective-permute-start.1
  9.2 3.4 %collective-permute-start.7 = (bf16[1088,128]{1,0:T(8,128)(2,1)S(1)}, bf16[1088,128]{1,0:T(8,128)(2,1)S(1)}, u32[]{:S(2)}, u32[]{:S(2)}) collective-permute-start(bf16[1088,128]{1,0:T(8,128)(2,1)S(1)} %get-tuple-element.36), channel_id=1, source_target_pairs={{1,2},{2,1},{3,4},{4,3},{5,6},{6,5},{7,8},{8,7},{9,10},{10,9},{11,... | collective-permute-start | bytes 835592 | tf_op jit(solution)/shard_map/ppermute | solution.py:470
  12.6 0.1 collective-permute-start.2
  12.7 0.5 %collective-permute-start.3 = (bf16[4,2,128,128]{3,2,1,0:T(8,128)(2,1)S(1)}, bf16[4,2,128,128]{3,2,1,0:T(8,128)(2,1)S(1)}, u32[]{:S(2)}, u32[]{:S(2)}) collective-permute-start(bf16[4,2,128,128]{3,2,1,0:T(8,128)(2,1)S(1)} %get-tuple-element.31.refs_2_), channel_id=1, source_target_pairs={{0,1},{1,0},{2,3},{3,2},{4,5},{5,4},{6,7},{7,6},{8,9},{9,8},{10,11... | collective-permute-start | bytes 786440 | tf_op jit(solution)/shard_map/ppermute | solution.py:471
  13.2 1.1 %collective-permute-done.5.got_ref.refs_10_ = bf16[1248,128]{1,0:T(8,128)(2,1)S(1)} collective-permute-done((bf16[1248,128]{1,0:T(8,128)(2,1)S(1)}, bf16[1248,128]{1,0:T(8,128)(2,1)S(1)}, u32[]{:S(2)}, u32[]{:S(2)}) %collective-permute-start.5) | collective-permute-done | bytes 319520 | tf_op jit(solution)/shard_map/ppermute | solution.py:458
  14.3 0.0 collective-permute-start.4
  14.3 0.2 outermost_rows.1.refs_8_
  14.4 0.0 collective-permute-done.1.refs_4_
  14.5 0.6 %collective-permute-start.6 = (bf16[16,2048]{1,0:T(8,128)(2,1)S(1)}, bf16[16,2048]{1,0:T(8,128)(2,1)S(1)}, u32[]{:S(2)}, u32[]{:S(2)}) collective-permute-start(bf16[16,2048]{1,0:T(8,128)(2,1)S(1)} %outermost_rows.1.refs_8_), channel_id=1, source_target_pairs={{0,1},{1,0},{2,3},{3,2},{4,5},{5,4},{6,7},{7,6},{8,9},{9,8},{10,11... | collective-permute-start | bytes 196616 | tf_op jit(solution)/shard_map/ppermute | solution.py:480
  15.0 0.0 collective-permute-done.2.refs_5_
  15.0 0.0 collective-permute-done.3.refs_6_
  15.0 0.8 %collective-permute-done.4.refs_7_ = bf16[4,2,128,128]{3,2,1,0:T(8,128)(2,1)S(1)} collective-permute-done((bf16[4,2,128,128]{3,2,1,0:T(8,128)(2,1)S(1)}, bf16[4,2,128,128]{3,2,1,0:T(8,128)(2,1)S(1)}, u32[]{:S(2)}, u32[]{:S(2)}) %collective-permute-start.4) | collective-permute-done | bytes 262176 | tf_op jit(solution)/shard_map/ppermute | solution.py:471
  15.8 0.1 collective-permute-done.6.refs_9_
  15.9 2.0 %near_part.1 = (f32[2,64,2048]{2,1,0:T(8,128)S(1)}, bf16[8,64,80]{2,1,0:T(8,128)(2,1)S(1)}) custom-call(bf16[4,2,128,128]{3,2,1,0:T(8,128)(2,1)S(1)} %get-tuple-element.29.refs_0_, bf16[4,2,128,128]{3,2,1,0:T(8,128)(2,1)S(1)} %get-tuple-element.30.refs_1_, bf16[4,2,128,128]{3,2,1,0:T(8,128)(2,1)S(1)} %get-tuple-element.31.refs_2_, ...), custom_call_target="tpu_custom_call" | custom-call | tf_op jit(solution)/shard_map/near_part/pallas_call | solution.py:481
  17.9 2.3 %collective-permute-done.7.msg_ref = bf16[1088,128]{1,0:T(8,128)(2,1)S(1)} collective-permute-done((bf16[1088,128]{1,0:T(8,128)(2,1)S(1)}, bf16[1088,128]{1,0:T(8,128)(2,1)S(1)}, u32[]{:S(2)}, u32[]{:S(2)}) %collective-permute-start.7) | collective-permute-done | bytes 278560 | tf_op jit(solution)/shard_map/ppermute | solution.py:470
  20.2 1.2 %last_part.1 = f32[2,64,2048]{2,1,0:T(8,128)} custom-call(bf16[8,64,80]{2,1,0:T(8,128)(2,1)S(1)} %get-tuple-element.34.taps_ref, f32[2,64,2048]{2,1,0:T(8,128)S(1)} %get-tuple-element.35.part_ref, bf16[1088,128]{1,0:T(8,128)(2,1)S(1)} %collective-permute-done.7.msg_ref), custom_call_target="tpu_custom_call" | custom-call | tf_op jit(solution)/shard_map/last_part/pallas_call | solution.py:490
Async XLA Ops:
  0.0 7.5 %copy-start = (bf16[2,512,256]{2,1,0:T(8,128)(2,1)S(1)}, bf16[2,512,256]{2,1,0:T(8,128)(2,1)}, u32[]{:S(2)}) copy-start(bf16[2,512,256]{2,1,0:T(8,128)(2,1)} %constant.2.clone.band_ref.refs_11_) | copy-start | bytes 1572868
  2.5 11.8 %collective-permute-start.5 = (bf16[1248,128]{1,0:T(8,128)(2,1)S(1)}, bf16[1248,128]{1,0:T(8,128)(2,1)S(1)}, u32[]{:S(2)}, u32[]{:S(2)}) collective-permute-start(bf16[1248,128]{1,0:T(8,128)(2,1)S(1)} %get-tuple-element.33.own_ref), channel_id=1, source_target_pairs={{1,2},{2,1},{3,4},{4,3},{5,6},{6,5},{7,8},{8,7},{9,10},{10,9},{11,... | collective-permute-start | bytes 958472 | tf_op jit(solution)/shard_map/ppermute | solution.py:458
  6.2 1.3 %collective-permute-start = (bf16[16,2048]{1,0:T(8,128)(2,1)S(1)}, bf16[16,2048]{1,0:T(8,128)(2,1)S(1)}, u32[]{:S(2)}, u32[]{:S(2)}) collective-permute-start(bf16[16,2048]{1,0:T(8,128)(2,1)S(1)} %get-tuple-element.24), channel_id=1, source_target_pairs={{0,1},{1,0},{2,3},{3,2},{4,5},{5,4},{6,7},{7,6},{8,9},{9,8},{10,11... | collective-permute-start | bytes 196616 | tf_op jit(solution)/shard_map/ppermute | solution.py:459
  9.0 5.4 %collective-permute-start.1 = (bf16[4,2,128,128]{3,2,1,0:T(8,128)(2,1)S(1)}, bf16[4,2,128,128]{3,2,1,0:T(8,128)(2,1)S(1)}, u32[]{:S(2)}, u32[]{:S(2)}) collective-permute-start(bf16[4,2,128,128]{3,2,1,0:T(8,128)(2,1)S(1)} %get-tuple-element.29.refs_0_), channel_id=1, source_target_pairs={{0,1},{1,0},{2,3},{3,2},{4,5},{5,4},{6,7},{7,6},{8,9},{9,8},{10,11... | collective-permute-start | bytes 786440 | tf_op jit(solution)/shard_map/ppermute | solution.py:471
  9.2 11.0 %collective-permute-start.7 = (bf16[1088,128]{1,0:T(8,128)(2,1)S(1)}, bf16[1088,128]{1,0:T(8,128)(2,1)S(1)}, u32[]{:S(2)}, u32[]{:S(2)}) collective-permute-start(bf16[1088,128]{1,0:T(8,128)(2,1)S(1)} %get-tuple-element.36), channel_id=1, source_target_pairs={{1,2},{2,1},{3,4},{4,3},{5,6},{6,5},{7,8},{8,7},{9,10},{10,9},{11,... | collective-permute-start | bytes 835592 | tf_op jit(solution)/shard_map/ppermute | solution.py:470
  12.6 2.4 %collective-permute-start.2 = (bf16[4,2,128,128]{3,2,1,0:T(8,128)(2,1)S(1)}, bf16[4,2,128,128]{3,2,1,0:T(8,128)(2,1)S(1)}, u32[]{:S(2)}, u32[]{:S(2)}) collective-permute-start(bf16[4,2,128,128]{3,2,1,0:T(8,128)(2,1)S(1)} %get-tuple-element.30.refs_1_), channel_id=1, source_target_pairs={{0,1},{1,0},{2,3},{3,2},{4,5},{5,4},{6,7},{7,6},{8,9},{9,8},{10,11... | collective-permute-start | bytes 786440 | tf_op jit(solution)/shard_map/ppermute | solution.py:471
  12.7 2.4 %collective-permute-start.3 = (bf16[4,2,128,128]{3,2,1,0:T(8,128)(2,1)S(1)}, bf16[4,2,128,128]{3,2,1,0:T(8,128)(2,1)S(1)}, u32[]{:S(2)}, u32[]{:S(2)}) collective-permute-start(bf16[4,2,128,128]{3,2,1,0:T(8,128)(2,1)S(1)} %get-tuple-element.31.refs_2_), channel_id=1, source_target_pairs={{0,1},{1,0},{2,3},{3,2},{4,5},{5,4},{6,7},{7,6},{8,9},{9,8},{10,11... | collective-permute-start | bytes 786440 | tf_op jit(solution)/shard_map/ppermute | solution.py:471
  14.3 1.5 %collective-permute-start.4 = (bf16[4,2,128,128]{3,2,1,0:T(8,128)(2,1)S(1)}, bf16[4,2,128,128]{3,2,1,0:T(8,128)(2,1)S(1)}, u32[]{:S(2)}, u32[]{:S(2)}) collective-permute-start(bf16[4,2,128,128]{3,2,1,0:T(8,128)(2,1)S(1)} %get-tuple-element.32.refs_3_), channel_id=1, source_target_pairs={{0,1},{1,0},{2,3},{3,2},{4,5},{5,4},{6,7},{7,6},{8,9},{9,8},{10,11... | collective-permute-start | bytes 786440 | tf_op jit(solution)/shard_map/ppermute | solution.py:471
  14.5 1.5 %collective-permute-start.6 = (bf16[16,2048]{1,0:T(8,128)(2,1)S(1)}, bf16[16,2048]{1,0:T(8,128)(2,1)S(1)}, u32[]{:S(2)}, u32[]{:S(2)}) collective-permute-start(bf16[16,2048]{1,0:T(8,128)(2,1)S(1)} %outermost_rows.1.refs_8_), channel_id=1, source_target_pairs={{0,1},{1,0},{2,3},{3,2},{4,5},{5,4},{6,7},{7,6},{8,9},{9,8},{10,11... | collective-permute-start | bytes 196616 | tf_op jit(solution)/shard_map/ppermute | solution.py:480

commit v8 on v7

--- a/solution.py
+++ b/solution.py
@@ -14,7 +14,7 @@
 TILE = 16
 SHIFT_Y, SHIFT_X, SHIFT_Z = 2, 3, 4
 SPAN = LANES << SHIFT_X
-PACK = 4
+PACK = 8
 CUTS = (0, 8, 16)
 PIECES = 4
 F32 = jnp.float32
@@ -114,11 +114,12 @@
         numer_x += scaled * grad_x
         denom += (0.25 * weight(level)) * (grad_y * grad_y + grad_x * grad_x)
     inverse = 1.0 / denom
-    if extra is None:
-        inverse = jnp.where(iota(inverse.shape, 0) == jnp.where(upper, 0, half - 1), 0.0, inverse)
     found = []
     for comp, numer in enumerate((numer_y, numer_x)):
         raw = numer * inverse
+        if extra is None:
+            other = inno_ref[comp, exact, here].astype(F32)
+            raw = jnp.where(iota(raw.shape, 0) == jnp.where(upper, 0, half - 1), other, raw)
         found.append(split(raw))
         at = pl.ds(pl.multiple_of(comp * rows + start, TILE), half)
         for part, values in enumerate(found[-1]):
@@ -189,7 +190,7 @@
     for total in totals:
         msg_ref[pl.ds(at, groups), :] = dot(sum_y, total.astype(BF16)).astype(BF16)
         at += groups
-    kinds = 3 * levels
+    kinds = 3 * levels - 2
     shape = (PACK * kinds, PACK * levels * TILE)
     row, col = iota(shape, 0), iota(shape, 1)
     want = row - (col >> 6) * kinds
@@ -198,7 +199,7 @@
     outermost = place == jnp.where(upper, 0, TILE - 1)
     next_row = place == jnp.where(upper, 1, TILE - 2)
     of_back = one_hot(((want == level) & outermost) | ((want == levels + level) & next_row))
-    of_inno = one_hot((want == 2 * levels + level) & outermost)
+    of_inno = one_hot((want == 2 * levels + level - 2) & (level >= 2) & outermost)
     edge_at = tile_at(jnp.where(upper, 0, rows - TILE))
     for first in range(0, nblocks, PACK):
         back, inno = [], []
@@ -219,7 +220,7 @@
 
 
 def outer_rows(rows, nblocks, levels):
-    return nblocks * rows + (nblocks * LANES // SPAN) * (rows >> SHIFT_Y) + nblocks * 3 * levels
+    return nblocks * rows + (nblocks * LANES // SPAN) * (rows >> SHIFT_Y) + nblocks * (3 * levels - 2)
 
 
 def inner_kernel(weight_ref, inno_ref, back_ref, row_ref, band_ref, *refs):
@@ -270,25 +271,32 @@
 def outermost_kernel(weight_ref, own_ref, got_ref, out_ref):
     nblocks = out_ref.shape[1] // LANES
     levels = weight_ref.shape[0] // 2
-    kinds = 3 * levels
+    kinds = 3 * levels - 2
     base = own_ref.shape[0] - nblocks * kinds
-
-    def unpacked(ref):
+    rows, half = HALF, HALF // 2
+    first_core = parity() == 0
+    at = iota((8, rows), 0) * half
+
+    def unpacked(ref, upper):
         packs = [ref[pl.ds(base + k * kinds, PACK * kinds), :].astype(F32) for k in range(0, nblocks, PACK)]
-        return [
-            jnp.concatenate(
-                [p[j * kinds + kind * levels : j * kinds + (kind + 1) * levels] for p in packs for j in range(PACK)], axis=1
-            )
-            for kind in range(3)
-        ]
-
-    own, got = unpacked(own_ref), unpacked(got_ref)
+        pick = one_hot((iota((8, rows), 1) == at + jnp.where(upper, 0, half - 1)) & (at < rows))
+        some = []
+        for k in range(0, nblocks, 2):
+            pair = [ref[pl.ds((k + j) * rows, rows), :] for j in range(2)]
+            some.append(dot(pick, jnp.concatenate(pair, axis=1))[:2])
+        found = []
+        for low, high in ((0, levels), (levels, 2 * levels), (2 * levels, kinds)):
+            parts = [p[j * kinds + low : j * kinds + high] for p in packs for j in range(PACK)]
+            found.append(jnp.concatenate(parts, axis=1))
+        found[2] = jnp.concatenate([jnp.concatenate(some, axis=1), found[2]], axis=0)
+        return found
+
+    own, got = unpacked(own_ref, first_core), unpacked(got_ref, jnp.logical_not(first_core))
     here = jnp.concatenate([own[0], got[0]], axis=0)
     beyond = jnp.concatenate([got[0], own[0]], axis=0)
     before = jnp.concatenate([own[1], got[1]], axis=0)
     inno = jnp.concatenate([own[2], got[2]], axis=0)
     shape = here.shape
-    first_core = parity() == 0
     grad_y = jnp.where((iota(shape, 0) < levels) == first_core, before - beyond, beyond - before)
     lane = iota(shape, 1)
     left = jnp.where(lane == 0, 0.0, pltpu.roll(here, 1, 1))
@@ -320,7 +328,7 @@
 
 def near_kernel(*refs):
     raw_refs, near_refs = refs[:PIECES], refs[PIECES : 2 * PIECES]
-    edges_ref, near_edges_ref, msg_ref, band_ref, out_ref, taps_ref, total_ref = refs[2 * PIECES :]
+    edges_ref, near_edges_ref, msg_ref, band_ref, out_hbm, out_ref, taps_ref, total_ref, sem = refs[2 * PIECES :]
     _, rows, width = out_ref.shape
     nblocks = width // LANES
     half = rows // 2
@@ -328,8 +336,13 @@
     side = 1 - 2 * par
     offset = iota((rows, rows), 1) - iota((rows, rows), 0)
     near_taps = jnp.concatenate([taps(offset), taps(offset + side * rows)], axis=1)
+    column = iota(near_taps.shape, 1)
+    outermost = (column == par * (rows - 1)) | (column == (2 - par) * rows - 1 + par)
+    near_taps = jnp.where(outermost, 0.0, near_taps)
     near_high = near_taps.astype(BF16)
     toward = far_taps(rows, True)
+    outermost = iota(toward.shape, 1) == jnp.where(par == 0, half - 1, 0)
+    toward_inner = jnp.where(outermost, 0.0, toward)
     shape = (rows, TILE)
     kind = iota(shape, 1)
     own_at = jnp.where(par == 0, 0, rows - 1)
@@ -340,7 +353,7 @@
     stacked = []
     for comp in range(2):
         here = (kind < 8) & (kind & 1 == comp)
-        all_taps = [near_taps, toward, jnp.where(here, own_edges, 0.0), jnp.where(here, near_edges, 0.0)]
+        all_taps = [near_taps, toward_inner, jnp.where(here, own_edges, 0.0), jnp.where(here, near_edges, 0.0)]
         stacked.append(jnp.concatenate(split(jnp.concatenate(all_taps, axis=1)), axis=0))
     groups = half >> SHIFT_Y
     shape = (half, groups)
@@ -377,14 +390,20 @@
         here = pl.ds(first * LANES, 2 * LANES)
         out_ref[0, :, here] = result[:rows]
         out_ref[1, :, here] = result[rows:]
+    rest = pl.ds(pl.multiple_of((1 - par) * half, 8), half)
+    copies = [pltpu.make_async_copy(out_ref.at[k, rest, :], out_hbm.at[k, rest, :], sem.at[k]) for k in range(2)]
+    for copy in copies:
+        copy.start()
     for index, matrix in enumerate(last_taps(rows)):
         taps_ref[index] = matrix
+    for copy in copies:
+        copy.wait()
 
 
 def last_taps(rows):
     half = rows // 2
     away = far_taps(rows, False)
-    high, low = split(away)
+    high, low = split(jnp.where(parity() == 0, away[:half], away[half:]))
     groups = rows >> SHIFT_Z
     shape = (half, TILE)
     found = []
@@ -396,26 +415,25 @@
     return found
 
 
-def last_kernel(taps_ref, part_ref, msg_ref, out_hbm, buf, sem):
+def last_kernel(taps_ref, part_ref, msg_ref, out_in, out_hbm, buf, sem):
     _, rows, width = part_ref.shape
     nblocks = width // LANES
     half = rows // 2
     places = TILE // (rows >> SHIFT_Z)
+    reached = pl.ds(pl.multiple_of(parity() * half, 8), half)
     copies = []
-    for index, first in enumerate(range(0, nblocks, 2)):
-        here = pl.ds(first * LANES, 2 * LANES)
-        tiles = [
-            msg_ref[pl.ds(nblocks * rows + (2 * (index // places) + j) * TILE, TILE), :] for j in range(2)
-        ]
-        sums = jnp.concatenate(tiles, axis=1)
-        for comp in range(2):
-            got = [msg_ref[pl.ds((first + j) * rows + comp * half, half), :] for j in range(2)]
-            got = jnp.concatenate(got, axis=1)
+    for comp in range(2):
+        for index, first in enumerate(range(0, nblocks, 2)):
+            here = pl.ds(first * LANES, 2 * LANES)
+            got, sums = [], []
+            for j in range(2):
+                got.append(msg_ref[pl.ds((first + j) * rows + comp * half, half), :])
+                sums.append(msg_ref[pl.ds(nblocks * rows + (2 * (index // places) + j) * TILE, TILE), :])
+            got, sums = jnp.concatenate(got, axis=1), jnp.concatenate(sums, axis=1)
             part = dot(taps_ref[index % places * 2 + comp], jnp.concatenate([got, got, sums], axis=0))
-            buf[comp, :, here] = part_ref[comp, :, here] + part
-        copy = pltpu.make_async_copy(buf.at[:, :, here], out_hbm.at[:, :, here], sem.at[index])
-        copy.start()
-        copies.append(copy)
+            buf[comp, :, here] = part_ref[comp, reached, here] + part
+        copies.append(pltpu.make_async_copy(buf.at[comp], out_hbm.at[comp, reached, :], sem.at[comp]))
+        copies[-1].start()
     for copy in copies:
         copy.wait()
 
@@ -478,24 +496,25 @@
         name="outermost_rows",
     )(weight, outer, outer_got)
     near_edges = lax.ppermute(edges, "row", chip)
-    part, last = pl.pallas_call(
+    out, part, last = pl.pallas_call(
         near_kernel,
-        out_shape=[result, jax.ShapeDtypeStruct((2 * TILE // (rows >> SHIFT_Z), rows, rows + TILE), BF16)],
+        out_shape=[result, result, jax.ShapeDtypeStruct((2 * TILE // (rows >> SHIFT_Z), half, rows + TILE), BF16)],
         in_specs=[VMEM] * (2 * PIECES + 4),
-        out_specs=[VMEM] * 2,
-        scratch_shapes=[pltpu.VMEM((nblocks, 2 * both, LANES), BF16)],
+        out_specs=[HBM] + [VMEM] * 2,
+        scratch_shapes=[pltpu.VMEM((nblocks, 2 * both, LANES), BF16), pltpu.SemaphoreType.DMA((2,))],
         compiler_params=PARAMS,
         name="near_part",
     )(*raws, *nears, edges, near_edges, outer_got, band)
     return pl.pallas_call(
         last_kernel,
         out_shape=result,
-        in_specs=[VMEM] * 3,
+        in_specs=[VMEM] * 3 + [HBM],
         out_specs=HBM,
-        scratch_shapes=[pltpu.VMEM((2, rows, width), F32), pltpu.SemaphoreType.DMA((nblocks // 2,))],
+        input_output_aliases={3: 0},
+        scratch_shapes=[pltpu.VMEM((2, half, width), F32), pltpu.SemaphoreType.DMA((2,))],
         compiler_params=PARAMS,
         name="last_part",
-    )(last, part, inner_got)
+    )(last, part, inner_got, out)
 
 
 def solution(mesh):

time: 21.7 us -> 21.3 us (0.982)
  waiting for transfers between devices: 5.51 us -> 4.6 us
  Pallas kernels: 7.38 us -> 7.94 us
    ppermute x1, waiting for transfers between devices: 2.28 us -> 1.46 us  [body(): inner_got = lax.ppermute(inner, 'row', away)]
    pallas_call x2, Pallas kernels: 3.2 us -> 3.71 us  [the longest x1 2.72 us: body(): pl.pallas_call(near_kernel, out_shape=[result, result, jax.ShapeDtypeStru...]
  transfers between devices with their start and end apart: 8 -> 8, of which waited for: 5 -> 5; matrix products, arithmetic and copies ran while one was open for 0% -> 0% of each run, Pallas kernels for 17% -> 21%
where the time goes in v8:
time: 21.3 us; the launch traced here: 21.1 us
  starting transfers between devices  8.46 us (40%)
  Pallas kernels  7.94 us (37%)
  waiting for transfers between devices  4.6 us (22%)
    ppermute x1, starting transfers between devices, body(): outer_got = lax.ppermute(outer, 'row', away)  3.7 us
    ppermute x1, starting transfers between devices, body(): inner_got = lax.ppermute(inner, 'row', away)  3.34 us
    pallas_call x1, Pallas kernels, body(): pl.pallas_call(near_kernel, out_shape=[result, result, jax.ShapeDtypeStru...  2.72 us
    pallas_call x1, Pallas kernels, body(): pl.pallas_call(outer_kernel, out_shape=[piece] * PIECES + [jax.ShapeDtype...  2.49 us
    ppermute x1, waiting for transfers between devices, body(): inner_got = lax.ppermute(inner, 'row', away)  1.46 us
    pallas_call x1, Pallas kernels, body(): pl.pallas_call(inner_kernel, out_shape=[piece] * PIECES + [jax.ShapeDtype...  1.46 us
    ppermute x1, waiting for transfers between devices, body(): row = lax.ppermute(row, 'row', chip)  1.24 us
    ppermute x1, waiting for transfers between devices, body(): outer_got = lax.ppermute(outer, 'row', away)  1 us
  transfers between devices with their start and end apart: 8, of which 5 were waited for; matrix products, arithmetic and copies ran while one was open for 0% of the time, Pallas kernels for 21%

profile of v8, /device:TPU:11, one launch (start us, length us, event | category | flops | bytes accessed | tf_op | source)
XLA Modules:
  0.0 21.1 jit_solution(15771063185572860910)
XLA Ops:
  0.0 0.0 copy-start
  0.0 2.5 %outer_half.1 = (bf16[4,2,128,128]{3,2,1,0:T(8,128)(2,1)S(1)}, bf16[4,2,128,128]{3,2,1,0:T(8,128)(2,1)S(1)}, bf16[4,2,128,128]{3,2,1,0:T(8,128)(2,1)S(1)}, bf16[...) custom-call(f32[4]{0:T(128)} %lw_hbm.1, ...), custom_call_target="tpu_custom_call" | custom-call | tf_op jit(solution)/shard_map/outer_half/pallas_call | solution.py:454
  2.5 3.7 %collective-permute-start.5 = (bf16[1216,128]{1,0:T(8,128)(2,1)S(1)}, bf16[1216,128]{1,0:T(8,128)(2,1)S(1)}, u32[]{:S(2)}, u32[]{:S(2)}) collective-permute-start(bf16[1216,128]{1,0:T(8,128)(2,1)S(1)} %get-tuple-element.34.own_ref), channel_id=1, source_target_pairs={{1,2},{2,1},{3,4},{4,3},{5,6},{6,5},{7,8},{8,7},{9,10},{10,9},{11,... | collective-permute-start | bytes 933896 | tf_op jit(solution)/shard_map/ppermute | solution.py:476
  6.2 0.1 collective-permute-start
  6.3 1.2 %collective-permute-done.row_ref = bf16[16,2048]{1,0:T(8,128)(2,1)S(1)} collective-permute-done((bf16[16,2048]{1,0:T(8,128)(2,1)S(1)}, bf16[16,2048]{1,0:T(8,128)(2,1)S(1)}, u32[]{:S(2)}, u32[]{:S(2)}) %collective-permute-start) | collective-permute-done | bytes 65568 | tf_op jit(solution)/shard_map/ppermute | solution.py:477
  7.5 0.0 copy-done
  7.5 1.5 %inner_half.1 = (bf16[4,2,128,128]{3,2,1,0:T(8,128)(2,1)S(1)}, bf16[4,2,128,128]{3,2,1,0:T(8,128)(2,1)S(1)}, bf16[4,2,128,128]{3,2,1,0:T(8,128)(2,1)S(1)}, bf16[...) custom-call(f32[8,256]{1,0:T(8,128)S(1)} %get-tuple-element.22.weigh, ...), custom_call_target="tpu_custom_call", output_to_operand_aliasing={{0}: (5, {}), {1}: (6, {}), {2}: (7, {}), {3}: (8, {})} | custom-call | tf_op jit(solution)/shard_map/inner_half/pallas_call | solution.py:478
  9.0 0.2 collective-permute-start.1
  9.2 3.3 %collective-permute-start.7 = (bf16[1088,128]{1,0:T(8,128)(2,1)S(1)}, bf16[1088,128]{1,0:T(8,128)(2,1)S(1)}, u32[]{:S(2)}, u32[]{:S(2)}) collective-permute-start(bf16[1088,128]{1,0:T(8,128)(2,1)S(1)} %get-tuple-element.37), channel_id=1, source_target_pairs={{1,2},{2,1},{3,4},{4,3},{5,6},{6,5},{7,8},{8,7},{9,10},{10,9},{11,... | collective-permute-start | bytes 835592 | tf_op jit(solution)/shard_map/ppermute | solution.py:488
  12.5 0.1 collective-permute-start.2
  12.7 0.4 %collective-permute-start.3 = (bf16[4,2,128,128]{3,2,1,0:T(8,128)(2,1)S(1)}, bf16[4,2,128,128]{3,2,1,0:T(8,128)(2,1)S(1)}, u32[]{:S(2)}, u32[]{:S(2)}) collective-permute-start(bf16[4,2,128,128]{3,2,1,0:T(8,128)(2,1)S(1)} %get-tuple-element.32.refs_2_), channel_id=1, source_target_pairs={{0,1},{1,0},{2,3},{3,2},{4,5},{5,4},{6,7},{7,6},{8,9},{9,8},{10,11... | collective-permute-start | bytes 786440 | tf_op jit(solution)/shard_map/ppermute | solution.py:489
  13.1 1.0 %collective-permute-done.5.got_ref.refs_10_ = bf16[1216,128]{1,0:T(8,128)(2,1)S(1)} collective-permute-done((bf16[1216,128]{1,0:T(8,128)(2,1)S(1)}, bf16[1216,128]{1,0:T(8,128)(2,1)S(1)}, u32[]{:S(2)}, u32[]{:S(2)}) %collective-permute-start.5) | collective-permute-done | bytes 311328 | tf_op jit(solution)/shard_map/ppermute | solution.py:476
  14.1 0.0 collective-permute-start.4
  14.1 0.3 %outermost_rows.1.refs_8_ = bf16[16,2048]{1,0:T(8,128)(2,1)S(1)} custom-call(f32[8,256]{1,0:T(8,128)S(1)} %get-tuple-element.22.weight_ref, bf16[1216,128]{1,0:T(8,128)(2,1)S(1)} %get-tuple-element.34.own_ref, bf16[1216,128]{1,0:T(8,128)(2,1)S(1)} %collective-permute-done.5.got_ref.refs_10_), custom_call_target="tpu_custom_call" | custom-call | tf_op jit(solution)/shard_map/outermost_rows/pallas_call | solution.py:490
  14.4 0.0 collective-permute-done.1.refs_4_
  14.4 0.6 %collective-permute-start.6 = (bf16[16,2048]{1,0:T(8,128)(2,1)S(1)}, bf16[16,2048]{1,0:T(8,128)(2,1)S(1)}, u32[]{:S(2)}, u32[]{:S(2)}) collective-permute-start(bf16[16,2048]{1,0:T(8,128)(2,1)S(1)} %outermost_rows.1.refs_8_), channel_id=1, source_target_pairs={{0,1},{1,0},{2,3},{3,2},{4,5},{5,4},{6,7},{7,6},{8,9},{9,8},{10,11... | collective-permute-start | bytes 196616 | tf_op jit(solution)/shard_map/ppermute | solution.py:498
  15.0 0.0 collective-permute-done.2.refs_5_
  15.0 0.0 collective-permute-done.3.refs_6_
  15.0 0.7 %collective-permute-done.4.refs_7_ = bf16[4,2,128,128]{3,2,1,0:T(8,128)(2,1)S(1)} collective-permute-done((bf16[4,2,128,128]{3,2,1,0:T(8,128)(2,1)S(1)}, bf16[4,2,128,128]{3,2,1,0:T(8,128)(2,1)S(1)}, u32[]{:S(2)}, u32[]{:S(2)}) %collective-permute-start.4) | collective-permute-done | bytes 262176 | tf_op jit(solution)/shard_map/ppermute | solution.py:489
  15.6 0.2 %collective-permute-done.6.refs_9_ = bf16[16,2048]{1,0:T(8,128)(2,1)S(1)} collective-permute-done((bf16[16,2048]{1,0:T(8,128)(2,1)S(1)}, bf16[16,2048]{1,0:T(8,128)(2,1)S(1)}, u32[]{:S(2)}, u32[]{:S(2)}) %collective-permute-start.6) | collective-permute-done | bytes 65568 | tf_op jit(solution)/shard_map/ppermute | solution.py:498
  15.9 2.7 %near_part.1 = (f32[2,64,2048]{2,1,0:T(8,128)}, f32[2,64,2048]{2,1,0:T(8,128)S(1)}, bf16[8,32,80]{2,1,0:T(8,128)(2,1)S(1)}) custom-call(bf16[4,2,128,128]{3,2,1,0:T(8,128)(2,1)S(1)} %get-tuple-element.30.refs_0_, bf16[4,2,128,128]{3,2,1,0:T(8,128)(2,1)S(1)} %get-tuple-element.31.refs_1_, bf16[4,2,128,128]{3,2,1,0:T(8,128)(2,1)S(1)} %get-tuple-element.32.refs_2_, ...), custom_call_target="tpu_custom_call" | custom-call | tf_op jit(solution)/shard_map/near_part/pallas_call | solution.py:499
  18.6 1.5 %collective-permute-done.7.msg_ref = bf16[1088,128]{1,0:T(8,128)(2,1)S(1)} collective-permute-done((bf16[1088,128]{1,0:T(8,128)(2,1)S(1)}, bf16[1088,128]{1,0:T(8,128)(2,1)S(1)}, u32[]{:S(2)}, u32[]{:S(2)}) %collective-permute-start.7) | collective-permute-done | bytes 278560 | tf_op jit(solution)/shard_map/ppermute | solution.py:488
  20.1 1.0 %last_part.1 = f32[2,64,2048]{2,1,0:T(8,128)} custom-call(bf16[8,32,80]{2,1,0:T(8,128)(2,1)S(1)} %get-tuple-element.35.taps_ref, f32[2,64,2048]{2,1,0:T(8,128)S(1)} %get-tuple-element.36.part_ref, bf16[1088,128]{1,0:T(8,128)(2,1)S(1)} %collective-permute-done.7.msg_ref, f32[2,64,2048]{2,1,0:T(8,128)} %get-tuple-element.38.out_in), custom_call_target="tpu_custom_call", output_to_operand_aliasing={{}: (3, {})} | custom-call | tf_op jit(solution)/shard_map/last_part/pallas_call | solution.py:508
Async XLA Ops:
  0.0 7.5 %copy-start = (bf16[2,512,256]{2,1,0:T(8,128)(2,1)S(1)}, bf16[2,512,256]{2,1,0:T(8,128)(2,1)}, u32[]{:S(2)}) copy-start(bf16[2,512,256]{2,1,0:T(8,128)(2,1)} %constant.2.clone.band_ref.refs_11_) | copy-start | bytes 1572868
  2.5 11.6 %collective-permute-start.5 = (bf16[1216,128]{1,0:T(8,128)(2,1)S(1)}, bf16[1216,128]{1,0:T(8,128)(2,1)S(1)}, u32[]{:S(2)}, u32[]{:S(2)}) collective-permute-start(bf16[1216,128]{1,0:T(8,128)(2,1)S(1)} %get-tuple-element.34.own_ref), channel_id=1, source_target_pairs={{1,2},{2,1},{3,4},{4,3},{5,6},{6,5},{7,8},{8,7},{9,10},{10,9},{11,... | collective-permute-start | bytes 933896 | tf_op jit(solution)/shard_map/ppermute | solution.py:476
  6.2 1.3 %collective-permute-start = (bf16[16,2048]{1,0:T(8,128)(2,1)S(1)}, bf16[16,2048]{1,0:T(8,128)(2,1)S(1)}, u32[]{:S(2)}, u32[]{:S(2)}) collective-permute-start(bf16[16,2048]{1,0:T(8,128)(2,1)S(1)} %get-tuple-element.25), channel_id=1, source_target_pairs={{0,1},{1,0},{2,3},{3,2},{4,5},{5,4},{6,7},{7,6},{8,9},{9,8},{10,11... | collective-permute-start | bytes 196616 | tf_op jit(solution)/shard_map/ppermute | solution.py:477
  9.0 5.4 %collective-permute-start.1 = (bf16[4,2,128,128]{3,2,1,0:T(8,128)(2,1)S(1)}, bf16[4,2,128,128]{3,2,1,0:T(8,128)(2,1)S(1)}, u32[]{:S(2)}, u32[]{:S(2)}) collective-permute-start(bf16[4,2,128,128]{3,2,1,0:T(8,128)(2,1)S(1)} %get-tuple-element.30.refs_0_), channel_id=1, source_target_pairs={{0,1},{1,0},{2,3},{3,2},{4,5},{5,4},{6,7},{7,6},{8,9},{9,8},{10,11... | collective-permute-start | bytes 786440 | tf_op jit(solution)/shard_map/ppermute | solution.py:489
  9.2 10.9 %collective-permute-start.7 = (bf16[1088,128]{1,0:T(8,128)(2,1)S(1)}, bf16[1088,128]{1,0:T(8,128)(2,1)S(1)}, u32[]{:S(2)}, u32[]{:S(2)}) collective-permute-start(bf16[1088,128]{1,0:T(8,128)(2,1)S(1)} %get-tuple-element.37), channel_id=1, source_target_pairs={{1,2},{2,1},{3,4},{4,3},{5,6},{6,5},{7,8},{8,7},{9,10},{10,9},{11,... | collective-permute-start | bytes 835592 | tf_op jit(solution)/shard_map/ppermute | solution.py:488
  12.5 2.5 %collective-permute-start.2 = (bf16[4,2,128,128]{3,2,1,0:T(8,128)(2,1)S(1)}, bf16[4,2,128,128]{3,2,1,0:T(8,128)(2,1)S(1)}, u32[]{:S(2)}, u32[]{:S(2)}) collective-permute-start(bf16[4,2,128,128]{3,2,1,0:T(8,128)(2,1)S(1)} %get-tuple-element.31.refs_1_), channel_id=1, source_target_pairs={{0,1},{1,0},{2,3},{3,2},{4,5},{5,4},{6,7},{7,6},{8,9},{9,8},{10,11... | collective-permute-start | bytes 786440 | tf_op jit(solution)/shard_map/ppermute | solution.py:489
  12.7 2.3 %collective-permute-start.3 = (bf16[4,2,128,128]{3,2,1,0:T(8,128)(2,1)S(1)}, bf16[4,2,128,128]{3,2,1,0:T(8,128)(2,1)S(1)}, u32[]{:S(2)}, u32[]{:S(2)}) collective-permute-start(bf16[4,2,128,128]{3,2,1,0:T(8,128)(2,1)S(1)} %get-tuple-element.32.refs_2_), channel_id=1, source_target_pairs={{0,1},{1,0},{2,3},{3,2},{4,5},{5,4},{6,7},{7,6},{8,9},{9,8},{10,11... | collective-permute-start | bytes 786440 | tf_op jit(solution)/shard_map/ppermute | solution.py:489
  14.1 1.5 %collective-permute-start.4 = (bf16[4,2,128,128]{3,2,1,0:T(8,128)(2,1)S(1)}, bf16[4,2,128,128]{3,2,1,0:T(8,128)(2,1)S(1)}, u32[]{:S(2)}, u32[]{:S(2)}) collective-permute-start(bf16[4,2,128,128]{3,2,1,0:T(8,128)(2,1)S(1)} %get-tuple-element.33.refs_3_), channel_id=1, source_target_pairs={{0,1},{1,0},{2,3},{3,2},{4,5},{5,4},{6,7},{7,6},{8,9},{9,8},{10,11... | collective-permute-start | bytes 786440 | tf_op jit(solution)/shard_map/ppermute | solution.py:489
  14.4 1.5 %collective-permute-start.6 = (bf16[16,2048]{1,0:T(8,128)(2,1)S(1)}, bf16[16,2048]{1,0:T(8,128)(2,1)S(1)}, u32[]{:S(2)}, u32[]{:S(2)}) collective-permute-start(bf16[16,2048]{1,0:T(8,128)(2,1)S(1)} %outermost_rows.1.refs_8_), channel_id=1, source_target_pairs={{0,1},{1,0},{2,3},{3,2},{4,5},{5,4},{6,7},{7,6},{8,9},{9,8},{10,11... | collective-permute-start | bytes 196616 | tf_op jit(solution)/shard_map/ppermute | solution.py:498

commit v9 on v8

--- a/solution.py
+++ b/solution.py
@@ -136,7 +136,7 @@
 
 
 def outer_kernel(lw_hbm, inno_hbm, back_hbm, *refs):
-    *raw_refs, msg_ref, row_ref, inno_ref, back_ref, weight_ref, lw_ref, sum_ref, sems, rest_sems, lw_sem = refs
+    *raw_refs, msg_ref, row_ref, inno_ref, back_ref, weight_ref, lw_ref, sum_ref, pick_ref, total_ref, sems, rest_sems, lw_sem = refs
     levels, rows, width = inno_ref.shape
     half = rows // 2
     deep = half + TILE
@@ -168,11 +168,47 @@
     diff_y, diff_x = differences(upper, half)
     sum_ref[...] = one_hot(iota(sum_ref.shape, 0) >> SHIFT_X == iota(sum_ref.shape, 1))
     groups = rows >> SHIFT_Y
-    shape = (groups, rows)
-    sum_y = one_hot(iota(shape, 1) >> SHIFT_Y == iota(shape, 0))
+    kinds = 3 * levels - 2
+    row, col = iota(pick_ref.shape[1:], 0), iota(pick_ref.shape[1:], 1)
+    want = row - (col >> 6) * kinds
+    level = (col >> 4) & (levels - 1)
+    place = col & (TILE - 1)
+    outermost = place == jnp.where(upper, 0, TILE - 1)
+    next_row = place == jnp.where(upper, 1, TILE - 2)
+    pick_ref[0] = one_hot(((want == level) & outermost) | ((want == levels + level) & next_row))
+    pick_ref[1] = one_hot((want == 2 * levels + level - 2) & (level >= 2) & outermost)
+    shape = (TILE, levels * TILE)
+    pick_near = one_hot(iota(shape, 1) == iota(shape, 0) * TILE + jnp.where(upper, TILE - 1, 0))
     weights.wait()
+    for level in range(2 * levels):
+        weight_ref[level : level + 1, :] = jnp.full((1, weight_ref.shape[1]), lw_ref[level % levels])
+    base = nblocks * rows
+    spans = range(0, nblocks, SPAN // LANES)
+
+    def input_rows():
+        near_rows = back_ref[:, tile_at(jnp.where(upper, rows - TILE, 0)), :]
+        row_ref[...] = dot(pick_near, near_rows.reshape(levels * TILE, -1)).astype(BF16)
+        edge_at = tile_at(jnp.where(upper, 0, rows - TILE))
+        for first in range(0, nblocks, PACK):
+            back, inno = [], []
+            for k in range(first, first + PACK):
+                here = pl.ds(k * LANES, LANES)
+                back.append(back_ref[:, edge_at, here].reshape(levels * TILE, LANES))
+                inno.append(inno_ref[:, edge_at, here].reshape(levels * TILE, LANES))
+            tile = dot(pick_ref[0], jnp.concatenate(back, axis=0)) + dot(pick_ref[1], jnp.concatenate(inno, axis=0))
+            at = base + len(spans) * groups + first * kinds
+            msg_ref[pl.ds(at, PACK * kinds), :] = tile.astype(BF16)
+
+    def residuals(span):
+        lows = [
+            jnp.concatenate(half_of(block_of(raw_refs, k), rows, start, 1), axis=0)
+            for k in range(span, span + SPAN // LANES)
+        ]
+        total_ref[...] = dot(jnp.concatenate(lows, axis=1), sum_ref[...])
+        found = sum(total_ref[pl.ds(k, groups, stride=1 << SHIFT_Y), :] for k in range(1 << SHIFT_Y))
+        msg_ref[pl.ds(base + span // (SPAN // LANES) * groups, groups), :] = found.astype(BF16)
+
     waited = 0
-    at = nblocks * rows
     for first in range(0, nblocks, 2):
         while cuts[waited] < window(first, nblocks)[1] * LANES:
             for copy in copies[waited]:
@@ -182,40 +218,11 @@
         for comp, (high, _) in enumerate(found):
             for j in range(2):
                 msg_ref[pl.ds((first + j) * rows + comp * half, half), :] = high[:, j * LANES : (j + 1) * LANES]
-    totals = []
-    for span in range(0, nblocks, SPAN // LANES):
-        blocks = range(span, span + SPAN // LANES)
-        lows = [jnp.concatenate(half_of(block_of(raw_refs, k), rows, start, 1), axis=0) for k in blocks]
-        totals.append(dot(jnp.concatenate(lows, axis=1), sum_ref[...]))
-    for total in totals:
-        msg_ref[pl.ds(at, groups), :] = dot(sum_y, total.astype(BF16)).astype(BF16)
-        at += groups
-    kinds = 3 * levels - 2
-    shape = (PACK * kinds, PACK * levels * TILE)
-    row, col = iota(shape, 0), iota(shape, 1)
-    want = row - (col >> 6) * kinds
-    level = (col >> 4) & (levels - 1)
-    place = col & (TILE - 1)
-    outermost = place == jnp.where(upper, 0, TILE - 1)
-    next_row = place == jnp.where(upper, 1, TILE - 2)
-    of_back = one_hot(((want == level) & outermost) | ((want == levels + level) & next_row))
-    of_inno = one_hot((want == 2 * levels + level - 2) & (level >= 2) & outermost)
-    edge_at = tile_at(jnp.where(upper, 0, rows - TILE))
-    for first in range(0, nblocks, PACK):
-        back, inno = [], []
-        for k in range(first, first + PACK):
-            here = pl.ds(k * LANES, LANES)
-            back.append(back_ref[:, edge_at, here].reshape(levels * TILE, LANES))
-            inno.append(inno_ref[:, edge_at, here].reshape(levels * TILE, LANES))
-        tile = dot(of_back, jnp.concatenate(back, axis=0)) + dot(of_inno, jnp.concatenate(inno, axis=0))
-        msg_ref[pl.ds(at, PACK * kinds), :] = tile.astype(BF16)
-        at += PACK * kinds
-    for level in range(2 * levels):
-        weight_ref[level : level + 1, :] = jnp.full((1, weight_ref.shape[1]), lw_ref[level % levels])
-    shape = (TILE, levels * TILE)
-    pick = one_hot(iota(shape, 1) == iota(shape, 0) * TILE + jnp.where(upper, TILE - 1, 0))
-    near_rows = back_ref[:, tile_at(jnp.where(upper, rows - TILE, 0)), :]
-    row_ref[...] = dot(pick, near_rows.reshape(levels * TILE, -1)).astype(BF16)
+        if first == spans[-1]:
+            for span in spans[:-1]:
+                residuals(span)
+    input_rows()
+    residuals(spans[-1])
     other.wait()
 
 
@@ -466,6 +473,8 @@
         scratch_shapes=[
             pltpu.SMEM((levels,), F32),
             pltpu.VMEM((SPAN, LANES), BF16),
+            pltpu.VMEM((2, PACK * (3 * levels - 2), PACK * levels * TILE), BF16),
+            pltpu.VMEM((rows, LANES), F32),
             pltpu.SemaphoreType.DMA((2, len(CUTS) - 1)),
             pltpu.SemaphoreType.DMA((2,)),
             pltpu.SemaphoreType.DMA,

time: 21.3 us -> 21.2 us (level)
  no operation moved by 1% of the time
where the time goes in v9:
time: 21.2 us; the launch traced here: 21 us
  starting transfers between devices  8.47 us (40%)
  Pallas kernels  7.81 us (37%)
  waiting for transfers between devices  4.61 us (22%)
    ppermute x1, starting transfers between devices, body(): outer_got = lax.ppermute(outer, 'row', away)  3.71 us
    ppermute x1, starting transfers between devices, body(): inner_got = lax.ppermute(inner, 'row', away)  3.34 us
    pallas_call x1, Pallas kernels, body(): pl.pallas_call(near_kernel, out_shape=[result, result, jax.ShapeDtypeStru...  2.72 us
    pallas_call x1, Pallas kernels, body(): pl.pallas_call(outer_kernel, out_shape=[piece] * PIECES + [jax.ShapeDtype...  2.37 us
    ppermute x1, waiting for transfers between devices, body(): inner_got = lax.ppermute(inner, 'row', away)  1.47 us
    pallas_call x1, Pallas kernels, body(): pl.pallas_call(inner_kernel, out_shape=[piece] * PIECES + [jax.ShapeDtype...  1.46 us
    ppermute x1, waiting for transfers between devices, body(): row = lax.ppermute(row, 'row', chip)  1.24 us
    ppermute x1, waiting for transfers between devices, body(): outer_got = lax.ppermute(outer, 'row', away)  1 us
  transfers between devices with their start and end apart: 8, of which 5 were waited for; matrix products, arithmetic and copies ran while one was open for 0% of the time, Pallas kernels for 21%

profile of v9, /device:TPU:11, one launch (start us, length us, event | category | flops | bytes accessed | tf_op | source)
XLA Modules:
  0.0 21.0 jit_solution(547590032400840823)
XLA Ops:
  0.0 0.0 copy-start
  0.0 2.4 %outer_half.1 = (bf16[4,2,128,128]{3,2,1,0:T(8,128)(2,1)S(1)}, bf16[4,2,128,128]{3,2,1,0:T(8,128)(2,1)S(1)}, bf16[4,2,128,128]{3,2,1,0:T(8,128)(2,1)S(1)}, bf16[...) custom-call(f32[4]{0:T(128)} %lw_hbm.1, ...), custom_call_target="tpu_custom_call" | custom-call | tf_op jit(solution)/shard_map/outer_half/pallas_call | solution.py:461
  2.4 3.7 %collective-permute-start.5 = (bf16[1216,128]{1,0:T(8,128)(2,1)S(1)}, bf16[1216,128]{1,0:T(8,128)(2,1)S(1)}, u32[]{:S(2)}, u32[]{:S(2)}) collective-permute-start(bf16[1216,128]{1,0:T(8,128)(2,1)S(1)} %get-tuple-element.34.own_ref), channel_id=1, source_target_pairs={{1,2},{2,1},{3,4},{4,3},{5,6},{6,5},{7,8},{8,7},{9,10},{10,9},{11,... | collective-permute-start | bytes 933896 | tf_op jit(solution)/shard_map/ppermute | solution.py:485
  6.1 0.1 collective-permute-start
  6.2 1.2 %collective-permute-done.row_ref = bf16[16,2048]{1,0:T(8,128)(2,1)S(1)} collective-permute-done((bf16[16,2048]{1,0:T(8,128)(2,1)S(1)}, bf16[16,2048]{1,0:T(8,128)(2,1)S(1)}, u32[]{:S(2)}, u32[]{:S(2)}) %collective-permute-start) | collective-permute-done | bytes 65568 | tf_op jit(solution)/shard_map/ppermute | solution.py:486
  7.4 0.0 copy-done
  7.4 1.5 %inner_half.1 = (bf16[4,2,128,128]{3,2,1,0:T(8,128)(2,1)S(1)}, bf16[4,2,128,128]{3,2,1,0:T(8,128)(2,1)S(1)}, bf16[4,2,128,128]{3,2,1,0:T(8,128)(2,1)S(1)}, bf16[...) custom-call(f32[8,256]{1,0:T(8,128)S(1)} %get-tuple-element.22.weigh, ...), custom_call_target="tpu_custom_call", output_to_operand_aliasing={{0}: (5, {}), {1}: (6, {}), {2}: (7, {}), {3}: (8, {})} | custom-call | tf_op jit(solution)/shard_map/inner_half/pallas_call | solution.py:487
  8.9 0.2 collective-permute-start.1
  9.1 3.3 %collective-permute-start.7 = (bf16[1088,128]{1,0:T(8,128)(2,1)S(1)}, bf16[1088,128]{1,0:T(8,128)(2,1)S(1)}, u32[]{:S(2)}, u32[]{:S(2)}) collective-permute-start(bf16[1088,128]{1,0:T(8,128)(2,1)S(1)} %get-tuple-element.37), channel_id=1, source_target_pairs={{1,2},{2,1},{3,4},{4,3},{5,6},{6,5},{7,8},{8,7},{9,10},{10,9},{11,... | collective-permute-start | bytes 835592 | tf_op jit(solution)/shard_map/ppermute | solution.py:497
  12.4 0.1 collective-permute-start.2
  12.6 0.4 %collective-permute-start.3 = (bf16[4,2,128,128]{3,2,1,0:T(8,128)(2,1)S(1)}, bf16[4,2,128,128]{3,2,1,0:T(8,128)(2,1)S(1)}, u32[]{:S(2)}, u32[]{:S(2)}) collective-permute-start(bf16[4,2,128,128]{3,2,1,0:T(8,128)(2,1)S(1)} %get-tuple-element.32.refs_2_), channel_id=1, source_target_pairs={{0,1},{1,0},{2,3},{3,2},{4,5},{5,4},{6,7},{7,6},{8,9},{9,8},{10,11... | collective-permute-start | bytes 786440 | tf_op jit(solution)/shard_map/ppermute | solution.py:498
  13.0 1.0 %collective-permute-done.5.got_ref.refs_10_ = bf16[1216,128]{1,0:T(8,128)(2,1)S(1)} collective-permute-done((bf16[1216,128]{1,0:T(8,128)(2,1)S(1)}, bf16[1216,128]{1,0:T(8,128)(2,1)S(1)}, u32[]{:S(2)}, u32[]{:S(2)}) %collective-permute-start.5) | collective-permute-done | bytes 311328 | tf_op jit(solution)/shard_map/ppermute | solution.py:485
  14.0 0.0 collective-permute-start.4
  14.0 0.3 %outermost_rows.1.refs_8_ = bf16[16,2048]{1,0:T(8,128)(2,1)S(1)} custom-call(f32[8,256]{1,0:T(8,128)S(1)} %get-tuple-element.22.weight_ref, bf16[1216,128]{1,0:T(8,128)(2,1)S(1)} %get-tuple-element.34.own_ref, bf16[1216,128]{1,0:T(8,128)(2,1)S(1)} %collective-permute-done.5.got_ref.refs_10_), custom_call_target="tpu_custom_call" | custom-call | tf_op jit(solution)/shard_map/outermost_rows/pallas_call | solution.py:499
  14.3 0.0 collective-permute-done.1.refs_4_
  14.3 0.6 %collective-permute-start.6 = (bf16[16,2048]{1,0:T(8,128)(2,1)S(1)}, bf16[16,2048]{1,0:T(8,128)(2,1)S(1)}, u32[]{:S(2)}, u32[]{:S(2)}) collective-permute-start(bf16[16,2048]{1,0:T(8,128)(2,1)S(1)} %outermost_rows.1.refs_8_), channel_id=1, source_target_pairs={{0,1},{1,0},{2,3},{3,2},{4,5},{5,4},{6,7},{7,6},{8,9},{9,8},{10,11... | collective-permute-start | bytes 196616 | tf_op jit(solution)/shard_map/ppermute | solution.py:507
  14.9 0.0 collective-permute-done.2.refs_5_
  14.9 0.0 collective-permute-done.3.refs_6_
  14.9 0.7 %collective-permute-done.4.refs_7_ = bf16[4,2,128,128]{3,2,1,0:T(8,128)(2,1)S(1)} collective-permute-done((bf16[4,2,128,128]{3,2,1,0:T(8,128)(2,1)S(1)}, bf16[4,2,128,128]{3,2,1,0:T(8,128)(2,1)S(1)}, u32[]{:S(2)}, u32[]{:S(2)}) %collective-permute-start.4) | collective-permute-done | bytes 262176 | tf_op jit(solution)/shard_map/ppermute | solution.py:498
  15.5 0.2 %collective-permute-done.6.refs_9_ = bf16[16,2048]{1,0:T(8,128)(2,1)S(1)} collective-permute-done((bf16[16,2048]{1,0:T(8,128)(2,1)S(1)}, bf16[16,2048]{1,0:T(8,128)(2,1)S(1)}, u32[]{:S(2)}, u32[]{:S(2)}) %collective-permute-start.6) | collective-permute-done | bytes 65568 | tf_op jit(solution)/shard_map/ppermute | solution.py:507
  15.8 2.7 %near_part.1 = (f32[2,64,2048]{2,1,0:T(8,128)}, f32[2,64,2048]{2,1,0:T(8,128)S(1)}, bf16[8,32,80]{2,1,0:T(8,128)(2,1)S(1)}) custom-call(bf16[4,2,128,128]{3,2,1,0:T(8,128)(2,1)S(1)} %get-tuple-element.30.refs_0_, bf16[4,2,128,128]{3,2,1,0:T(8,128)(2,1)S(1)} %get-tuple-element.31.refs_1_, bf16[4,2,128,128]{3,2,1,0:T(8,128)(2,1)S(1)} %get-tuple-element.32.refs_2_, ...), custom_call_target="tpu_custom_call" | custom-call | tf_op jit(solution)/shard_map/near_part/pallas_call | solution.py:508
  18.5 1.5 %collective-permute-done.7.msg_ref = bf16[1088,128]{1,0:T(8,128)(2,1)S(1)} collective-permute-done((bf16[1088,128]{1,0:T(8,128)(2,1)S(1)}, bf16[1088,128]{1,0:T(8,128)(2,1)S(1)}, u32[]{:S(2)}, u32[]{:S(2)}) %collective-permute-start.7) | collective-permute-done | bytes 278560 | tf_op jit(solution)/shard_map/ppermute | solution.py:497
  20.0 1.0 %last_part.1 = f32[2,64,2048]{2,1,0:T(8,128)} custom-call(bf16[8,32,80]{2,1,0:T(8,128)(2,1)S(1)} %get-tuple-element.35.taps_ref, f32[2,64,2048]{2,1,0:T(8,128)S(1)} %get-tuple-element.36.part_ref, bf16[1088,128]{1,0:T(8,128)(2,1)S(1)} %collective-permute-done.7.msg_ref, f32[2,64,2048]{2,1,0:T(8,128)} %get-tuple-element.38.out_in), custom_call_target="tpu_custom_call", output_to_operand_aliasing={{}: (3, {})} | custom-call | tf_op jit(solution)/shard_map/last_part/pallas_call | solution.py:517
Async XLA Ops:
  0.0 7.4 %copy-start = (bf16[2,512,256]{2,1,0:T(8,128)(2,1)S(1)}, bf16[2,512,256]{2,1,0:T(8,128)(2,1)}, u32[]{:S(2)}) copy-start(bf16[2,512,256]{2,1,0:T(8,128)(2,1)} %constant.2.clone.band_ref.refs_11_) | copy-start | bytes 1572868
  2.4 11.6 %collective-permute-start.5 = (bf16[1216,128]{1,0:T(8,128)(2,1)S(1)}, bf16[1216,128]{1,0:T(8,128)(2,1)S(1)}, u32[]{:S(2)}, u32[]{:S(2)}) collective-permute-start(bf16[1216,128]{1,0:T(8,128)(2,1)S(1)} %get-tuple-element.34.own_ref), channel_id=1, source_target_pairs={{1,2},{2,1},{3,4},{4,3},{5,6},{6,5},{7,8},{8,7},{9,10},{10,9},{11,... | collective-permute-start | bytes 933896 | tf_op jit(solution)/shard_map/ppermute | solution.py:485
  6.1 1.3 %collective-permute-start = (bf16[16,2048]{1,0:T(8,128)(2,1)S(1)}, bf16[16,2048]{1,0:T(8,128)(2,1)S(1)}, u32[]{:S(2)}, u32[]{:S(2)}) collective-permute-start(bf16[16,2048]{1,0:T(8,128)(2,1)S(1)} %get-tuple-element.25), channel_id=1, source_target_pairs={{0,1},{1,0},{2,3},{3,2},{4,5},{5,4},{6,7},{7,6},{8,9},{9,8},{10,11... | collective-permute-start | bytes 196616 | tf_op jit(solution)/shard_map/ppermute | solution.py:486
  8.9 5.4 %collective-permute-start.1 = (bf16[4,2,128,128]{3,2,1,0:T(8,128)(2,1)S(1)}, bf16[4,2,128,128]{3,2,1,0:T(8,128)(2,1)S(1)}, u32[]{:S(2)}, u32[]{:S(2)}) collective-permute-start(bf16[4,2,128,128]{3,2,1,0:T(8,128)(2,1)S(1)} %get-tuple-element.30.refs_0_), channel_id=1, source_target_pairs={{0,1},{1,0},{2,3},{3,2},{4,5},{5,4},{6,7},{7,6},{8,9},{9,8},{10,11... | collective-permute-start | bytes 786440 | tf_op jit(solution)/shard_map/ppermute | solution.py:498
  9.1 10.9 %collective-permute-start.7 = (bf16[1088,128]{1,0:T(8,128)(2,1)S(1)}, bf16[1088,128]{1,0:T(8,128)(2,1)S(1)}, u32[]{:S(2)}, u32[]{:S(2)}) collective-permute-start(bf16[1088,128]{1,0:T(8,128)(2,1)S(1)} %get-tuple-element.37), channel_id=1, source_target_pairs={{1,2},{2,1},{3,4},{4,3},{5,6},{6,5},{7,8},{8,7},{9,10},{10,9},{11,... | collective-permute-start | bytes 835592 | tf_op jit(solution)/shard_map/ppermute | solution.py:497
  12.4 2.4 %collective-permute-start.2 = (bf16[4,2,128,128]{3,2,1,0:T(8,128)(2,1)S(1)}, bf16[4,2,128,128]{3,2,1,0:T(8,128)(2,1)S(1)}, u32[]{:S(2)}, u32[]{:S(2)}) collective-permute-start(bf16[4,2,128,128]{3,2,1,0:T(8,128)(2,1)S(1)} %get-tuple-element.31.refs_1_), channel_id=1, source_target_pairs={{0,1},{1,0},{2,3},{3,2},{4,5},{5,4},{6,7},{7,6},{8,9},{9,8},{10,11... | collective-permute-start | bytes 786440 | tf_op jit(solution)/shard_map/ppermute | solution.py:498
  12.6 2.3 %collective-permute-start.3 = (bf16[4,2,128,128]{3,2,1,0:T(8,128)(2,1)S(1)}, bf16[4,2,128,128]{3,2,1,0:T(8,128)(2,1)S(1)}, u32[]{:S(2)}, u32[]{:S(2)}) collective-permute-start(bf16[4,2,128,128]{3,2,1,0:T(8,128)(2,1)S(1)} %get-tuple-element.32.refs_2_), channel_id=1, source_target_pairs={{0,1},{1,0},{2,3},{3,2},{4,5},{5,4},{6,7},{7,6},{8,9},{9,8},{10,11... | collective-permute-start | bytes 786440 | tf_op jit(solution)/shard_map/ppermute | solution.py:498
  14.0 1.5 %collective-permute-start.4 = (bf16[4,2,128,128]{3,2,1,0:T(8,128)(2,1)S(1)}, bf16[4,2,128,128]{3,2,1,0:T(8,128)(2,1)S(1)}, u32[]{:S(2)}, u32[]{:S(2)}) collective-permute-start(bf16[4,2,128,128]{3,2,1,0:T(8,128)(2,1)S(1)} %get-tuple-element.33.refs_3_), channel_id=1, source_target_pairs={{0,1},{1,0},{2,3},{3,2},{4,5},{5,4},{6,7},{7,6},{8,9},{9,8},{10,11... | collective-permute-start | bytes 786440 | tf_op jit(solution)/shard_map/ppermute | solution.py:498
  14.3 1.5 %collective-permute-start.6 = (bf16[16,2048]{1,0:T(8,128)(2,1)S(1)}, bf16[16,2048]{1,0:T(8,128)(2,1)S(1)}, u32[]{:S(2)}, u32[]{:S(2)}) collective-permute-start(bf16[16,2048]{1,0:T(8,128)(2,1)S(1)} %outermost_rows.1.refs_8_), channel_id=1, source_target_pairs={{0,1},{1,0},{2,3},{3,2},{4,5},{5,4},{6,7},{7,6},{8,9},{9,8},{10,11... | collective-permute-start | bytes 196616 | tf_op jit(solution)/shard_map/ppermute | solution.py:507

commit v10 on v9

--- a/solution.py
+++ b/solution.py
@@ -12,8 +12,7 @@
 SIGMA = 64
 LANES = 128
 TILE = 16
-SHIFT_Y, SHIFT_X, SHIFT_Z = 2, 3, 4
-SPAN = LANES << SHIFT_X
+SPREAD, LOWEST = 250.0, 125.0
 PACK = 8
 CUTS = (0, 8, 16)
 PIECES = 4
@@ -29,6 +28,23 @@
 def split(values):
     high = values.astype(BF16)
     return high, (values - high.astype(F32)).astype(BF16)
+
+
+def encode(parts):
+    top = jnp.max(jnp.concatenate([jnp.abs(x) for x in parts], axis=0), axis=0, keepdims=True)
+    top = (top * 1.01).astype(BF16).astype(F32)
+    scale = SPREAD / jnp.maximum(top, 1e-35)
+    codes = []
+    for x in parts:
+        size = jnp.exp2(jnp.abs(x) * scale - LOWEST)
+        codes.append(jnp.where(x < 0, -size, size))
+    return codes, top
+
+
+def decode(codes, top):
+    codes = codes.astype(F32)
+    size = (jnp.log2(jnp.maximum(jnp.abs(codes), 2.0**-LOWEST)) + LOWEST) * (top * (1.0 / SPREAD))
+    return jnp.where(codes < 0, -size, size)
 
 
 def dot(left, right):
@@ -118,11 +134,10 @@
     for comp, numer in enumerate((numer_y, numer_x)):
         raw = numer * inverse
         if extra is None:
-            other = inno_ref[comp, exact, here].astype(F32)
-            raw = jnp.where(iota(raw.shape, 0) == jnp.where(upper, 0, half - 1), other, raw)
-        found.append(split(raw))
+            raw = jnp.where(iota(raw.shape, 0) == jnp.where(upper, 0, half - 1), 0.0, raw)
+        found.append(raw)
         at = pl.ds(pl.multiple_of(comp * rows + start, TILE), half)
-        for part, values in enumerate(found[-1]):
+        for part, values in enumerate(split(raw)):
             for j in range(2):
                 block_of(raw_refs, first + j)[part, at, :] = values[:, j * LANES : (j + 1) * LANES]
     return found
@@ -136,7 +151,7 @@
 
 
 def outer_kernel(lw_hbm, inno_hbm, back_hbm, *refs):
-    *raw_refs, msg_ref, row_ref, inno_ref, back_ref, weight_ref, lw_ref, sum_ref, pick_ref, total_ref, sems, rest_sems, lw_sem = refs
+    *raw_refs, msg_ref, row_ref, inno_ref, back_ref, weight_ref, lw_ref, pick_ref, top_ref, sems, rest_sems, lw_sem = refs
     levels, rows, width = inno_ref.shape
     half = rows // 2
     deep = half + TILE
@@ -166,8 +181,7 @@
     for copy in sum(copies, []) + [other]:
         copy.start()
     diff_y, diff_x = differences(upper, half)
-    sum_ref[...] = one_hot(iota(sum_ref.shape, 0) >> SHIFT_X == iota(sum_ref.shape, 1))
-    groups = rows >> SHIFT_Y
+    outermost_row = iota((half, 2 * LANES), 0) == jnp.where(upper, 0, half - 1)
     kinds = 3 * levels - 2
     row, col = iota(pick_ref.shape[1:], 0), iota(pick_ref.shape[1:], 1)
     want = row - (col >> 6) * kinds
@@ -183,7 +197,6 @@
     for level in range(2 * levels):
         weight_ref[level : level + 1, :] = jnp.full((1, weight_ref.shape[1]), lw_ref[level % levels])
     base = nblocks * rows
-    spans = range(0, nblocks, SPAN // LANES)
 
     def input_rows():
         near_rows = back_ref[:, tile_at(jnp.where(upper, rows - TILE, 0)), :]
@@ -196,17 +209,8 @@
                 back.append(back_ref[:, edge_at, here].reshape(levels * TILE, LANES))
                 inno.append(inno_ref[:, edge_at, here].reshape(levels * TILE, LANES))
             tile = dot(pick_ref[0], jnp.concatenate(back, axis=0)) + dot(pick_ref[1], jnp.concatenate(inno, axis=0))
-            at = base + len(spans) * groups + first * kinds
+            at = base + nblocks + first * kinds
             msg_ref[pl.ds(at, PACK * kinds), :] = tile.astype(BF16)
-
-    def residuals(span):
-        lows = [
-            jnp.concatenate(half_of(block_of(raw_refs, k), rows, start, 1), axis=0)
-            for k in range(span, span + SPAN // LANES)
-        ]
-        total_ref[...] = dot(jnp.concatenate(lows, axis=1), sum_ref[...])
-        found = sum(total_ref[pl.ds(k, groups, stride=1 << SHIFT_Y), :] for k in range(1 << SHIFT_Y))
-        msg_ref[pl.ds(base + span // (SPAN // LANES) * groups, groups), :] = found.astype(BF16)
 
     waited = 0
     for first in range(0, nblocks, 2):
@@ -215,24 +219,26 @@
                 copy.wait()
             waited += 1
         found = raw_pair(first, lambda k: lw_ref[k], inno_ref, back_ref, upper, diff_y, diff_x, None, raw_refs)
-        for comp, (high, _) in enumerate(found):
+        codes, top = encode(found)
+        for comp, code in enumerate(codes):
+            inno = inno_ref[comp, pl.ds(pl.multiple_of(start, TILE), half), pl.ds(first * LANES, 2 * LANES)]
+            code = jnp.where(outermost_row, inno.astype(F32), code).astype(BF16)
             for j in range(2):
-                msg_ref[pl.ds((first + j) * rows + comp * half, half), :] = high[:, j * LANES : (j + 1) * LANES]
-        if first == spans[-1]:
-            for span in spans[:-1]:
-                residuals(span)
+                msg_ref[pl.ds((first + j) * rows + comp * half, half), :] = code[:, j * LANES : (j + 1) * LANES]
+        for j in range(2):
+            top_ref[first + j : first + j + 1, :] = top[:, j * LANES : (j + 1) * LANES]
     input_rows()
-    residuals(spans[-1])
+    msg_ref[pl.ds(base, nblocks), :] = top_ref[...].astype(BF16)
     other.wait()
 
 
 def outer_rows(rows, nblocks, levels):
-    return nblocks * rows + (nblocks * LANES // SPAN) * (rows >> SHIFT_Y) + nblocks * (3 * levels - 2)
+    return nblocks * rows + nblocks + nblocks * (3 * levels - 2)
 
 
 def inner_kernel(weight_ref, inno_ref, back_ref, row_ref, band_ref, *refs):
     raw_refs = refs[PIECES : 2 * PIECES]
-    msg_ref, rest_ref = refs[2 * PIECES :]
+    msg_ref, top_ref = refs[2 * PIECES :]
     _, rows, width = inno_ref.shape
     half = rows // 2
     nblocks = width // LANES
@@ -252,27 +258,19 @@
         block = block_of(raw_refs, k)
         return jnp.concatenate(half_of(block, rows, start, 0) + half_of(block, rows, start, 1), axis=0)
 
-    groups = rows >> SHIFT_Z
-    shape = (2 * groups, rows)
-    sum_y = one_hot(iota(shape, 1) >> SHIFT_Z == iota(shape, 0))
     for first in range(0, nblocks, 2):
         raw_pair(first, weight, inno_ref, back_ref, upper, diff_y, diff_x, extra, raw_refs)
     for first in range(0, nblocks, 2):
-        high, low = split(smooth_x(band_ref, load, first, nblocks))
-        rest_ref[:, first * LANES : (first + 2) * LANES] = low
+        (code,), top = encode([smooth_x(band_ref, load, first, nblocks)])
+        code = code.astype(BF16)
         for j in range(2):
-            msg_ref[pl.ds((first + j) * rows, rows), :] = high[:, j * LANES : (j + 1) * LANES]
-    sums = dot(sum_y, rest_ref[...])
-    per = TILE // groups
-    for first in range(0, nblocks, 2 * per):
-        for j in range(2):
-            parts = [sums[:groups, k * LANES : (k + 1) * LANES] for k in range(first + j, first + 2 * per, 2)]
-            tile = nblocks * rows + (first // per + j) * TILE
-            msg_ref[pl.ds(tile, TILE), :] = jnp.concatenate(parts, axis=0).astype(BF16)
+            msg_ref[pl.ds((first + j) * rows, rows), :] = code[:, j * LANES : (j + 1) * LANES]
+            top_ref[first + j : first + j + 1, :] = top[:, j * LANES : (j + 1) * LANES]
+    msg_ref[pl.ds(nblocks * rows, nblocks), :] = top_ref[...].astype(BF16)
 
 
 def inner_rows(rows, nblocks):
-    return nblocks * rows + nblocks * (rows >> SHIFT_Z)
+    return nblocks * rows + nblocks
 
 
 def outermost_kernel(weight_ref, own_ref, got_ref, out_ref):
@@ -346,10 +344,11 @@
     column = iota(near_taps.shape, 1)
     outermost = (column == par * (rows - 1)) | (column == (2 - par) * rows - 1 + par)
     near_taps = jnp.where(outermost, 0.0, near_taps)
-    near_high = near_taps.astype(BF16)
     toward = far_taps(rows, True)
     outermost = iota(toward.shape, 1) == jnp.where(par == 0, half - 1, 0)
-    toward_inner = jnp.where(outermost, 0.0, toward)
+    toward = jnp.where(outermost, 0.0, toward)
+    outermost = iota((half, 2 * LANES), 0) == jnp.where(par == 0, half - 1, 0)
+    low_taps = jnp.concatenate([near_taps, toward], axis=1).astype(BF16)
     shape = (rows, TILE)
     kind = iota(shape, 1)
     own_at = jnp.where(par == 0, 0, rows - 1)
@@ -360,34 +359,27 @@
     stacked = []
     for comp in range(2):
         here = (kind < 8) & (kind & 1 == comp)
-        all_taps = [near_taps, toward_inner, jnp.where(here, own_edges, 0.0), jnp.where(here, near_edges, 0.0)]
+        all_taps = [near_taps, toward, jnp.where(here, own_edges, 0.0), jnp.where(here, near_edges, 0.0)]
         stacked.append(jnp.concatenate(split(jnp.concatenate(all_taps, axis=1)), axis=0))
-    groups = half >> SHIFT_Y
-    shape = (half, groups)
-    mean_y = one_hot(iota(shape, 0) >> SHIFT_Y == iota(shape, 1), 1.0 / (1 << SHIFT_Y))
-    group_taps = dot(toward.astype(BF16), mean_y).astype(BF16)
-    shape = (LANES, SPAN)
-    mean_x = one_hot(iota(shape, 1) >> SHIFT_X == iota(shape, 0), 1.0 / (1 << SHIFT_X))
-    rest = []
-    for span in range(width // SPAN):
-        tile = msg_ref[pl.ds(nblocks * rows + span * 2 * groups, 2 * groups), :]
-        rest.append(jnp.concatenate([dot(group_taps, tile[:groups]), dot(group_taps, tile[groups:])], axis=0).astype(BF16))
+    tops = msg_ref[pl.ds(nblocks * rows, nblocks), :].astype(F32)
     for first in range(0, nblocks, 2):
         cols = pl.ds(first * LANES, 2 * LANES)
-        place = first * LANES % SPAN
-        spread = dot(rest[first * LANES // SPAN], mean_x[:, place : place + 2 * LANES])
+        top = jnp.concatenate([tops[k : k + 1] for k in (first, first + 1)], axis=1)
         edges = [edges_ref[:, cols], near_edges_ref[:, cols]]
         for comp in range(2):
             here = pl.ds(comp * rows, rows)
-            highs, lows = [], []
+            both, got = [], []
             for k in (first, first + 1):
-                both = (block_of(raw_refs, k), block_of(near_refs, k))
-                got = msg_ref[pl.ds(k * rows + comp * half, half), :]
-                highs.append(jnp.concatenate([ref[0, here, :] for ref in both] + [got], axis=0))
-                lows.append(jnp.concatenate([ref[1, here, :] for ref in both], axis=0))
-            part = dot(stacked[comp], jnp.concatenate([jnp.concatenate(highs, axis=1)] + edges, axis=0))
-            part = part[:rows] + part[rows:] + dot(near_high, jnp.concatenate(lows, axis=1))
-            high, low = split(part + spread[comp * rows : (comp + 1) * rows])
+                refs = (block_of(raw_refs, k), block_of(near_refs, k))
+                both.append([jnp.concatenate([ref[part, here, :] for ref in refs], axis=0) for part in range(2)])
+                got.append(msg_ref[pl.ds(k * rows + comp * half, half), :])
+            got = decode(jnp.concatenate(got, axis=1), top)
+            got = split(jnp.where(outermost, 0.0, got))
+            highs, lows = (
+                jnp.concatenate([jnp.concatenate([x[part] for x in both], axis=1), got[part]], axis=0) for part in range(2)
+            )
+            part = dot(stacked[comp], jnp.concatenate([highs] + edges, axis=0))
+            high, low = split(part[:rows] + part[rows:] + dot(low_taps, lows))
             for j in range(2):
                 cut = slice(j * LANES, (j + 1) * LANES)
                 total_ref[first + j, pl.ds(comp * rows, rows), :] = high[:, cut]
@@ -401,43 +393,27 @@
     copies = [pltpu.make_async_copy(out_ref.at[k, rest, :], out_hbm.at[k, rest, :], sem.at[k]) for k in range(2)]
     for copy in copies:
         copy.start()
-    for index, matrix in enumerate(last_taps(rows)):
-        taps_ref[index] = matrix
+    away = far_taps(rows, False)
+    high, low = split(jnp.where(par == 0, away[:half], away[half:]))
+    taps_ref[...] = jnp.concatenate([high, low, high], axis=1)
     for copy in copies:
         copy.wait()
-
-
-def last_taps(rows):
-    half = rows // 2
-    away = far_taps(rows, False)
-    high, low = split(jnp.where(parity() == 0, away[:half], away[half:]))
-    groups = rows >> SHIFT_Z
-    shape = (half, TILE)
-    found = []
-    for place in range(TILE // groups):
-        for comp in range(2):
-            of_group = (iota(shape, 0) >> SHIFT_Z) + place * groups + comp * (groups // 2) == iota(shape, 1)
-            mean = dot(high, one_hot(of_group, 1.0 / (1 << SHIFT_Z))).astype(BF16)
-            found.append(jnp.concatenate([high, low, mean], axis=1))
-    return found
 
 
 def last_kernel(taps_ref, part_ref, msg_ref, out_in, out_hbm, buf, sem):
     _, rows, width = part_ref.shape
     nblocks = width // LANES
     half = rows // 2
-    places = TILE // (rows >> SHIFT_Z)
+    tops = msg_ref[pl.ds(nblocks * rows, nblocks), :].astype(F32)
     reached = pl.ds(pl.multiple_of(parity() * half, 8), half)
     copies = []
     for comp in range(2):
-        for index, first in enumerate(range(0, nblocks, 2)):
+        for first in range(0, nblocks, 2):
             here = pl.ds(first * LANES, 2 * LANES)
-            got, sums = [], []
-            for j in range(2):
-                got.append(msg_ref[pl.ds((first + j) * rows + comp * half, half), :])
-                sums.append(msg_ref[pl.ds(nblocks * rows + (2 * (index // places) + j) * TILE, TILE), :])
-            got, sums = jnp.concatenate(got, axis=1), jnp.concatenate(sums, axis=1)
-            part = dot(taps_ref[index % places * 2 + comp], jnp.concatenate([got, got, sums], axis=0))
+            top = jnp.concatenate([tops[k : k + 1] for k in (first, first + 1)], axis=1)
+            got = [msg_ref[pl.ds((first + j) * rows + comp * half, half), :] for j in range(2)]
+            high, low = split(decode(jnp.concatenate(got, axis=1), top))
+            part = dot(taps_ref[...], jnp.concatenate([high, high, low], axis=0))
             buf[comp, :, here] = part_ref[comp, reached, here] + part
         copies.append(pltpu.make_async_copy(buf.at[comp], out_hbm.at[comp, reached, :], sem.at[comp]))
         copies[-1].start()
@@ -447,7 +423,7 @@
 
 def body(innovation, background, level_weight):
     levels, rows, width = innovation.shape
-    if rows != HALF or width % SPAN or levels != 4:
+    if rows != HALF or width % (PACK * LANES) or levels != 4:
         raise NotImplementedError("slab shape")
     nblocks = width // LANES
     both, half = 2 * rows, rows // 2
@@ -472,9 +448,8 @@
         out_specs=[VMEM] * (PIECES + 5),
         scratch_shapes=[
             pltpu.SMEM((levels,), F32),
-            pltpu.VMEM((SPAN, LANES), BF16),
             pltpu.VMEM((2, PACK * (3 * levels - 2), PACK * levels * TILE), BF16),
-            pltpu.VMEM((rows, LANES), F32),
+            pltpu.VMEM((nblocks, LANES), F32),
             pltpu.SemaphoreType.DMA((2, len(CUTS) - 1)),
             pltpu.SemaphoreType.DMA((2,)),
             pltpu.SemaphoreType.DMA,
@@ -489,7 +464,7 @@
         out_shape=[piece] * PIECES + [jax.ShapeDtypeStruct((inner_rows(rows, nblocks), LANES), BF16)],
         in_specs=[VMEM] * (5 + PIECES),
         out_specs=[VMEM] * (PIECES + 1),
-        scratch_shapes=[pltpu.VMEM((rows, width), BF16)],
+        scratch_shapes=[pltpu.VMEM((nblocks, LANES), F32)],
         input_output_aliases={5 + k: k for k in range(PIECES)},
         compiler_params=PARAMS,
         name="inner_half",
@@ -507,7 +482,7 @@
     near_edges = lax.ppermute(edges, "row", chip)
     out, part, last = pl.pallas_call(
         near_kernel,
-        out_shape=[result, result, jax.ShapeDtypeStruct((2 * TILE // (rows >> SHIFT_Z), half, rows + TILE), BF16)],
+        out_shape=[result, result, jax.ShapeDtypeStruct((half, 3 * half), BF16)],
         in_specs=[VMEM] * (2 * PIECES + 4),
         out_specs=[HBM] + [VMEM] * 2,
         scratch_shapes=[pltpu.VMEM((nblocks, 2 * both, LANES), BF16), pltpu.SemaphoreType.DMA((2,))],

time: 21.2 us -> 21.1 us (level)
  transfers between devices with their start and end apart: 8 -> 8, of which waited for: 5 -> 5; matrix products, arithmetic and copies ran while one was open for 0% -> 0% of each run, Pallas kernels for 21% -> 20%
where the time goes in v10:
time: 21.1 us; the launch traced here: 20.9 us
  starting transfers between devices  8.52 us (40%)
  Pallas kernels  7.88 us (37%)
  waiting for transfers between devices  4.47 us (21%)
    ppermute x1, starting transfers between devices, body(): outer_got = lax.ppermute(outer, 'row', away)  3.71 us
    ppermute x1, starting transfers between devices, body(): inner_got = lax.ppermute(inner, 'row', away)  3.36 us
    pallas_call x1, Pallas kernels, body(): pl.pallas_call(outer_kernel, out_shape=[piece] * PIECES + [jax.ShapeDtype...  2.53 us
    pallas_call x1, Pallas kernels, body(): pl.pallas_call(near_kernel, out_shape=[result, result, jax.ShapeDtypeStru...  2.52 us
    ppermute x1, waiting for transfers between devices, body(): inner_got = lax.ppermute(inner, 'row', away)  1.45 us
    pallas_call x1, Pallas kernels, body(): pl.pallas_call(inner_kernel, out_shape=[piece] * PIECES + [jax.ShapeDtype...  1.44 us
    ppermute x1, waiting for transfers between devices, body(): row = lax.ppermute(row, 'row', chip)  1.24 us
    pallas_call x1, Pallas kernels, body(): pl.pallas_call(last_kernel, out_shape=result, in_specs=[VMEM] * 3 + [HBM]...  1.11 us
  transfers between devices with their start and end apart: 8, of which 5 were waited for; matrix products, arithmetic and copies ran while one was open for 0% of the time, Pallas kernels for 20%

profile of v10, /device:TPU:11, one launch (start us, length us, event | category | flops | bytes accessed | tf_op | source)
XLA Modules:
  0.0 20.9 jit_solution(8579990105191769299)
XLA Ops:
  0.0 0.0 copy-start
  0.0 2.5 %outer_half.1 = (bf16[4,2,128,128]{3,2,1,0:T(8,128)(2,1)S(1)}, bf16[4,2,128,128]{3,2,1,0:T(8,128)(2,1)S(1)}, bf16[4,2,128,128]{3,2,1,0:T(8,128)(2,1)S(1)}, bf16[...) custom-call(f32[4]{0:T(128)} %lw_hbm.1, ...), custom_call_target="tpu_custom_call" | custom-call | tf_op jit(solution)/shard_map/outer_half/pallas_call | solution.py:437
  2.5 3.7 %collective-permute-start.5 = (bf16[1200,128]{1,0:T(8,128)(2,1)S(1)}, bf16[1200,128]{1,0:T(8,128)(2,1)S(1)}, u32[]{:S(2)}, u32[]{:S(2)}) collective-permute-start(bf16[1200,128]{1,0:T(8,128)(2,1)S(1)} %get-tuple-element.34.own_ref), channel_id=1, source_target_pairs={{1,2},{2,1},{3,4},{4,3},{5,6},{6,5},{7,8},{8,7},{9,10},{10,9},{11,... | collective-permute-start | bytes 921608 | tf_op jit(solution)/shard_map/ppermute | solution.py:460
  6.3 0.1 collective-permute-start
  6.3 1.2 %collective-permute-done.row_ref = bf16[16,2048]{1,0:T(8,128)(2,1)S(1)} collective-permute-done((bf16[16,2048]{1,0:T(8,128)(2,1)S(1)}, bf16[16,2048]{1,0:T(8,128)(2,1)S(1)}, u32[]{:S(2)}, u32[]{:S(2)}) %collective-permute-start) | collective-permute-done | bytes 65568 | tf_op jit(solution)/shard_map/ppermute | solution.py:461
  7.6 0.0 copy-done
  7.6 1.4 %inner_half.1 = (bf16[4,2,128,128]{3,2,1,0:T(8,128)(2,1)S(1)}, bf16[4,2,128,128]{3,2,1,0:T(8,128)(2,1)S(1)}, bf16[4,2,128,128]{3,2,1,0:T(8,128)(2,1)S(1)}, bf16[...) custom-call(f32[8,256]{1,0:T(8,128)S(1)} %get-tuple-element.22.weigh, ...), custom_call_target="tpu_custom_call", output_to_operand_aliasing={{0}: (5, {}), {1}: (6, {}), {2}: (7, {}), {3}: (8, {})} | custom-call | tf_op jit(solution)/shard_map/inner_half/pallas_call | solution.py:462
  9.0 0.2 %collective-permute-start.1 = (bf16[4,2,128,128]{3,2,1,0:T(8,128)(2,1)S(1)}, bf16[4,2,128,128]{3,2,1,0:T(8,128)(2,1)S(1)}, u32[]{:S(2)}, u32[]{:S(2)}) collective-permute-start(bf16[4,2,128,128]{3,2,1,0:T(8,128)(2,1)S(1)} %get-tuple-element.30.refs_0_), channel_id=1, source_target_pairs={{0,1},{1,0},{2,3},{3,2},{4,5},{5,4},{6,7},{7,6},{8,9},{9,8},{10,11... | collective-permute-start | bytes 786440 | tf_op jit(solution)/shard_map/ppermute | solution.py:473
  9.3 3.4 %collective-permute-start.7 = (bf16[1040,128]{1,0:T(8,128)(2,1)S(1)}, bf16[1040,128]{1,0:T(8,128)(2,1)S(1)}, u32[]{:S(2)}, u32[]{:S(2)}) collective-permute-start(bf16[1040,128]{1,0:T(8,128)(2,1)S(1)} %get-tuple-element.37), channel_id=1, source_target_pairs={{1,2},{2,1},{3,4},{4,3},{5,6},{6,5},{7,8},{8,7},{9,10},{10,9},{11,... | collective-permute-start | bytes 798728 | tf_op jit(solution)/shard_map/ppermute | solution.py:472
  12.6 0.1 collective-permute-start.2
  12.7 0.5 %collective-permute-start.3 = (bf16[4,2,128,128]{3,2,1,0:T(8,128)(2,1)S(1)}, bf16[4,2,128,128]{3,2,1,0:T(8,128)(2,1)S(1)}, u32[]{:S(2)}, u32[]{:S(2)}) collective-permute-start(bf16[4,2,128,128]{3,2,1,0:T(8,128)(2,1)S(1)} %get-tuple-element.32.refs_2_), channel_id=1, source_target_pairs={{0,1},{1,0},{2,3},{3,2},{4,5},{5,4},{6,7},{7,6},{8,9},{9,8},{10,11... | collective-permute-start | bytes 786440 | tf_op jit(solution)/shard_map/ppermute | solution.py:473
  13.2 0.9 %collective-permute-done.5.got_ref.refs_10_ = bf16[1200,128]{1,0:T(8,128)(2,1)S(1)} collective-permute-done((bf16[1200,128]{1,0:T(8,128)(2,1)S(1)}, bf16[1200,128]{1,0:T(8,128)(2,1)S(1)}, u32[]{:S(2)}, u32[]{:S(2)}) %collective-permute-start.5) | collective-permute-done | bytes 307232 | tf_op jit(solution)/shard_map/ppermute | solution.py:460
  14.1 0.0 collective-permute-start.4
  14.1 0.3 %outermost_rows.1.refs_8_ = bf16[16,2048]{1,0:T(8,128)(2,1)S(1)} custom-call(f32[8,256]{1,0:T(8,128)S(1)} %get-tuple-element.22.weight_ref, bf16[1200,128]{1,0:T(8,128)(2,1)S(1)} %get-tuple-element.34.own_ref, bf16[1200,128]{1,0:T(8,128)(2,1)S(1)} %collective-permute-done.5.got_ref.refs_10_), custom_call_target="tpu_custom_call" | custom-call | tf_op jit(solution)/shard_map/outermost_rows/pallas_call | solution.py:474
  14.4 0.0 collective-permute-done.1.refs_4_
  14.4 0.6 %collective-permute-start.6 = (bf16[16,2048]{1,0:T(8,128)(2,1)S(1)}, bf16[16,2048]{1,0:T(8,128)(2,1)S(1)}, u32[]{:S(2)}, u32[]{:S(2)}) collective-permute-start(bf16[16,2048]{1,0:T(8,128)(2,1)S(1)} %outermost_rows.1.refs_8_), channel_id=1, source_target_pairs={{0,1},{1,0},{2,3},{3,2},{4,5},{5,4},{6,7},{7,6},{8,9},{9,8},{10,11... | collective-permute-start | bytes 196616 | tf_op jit(solution)/shard_map/ppermute | solution.py:482
  15.0 0.0 collective-permute-done.2.refs_5_
  15.0 0.0 collective-permute-done.3.refs_6_
  15.0 0.7 %collective-permute-done.4.refs_7_ = bf16[4,2,128,128]{3,2,1,0:T(8,128)(2,1)S(1)} collective-permute-done((bf16[4,2,128,128]{3,2,1,0:T(8,128)(2,1)S(1)}, bf16[4,2,128,128]{3,2,1,0:T(8,128)(2,1)S(1)}, u32[]{:S(2)}, u32[]{:S(2)}) %collective-permute-start.4) | collective-permute-done | bytes 262176 | tf_op jit(solution)/shard_map/ppermute | solution.py:473
  15.6 0.2 %collective-permute-done.6.refs_9_ = bf16[16,2048]{1,0:T(8,128)(2,1)S(1)} collective-permute-done((bf16[16,2048]{1,0:T(8,128)(2,1)S(1)}, bf16[16,2048]{1,0:T(8,128)(2,1)S(1)}, u32[]{:S(2)}, u32[]{:S(2)}) %collective-permute-start.6) | collective-permute-done | bytes 65568 | tf_op jit(solution)/shard_map/ppermute | solution.py:482
  15.9 2.5 %near_part.1 = (f32[2,64,2048]{2,1,0:T(8,128)}, f32[2,64,2048]{2,1,0:T(8,128)S(1)}, bf16[32,96]{1,0:T(8,128)(2,1)S(1)}) custom-call(bf16[4,2,128,128]{3,2,1,0:T(8,128)(2,1)S(1)} %get-tuple-element.30.refs_0_, bf16[4,2,128,128]{3,2,1,0:T(8,128)(2,1)S(1)} %get-tuple-element.31.refs_1_, bf16[4,2,128,128]{3,2,1,0:T(8,128)(2,1)S(1)} %get-tuple-element.32.refs_2_, ...), custom_call_target="tpu_custom_call" | custom-call | tf_op jit(solution)/shard_map/near_part/pallas_call | solution.py:483
  18.4 1.5 %collective-permute-done.7.msg_ref = bf16[1040,128]{1,0:T(8,128)(2,1)S(1)} collective-permute-done((bf16[1040,128]{1,0:T(8,128)(2,1)S(1)}, bf16[1040,128]{1,0:T(8,128)(2,1)S(1)}, u32[]{:S(2)}, u32[]{:S(2)}) %collective-permute-start.7) | collective-permute-done | bytes 266272 | tf_op jit(solution)/shard_map/ppermute | solution.py:472
  19.8 1.1 %last_part.1 = f32[2,64,2048]{2,1,0:T(8,128)} custom-call(bf16[32,96]{1,0:T(8,128)(2,1)S(1)} %get-tuple-element.35.taps_ref, f32[2,64,2048]{2,1,0:T(8,128)S(1)} %get-tuple-element.36.part_ref, bf16[1040,128]{1,0:T(8,128)(2,1)S(1)} %collective-permute-done.7.msg_ref, f32[2,64,2048]{2,1,0:T(8,128)} %get-tuple-element.38.out_in), custom_call_target="tpu_custom_call", output_to_operand_aliasing={{}: (3, {})} | custom-call | tf_op jit(solution)/shard_map/last_part/pallas_call | solution.py:492
Async XLA Ops:
  0.0 7.6 %copy-start = (bf16[2,512,256]{2,1,0:T(8,128)(2,1)S(1)}, bf16[2,512,256]{2,1,0:T(8,128)(2,1)}, u32[]{:S(2)}) copy-start(bf16[2,512,256]{2,1,0:T(8,128)(2,1)} %constant.2.clone.band_ref.refs_11_) | copy-start | bytes 1572868
  2.5 11.5 %collective-permute-start.5 = (bf16[1200,128]{1,0:T(8,128)(2,1)S(1)}, bf16[1200,128]{1,0:T(8,128)(2,1)S(1)}, u32[]{:S(2)}, u32[]{:S(2)}) collective-permute-start(bf16[1200,128]{1,0:T(8,128)(2,1)S(1)} %get-tuple-element.34.own_ref), channel_id=1, source_target_pairs={{1,2},{2,1},{3,4},{4,3},{5,6},{6,5},{7,8},{8,7},{9,10},{10,9},{11,... | collective-permute-start | bytes 921608 | tf_op jit(solution)/shard_map/ppermute | solution.py:460
  6.3 1.3 %collective-permute-start = (bf16[16,2048]{1,0:T(8,128)(2,1)S(1)}, bf16[16,2048]{1,0:T(8,128)(2,1)S(1)}, u32[]{:S(2)}, u32[]{:S(2)}) collective-permute-start(bf16[16,2048]{1,0:T(8,128)(2,1)S(1)} %get-tuple-element.25), channel_id=1, source_target_pairs={{0,1},{1,0},{2,3},{3,2},{4,5},{5,4},{6,7},{7,6},{8,9},{9,8},{10,11... | collective-permute-start | bytes 196616 | tf_op jit(solution)/shard_map/ppermute | solution.py:461
  9.0 5.3 %collective-permute-start.1 = (bf16[4,2,128,128]{3,2,1,0:T(8,128)(2,1)S(1)}, bf16[4,2,128,128]{3,2,1,0:T(8,128)(2,1)S(1)}, u32[]{:S(2)}, u32[]{:S(2)}) collective-permute-start(bf16[4,2,128,128]{3,2,1,0:T(8,128)(2,1)S(1)} %get-tuple-element.30.refs_0_), channel_id=1, source_target_pairs={{0,1},{1,0},{2,3},{3,2},{4,5},{5,4},{6,7},{7,6},{8,9},{9,8},{10,11... | collective-permute-start | bytes 786440 | tf_op jit(solution)/shard_map/ppermute | solution.py:473
  9.3 10.6 %collective-permute-start.7 = (bf16[1040,128]{1,0:T(8,128)(2,1)S(1)}, bf16[1040,128]{1,0:T(8,128)(2,1)S(1)}, u32[]{:S(2)}, u32[]{:S(2)}) collective-permute-start(bf16[1040,128]{1,0:T(8,128)(2,1)S(1)} %get-tuple-element.37), channel_id=1, source_target_pairs={{1,2},{2,1},{3,4},{4,3},{5,6},{6,5},{7,8},{8,7},{9,10},{10,9},{11,... | collective-permute-start | bytes 798728 | tf_op jit(solution)/shard_map/ppermute | solution.py:472
  12.6 2.3 %collective-permute-start.2 = (bf16[4,2,128,128]{3,2,1,0:T(8,128)(2,1)S(1)}, bf16[4,2,128,128]{3,2,1,0:T(8,128)(2,1)S(1)}, u32[]{:S(2)}, u32[]{:S(2)}) collective-permute-start(bf16[4,2,128,128]{3,2,1,0:T(8,128)(2,1)S(1)} %get-tuple-element.31.refs_1_), channel_id=1, source_target_pairs={{0,1},{1,0},{2,3},{3,2},{4,5},{5,4},{6,7},{7,6},{8,9},{9,8},{10,11... | collective-permute-start | bytes 786440 | tf_op jit(solution)/shard_map/ppermute | solution.py:473
  12.7 2.2 %collective-permute-start.3 = (bf16[4,2,128,128]{3,2,1,0:T(8,128)(2,1)S(1)}, bf16[4,2,128,128]{3,2,1,0:T(8,128)(2,1)S(1)}, u32[]{:S(2)}, u32[]{:S(2)}) collective-permute-start(bf16[4,2,128,128]{3,2,1,0:T(8,128)(2,1)S(1)} %get-tuple-element.32.refs_2_), channel_id=1, source_target_pairs={{0,1},{1,0},{2,3},{3,2},{4,5},{5,4},{6,7},{7,6},{8,9},{9,8},{10,11... | collective-permute-start | bytes 786440 | tf_op jit(solution)/shard_map/ppermute | solution.py:473
  14.1 1.5 %collective-permute-start.4 = (bf16[4,2,128,128]{3,2,1,0:T(8,128)(2,1)S(1)}, bf16[4,2,128,128]{3,2,1,0:T(8,128)(2,1)S(1)}, u32[]{:S(2)}, u32[]{:S(2)}) collective-permute-start(bf16[4,2,128,128]{3,2,1,0:T(8,128)(2,1)S(1)} %get-tuple-element.33.refs_3_), channel_id=1, source_target_pairs={{0,1},{1,0},{2,3},{3,2},{4,5},{5,4},{6,7},{7,6},{8,9},{9,8},{10,11... | collective-permute-start | bytes 786440 | tf_op jit(solution)/shard_map/ppermute | solution.py:473
  14.4 1.5 %collective-permute-start.6 = (bf16[16,2048]{1,0:T(8,128)(2,1)S(1)}, bf16[16,2048]{1,0:T(8,128)(2,1)S(1)}, u32[]{:S(2)}, u32[]{:S(2)}) collective-permute-start(bf16[16,2048]{1,0:T(8,128)(2,1)S(1)} %outermost_rows.1.refs_8_), channel_id=1, source_target_pairs={{0,1},{1,0},{2,3},{3,2},{4,5},{5,4},{6,7},{7,6},{8,9},{9,8},{10,11... | collective-permute-start | bytes 196616 | tf_op jit(solution)/shard_map/ppermute | solution.py:482

commit v11 on v10

--- a/solution.py
+++ b/solution.py
@@ -12,7 +12,7 @@
 SIGMA = 64
 LANES = 128
 TILE = 16
-SPREAD, LOWEST = 250.0, 125.0
+SPREAD, LOWEST, LEAST = 250.0, 125.0, 1e-35
 PACK = 8
 CUTS = (0, 8, 16)
 PIECES = 4
@@ -33,7 +33,7 @@
 def encode(parts):
     top = jnp.max(jnp.concatenate([jnp.abs(x) for x in parts], axis=0), axis=0, keepdims=True)
     top = (top * 1.01).astype(BF16).astype(F32)
-    scale = SPREAD / jnp.maximum(top, 1e-35)
+    scale = SPREAD / jnp.maximum(top, LEAST)
     codes = []
     for x in parts:
         size = jnp.exp2(jnp.abs(x) * scale - LOWEST)
@@ -43,7 +43,7 @@
 
 def decode(codes, top):
     codes = codes.astype(F32)
-    size = (jnp.log2(jnp.maximum(jnp.abs(codes), 2.0**-LOWEST)) + LOWEST) * (top * (1.0 / SPREAD))
+    size = (jnp.log2(jnp.maximum(jnp.abs(codes), 2.0**-LOWEST)) + LOWEST) * (jnp.maximum(top, LEAST) * (1.0 / SPREAD))
     return jnp.where(codes < 0, -size, size)
 
 
@@ -218,6 +218,8 @@
             for copy in copies[waited]:
                 copy.wait()
             waited += 1
+        if first == cuts[-2] // LANES:
+            input_rows()
         found = raw_pair(first, lambda k: lw_ref[k], inno_ref, back_ref, upper, diff_y, diff_x, None, raw_refs)
         codes, top = encode(found)
         for comp, code in enumerate(codes):
@@ -227,7 +229,6 @@
                 msg_ref[pl.ds((first + j) * rows + comp * half, half), :] = code[:, j * LANES : (j + 1) * LANES]
         for j in range(2):
             top_ref[first + j : first + j + 1, :] = top[:, j * LANES : (j + 1) * LANES]
-    input_rows()
     msg_ref[pl.ds(base, nblocks), :] = top_ref[...].astype(BF16)
     other.wait()
 
@@ -333,7 +334,7 @@
 
 def near_kernel(*refs):
     raw_refs, near_refs = refs[:PIECES], refs[PIECES : 2 * PIECES]
-    edges_ref, near_edges_ref, msg_ref, band_ref, out_hbm, out_ref, taps_ref, total_ref, sem = refs[2 * PIECES :]
+    edges_ref, near_edges_ref, msg_ref, band_ref, out_ref, taps_ref, total_ref = refs[2 * PIECES :]
     _, rows, width = out_ref.shape
     nblocks = width // LANES
     half = rows // 2
@@ -389,24 +390,21 @@
         here = pl.ds(first * LANES, 2 * LANES)
         out_ref[0, :, here] = result[:rows]
         out_ref[1, :, here] = result[rows:]
-    rest = pl.ds(pl.multiple_of((1 - par) * half, 8), half)
-    copies = [pltpu.make_async_copy(out_ref.at[k, rest, :], out_hbm.at[k, rest, :], sem.at[k]) for k in range(2)]
-    for copy in copies:
-        copy.start()
     away = far_taps(rows, False)
     high, low = split(jnp.where(par == 0, away[:half], away[half:]))
     taps_ref[...] = jnp.concatenate([high, low, high], axis=1)
-    for copy in copies:
-        copy.wait()
-
-
-def last_kernel(taps_ref, part_ref, msg_ref, out_in, out_hbm, buf, sem):
+
+
+def last_kernel(taps_ref, part_ref, msg_ref, out_hbm, buf, sem):
     _, rows, width = part_ref.shape
     nblocks = width // LANES
     half = rows // 2
     tops = msg_ref[pl.ds(nblocks * rows, nblocks), :].astype(F32)
     reached = pl.ds(pl.multiple_of(parity() * half, 8), half)
-    copies = []
+    rest = pl.ds(pl.multiple_of((1 - parity()) * half, 8), half)
+    copies = [pltpu.make_async_copy(part_ref.at[k, rest, :], out_hbm.at[k, rest, :], sem.at[2 + k]) for k in range(2)]
+    for copy in copies:
+        copy.start()
     for comp in range(2):
         for first in range(0, nblocks, 2):
             here = pl.ds(first * LANES, 2 * LANES)
@@ -480,25 +478,24 @@
         name="outermost_rows",
     )(weight, outer, outer_got)
     near_edges = lax.ppermute(edges, "row", chip)
-    out, part, last = pl.pallas_call(
+    part, last = pl.pallas_call(
         near_kernel,
-        out_shape=[result, result, jax.ShapeDtypeStruct((half, 3 * half), BF16)],
+        out_shape=[result, jax.ShapeDtypeStruct((half, 3 * half), BF16)],
         in_specs=[VMEM] * (2 * PIECES + 4),
-        out_specs=[HBM] + [VMEM] * 2,
-        scratch_shapes=[pltpu.VMEM((nblocks, 2 * both, LANES), BF16), pltpu.SemaphoreType.DMA((2,))],
+        out_specs=[VMEM] * 2,
+        scratch_shapes=[pltpu.VMEM((nblocks, 2 * both, LANES), BF16)],
         compiler_params=PARAMS,
         name="near_part",
     )(*raws, *nears, edges, near_edges, outer_got, band)
     return pl.pallas_call(
         last_kernel,
         out_shape=result,
-        in_specs=[VMEM] * 3 + [HBM],
+        in_specs=[VMEM] * 3,
         out_specs=HBM,
-        input_output_aliases={3: 0},
-        scratch_shapes=[pltpu.VMEM((2, half, width), F32), pltpu.SemaphoreType.DMA((2,))],
+        scratch_shapes=[pltpu.VMEM((2, half, width), F32), pltpu.SemaphoreType.DMA((4,))],
         compiler_params=PARAMS,
         name="last_part",
-    )(last, part, inner_got, out)
+    )(last, part, inner_got)
 
 
 def solution(mesh):

time: 21.1 us -> 21.1 us (level)
  Pallas kernels: 7.88 us -> 7 us
  waiting for transfers between devices: 4.47 us -> 5.28 us
    ppermute x1, waiting for transfers between devices: 1.45 us -> 2.27 us  [body(): inner_got = lax.ppermute(inner, 'row', away)]
    pallas_call x2, Pallas kernels: 3.63 us -> 2.84 us  [the longest x1 1.71 us: body(): pl.pallas_call(near_kernel, out_shape=[result, jax.ShapeDtypeStruct((half...]
  transfers between devices with their start and end apart: 8 -> 8, of which waited for: 5 -> 5; matrix products, arithmetic and copies ran while one was open for 0% -> 0% of each run, Pallas kernels for 20% -> 16%
where the time goes in v11:
time: 21.1 us; the launch traced here: 20.9 us
  starting transfers between devices  8.52 us (40%)
  Pallas kernels  7 us (33%)
  waiting for transfers between devices  5.28 us (25%)
    ppermute x1, starting transfers between devices, body(): outer_got = lax.ppermute(outer, 'row', away)  3.71 us
    ppermute x1, starting transfers between devices, body(): inner_got = lax.ppermute(inner, 'row', away)  3.37 us
    pallas_call x1, Pallas kernels, body(): pl.pallas_call(outer_kernel, out_shape=[piece] * PIECES + [jax.ShapeDtype...  2.45 us
    ppermute x1, waiting for transfers between devices, body(): inner_got = lax.ppermute(inner, 'row', away)  2.27 us
    pallas_call x1, Pallas kernels, body(): pl.pallas_call(near_kernel, out_shape=[result, jax.ShapeDtypeStruct((half...  1.71 us
    pallas_call x1, Pallas kernels, body(): pl.pallas_call(inner_kernel, out_shape=[piece] * PIECES + [jax.ShapeDtype...  1.43 us
    ppermute x1, waiting for transfers between devices, body(): row = lax.ppermute(row, 'row', chip)  1.24 us
    pallas_call x1, Pallas kernels, body(): pl.pallas_call(last_kernel, out_shape=result, in_specs=[VMEM] * 3, out_sp...  1.14 us
  transfers between devices with their start and end apart: 8, of which 5 were waited for; matrix products, arithmetic and copies ran while one was open for 0% of the time, Pallas kernels for 16%

profile of v11, /device:TPU:11, one launch (start us, length us, event | category | flops | bytes accessed | tf_op | source)
XLA Modules:
  0.0 20.9 jit_solution(10407845360361984393)
XLA Ops:
  0.0 0.0 copy-start
  0.0 2.4 %outer_half.1 = (bf16[4,2,128,128]{3,2,1,0:T(8,128)(2,1)S(1)}, bf16[4,2,128,128]{3,2,1,0:T(8,128)(2,1)S(1)}, bf16[4,2,128,128]{3,2,1,0:T(8,128)(2,1)S(1)}, bf16[...) custom-call(f32[4]{0:T(128)} %lw_hbm.1, ...), custom_call_target="tpu_custom_call" | custom-call | tf_op jit(solution)/shard_map/outer_half/pallas_call | solution.py:435
  2.5 3.7 %collective-permute-start.5 = (bf16[1200,128]{1,0:T(8,128)(2,1)S(1)}, bf16[1200,128]{1,0:T(8,128)(2,1)S(1)}, u32[]{:S(2)}, u32[]{:S(2)}) collective-permute-start(bf16[1200,128]{1,0:T(8,128)(2,1)S(1)} %get-tuple-element.33.own_ref), channel_id=1, source_target_pairs={{1,2},{2,1},{3,4},{4,3},{5,6},{6,5},{7,8},{8,7},{9,10},{10,9},{11,... | collective-permute-start | bytes 921608 | tf_op jit(solution)/shard_map/ppermute | solution.py:458
  6.2 0.1 collective-permute-start
  6.3 1.2 %collective-permute-done.row_ref = bf16[16,2048]{1,0:T(8,128)(2,1)S(1)} collective-permute-done((bf16[16,2048]{1,0:T(8,128)(2,1)S(1)}, bf16[16,2048]{1,0:T(8,128)(2,1)S(1)}, u32[]{:S(2)}, u32[]{:S(2)}) %collective-permute-start) | collective-permute-done | bytes 65568 | tf_op jit(solution)/shard_map/ppermute | solution.py:459
  7.5 0.0 copy-done
  7.5 1.4 %inner_half.1 = (bf16[4,2,128,128]{3,2,1,0:T(8,128)(2,1)S(1)}, bf16[4,2,128,128]{3,2,1,0:T(8,128)(2,1)S(1)}, bf16[4,2,128,128]{3,2,1,0:T(8,128)(2,1)S(1)}, bf16[...) custom-call(f32[8,256]{1,0:T(8,128)S(1)} %get-tuple-element.21.weigh, ...), custom_call_target="tpu_custom_call", output_to_operand_aliasing={{0}: (5, {}), {1}: (6, {}), {2}: (7, {}), {3}: (8, {})} | custom-call | tf_op jit(solution)/shard_map/inner_half/pallas_call | solution.py:460
  8.9 0.2 %collective-permute-start.1 = (bf16[4,2,128,128]{3,2,1,0:T(8,128)(2,1)S(1)}, bf16[4,2,128,128]{3,2,1,0:T(8,128)(2,1)S(1)}, u32[]{:S(2)}, u32[]{:S(2)}) collective-permute-start(bf16[4,2,128,128]{3,2,1,0:T(8,128)(2,1)S(1)} %get-tuple-element.29.refs_0_), channel_id=1, source_target_pairs={{0,1},{1,0},{2,3},{3,2},{4,5},{5,4},{6,7},{7,6},{8,9},{9,8},{10,11... | collective-permute-start | bytes 786440 | tf_op jit(solution)/shard_map/ppermute | solution.py:471
  9.2 3.4 %collective-permute-start.7 = (bf16[1040,128]{1,0:T(8,128)(2,1)S(1)}, bf16[1040,128]{1,0:T(8,128)(2,1)S(1)}, u32[]{:S(2)}, u32[]{:S(2)}) collective-permute-start(bf16[1040,128]{1,0:T(8,128)(2,1)S(1)} %get-tuple-element.36), channel_id=1, source_target_pairs={{1,2},{2,1},{3,4},{4,3},{5,6},{6,5},{7,8},{8,7},{9,10},{10,9},{11,... | collective-permute-start | bytes 798728 | tf_op jit(solution)/shard_map/ppermute | solution.py:470
  12.5 0.1 collective-permute-start.2
  12.7 0.5 %collective-permute-start.3 = (bf16[4,2,128,128]{3,2,1,0:T(8,128)(2,1)S(1)}, bf16[4,2,128,128]{3,2,1,0:T(8,128)(2,1)S(1)}, u32[]{:S(2)}, u32[]{:S(2)}) collective-permute-start(bf16[4,2,128,128]{3,2,1,0:T(8,128)(2,1)S(1)} %get-tuple-element.31.refs_2_), channel_id=1, source_target_pairs={{0,1},{1,0},{2,3},{3,2},{4,5},{5,4},{6,7},{7,6},{8,9},{9,8},{10,11... | collective-permute-start | bytes 786440 | tf_op jit(solution)/shard_map/ppermute | solution.py:471
  13.1 0.9 %collective-permute-done.5.got_ref.refs_10_ = bf16[1200,128]{1,0:T(8,128)(2,1)S(1)} collective-permute-done((bf16[1200,128]{1,0:T(8,128)(2,1)S(1)}, bf16[1200,128]{1,0:T(8,128)(2,1)S(1)}, u32[]{:S(2)}, u32[]{:S(2)}) %collective-permute-start.5) | collective-permute-done | bytes 307232 | tf_op jit(solution)/shard_map/ppermute | solution.py:458
  14.0 0.0 collective-permute-start.4
  14.0 0.3 %outermost_rows.1.refs_8_ = bf16[16,2048]{1,0:T(8,128)(2,1)S(1)} custom-call(f32[8,256]{1,0:T(8,128)S(1)} %get-tuple-element.21.weight_ref, bf16[1200,128]{1,0:T(8,128)(2,1)S(1)} %get-tuple-element.33.own_ref, bf16[1200,128]{1,0:T(8,128)(2,1)S(1)} %collective-permute-done.5.got_ref.refs_10_), custom_call_target="tpu_custom_call" | custom-call | tf_op jit(solution)/shard_map/outermost_rows/pallas_call | solution.py:472
  14.3 0.0 collective-permute-done.1.refs_4_
  14.3 0.6 %collective-permute-start.6 = (bf16[16,2048]{1,0:T(8,128)(2,1)S(1)}, bf16[16,2048]{1,0:T(8,128)(2,1)S(1)}, u32[]{:S(2)}, u32[]{:S(2)}) collective-permute-start(bf16[16,2048]{1,0:T(8,128)(2,1)S(1)} %outermost_rows.1.refs_8_), channel_id=1, source_target_pairs={{0,1},{1,0},{2,3},{3,2},{4,5},{5,4},{6,7},{7,6},{8,9},{9,8},{10,11... | collective-permute-start | bytes 196616 | tf_op jit(solution)/shard_map/ppermute | solution.py:480
  14.9 0.0 collective-permute-done.2.refs_5_
  14.9 0.0 collective-permute-done.3.refs_6_
  14.9 0.7 %collective-permute-done.4.refs_7_ = bf16[4,2,128,128]{3,2,1,0:T(8,128)(2,1)S(1)} collective-permute-done((bf16[4,2,128,128]{3,2,1,0:T(8,128)(2,1)S(1)}, bf16[4,2,128,128]{3,2,1,0:T(8,128)(2,1)S(1)}, u32[]{:S(2)}, u32[]{:S(2)}) %collective-permute-start.4) | collective-permute-done | bytes 262176 | tf_op jit(solution)/shard_map/ppermute | solution.py:471
  15.5 0.2 %collective-permute-done.6.refs_9_ = bf16[16,2048]{1,0:T(8,128)(2,1)S(1)} collective-permute-done((bf16[16,2048]{1,0:T(8,128)(2,1)S(1)}, bf16[16,2048]{1,0:T(8,128)(2,1)S(1)}, u32[]{:S(2)}, u32[]{:S(2)}) %collective-permute-start.6) | collective-permute-done | bytes 65568 | tf_op jit(solution)/shard_map/ppermute | solution.py:480
  15.8 1.7 %near_part.1 = (f32[2,64,2048]{2,1,0:T(8,128)S(1)}, bf16[32,96]{1,0:T(8,128)(2,1)S(1)}) custom-call(bf16[4,2,128,128]{3,2,1,0:T(8,128)(2,1)S(1)} %get-tuple-element.29.refs_0_, bf16[4,2,128,128]{3,2,1,0:T(8,128)(2,1)S(1)} %get-tuple-element.30.refs_1_, bf16[4,2,128,128]{3,2,1,0:T(8,128)(2,1)S(1)} %get-tuple-element.31.refs_2_, ...), custom_call_target="tpu_custom_call" | custom-call | tf_op jit(solution)/shard_map/near_part/pallas_call | solution.py:481
  17.5 2.3 %collective-permute-done.7.msg_ref = bf16[1040,128]{1,0:T(8,128)(2,1)S(1)} collective-permute-done((bf16[1040,128]{1,0:T(8,128)(2,1)S(1)}, bf16[1040,128]{1,0:T(8,128)(2,1)S(1)}, u32[]{:S(2)}, u32[]{:S(2)}) %collective-permute-start.7) | collective-permute-done | bytes 266272 | tf_op jit(solution)/shard_map/ppermute | solution.py:470
  19.7 1.1 %last_part.1 = f32[2,64,2048]{2,1,0:T(8,128)} custom-call(bf16[32,96]{1,0:T(8,128)(2,1)S(1)} %get-tuple-element.34.taps_ref, f32[2,64,2048]{2,1,0:T(8,128)S(1)} %get-tuple-element.35.part_ref, bf16[1040,128]{1,0:T(8,128)(2,1)S(1)} %collective-permute-done.7.msg_ref), custom_call_target="tpu_custom_call" | custom-call | tf_op jit(solution)/shard_map/last_part/pallas_call | solution.py:490
Async XLA Ops:
  0.0 7.5 %copy-start = (bf16[2,512,256]{2,1,0:T(8,128)(2,1)S(1)}, bf16[2,512,256]{2,1,0:T(8,128)(2,1)}, u32[]{:S(2)}) copy-start(bf16[2,512,256]{2,1,0:T(8,128)(2,1)} %constant.2.clone.band_ref.refs_11_) | copy-start | bytes 1572868
  2.5 11.5 %collective-permute-start.5 = (bf16[1200,128]{1,0:T(8,128)(2,1)S(1)}, bf16[1200,128]{1,0:T(8,128)(2,1)S(1)}, u32[]{:S(2)}, u32[]{:S(2)}) collective-permute-start(bf16[1200,128]{1,0:T(8,128)(2,1)S(1)} %get-tuple-element.33.own_ref), channel_id=1, source_target_pairs={{1,2},{2,1},{3,4},{4,3},{5,6},{6,5},{7,8},{8,7},{9,10},{10,9},{11,... | collective-permute-start | bytes 921608 | tf_op jit(solution)/shard_map/ppermute | solution.py:458
  6.2 1.3 %collective-permute-start = (bf16[16,2048]{1,0:T(8,128)(2,1)S(1)}, bf16[16,2048]{1,0:T(8,128)(2,1)S(1)}, u32[]{:S(2)}, u32[]{:S(2)}) collective-permute-start(bf16[16,2048]{1,0:T(8,128)(2,1)S(1)} %get-tuple-element.24), channel_id=1, source_target_pairs={{0,1},{1,0},{2,3},{3,2},{4,5},{5,4},{6,7},{7,6},{8,9},{9,8},{10,11... | collective-permute-start | bytes 196616 | tf_op jit(solution)/shard_map/ppermute | solution.py:459
  8.9 5.3 %collective-permute-start.1 = (bf16[4,2,128,128]{3,2,1,0:T(8,128)(2,1)S(1)}, bf16[4,2,128,128]{3,2,1,0:T(8,128)(2,1)S(1)}, u32[]{:S(2)}, u32[]{:S(2)}) collective-permute-start(bf16[4,2,128,128]{3,2,1,0:T(8,128)(2,1)S(1)} %get-tuple-element.29.refs_0_), channel_id=1, source_target_pairs={{0,1},{1,0},{2,3},{3,2},{4,5},{5,4},{6,7},{7,6},{8,9},{9,8},{10,11... | collective-permute-start | bytes 786440 | tf_op jit(solution)/shard_map/ppermute | solution.py:471
  9.2 10.6 %collective-permute-start.7 = (bf16[1040,128]{1,0:T(8,128)(2,1)S(1)}, bf16[1040,128]{1,0:T(8,128)(2,1)S(1)}, u32[]{:S(2)}, u32[]{:S(2)}) collective-permute-start(bf16[1040,128]{1,0:T(8,128)(2,1)S(1)} %get-tuple-element.36), channel_id=1, source_target_pairs={{1,2},{2,1},{3,4},{4,3},{5,6},{6,5},{7,8},{8,7},{9,10},{10,9},{11,... | collective-permute-start | bytes 798728 | tf_op jit(solution)/shard_map/ppermute | solution.py:470
  12.5 2.3 %collective-permute-start.2 = (bf16[4,2,128,128]{3,2,1,0:T(8,128)(2,1)S(1)}, bf16[4,2,128,128]{3,2,1,0:T(8,128)(2,1)S(1)}, u32[]{:S(2)}, u32[]{:S(2)}) collective-permute-start(bf16[4,2,128,128]{3,2,1,0:T(8,128)(2,1)S(1)} %get-tuple-element.30.refs_1_), channel_id=1, source_target_pairs={{0,1},{1,0},{2,3},{3,2},{4,5},{5,4},{6,7},{7,6},{8,9},{9,8},{10,11... | collective-permute-start | bytes 786440 | tf_op jit(solution)/shard_map/ppermute | solution.py:471
  12.7 2.2 %collective-permute-start.3 = (bf16[4,2,128,128]{3,2,1,0:T(8,128)(2,1)S(1)}, bf16[4,2,128,128]{3,2,1,0:T(8,128)(2,1)S(1)}, u32[]{:S(2)}, u32[]{:S(2)}) collective-permute-start(bf16[4,2,128,128]{3,2,1,0:T(8,128)(2,1)S(1)} %get-tuple-element.31.refs_2_), channel_id=1, source_target_pairs={{0,1},{1,0},{2,3},{3,2},{4,5},{5,4},{6,7},{7,6},{8,9},{9,8},{10,11... | collective-permute-start | bytes 786440 | tf_op jit(solution)/shard_map/ppermute | solution.py:471
  14.0 1.5 %collective-permute-start.4 = (bf16[4,2,128,128]{3,2,1,0:T(8,128)(2,1)S(1)}, bf16[4,2,128,128]{3,2,1,0:T(8,128)(2,1)S(1)}, u32[]{:S(2)}, u32[]{:S(2)}) collective-permute-start(bf16[4,2,128,128]{3,2,1,0:T(8,128)(2,1)S(1)} %get-tuple-element.32.refs_3_), channel_id=1, source_target_pairs={{0,1},{1,0},{2,3},{3,2},{4,5},{5,4},{6,7},{7,6},{8,9},{9,8},{10,11... | collective-permute-start | bytes 786440 | tf_op jit(solution)/shard_map/ppermute | solution.py:471
  14.3 1.5 %collective-permute-start.6 = (bf16[16,2048]{1,0:T(8,128)(2,1)S(1)}, bf16[16,2048]{1,0:T(8,128)(2,1)S(1)}, u32[]{:S(2)}, u32[]{:S(2)}) collective-permute-start(bf16[16,2048]{1,0:T(8,128)(2,1)S(1)} %outermost_rows.1.refs_8_), channel_id=1, source_target_pairs={{0,1},{1,0},{2,3},{3,2},{4,5},{5,4},{6,7},{7,6},{8,9},{9,8},{10,11... | collective-permute-start | bytes 196616 | tf_op jit(solution)/shard_map/ppermute | solution.py:480

commit v12 on v11

--- a/solution.py
+++ b/solution.py
@@ -101,11 +101,6 @@
 
 def tile_at(row):
     return pl.ds(pl.multiple_of(row, TILE), TILE)
-
-
-def half_of(ref, comp_rows, start, part):
-    half = comp_rows // 2
-    return [ref[part, pl.ds(pl.multiple_of(comp * comp_rows + start, TILE), half), :] for comp in range(2)]
 
 
 def raw_pair(first, weight, inno_ref, back_ref, upper, diff_y, diff_x, extra, raw_refs):
@@ -137,9 +132,8 @@
             raw = jnp.where(iota(raw.shape, 0) == jnp.where(upper, 0, half - 1), 0.0, raw)
         found.append(raw)
         at = pl.ds(pl.multiple_of(comp * rows + start, TILE), half)
-        for part, values in enumerate(split(raw)):
-            for j in range(2):
-                block_of(raw_refs, first + j)[part, at, :] = values[:, j * LANES : (j + 1) * LANES]
+        for j in range(2):
+            block_of(raw_refs, first + j)[at, :] = raw[:, j * LANES : (j + 1) * LANES]
     return found
 
 
@@ -239,7 +233,7 @@
 
 def inner_kernel(weight_ref, inno_ref, back_ref, row_ref, band_ref, *refs):
     raw_refs = refs[PIECES : 2 * PIECES]
-    msg_ref, top_ref = refs[2 * PIECES :]
+    msg_ref, top_ref, both_ref = refs[2 * PIECES :]
     _, rows, width = inno_ref.shape
     half = rows // 2
     nblocks = width // LANES
@@ -255,14 +249,13 @@
     def weight(level):
         return weight_ref[level : level + 1, :]
 
-    def load(k):
-        block = block_of(raw_refs, k)
-        return jnp.concatenate(half_of(block, rows, start, 0) + half_of(block, rows, start, 1), axis=0)
-
     for first in range(0, nblocks, 2):
-        raw_pair(first, weight, inno_ref, back_ref, upper, diff_y, diff_x, extra, raw_refs)
+        found = raw_pair(first, weight, inno_ref, back_ref, upper, diff_y, diff_x, extra, raw_refs)
+        both = jnp.concatenate(split(jnp.concatenate(found, axis=0)), axis=0)
+        for j in range(2):
+            both_ref[first + j] = both[:, j * LANES : (j + 1) * LANES]
     for first in range(0, nblocks, 2):
-        (code,), top = encode([smooth_x(band_ref, load, first, nblocks)])
+        (code,), top = encode([smooth_x(band_ref, lambda k: both_ref[k], first, nblocks)])
         code = code.astype(BF16)
         for j in range(2):
             msg_ref[pl.ds((first + j) * rows, rows), :] = code[:, j * LANES : (j + 1) * LANES]
@@ -372,12 +365,12 @@
             both, got = [], []
             for k in (first, first + 1):
                 refs = (block_of(raw_refs, k), block_of(near_refs, k))
-                both.append([jnp.concatenate([ref[part, here, :] for ref in refs], axis=0) for part in range(2)])
+                both.append(jnp.concatenate([ref[here, :] for ref in refs], axis=0))
                 got.append(msg_ref[pl.ds(k * rows + comp * half, half), :])
             got = decode(jnp.concatenate(got, axis=1), top)
             got = split(jnp.where(outermost, 0.0, got))
             highs, lows = (
-                jnp.concatenate([jnp.concatenate([x[part] for x in both], axis=1), got[part]], axis=0) for part in range(2)
+                jnp.concatenate([x, y], axis=0) for x, y in zip(split(jnp.concatenate(both, axis=1)), got)
             )
             part = dot(stacked[comp], jnp.concatenate([highs] + edges, axis=0))
             high, low = split(part[:rows] + part[rows:] + dot(low_taps, lows))
@@ -430,7 +423,7 @@
     away = [(i, j) for i in range(count) for j in [((i + 1) ^ 1) - 1] if 0 <= j < count]
     hbm = [pltpu.with_memory_space_constraint(x, pltpu.HBM) for x in (level_weight, innovation, background)]
     band = jnp.asarray(zonal_band())
-    piece = jax.ShapeDtypeStruct((nblocks // PIECES, 2, both, LANES), BF16)
+    piece = jax.ShapeDtypeStruct((nblocks // PIECES, both, LANES), F32)
     result = jax.ShapeDtypeStruct((2, rows, width), F32)
     *raws, outer, row, inno, back, weight = pl.pallas_call(
         outer_kernel,
@@ -462,7 +455,7 @@
         out_shape=[piece] * PIECES + [jax.ShapeDtypeStruct((inner_rows(rows, nblocks), LANES), BF16)],
         in_specs=[VMEM] * (5 + PIECES),
         out_specs=[VMEM] * (PIECES + 1),
-        scratch_shapes=[pltpu.VMEM((nblocks, LANES), F32)],
+        scratch_shapes=[pltpu.VMEM((nblocks, LANES), F32), pltpu.VMEM((nblocks, both, LANES), BF16)],
         input_output_aliases={5 + k: k for k in range(PIECES)},
         compiler_params=PARAMS,
         name="inner_half",

time: 21.1 us -> 21 us (level)
  transfers between devices with their start and end apart: 8 -> 8, of which waited for: 5 -> 5; matrix products, arithmetic and copies ran while one was open for 0% -> 0% of each run, Pallas kernels for 16% -> 17%
where the time goes in v12:
time: 21 us; the launch traced here: 20.8 us
  starting transfers between devices  8.52 us (41%)
  Pallas kernels  7.06 us (34%)
  waiting for transfers between devices  5.19 us (25%)
    ppermute x1, starting transfers between devices, body(): outer_got = lax.ppermute(outer, 'row', away)  3.71 us
    ppermute x1, starting transfers between devices, body(): inner_got = lax.ppermute(inner, 'row', away)  3.37 us
    pallas_call x1, Pallas kernels, body(): pl.pallas_call(outer_kernel, out_shape=[piece] * PIECES + [jax.ShapeDtype...  2.4 us
    ppermute x1, waiting for transfers between devices, body(): inner_got = lax.ppermute(inner, 'row', away)  2.19 us
    pallas_call x1, Pallas kernels, body(): pl.pallas_call(near_kernel, out_shape=[result, jax.ShapeDtypeStruct((half...  1.79 us
    pallas_call x1, Pallas kernels, body(): pl.pallas_call(inner_kernel, out_shape=[piece] * PIECES + [jax.ShapeDtype...  1.46 us
    ppermute x1, waiting for transfers between devices, body(): row = lax.ppermute(row, 'row', chip)  1.24 us
    pallas_call x1, Pallas kernels, body(): pl.pallas_call(last_kernel, out_shape=result, in_specs=[VMEM] * 3, out_sp...  1.13 us
  transfers between devices with their start and end apart: 8, of which 5 were waited for; matrix products, arithmetic and copies ran while one was open for 0% of the time, Pallas kernels for 17%

profile of v12, /device:TPU:11, one launch (start us, length us, event | category | flops | bytes accessed | tf_op | source)
XLA Modules:
  0.0 20.8 jit_solution(4367852318922437280)
XLA Ops:
  0.0 0.0 copy-start
  0.0 2.4 %outer_half.1 = (f32[4,128,128]{2,1,0:T(8,128)S(1)}, f32[4,128,128]{2,1,0:T(8,128)S(1)}, f32[4,128,128]{2,1,0:T(8,128)S(1)}, f32[4,128,128]{2,1,0:T(8,128)S(1)},...) custom-call(f32[4]{0:T(128)} %lw_hbm.1, ...), custom_call_target="tpu_custom_call" | custom-call | tf_op jit(solution)/shard_map/outer_half/pallas_call | solution.py:428
  2.4 3.7 %collective-permute-start.5 = (bf16[1200,128]{1,0:T(8,128)(2,1)S(1)}, bf16[1200,128]{1,0:T(8,128)(2,1)S(1)}, u32[]{:S(2)}, u32[]{:S(2)}) collective-permute-start(bf16[1200,128]{1,0:T(8,128)(2,1)S(1)} %get-tuple-element.33.own_ref), channel_id=1, source_target_pairs={{1,2},{2,1},{3,4},{4,3},{5,6},{6,5},{7,8},{8,7},{9,10},{10,9},{11,... | collective-permute-start | bytes 921608 | tf_op jit(solution)/shard_map/ppermute | solution.py:451
  6.1 0.1 collective-permute-start
  6.2 1.2 %collective-permute-done.row_ref = bf16[16,2048]{1,0:T(8,128)(2,1)S(1)} collective-permute-done((bf16[16,2048]{1,0:T(8,128)(2,1)S(1)}, bf16[16,2048]{1,0:T(8,128)(2,1)S(1)}, u32[]{:S(2)}, u32[]{:S(2)}) %collective-permute-start) | collective-permute-done | bytes 65568 | tf_op jit(solution)/shard_map/ppermute | solution.py:452
  7.4 0.0 copy-done
  7.4 1.5 %inner_half.1 = (f32[4,128,128]{2,1,0:T(8,128)S(1)}, f32[4,128,128]{2,1,0:T(8,128)S(1)}, f32[4,128,128]{2,1,0:T(8,128)S(1)}, f32[4,128,128]{2,1,0:T(8,128)S(1)}, bf16[1040,128]{1,0:T(8,128)(2,1)S(1)}) custom-call(f32[8,256]{1,0:T(8,128)S(1)} %get-tuple-element.21.weight_ref, ...), custom_call_target="tpu_custom_call", output_to_operand_aliasing={{0}: (5, {}), {1}: (6, {}), {2}: (7, {}), {3}: (8, {})} | custom-call | tf_op jit(solution)/shard_map/inner_half/pallas_call | solution.py:453
  8.9 0.2 %collective-permute-start.1 = (f32[4,128,128]{2,1,0:T(8,128)S(1)}, f32[4,128,128]{2,1,0:T(8,128)S(1)}, u32[]{:S(2)}, u32[]{:S(2)}) collective-permute-start(f32[4,128,128]{2,1,0:T(8,128)S(1)} %get-tuple-element.29.refs_0_), channel_id=1, source_target_pairs={{0,1},{1,0},{2,3},{3,2},{4,5},{5,4},{6,7},{7,6},{8,9},{9,8},{10,11... | collective-permute-start | bytes 786440 | tf_op jit(solution)/shard_map/ppermute | solution.py:464
  9.1 3.4 %collective-permute-start.7 = (bf16[1040,128]{1,0:T(8,128)(2,1)S(1)}, bf16[1040,128]{1,0:T(8,128)(2,1)S(1)}, u32[]{:S(2)}, u32[]{:S(2)}) collective-permute-start(bf16[1040,128]{1,0:T(8,128)(2,1)S(1)} %get-tuple-element.36), channel_id=1, source_target_pairs={{1,2},{2,1},{3,4},{4,3},{5,6},{6,5},{7,8},{8,7},{9,10},{10,9},{11,... | collective-permute-start | bytes 798728 | tf_op jit(solution)/shard_map/ppermute | solution.py:463
  12.5 0.1 collective-permute-start.2
  12.6 0.5 %collective-permute-start.3 = (f32[4,128,128]{2,1,0:T(8,128)S(1)}, f32[4,128,128]{2,1,0:T(8,128)S(1)}, u32[]{:S(2)}, u32[]{:S(2)}) collective-permute-start(f32[4,128,128]{2,1,0:T(8,128)S(1)} %get-tuple-element.31.refs_2_), channel_id=1, source_target_pairs={{0,1},{1,0},{2,3},{3,2},{4,5},{5,4},{6,7},{7,6},{8,9},{9,8},{10,11... | collective-permute-start | bytes 786440 | tf_op jit(solution)/shard_map/ppermute | solution.py:464
  13.1 0.8 %collective-permute-done.5.got_ref.refs_10_ = bf16[1200,128]{1,0:T(8,128)(2,1)S(1)} collective-permute-done((bf16[1200,128]{1,0:T(8,128)(2,1)S(1)}, bf16[1200,128]{1,0:T(8,128)(2,1)S(1)}, u32[]{:S(2)}, u32[]{:S(2)}) %collective-permute-start.5) | collective-permute-done | bytes 307232 | tf_op jit(solution)/shard_map/ppermute | solution.py:451
  13.9 0.0 collective-permute-start.4
  13.9 0.3 %outermost_rows.1.refs_8_ = bf16[16,2048]{1,0:T(8,128)(2,1)S(1)} custom-call(f32[8,256]{1,0:T(8,128)S(1)} %get-tuple-element.21.weight_ref, bf16[1200,128]{1,0:T(8,128)(2,1)S(1)} %get-tuple-element.33.own_ref, bf16[1200,128]{1,0:T(8,128)(2,1)S(1)} %collective-permute-done.5.got_ref.refs_10_), custom_call_target="tpu_custom_call" | custom-call | tf_op jit(solution)/shard_map/outermost_rows/pallas_call | solution.py:465
  14.2 0.0 collective-permute-done.1.refs_4_
  14.2 0.6 %collective-permute-start.6 = (bf16[16,2048]{1,0:T(8,128)(2,1)S(1)}, bf16[16,2048]{1,0:T(8,128)(2,1)S(1)}, u32[]{:S(2)}, u32[]{:S(2)}) collective-permute-start(bf16[16,2048]{1,0:T(8,128)(2,1)S(1)} %outermost_rows.1.refs_8_), channel_id=1, source_target_pairs={{0,1},{1,0},{2,3},{3,2},{4,5},{5,4},{6,7},{7,6},{8,9},{9,8},{10,11... | collective-permute-start | bytes 196616 | tf_op jit(solution)/shard_map/ppermute | solution.py:473
  14.8 0.0 collective-permute-done.2.refs_5_
  14.8 0.0 collective-permute-done.3.refs_6_
  14.8 0.7 %collective-permute-done.4.refs_7_ = f32[4,128,128]{2,1,0:T(8,128)S(1)} collective-permute-done((f32[4,128,128]{2,1,0:T(8,128)S(1)}, f32[4,128,128]{2,1,0:T(8,128)S(1)}, u32[]{:S(2)}, u32[]{:S(2)}) %collective-permute-start.4) | collective-permute-done | bytes 262176 | tf_op jit(solution)/shard_map/ppermute | solution.py:464
  15.5 0.2 %collective-permute-done.6.refs_9_ = bf16[16,2048]{1,0:T(8,128)(2,1)S(1)} collective-permute-done((bf16[16,2048]{1,0:T(8,128)(2,1)S(1)}, bf16[16,2048]{1,0:T(8,128)(2,1)S(1)}, u32[]{:S(2)}, u32[]{:S(2)}) %collective-permute-start.6) | collective-permute-done | bytes 65568 | tf_op jit(solution)/shard_map/ppermute | solution.py:473
  15.7 1.8 %near_part.1 = (f32[2,64,2048]{2,1,0:T(8,128)S(1)}, bf16[32,96]{1,0:T(8,128)(2,1)S(1)}) custom-call(f32[4,128,128]{2,1,0:T(8,128)S(1)} %get-tuple-element.29.refs_0_, f32[4,128,128]{2,1,0:T(8,128)S(1)} %get-tuple-element.30.refs_1_, f32[4,128,128]{2,1,0:T(8,128)S(1)} %get-tuple-element.31.refs_2_, f32[4,128,128]{2,1,0:T(8,128)S(1)} %get-tuple-element.32.refs_3_, ...), custom_call_target="tpu_custom_call" | custom-call | tf_op jit(solution)/shard_map/near_part/pallas_call | solution.py:474
  17.5 2.2 %collective-permute-done.7.msg_ref = bf16[1040,128]{1,0:T(8,128)(2,1)S(1)} collective-permute-done((bf16[1040,128]{1,0:T(8,128)(2,1)S(1)}, bf16[1040,128]{1,0:T(8,128)(2,1)S(1)}, u32[]{:S(2)}, u32[]{:S(2)}) %collective-permute-start.7) | collective-permute-done | bytes 266272 | tf_op jit(solution)/shard_map/ppermute | solution.py:463
  19.7 1.1 %last_part.1 = f32[2,64,2048]{2,1,0:T(8,128)} custom-call(bf16[32,96]{1,0:T(8,128)(2,1)S(1)} %get-tuple-element.34.taps_ref, f32[2,64,2048]{2,1,0:T(8,128)S(1)} %get-tuple-element.35.part_ref, bf16[1040,128]{1,0:T(8,128)(2,1)S(1)} %collective-permute-done.7.msg_ref), custom_call_target="tpu_custom_call" | custom-call | tf_op jit(solution)/shard_map/last_part/pallas_call | solution.py:483
Async XLA Ops:
  0.0 7.4 %copy-start = (bf16[2,512,256]{2,1,0:T(8,128)(2,1)S(1)}, bf16[2,512,256]{2,1,0:T(8,128)(2,1)}, u32[]{:S(2)}) copy-start(bf16[2,512,256]{2,1,0:T(8,128)(2,1)} %constant.2.clone.band_ref.refs_11_) | copy-start | bytes 1572868
  2.4 11.5 %collective-permute-start.5 = (bf16[1200,128]{1,0:T(8,128)(2,1)S(1)}, bf16[1200,128]{1,0:T(8,128)(2,1)S(1)}, u32[]{:S(2)}, u32[]{:S(2)}) collective-permute-start(bf16[1200,128]{1,0:T(8,128)(2,1)S(1)} %get-tuple-element.33.own_ref), channel_id=1, source_target_pairs={{1,2},{2,1},{3,4},{4,3},{5,6},{6,5},{7,8},{8,7},{9,10},{10,9},{11,... | collective-permute-start | bytes 921608 | tf_op jit(solution)/shard_map/ppermute | solution.py:451
  6.1 1.3 %collective-permute-start = (bf16[16,2048]{1,0:T(8,128)(2,1)S(1)}, bf16[16,2048]{1,0:T(8,128)(2,1)S(1)}, u32[]{:S(2)}, u32[]{:S(2)}) collective-permute-start(bf16[16,2048]{1,0:T(8,128)(2,1)S(1)} %get-tuple-element.24), channel_id=1, source_target_pairs={{0,1},{1,0},{2,3},{3,2},{4,5},{5,4},{6,7},{7,6},{8,9},{9,8},{10,11... | collective-permute-start | bytes 196616 | tf_op jit(solution)/shard_map/ppermute | solution.py:452
  8.9 5.3 %collective-permute-start.1 = (f32[4,128,128]{2,1,0:T(8,128)S(1)}, f32[4,128,128]{2,1,0:T(8,128)S(1)}, u32[]{:S(2)}, u32[]{:S(2)}) collective-permute-start(f32[4,128,128]{2,1,0:T(8,128)S(1)} %get-tuple-element.29.refs_0_), channel_id=1, source_target_pairs={{0,1},{1,0},{2,3},{3,2},{4,5},{5,4},{6,7},{7,6},{8,9},{9,8},{10,11... | collective-permute-start | bytes 786440 | tf_op jit(solution)/shard_map/ppermute | solution.py:464
  9.1 10.6 %collective-permute-start.7 = (bf16[1040,128]{1,0:T(8,128)(2,1)S(1)}, bf16[1040,128]{1,0:T(8,128)(2,1)S(1)}, u32[]{:S(2)}, u32[]{:S(2)}) collective-permute-start(bf16[1040,128]{1,0:T(8,128)(2,1)S(1)} %get-tuple-element.36), channel_id=1, source_target_pairs={{1,2},{2,1},{3,4},{4,3},{5,6},{6,5},{7,8},{8,7},{9,10},{10,9},{11,... | collective-permute-start | bytes 798728 | tf_op jit(solution)/shard_map/ppermute | solution.py:463
  12.5 2.3 %collective-permute-start.2 = (f32[4,128,128]{2,1,0:T(8,128)S(1)}, f32[4,128,128]{2,1,0:T(8,128)S(1)}, u32[]{:S(2)}, u32[]{:S(2)}) collective-permute-start(f32[4,128,128]{2,1,0:T(8,128)S(1)} %get-tuple-element.30.refs_1_), channel_id=1, source_target_pairs={{0,1},{1,0},{2,3},{3,2},{4,5},{5,4},{6,7},{7,6},{8,9},{9,8},{10,11... | collective-permute-start | bytes 786440 | tf_op jit(solution)/shard_map/ppermute | solution.py:464
  12.6 2.2 %collective-permute-start.3 = (f32[4,128,128]{2,1,0:T(8,128)S(1)}, f32[4,128,128]{2,1,0:T(8,128)S(1)}, u32[]{:S(2)}, u32[]{:S(2)}) collective-permute-start(f32[4,128,128]{2,1,0:T(8,128)S(1)} %get-tuple-element.31.refs_2_), channel_id=1, source_target_pairs={{0,1},{1,0},{2,3},{3,2},{4,5},{5,4},{6,7},{7,6},{8,9},{9,8},{10,11... | collective-permute-start | bytes 786440 | tf_op jit(solution)/shard_map/ppermute | solution.py:464
  13.9 1.5 %collective-permute-start.4 = (f32[4,128,128]{2,1,0:T(8,128)S(1)}, f32[4,128,128]{2,1,0:T(8,128)S(1)}, u32[]{:S(2)}, u32[]{:S(2)}) collective-permute-start(f32[4,128,128]{2,1,0:T(8,128)S(1)} %get-tuple-element.32.refs_3_), channel_id=1, source_target_pairs={{0,1},{1,0},{2,3},{3,2},{4,5},{5,4},{6,7},{7,6},{8,9},{9,8},{10,11... | collective-permute-start | bytes 786440 | tf_op jit(solution)/shard_map/ppermute | solution.py:464
  14.2 1.5 %collective-permute-start.6 = (bf16[16,2048]{1,0:T(8,128)(2,1)S(1)}, bf16[16,2048]{1,0:T(8,128)(2,1)S(1)}, u32[]{:S(2)}, u32[]{:S(2)}) collective-permute-start(bf16[16,2048]{1,0:T(8,128)(2,1)S(1)} %outermost_rows.1.refs_8_), channel_id=1, source_target_pairs={{0,1},{1,0},{2,3},{3,2},{4,5},{5,4},{6,7},{7,6},{8,9},{9,8},{10,11... | collective-permute-start | bytes 196616 | tf_op jit(solution)/shard_map/ppermute | solution.py:473

commit v13 on v12

--- a/solution.py
+++ b/solution.py
@@ -184,7 +184,11 @@
     outermost = place == jnp.where(upper, 0, TILE - 1)
     next_row = place == jnp.where(upper, 1, TILE - 2)
     pick_ref[0] = one_hot(((want == level) & outermost) | ((want == levels + level) & next_row))
-    pick_ref[1] = one_hot((want == 2 * levels + level - 2) & (level >= 2) & outermost)
+    half_cols = PACK * (levels - 2) * TILE
+    row, col = iota((PACK * kinds, half_cols), 0), iota((PACK * kinds, half_cols), 1)
+    want = row - (col >> 5) * kinds
+    level = (col >> 4) & 1
+    pick_ref[1, :, :half_cols] = one_hot((want == 2 * levels + level) & (col & (TILE - 1) == jnp.where(upper, 0, TILE - 1)))
     shape = (TILE, levels * TILE)
     pick_near = one_hot(iota(shape, 1) == iota(shape, 0) * TILE + jnp.where(upper, TILE - 1, 0))
     weights.wait()
@@ -201,8 +205,8 @@
             for k in range(first, first + PACK):
                 here = pl.ds(k * LANES, LANES)
                 back.append(back_ref[:, edge_at, here].reshape(levels * TILE, LANES))
-                inno.append(inno_ref[:, edge_at, here].reshape(levels * TILE, LANES))
-            tile = dot(pick_ref[0], jnp.concatenate(back, axis=0)) + dot(pick_ref[1], jnp.concatenate(inno, axis=0))
+                inno.append(inno_ref[2:, edge_at, here].reshape((levels - 2) * TILE, LANES))
+            tile = dot(pick_ref[0], jnp.concatenate(back, axis=0)) + dot(pick_ref[1, :, :half_cols], jnp.concatenate(inno, axis=0))
             at = base + nblocks + first * kinds
             msg_ref[pl.ds(at, PACK * kinds), :] = tile.astype(BF16)
 

time: 21 us -> 21 us (level)
  no operation moved by 1% of the time
where the time goes in v13:
time: 21 us; the launch traced here: 20.8 us
  starting transfers between devices  8.52 us (41%)
  Pallas kernels  7.03 us (33%)
  waiting for transfers between devices  5.18 us (25%)
    ppermute x1, starting transfers between devices, body(): outer_got = lax.ppermute(outer, 'row', away)  3.71 us
    ppermute x1, starting transfers between devices, body(): inner_got = lax.ppermute(inner, 'row', away)  3.37 us
    pallas_call x1, Pallas kernels, body(): pl.pallas_call(outer_kernel, out_shape=[piece] * PIECES + [jax.ShapeDtype...  2.37 us
    ppermute x1, waiting for transfers between devices, body(): inner_got = lax.ppermute(inner, 'row', away)  2.19 us
    pallas_call x1, Pallas kernels, body(): pl.pallas_call(near_kernel, out_shape=[result, jax.ShapeDtypeStruct((half...  1.8 us
    pallas_call x1, Pallas kernels, body(): pl.pallas_call(inner_kernel, out_shape=[piece] * PIECES + [jax.ShapeDtype...  1.45 us
    ppermute x1, waiting for transfers between devices, body(): row = lax.ppermute(row, 'row', chip)  1.24 us
    pallas_call x1, Pallas kernels, body(): pl.pallas_call(last_kernel, out_shape=result, in_specs=[VMEM] * 3, out_sp...  1.14 us
  transfers between devices with their start and end apart: 8, of which 5 were waited for; matrix products, arithmetic and copies ran while one was open for 0% of the time, Pallas kernels for 17%

profile of v13, /device:TPU:11, one launch (start us, length us, event | category | flops | bytes accessed | tf_op | source)
XLA Modules:
  0.0 20.8 jit_solution(2327252447410840175)
XLA Ops:
  0.0 0.0 copy-start
  0.0 2.4 %outer_half.1 = (f32[4,128,128]{2,1,0:T(8,128)S(1)}, f32[4,128,128]{2,1,0:T(8,128)S(1)}, f32[4,128,128]{2,1,0:T(8,128)S(1)}, f32[4,128,128]{2,1,0:T(8,128)S(1)},...) custom-call(f32[4]{0:T(128)} %lw_hbm.1, ...), custom_call_target="tpu_custom_call" | custom-call | tf_op jit(solution)/shard_map/outer_half/pallas_call | solution.py:432
  2.4 3.7 %collective-permute-start.5 = (bf16[1200,128]{1,0:T(8,128)(2,1)S(1)}, bf16[1200,128]{1,0:T(8,128)(2,1)S(1)}, u32[]{:S(2)}, u32[]{:S(2)}) collective-permute-start(bf16[1200,128]{1,0:T(8,128)(2,1)S(1)} %get-tuple-element.33.own_ref), channel_id=1, source_target_pairs={{1,2},{2,1},{3,4},{4,3},{5,6},{6,5},{7,8},{8,7},{9,10},{10,9},{11,... | collective-permute-start | bytes 921608 | tf_op jit(solution)/shard_map/ppermute | solution.py:455
  6.1 0.1 collective-permute-start
  6.2 1.2 %collective-permute-done.row_ref = bf16[16,2048]{1,0:T(8,128)(2,1)S(1)} collective-permute-done((bf16[16,2048]{1,0:T(8,128)(2,1)S(1)}, bf16[16,2048]{1,0:T(8,128)(2,1)S(1)}, u32[]{:S(2)}, u32[]{:S(2)}) %collective-permute-start) | collective-permute-done | bytes 65568 | tf_op jit(solution)/shard_map/ppermute | solution.py:456
  7.4 0.0 copy-done
  7.4 1.5 %inner_half.1 = (f32[4,128,128]{2,1,0:T(8,128)S(1)}, f32[4,128,128]{2,1,0:T(8,128)S(1)}, f32[4,128,128]{2,1,0:T(8,128)S(1)}, f32[4,128,128]{2,1,0:T(8,128)S(1)}, bf16[1040,128]{1,0:T(8,128)(2,1)S(1)}) custom-call(f32[8,256]{1,0:T(8,128)S(1)} %get-tuple-element.21.weight_ref, ...), custom_call_target="tpu_custom_call", output_to_operand_aliasing={{0}: (5, {}), {1}: (6, {}), {2}: (7, {}), {3}: (8, {})} | custom-call | tf_op jit(solution)/shard_map/inner_half/pallas_call | solution.py:457
  8.9 0.2 %collective-permute-start.1 = (f32[4,128,128]{2,1,0:T(8,128)S(1)}, f32[4,128,128]{2,1,0:T(8,128)S(1)}, u32[]{:S(2)}, u32[]{:S(2)}) collective-permute-start(f32[4,128,128]{2,1,0:T(8,128)S(1)} %get-tuple-element.29.refs_0_), channel_id=1, source_target_pairs={{0,1},{1,0},{2,3},{3,2},{4,5},{5,4},{6,7},{7,6},{8,9},{9,8},{10,11... | collective-permute-start | bytes 786440 | tf_op jit(solution)/shard_map/ppermute | solution.py:468
  9.1 3.4 %collective-permute-start.7 = (bf16[1040,128]{1,0:T(8,128)(2,1)S(1)}, bf16[1040,128]{1,0:T(8,128)(2,1)S(1)}, u32[]{:S(2)}, u32[]{:S(2)}) collective-permute-start(bf16[1040,128]{1,0:T(8,128)(2,1)S(1)} %get-tuple-element.36), channel_id=1, source_target_pairs={{1,2},{2,1},{3,4},{4,3},{5,6},{6,5},{7,8},{8,7},{9,10},{10,9},{11,... | collective-permute-start | bytes 798728 | tf_op jit(solution)/shard_map/ppermute | solution.py:467
  12.5 0.1 collective-permute-start.2
  12.6 0.5 %collective-permute-start.3 = (f32[4,128,128]{2,1,0:T(8,128)S(1)}, f32[4,128,128]{2,1,0:T(8,128)S(1)}, u32[]{:S(2)}, u32[]{:S(2)}) collective-permute-start(f32[4,128,128]{2,1,0:T(8,128)S(1)} %get-tuple-element.31.refs_2_), channel_id=1, source_target_pairs={{0,1},{1,0},{2,3},{3,2},{4,5},{5,4},{6,7},{7,6},{8,9},{9,8},{10,11... | collective-permute-start | bytes 786440 | tf_op jit(solution)/shard_map/ppermute | solution.py:468
  13.1 0.9 %collective-permute-done.5.got_ref.refs_10_ = bf16[1200,128]{1,0:T(8,128)(2,1)S(1)} collective-permute-done((bf16[1200,128]{1,0:T(8,128)(2,1)S(1)}, bf16[1200,128]{1,0:T(8,128)(2,1)S(1)}, u32[]{:S(2)}, u32[]{:S(2)}) %collective-permute-start.5) | collective-permute-done | bytes 307232 | tf_op jit(solution)/shard_map/ppermute | solution.py:455
  13.9 0.0 collective-permute-start.4
  13.9 0.3 %outermost_rows.1.refs_8_ = bf16[16,2048]{1,0:T(8,128)(2,1)S(1)} custom-call(f32[8,256]{1,0:T(8,128)S(1)} %get-tuple-element.21.weight_ref, bf16[1200,128]{1,0:T(8,128)(2,1)S(1)} %get-tuple-element.33.own_ref, bf16[1200,128]{1,0:T(8,128)(2,1)S(1)} %collective-permute-done.5.got_ref.refs_10_), custom_call_target="tpu_custom_call" | custom-call | tf_op jit(solution)/shard_map/outermost_rows/pallas_call | solution.py:469
  14.2 0.0 collective-permute-done.1.refs_4_
  14.2 0.6 %collective-permute-start.6 = (bf16[16,2048]{1,0:T(8,128)(2,1)S(1)}, bf16[16,2048]{1,0:T(8,128)(2,1)S(1)}, u32[]{:S(2)}, u32[]{:S(2)}) collective-permute-start(bf16[16,2048]{1,0:T(8,128)(2,1)S(1)} %outermost_rows.1.refs_8_), channel_id=1, source_target_pairs={{0,1},{1,0},{2,3},{3,2},{4,5},{5,4},{6,7},{7,6},{8,9},{9,8},{10,11... | collective-permute-start | bytes 196616 | tf_op jit(solution)/shard_map/ppermute | solution.py:477
  14.8 0.0 collective-permute-done.2.refs_5_
  14.8 0.0 collective-permute-done.3.refs_6_
  14.8 0.7 %collective-permute-done.4.refs_7_ = f32[4,128,128]{2,1,0:T(8,128)S(1)} collective-permute-done((f32[4,128,128]{2,1,0:T(8,128)S(1)}, f32[4,128,128]{2,1,0:T(8,128)S(1)}, u32[]{:S(2)}, u32[]{:S(2)}) %collective-permute-start.4) | collective-permute-done | bytes 262176 | tf_op jit(solution)/shard_map/ppermute | solution.py:468
  15.4 0.2 %collective-permute-done.6.refs_9_ = bf16[16,2048]{1,0:T(8,128)(2,1)S(1)} collective-permute-done((bf16[16,2048]{1,0:T(8,128)(2,1)S(1)}, bf16[16,2048]{1,0:T(8,128)(2,1)S(1)}, u32[]{:S(2)}, u32[]{:S(2)}) %collective-permute-start.6) | collective-permute-done | bytes 65568 | tf_op jit(solution)/shard_map/ppermute | solution.py:477
  15.7 1.8 %near_part.1 = (f32[2,64,2048]{2,1,0:T(8,128)S(1)}, bf16[32,96]{1,0:T(8,128)(2,1)S(1)}) custom-call(f32[4,128,128]{2,1,0:T(8,128)S(1)} %get-tuple-element.29.refs_0_, f32[4,128,128]{2,1,0:T(8,128)S(1)} %get-tuple-element.30.refs_1_, f32[4,128,128]{2,1,0:T(8,128)S(1)} %get-tuple-element.31.refs_2_, f32[4,128,128]{2,1,0:T(8,128)S(1)} %get-tuple-element.32.refs_3_, ...), custom_call_target="tpu_custom_call" | custom-call | tf_op jit(solution)/shard_map/near_part/pallas_call | solution.py:478
  17.5 2.2 %collective-permute-done.7.msg_ref = bf16[1040,128]{1,0:T(8,128)(2,1)S(1)} collective-permute-done((bf16[1040,128]{1,0:T(8,128)(2,1)S(1)}, bf16[1040,128]{1,0:T(8,128)(2,1)S(1)}, u32[]{:S(2)}, u32[]{:S(2)}) %collective-permute-start.7) | collective-permute-done | bytes 266272 | tf_op jit(solution)/shard_map/ppermute | solution.py:467
  19.7 1.1 %last_part.1 = f32[2,64,2048]{2,1,0:T(8,128)} custom-call(bf16[32,96]{1,0:T(8,128)(2,1)S(1)} %get-tuple-element.34.taps_ref, f32[2,64,2048]{2,1,0:T(8,128)S(1)} %get-tuple-element.35.part_ref, bf16[1040,128]{1,0:T(8,128)(2,1)S(1)} %collective-permute-done.7.msg_ref), custom_call_target="tpu_custom_call" | custom-call | tf_op jit(solution)/shard_map/last_part/pallas_call | solution.py:487
Async XLA Ops:
  0.0 7.4 %copy-start = (bf16[2,512,256]{2,1,0:T(8,128)(2,1)S(1)}, bf16[2,512,256]{2,1,0:T(8,128)(2,1)}, u32[]{:S(2)}) copy-start(bf16[2,512,256]{2,1,0:T(8,128)(2,1)} %constant.2.clone.band_ref.refs_11_) | copy-start | bytes 1572868
  2.4 11.5 %collective-permute-start.5 = (bf16[1200,128]{1,0:T(8,128)(2,1)S(1)}, bf16[1200,128]{1,0:T(8,128)(2,1)S(1)}, u32[]{:S(2)}, u32[]{:S(2)}) collective-permute-start(bf16[1200,128]{1,0:T(8,128)(2,1)S(1)} %get-tuple-element.33.own_ref), channel_id=1, source_target_pairs={{1,2},{2,1},{3,4},{4,3},{5,6},{6,5},{7,8},{8,7},{9,10},{10,9},{11,... | collective-permute-start | bytes 921608 | tf_op jit(solution)/shard_map/ppermute | solution.py:455
  6.1 1.3 %collective-permute-start = (bf16[16,2048]{1,0:T(8,128)(2,1)S(1)}, bf16[16,2048]{1,0:T(8,128)(2,1)S(1)}, u32[]{:S(2)}, u32[]{:S(2)}) collective-permute-start(bf16[16,2048]{1,0:T(8,128)(2,1)S(1)} %get-tuple-element.24), channel_id=1, source_target_pairs={{0,1},{1,0},{2,3},{3,2},{4,5},{5,4},{6,7},{7,6},{8,9},{9,8},{10,11... | collective-permute-start | bytes 196616 | tf_op jit(solution)/shard_map/ppermute | solution.py:456
  8.9 5.3 %collective-permute-start.1 = (f32[4,128,128]{2,1,0:T(8,128)S(1)}, f32[4,128,128]{2,1,0:T(8,128)S(1)}, u32[]{:S(2)}, u32[]{:S(2)}) collective-permute-start(f32[4,128,128]{2,1,0:T(8,128)S(1)} %get-tuple-element.29.refs_0_), channel_id=1, source_target_pairs={{0,1},{1,0},{2,3},{3,2},{4,5},{5,4},{6,7},{7,6},{8,9},{9,8},{10,11... | collective-permute-start | bytes 786440 | tf_op jit(solution)/shard_map/ppermute | solution.py:468
  9.1 10.6 %collective-permute-start.7 = (bf16[1040,128]{1,0:T(8,128)(2,1)S(1)}, bf16[1040,128]{1,0:T(8,128)(2,1)S(1)}, u32[]{:S(2)}, u32[]{:S(2)}) collective-permute-start(bf16[1040,128]{1,0:T(8,128)(2,1)S(1)} %get-tuple-element.36), channel_id=1, source_target_pairs={{1,2},{2,1},{3,4},{4,3},{5,6},{6,5},{7,8},{8,7},{9,10},{10,9},{11,... | collective-permute-start | bytes 798728 | tf_op jit(solution)/shard_map/ppermute | solution.py:467
  12.5 2.3 %collective-permute-start.2 = (f32[4,128,128]{2,1,0:T(8,128)S(1)}, f32[4,128,128]{2,1,0:T(8,128)S(1)}, u32[]{:S(2)}, u32[]{:S(2)}) collective-permute-start(f32[4,128,128]{2,1,0:T(8,128)S(1)} %get-tuple-element.30.refs_1_), channel_id=1, source_target_pairs={{0,1},{1,0},{2,3},{3,2},{4,5},{5,4},{6,7},{7,6},{8,9},{9,8},{10,11... | collective-permute-start | bytes 786440 | tf_op jit(solution)/shard_map/ppermute | solution.py:468
  12.6 2.2 %collective-permute-start.3 = (f32[4,128,128]{2,1,0:T(8,128)S(1)}, f32[4,128,128]{2,1,0:T(8,128)S(1)}, u32[]{:S(2)}, u32[]{:S(2)}) collective-permute-start(f32[4,128,128]{2,1,0:T(8,128)S(1)} %get-tuple-element.31.refs_2_), channel_id=1, source_target_pairs={{0,1},{1,0},{2,3},{3,2},{4,5},{5,4},{6,7},{7,6},{8,9},{9,8},{10,11... | collective-permute-start | bytes 786440 | tf_op jit(solution)/shard_map/ppermute | solution.py:468
  13.9 1.5 %collective-permute-start.4 = (f32[4,128,128]{2,1,0:T(8,128)S(1)}, f32[4,128,128]{2,1,0:T(8,128)S(1)}, u32[]{:S(2)}, u32[]{:S(2)}) collective-permute-start(f32[4,128,128]{2,1,0:T(8,128)S(1)} %get-tuple-element.32.refs_3_), channel_id=1, source_target_pairs={{0,1},{1,0},{2,3},{3,2},{4,5},{5,4},{6,7},{7,6},{8,9},{9,8},{10,11... | collective-permute-start | bytes 786440 | tf_op jit(solution)/shard_map/ppermute | solution.py:468
  14.2 1.5 %collective-permute-start.6 = (bf16[16,2048]{1,0:T(8,128)(2,1)S(1)}, bf16[16,2048]{1,0:T(8,128)(2,1)S(1)}, u32[]{:S(2)}, u32[]{:S(2)}) collective-permute-start(bf16[16,2048]{1,0:T(8,128)(2,1)S(1)} %outermost_rows.1.refs_8_), channel_id=1, source_target_pairs={{0,1},{1,0},{2,3},{3,2},{4,5},{5,4},{6,7},{7,6},{8,9},{9,8},{10,11... | collective-permute-start | bytes 196616 | tf_op jit(solution)/shard_map/ppermute | solution.py:477

commit v14 on v13

--- a/solution.py
+++ b/solution.py
@@ -399,7 +399,7 @@
     tops = msg_ref[pl.ds(nblocks * rows, nblocks), :].astype(F32)
     reached = pl.ds(pl.multiple_of(parity() * half, 8), half)
     rest = pl.ds(pl.multiple_of((1 - parity()) * half, 8), half)
-    copies = [pltpu.make_async_copy(part_ref.at[k, rest, :], out_hbm.at[k, rest, :], sem.at[2 + k]) for k in range(2)]
+    copies = [pltpu.make_async_copy(part_ref.at[k, rest, :], out_hbm.at[k, rest, :], sem.at[k]) for k in range(2)]
     for copy in copies:
         copy.start()
     for comp in range(2):
@@ -410,8 +410,11 @@
             high, low = split(decode(jnp.concatenate(got, axis=1), top))
             part = dot(taps_ref[...], jnp.concatenate([high, high, low], axis=0))
             buf[comp, :, here] = part_ref[comp, reached, here] + part
-        copies.append(pltpu.make_async_copy(buf.at[comp], out_hbm.at[comp, reached, :], sem.at[comp]))
-        copies[-1].start()
+            if first + 2 in (nblocks // 2, nblocks):
+                cols = pl.ds((first + 2 - nblocks // 2) * LANES, width // 2)
+                at = 2 * comp + (first + 2) // nblocks
+                copies.append(pltpu.make_async_copy(buf.at[comp, :, cols], out_hbm.at[comp, reached, cols], sem.at[2 + at]))
+                copies[-1].start()
     for copy in copies:
         copy.wait()
 
@@ -489,7 +492,7 @@
         out_shape=result,
         in_specs=[VMEM] * 3,
         out_specs=HBM,
-        scratch_shapes=[pltpu.VMEM((2, half, width), F32), pltpu.SemaphoreType.DMA((4,))],
+        scratch_shapes=[pltpu.VMEM((2, half, width), F32), pltpu.SemaphoreType.DMA((6,))],
         compiler_params=PARAMS,
         name="last_part",
     )(last, part, inner_got)

time: 21 us -> 20.9 us (level)
  no operation moved by 1% of the time
where the time goes in v14:
time: 20.9 us; the launch traced here: 20.8 us
  starting transfers between devices  8.52 us (41%)
  Pallas kernels  7 us (33%)
  waiting for transfers between devices  5.18 us (25%)
    ppermute x1, starting transfers between devices, body(): outer_got = lax.ppermute(outer, 'row', away)  3.71 us
    ppermute x1, starting transfers between devices, body(): inner_got = lax.ppermute(inner, 'row', away)  3.37 us
    pallas_call x1, Pallas kernels, body(): pl.pallas_call(outer_kernel, out_shape=[piece] * PIECES + [jax.ShapeDtype...  2.37 us
    ppermute x1, waiting for transfers between devices, body(): inner_got = lax.ppermute(inner, 'row', away)  2.19 us
    pallas_call x1, Pallas kernels, body(): pl.pallas_call(near_kernel, out_shape=[result, jax.ShapeDtypeStruct((half...  1.8 us
    pallas_call x1, Pallas kernels, body(): pl.pallas_call(inner_kernel, out_shape=[piece] * PIECES + [jax.ShapeDtype...  1.45 us
    ppermute x1, waiting for transfers between devices, body(): row = lax.ppermute(row, 'row', chip)  1.24 us
    pallas_call x1, Pallas kernels, body(): pl.pallas_call(last_kernel, out_shape=result, in_specs=[VMEM] * 3, out_sp...  1.1 us
  transfers between devices with their start and end apart: 8, of which 5 were waited for; matrix products, arithmetic and copies ran while one was open for 0% of the time, Pallas kernels for 17%

profile of v14, /device:TPU:11, one launch (start us, length us, event | category | flops | bytes accessed | tf_op | source)
XLA Modules:
  0.0 20.8 jit_solution(10781734850134307544)
XLA Ops:
  0.0 0.0 copy-start
  0.0 2.4 %outer_half.1 = (f32[4,128,128]{2,1,0:T(8,128)S(1)}, f32[4,128,128]{2,1,0:T(8,128)S(1)}, f32[4,128,128]{2,1,0:T(8,128)S(1)}, f32[4,128,128]{2,1,0:T(8,128)S(1)},...) custom-call(f32[4]{0:T(128)} %lw_hbm.1, ...), custom_call_target="tpu_custom_call" | custom-call | tf_op jit(solution)/shard_map/outer_half/pallas_call | solution.py:435
  2.4 3.7 %collective-permute-start.5 = (bf16[1200,128]{1,0:T(8,128)(2,1)S(1)}, bf16[1200,128]{1,0:T(8,128)(2,1)S(1)}, u32[]{:S(2)}, u32[]{:S(2)}) collective-permute-start(bf16[1200,128]{1,0:T(8,128)(2,1)S(1)} %get-tuple-element.33.own_ref), channel_id=1, source_target_pairs={{1,2},{2,1},{3,4},{4,3},{5,6},{6,5},{7,8},{8,7},{9,10},{10,9},{11,... | collective-permute-start | bytes 921608 | tf_op jit(solution)/shard_map/ppermute | solution.py:458
  6.1 0.1 collective-permute-start
  6.2 1.2 %collective-permute-done.row_ref = bf16[16,2048]{1,0:T(8,128)(2,1)S(1)} collective-permute-done((bf16[16,2048]{1,0:T(8,128)(2,1)S(1)}, bf16[16,2048]{1,0:T(8,128)(2,1)S(1)}, u32[]{:S(2)}, u32[]{:S(2)}) %collective-permute-start) | collective-permute-done | bytes 65568 | tf_op jit(solution)/shard_map/ppermute | solution.py:459
  7.4 0.0 copy-done
  7.4 1.5 %inner_half.1 = (f32[4,128,128]{2,1,0:T(8,128)S(1)}, f32[4,128,128]{2,1,0:T(8,128)S(1)}, f32[4,128,128]{2,1,0:T(8,128)S(1)}, f32[4,128,128]{2,1,0:T(8,128)S(1)}, bf16[1040,128]{1,0:T(8,128)(2,1)S(1)}) custom-call(f32[8,256]{1,0:T(8,128)S(1)} %get-tuple-element.21.weight_ref, ...), custom_call_target="tpu_custom_call", output_to_operand_aliasing={{0}: (5, {}), {1}: (6, {}), {2}: (7, {}), {3}: (8, {})} | custom-call | tf_op jit(solution)/shard_map/inner_half/pallas_call | solution.py:460
  8.9 0.2 %collective-permute-start.1 = (f32[4,128,128]{2,1,0:T(8,128)S(1)}, f32[4,128,128]{2,1,0:T(8,128)S(1)}, u32[]{:S(2)}, u32[]{:S(2)}) collective-permute-start(f32[4,128,128]{2,1,0:T(8,128)S(1)} %get-tuple-element.29.refs_0_), channel_id=1, source_target_pairs={{0,1},{1,0},{2,3},{3,2},{4,5},{5,4},{6,7},{7,6},{8,9},{9,8},{10,11... | collective-permute-start | bytes 786440 | tf_op jit(solution)/shard_map/ppermute | solution.py:471
  9.1 3.4 %collective-permute-start.7 = (bf16[1040,128]{1,0:T(8,128)(2,1)S(1)}, bf16[1040,128]{1,0:T(8,128)(2,1)S(1)}, u32[]{:S(2)}, u32[]{:S(2)}) collective-permute-start(bf16[1040,128]{1,0:T(8,128)(2,1)S(1)} %get-tuple-element.36), channel_id=1, source_target_pairs={{1,2},{2,1},{3,4},{4,3},{5,6},{6,5},{7,8},{8,7},{9,10},{10,9},{11,... | collective-permute-start | bytes 798728 | tf_op jit(solution)/shard_map/ppermute | solution.py:470
  12.5 0.1 collective-permute-start.2
  12.6 0.5 %collective-permute-start.3 = (f32[4,128,128]{2,1,0:T(8,128)S(1)}, f32[4,128,128]{2,1,0:T(8,128)S(1)}, u32[]{:S(2)}, u32[]{:S(2)}) collective-permute-start(f32[4,128,128]{2,1,0:T(8,128)S(1)} %get-tuple-element.31.refs_2_), channel_id=1, source_target_pairs={{0,1},{1,0},{2,3},{3,2},{4,5},{5,4},{6,7},{7,6},{8,9},{9,8},{10,11... | collective-permute-start | bytes 786440 | tf_op jit(solution)/shard_map/ppermute | solution.py:471
  13.1 0.9 %collective-permute-done.5.got_ref.refs_10_ = bf16[1200,128]{1,0:T(8,128)(2,1)S(1)} collective-permute-done((bf16[1200,128]{1,0:T(8,128)(2,1)S(1)}, bf16[1200,128]{1,0:T(8,128)(2,1)S(1)}, u32[]{:S(2)}, u32[]{:S(2)}) %collective-permute-start.5) | collective-permute-done | bytes 307232 | tf_op jit(solution)/shard_map/ppermute | solution.py:458
  13.9 0.0 collective-permute-start.4
  13.9 0.3 %outermost_rows.1.refs_8_ = bf16[16,2048]{1,0:T(8,128)(2,1)S(1)} custom-call(f32[8,256]{1,0:T(8,128)S(1)} %get-tuple-element.21.weight_ref, bf16[1200,128]{1,0:T(8,128)(2,1)S(1)} %get-tuple-element.33.own_ref, bf16[1200,128]{1,0:T(8,128)(2,1)S(1)} %collective-permute-done.5.got_ref.refs_10_), custom_call_target="tpu_custom_call" | custom-call | tf_op jit(solution)/shard_map/outermost_rows/pallas_call | solution.py:472
  14.2 0.0 collective-permute-done.1.refs_4_
  14.2 0.6 %collective-permute-start.6 = (bf16[16,2048]{1,0:T(8,128)(2,1)S(1)}, bf16[16,2048]{1,0:T(8,128)(2,1)S(1)}, u32[]{:S(2)}, u32[]{:S(2)}) collective-permute-start(bf16[16,2048]{1,0:T(8,128)(2,1)S(1)} %outermost_rows.1.refs_8_), channel_id=1, source_target_pairs={{0,1},{1,0},{2,3},{3,2},{4,5},{5,4},{6,7},{7,6},{8,9},{9,8},{10,11... | collective-permute-start | bytes 196616 | tf_op jit(solution)/shard_map/ppermute | solution.py:480
  14.8 0.0 collective-permute-done.2.refs_5_
  14.8 0.0 collective-permute-done.3.refs_6_
  14.8 0.7 %collective-permute-done.4.refs_7_ = f32[4,128,128]{2,1,0:T(8,128)S(1)} collective-permute-done((f32[4,128,128]{2,1,0:T(8,128)S(1)}, f32[4,128,128]{2,1,0:T(8,128)S(1)}, u32[]{:S(2)}, u32[]{:S(2)}) %collective-permute-start.4) | collective-permute-done | bytes 262176 | tf_op jit(solution)/shard_map/ppermute | solution.py:471
  15.4 0.2 %collective-permute-done.6.refs_9_ = bf16[16,2048]{1,0:T(8,128)(2,1)S(1)} collective-permute-done((bf16[16,2048]{1,0:T(8,128)(2,1)S(1)}, bf16[16,2048]{1,0:T(8,128)(2,1)S(1)}, u32[]{:S(2)}, u32[]{:S(2)}) %collective-permute-start.6) | collective-permute-done | bytes 65568 | tf_op jit(solution)/shard_map/ppermute | solution.py:480
  15.7 1.8 %near_part.1 = (f32[2,64,2048]{2,1,0:T(8,128)S(1)}, bf16[32,96]{1,0:T(8,128)(2,1)S(1)}) custom-call(f32[4,128,128]{2,1,0:T(8,128)S(1)} %get-tuple-element.29.refs_0_, f32[4,128,128]{2,1,0:T(8,128)S(1)} %get-tuple-element.30.refs_1_, f32[4,128,128]{2,1,0:T(8,128)S(1)} %get-tuple-element.31.refs_2_, f32[4,128,128]{2,1,0:T(8,128)S(1)} %get-tuple-element.32.refs_3_, ...), custom_call_target="tpu_custom_call" | custom-call | tf_op jit(solution)/shard_map/near_part/pallas_call | solution.py:481
  17.5 2.2 %collective-permute-done.7.msg_ref = bf16[1040,128]{1,0:T(8,128)(2,1)S(1)} collective-permute-done((bf16[1040,128]{1,0:T(8,128)(2,1)S(1)}, bf16[1040,128]{1,0:T(8,128)(2,1)S(1)}, u32[]{:S(2)}, u32[]{:S(2)}) %collective-permute-start.7) | collective-permute-done | bytes 266272 | tf_op jit(solution)/shard_map/ppermute | solution.py:470
  19.7 1.1 %last_part.1 = f32[2,64,2048]{2,1,0:T(8,128)} custom-call(bf16[32,96]{1,0:T(8,128)(2,1)S(1)} %get-tuple-element.34.taps_ref, f32[2,64,2048]{2,1,0:T(8,128)S(1)} %get-tuple-element.35.part_ref, bf16[1040,128]{1,0:T(8,128)(2,1)S(1)} %collective-permute-done.7.msg_ref), custom_call_target="tpu_custom_call" | custom-call | tf_op jit(solution)/shard_map/last_part/pallas_call | solution.py:490
Async XLA Ops:
  0.0 7.4 %copy-start = (bf16[2,512,256]{2,1,0:T(8,128)(2,1)S(1)}, bf16[2,512,256]{2,1,0:T(8,128)(2,1)}, u32[]{:S(2)}) copy-start(bf16[2,512,256]{2,1,0:T(8,128)(2,1)} %constant.2.clone.band_ref.refs_11_) | copy-start | bytes 1572868
  2.4 11.5 %collective-permute-start.5 = (bf16[1200,128]{1,0:T(8,128)(2,1)S(1)}, bf16[1200,128]{1,0:T(8,128)(2,1)S(1)}, u32[]{:S(2)}, u32[]{:S(2)}) collective-permute-start(bf16[1200,128]{1,0:T(8,128)(2,1)S(1)} %get-tuple-element.33.own_ref), channel_id=1, source_target_pairs={{1,2},{2,1},{3,4},{4,3},{5,6},{6,5},{7,8},{8,7},{9,10},{10,9},{11,... | collective-permute-start | bytes 921608 | tf_op jit(solution)/shard_map/ppermute | solution.py:458
  6.1 1.3 %collective-permute-start = (bf16[16,2048]{1,0:T(8,128)(2,1)S(1)}, bf16[16,2048]{1,0:T(8,128)(2,1)S(1)}, u32[]{:S(2)}, u32[]{:S(2)}) collective-permute-start(bf16[16,2048]{1,0:T(8,128)(2,1)S(1)} %get-tuple-element.24), channel_id=1, source_target_pairs={{0,1},{1,0},{2,3},{3,2},{4,5},{5,4},{6,7},{7,6},{8,9},{9,8},{10,11... | collective-permute-start | bytes 196616 | tf_op jit(solution)/shard_map/ppermute | solution.py:459
  8.9 5.3 %collective-permute-start.1 = (f32[4,128,128]{2,1,0:T(8,128)S(1)}, f32[4,128,128]{2,1,0:T(8,128)S(1)}, u32[]{:S(2)}, u32[]{:S(2)}) collective-permute-start(f32[4,128,128]{2,1,0:T(8,128)S(1)} %get-tuple-element.29.refs_0_), channel_id=1, source_target_pairs={{0,1},{1,0},{2,3},{3,2},{4,5},{5,4},{6,7},{7,6},{8,9},{9,8},{10,11... | collective-permute-start | bytes 786440 | tf_op jit(solution)/shard_map/ppermute | solution.py:471
  9.1 10.6 %collective-permute-start.7 = (bf16[1040,128]{1,0:T(8,128)(2,1)S(1)}, bf16[1040,128]{1,0:T(8,128)(2,1)S(1)}, u32[]{:S(2)}, u32[]{:S(2)}) collective-permute-start(bf16[1040,128]{1,0:T(8,128)(2,1)S(1)} %get-tuple-element.36), channel_id=1, source_target_pairs={{1,2},{2,1},{3,4},{4,3},{5,6},{6,5},{7,8},{8,7},{9,10},{10,9},{11,... | collective-permute-start | bytes 798728 | tf_op jit(solution)/shard_map/ppermute | solution.py:470
  12.5 2.3 %collective-permute-start.2 = (f32[4,128,128]{2,1,0:T(8,128)S(1)}, f32[4,128,128]{2,1,0:T(8,128)S(1)}, u32[]{:S(2)}, u32[]{:S(2)}) collective-permute-start(f32[4,128,128]{2,1,0:T(8,128)S(1)} %get-tuple-element.30.refs_1_), channel_id=1, source_target_pairs={{0,1},{1,0},{2,3},{3,2},{4,5},{5,4},{6,7},{7,6},{8,9},{9,8},{10,11... | collective-permute-start | bytes 786440 | tf_op jit(solution)/shard_map/ppermute | solution.py:471
  12.6 2.2 %collective-permute-start.3 = (f32[4,128,128]{2,1,0:T(8,128)S(1)}, f32[4,128,128]{2,1,0:T(8,128)S(1)}, u32[]{:S(2)}, u32[]{:S(2)}) collective-permute-start(f32[4,128,128]{2,1,0:T(8,128)S(1)} %get-tuple-element.31.refs_2_), channel_id=1, source_target_pairs={{0,1},{1,0},{2,3},{3,2},{4,5},{5,4},{6,7},{7,6},{8,9},{9,8},{10,11... | collective-permute-start | bytes 786440 | tf_op jit(solution)/shard_map/ppermute | solution.py:471
  13.9 1.5 %collective-permute-start.4 = (f32[4,128,128]{2,1,0:T(8,128)S(1)}, f32[4,128,128]{2,1,0:T(8,128)S(1)}, u32[]{:S(2)}, u32[]{:S(2)}) collective-permute-start(f32[4,128,128]{2,1,0:T(8,128)S(1)} %get-tuple-element.32.refs_3_), channel_id=1, source_target_pairs={{0,1},{1,0},{2,3},{3,2},{4,5},{5,4},{6,7},{7,6},{8,9},{9,8},{10,11... | collective-permute-start | bytes 786440 | tf_op jit(solution)/shard_map/ppermute | solution.py:471
  14.2 1.5 %collective-permute-start.6 = (bf16[16,2048]{1,0:T(8,128)(2,1)S(1)}, bf16[16,2048]{1,0:T(8,128)(2,1)S(1)}, u32[]{:S(2)}, u32[]{:S(2)}) collective-permute-start(bf16[16,2048]{1,0:T(8,128)(2,1)S(1)} %outermost_rows.1.refs_8_), channel_id=1, source_target_pairs={{0,1},{1,0},{2,3},{3,2},{4,5},{5,4},{6,7},{7,6},{8,9},{9,8},{10,11... | collective-permute-start | bytes 196616 | tf_op jit(solution)/shard_map/ppermute | solution.py:480

commit v15 on v13

--- a/solution.py
+++ b/solution.py
@@ -197,8 +197,12 @@
     base = nblocks * rows
 
     def input_rows():
-        near_rows = back_ref[:, tile_at(jnp.where(upper, rows - TILE, 0)), :]
-        row_ref[...] = dot(pick_near, near_rows.reshape(levels * TILE, -1)).astype(BF16)
+        near_rows = []
+        for level in range(levels):
+            ends = [back_ref[level, k : k + 1, :].astype(F32) for k in (rows - 1, 0)]
+            near_rows.append(jnp.where(upper, *ends))
+        near_rows.append(jnp.zeros((TILE - levels, width), F32))
+        row_ref[...] = jnp.concatenate(near_rows, axis=0).astype(BF16)
         edge_at = tile_at(jnp.where(upper, 0, rows - TILE))
         for first in range(0, nblocks, PACK):
             back, inno = [], []

time: 21 us -> 21 us (level)
  no operation moved by 1% of the time
where the time goes in v15:
time: 21 us; the launch traced here: 20.8 us
  starting transfers between devices  8.52 us (41%)
  Pallas kernels  7.05 us (34%)
  waiting for transfers between devices  5.18 us (25%)
    ppermute x1, starting transfers between devices, body(): outer_got = lax.ppermute(outer, 'row', away)  3.71 us
    ppermute x1, starting transfers between devices, body(): inner_got = lax.ppermute(inner, 'row', away)  3.37 us
    pallas_call x1, Pallas kernels, body(): pl.pallas_call(outer_kernel, out_shape=[piece] * PIECES + [jax.ShapeDtype...  2.37 us
    ppermute x1, waiting for transfers between devices, body(): inner_got = lax.ppermute(inner, 'row', away)  2.19 us
    pallas_call x1, Pallas kernels, body(): pl.pallas_call(near_kernel, out_shape=[result, jax.ShapeDtypeStruct((half...  1.79 us
    pallas_call x1, Pallas kernels, body(): pl.pallas_call(inner_kernel, out_shape=[piece] * PIECES + [jax.ShapeDtype...  1.46 us
    ppermute x1, waiting for transfers between devices, body(): row = lax.ppermute(row, 'row', chip)  1.24 us
    pallas_call x1, Pallas kernels, body(): pl.pallas_call(last_kernel, out_shape=result, in_specs=[VMEM] * 3, out_sp...  1.14 us
  transfers between devices with their start and end apart: 8, of which 5 were waited for; matrix products, arithmetic and copies ran while one was open for 0% of the time, Pallas kernels for 17%

profile of v15, /device:TPU:11, one launch (start us, length us, event | category | flops | bytes accessed | tf_op | source)
XLA Modules:
  0.0 20.8 jit_solution(10298915033333059679)
XLA Ops:
  0.0 0.0 copy-start
  0.0 2.4 %outer_half.1 = (f32[4,128,128]{2,1,0:T(8,128)S(1)}, f32[4,128,128]{2,1,0:T(8,128)S(1)}, f32[4,128,128]{2,1,0:T(8,128)S(1)}, f32[4,128,128]{2,1,0:T(8,128)S(1)},...) custom-call(f32[4]{0:T(128)} %lw_hbm.1, ...), custom_call_target="tpu_custom_call" | custom-call | tf_op jit(solution)/shard_map/outer_half/pallas_call | solution.py:436
  2.4 3.7 %collective-permute-start.5 = (bf16[1200,128]{1,0:T(8,128)(2,1)S(1)}, bf16[1200,128]{1,0:T(8,128)(2,1)S(1)}, u32[]{:S(2)}, u32[]{:S(2)}) collective-permute-start(bf16[1200,128]{1,0:T(8,128)(2,1)S(1)} %get-tuple-element.33.own_ref), channel_id=1, source_target_pairs={{1,2},{2,1},{3,4},{4,3},{5,6},{6,5},{7,8},{8,7},{9,10},{10,9},{11,... | collective-permute-start | bytes 921608 | tf_op jit(solution)/shard_map/ppermute | solution.py:459
  6.1 0.1 collective-permute-start
  6.2 1.2 %collective-permute-done.row_ref = bf16[16,2048]{1,0:T(8,128)(2,1)S(1)} collective-permute-done((bf16[16,2048]{1,0:T(8,128)(2,1)S(1)}, bf16[16,2048]{1,0:T(8,128)(2,1)S(1)}, u32[]{:S(2)}, u32[]{:S(2)}) %collective-permute-start) | collective-permute-done | bytes 65568 | tf_op jit(solution)/shard_map/ppermute | solution.py:460
  7.4 0.0 copy-done
  7.4 1.5 %inner_half.1 = (f32[4,128,128]{2,1,0:T(8,128)S(1)}, f32[4,128,128]{2,1,0:T(8,128)S(1)}, f32[4,128,128]{2,1,0:T(8,128)S(1)}, f32[4,128,128]{2,1,0:T(8,128)S(1)}, bf16[1040,128]{1,0:T(8,128)(2,1)S(1)}) custom-call(f32[8,256]{1,0:T(8,128)S(1)} %get-tuple-element.21.weight_ref, ...), custom_call_target="tpu_custom_call", output_to_operand_aliasing={{0}: (5, {}), {1}: (6, {}), {2}: (7, {}), {3}: (8, {})} | custom-call | tf_op jit(solution)/shard_map/inner_half/pallas_call | solution.py:461
  8.9 0.2 %collective-permute-start.1 = (f32[4,128,128]{2,1,0:T(8,128)S(1)}, f32[4,128,128]{2,1,0:T(8,128)S(1)}, u32[]{:S(2)}, u32[]{:S(2)}) collective-permute-start(f32[4,128,128]{2,1,0:T(8,128)S(1)} %get-tuple-element.29.refs_0_), channel_id=1, source_target_pairs={{0,1},{1,0},{2,3},{3,2},{4,5},{5,4},{6,7},{7,6},{8,9},{9,8},{10,11... | collective-permute-start | bytes 786440 | tf_op jit(solution)/shard_map/ppermute | solution.py:472
  9.1 3.4 %collective-permute-start.7 = (bf16[1040,128]{1,0:T(8,128)(2,1)S(1)}, bf16[1040,128]{1,0:T(8,128)(2,1)S(1)}, u32[]{:S(2)}, u32[]{:S(2)}) collective-permute-start(bf16[1040,128]{1,0:T(8,128)(2,1)S(1)} %get-tuple-element.36), channel_id=1, source_target_pairs={{1,2},{2,1},{3,4},{4,3},{5,6},{6,5},{7,8},{8,7},{9,10},{10,9},{11,... | collective-permute-start | bytes 798728 | tf_op jit(solution)/shard_map/ppermute | solution.py:471
  12.5 0.1 collective-permute-start.2
  12.6 0.5 %collective-permute-start.3 = (f32[4,128,128]{2,1,0:T(8,128)S(1)}, f32[4,128,128]{2,1,0:T(8,128)S(1)}, u32[]{:S(2)}, u32[]{:S(2)}) collective-permute-start(f32[4,128,128]{2,1,0:T(8,128)S(1)} %get-tuple-element.31.refs_2_), channel_id=1, source_target_pairs={{0,1},{1,0},{2,3},{3,2},{4,5},{5,4},{6,7},{7,6},{8,9},{9,8},{10,11... | collective-permute-start | bytes 786440 | tf_op jit(solution)/shard_map/ppermute | solution.py:472
  13.1 0.9 %collective-permute-done.5.got_ref.refs_10_ = bf16[1200,128]{1,0:T(8,128)(2,1)S(1)} collective-permute-done((bf16[1200,128]{1,0:T(8,128)(2,1)S(1)}, bf16[1200,128]{1,0:T(8,128)(2,1)S(1)}, u32[]{:S(2)}, u32[]{:S(2)}) %collective-permute-start.5) | collective-permute-done | bytes 307232 | tf_op jit(solution)/shard_map/ppermute | solution.py:459
  13.9 0.0 collective-permute-start.4
  13.9 0.3 %outermost_rows.1.refs_8_ = bf16[16,2048]{1,0:T(8,128)(2,1)S(1)} custom-call(f32[8,256]{1,0:T(8,128)S(1)} %get-tuple-element.21.weight_ref, bf16[1200,128]{1,0:T(8,128)(2,1)S(1)} %get-tuple-element.33.own_ref, bf16[1200,128]{1,0:T(8,128)(2,1)S(1)} %collective-permute-done.5.got_ref.refs_10_), custom_call_target="tpu_custom_call" | custom-call | tf_op jit(solution)/shard_map/outermost_rows/pallas_call | solution.py:473
  14.2 0.0 collective-permute-done.1.refs_4_
  14.2 0.6 %collective-permute-start.6 = (bf16[16,2048]{1,0:T(8,128)(2,1)S(1)}, bf16[16,2048]{1,0:T(8,128)(2,1)S(1)}, u32[]{:S(2)}, u32[]{:S(2)}) collective-permute-start(bf16[16,2048]{1,0:T(8,128)(2,1)S(1)} %outermost_rows.1.refs_8_), channel_id=1, source_target_pairs={{0,1},{1,0},{2,3},{3,2},{4,5},{5,4},{6,7},{7,6},{8,9},{9,8},{10,11... | collective-permute-start | bytes 196616 | tf_op jit(solution)/shard_map/ppermute | solution.py:481
  14.8 0.0 collective-permute-done.2.refs_5_
  14.8 0.0 collective-permute-done.3.refs_6_
  14.8 0.7 %collective-permute-done.4.refs_7_ = f32[4,128,128]{2,1,0:T(8,128)S(1)} collective-permute-done((f32[4,128,128]{2,1,0:T(8,128)S(1)}, f32[4,128,128]{2,1,0:T(8,128)S(1)}, u32[]{:S(2)}, u32[]{:S(2)}) %collective-permute-start.4) | collective-permute-done | bytes 262176 | tf_op jit(solution)/shard_map/ppermute | solution.py:472
  15.5 0.2 %collective-permute-done.6.refs_9_ = bf16[16,2048]{1,0:T(8,128)(2,1)S(1)} collective-permute-done((bf16[16,2048]{1,0:T(8,128)(2,1)S(1)}, bf16[16,2048]{1,0:T(8,128)(2,1)S(1)}, u32[]{:S(2)}, u32[]{:S(2)}) %collective-permute-start.6) | collective-permute-done | bytes 65568 | tf_op jit(solution)/shard_map/ppermute | solution.py:481
  15.7 1.8 %near_part.1 = (f32[2,64,2048]{2,1,0:T(8,128)S(1)}, bf16[32,96]{1,0:T(8,128)(2,1)S(1)}) custom-call(f32[4,128,128]{2,1,0:T(8,128)S(1)} %get-tuple-element.29.refs_0_, f32[4,128,128]{2,1,0:T(8,128)S(1)} %get-tuple-element.30.refs_1_, f32[4,128,128]{2,1,0:T(8,128)S(1)} %get-tuple-element.31.refs_2_, f32[4,128,128]{2,1,0:T(8,128)S(1)} %get-tuple-element.32.refs_3_, ...), custom_call_target="tpu_custom_call" | custom-call | tf_op jit(solution)/shard_map/near_part/pallas_call | solution.py:482
  17.5 2.2 %collective-permute-done.7.msg_ref = bf16[1040,128]{1,0:T(8,128)(2,1)S(1)} collective-permute-done((bf16[1040,128]{1,0:T(8,128)(2,1)S(1)}, bf16[1040,128]{1,0:T(8,128)(2,1)S(1)}, u32[]{:S(2)}, u32[]{:S(2)}) %collective-permute-start.7) | collective-permute-done | bytes 266272 | tf_op jit(solution)/shard_map/ppermute | solution.py:471
  19.7 1.1 %last_part.1 = f32[2,64,2048]{2,1,0:T(8,128)} custom-call(bf16[32,96]{1,0:T(8,128)(2,1)S(1)} %get-tuple-element.34.taps_ref, f32[2,64,2048]{2,1,0:T(8,128)S(1)} %get-tuple-element.35.part_ref, bf16[1040,128]{1,0:T(8,128)(2,1)S(1)} %collective-permute-done.7.msg_ref), custom_call_target="tpu_custom_call" | custom-call | tf_op jit(solution)/shard_map/last_part/pallas_call | solution.py:491
Async XLA Ops:
  0.0 7.4 %copy-start = (bf16[2,512,256]{2,1,0:T(8,128)(2,1)S(1)}, bf16[2,512,256]{2,1,0:T(8,128)(2,1)}, u32[]{:S(2)}) copy-start(bf16[2,512,256]{2,1,0:T(8,128)(2,1)} %constant.2.clone.band_ref.refs_11_) | copy-start | bytes 1572868
  2.4 11.5 %collective-permute-start.5 = (bf16[1200,128]{1,0:T(8,128)(2,1)S(1)}, bf16[1200,128]{1,0:T(8,128)(2,1)S(1)}, u32[]{:S(2)}, u32[]{:S(2)}) collective-permute-start(bf16[1200,128]{1,0:T(8,128)(2,1)S(1)} %get-tuple-element.33.own_ref), channel_id=1, source_target_pairs={{1,2},{2,1},{3,4},{4,3},{5,6},{6,5},{7,8},{8,7},{9,10},{10,9},{11,... | collective-permute-start | bytes 921608 | tf_op jit(solution)/shard_map/ppermute | solution.py:459
  6.1 1.3 %collective-permute-start = (bf16[16,2048]{1,0:T(8,128)(2,1)S(1)}, bf16[16,2048]{1,0:T(8,128)(2,1)S(1)}, u32[]{:S(2)}, u32[]{:S(2)}) collective-permute-start(bf16[16,2048]{1,0:T(8,128)(2,1)S(1)} %get-tuple-element.24), channel_id=1, source_target_pairs={{0,1},{1,0},{2,3},{3,2},{4,5},{5,4},{6,7},{7,6},{8,9},{9,8},{10,11... | collective-permute-start | bytes 196616 | tf_op jit(solution)/shard_map/ppermute | solution.py:460
  8.9 5.3 %collective-permute-start.1 = (f32[4,128,128]{2,1,0:T(8,128)S(1)}, f32[4,128,128]{2,1,0:T(8,128)S(1)}, u32[]{:S(2)}, u32[]{:S(2)}) collective-permute-start(f32[4,128,128]{2,1,0:T(8,128)S(1)} %get-tuple-element.29.refs_0_), channel_id=1, source_target_pairs={{0,1},{1,0},{2,3},{3,2},{4,5},{5,4},{6,7},{7,6},{8,9},{9,8},{10,11... | collective-permute-start | bytes 786440 | tf_op jit(solution)/shard_map/ppermute | solution.py:472
  9.1 10.6 %collective-permute-start.7 = (bf16[1040,128]{1,0:T(8,128)(2,1)S(1)}, bf16[1040,128]{1,0:T(8,128)(2,1)S(1)}, u32[]{:S(2)}, u32[]{:S(2)}) collective-permute-start(bf16[1040,128]{1,0:T(8,128)(2,1)S(1)} %get-tuple-element.36), channel_id=1, source_target_pairs={{1,2},{2,1},{3,4},{4,3},{5,6},{6,5},{7,8},{8,7},{9,10},{10,9},{11,... | collective-permute-start | bytes 798728 | tf_op jit(solution)/shard_map/ppermute | solution.py:471
  12.5 2.3 %collective-permute-start.2 = (f32[4,128,128]{2,1,0:T(8,128)S(1)}, f32[4,128,128]{2,1,0:T(8,128)S(1)}, u32[]{:S(2)}, u32[]{:S(2)}) collective-permute-start(f32[4,128,128]{2,1,0:T(8,128)S(1)} %get-tuple-element.30.refs_1_), channel_id=1, source_target_pairs={{0,1},{1,0},{2,3},{3,2},{4,5},{5,4},{6,7},{7,6},{8,9},{9,8},{10,11... | collective-permute-start | bytes 786440 | tf_op jit(solution)/shard_map/ppermute | solution.py:472
  12.6 2.2 %collective-permute-start.3 = (f32[4,128,128]{2,1,0:T(8,128)S(1)}, f32[4,128,128]{2,1,0:T(8,128)S(1)}, u32[]{:S(2)}, u32[]{:S(2)}) collective-permute-start(f32[4,128,128]{2,1,0:T(8,128)S(1)} %get-tuple-element.31.refs_2_), channel_id=1, source_target_pairs={{0,1},{1,0},{2,3},{3,2},{4,5},{5,4},{6,7},{7,6},{8,9},{9,8},{10,11... | collective-permute-start | bytes 786440 | tf_op jit(solution)/shard_map/ppermute | solution.py:472
  13.9 1.5 %collective-permute-start.4 = (f32[4,128,128]{2,1,0:T(8,128)S(1)}, f32[4,128,128]{2,1,0:T(8,128)S(1)}, u32[]{:S(2)}, u32[]{:S(2)}) collective-permute-start(f32[4,128,128]{2,1,0:T(8,128)S(1)} %get-tuple-element.32.refs_3_), channel_id=1, source_target_pairs={{0,1},{1,0},{2,3},{3,2},{4,5},{5,4},{6,7},{7,6},{8,9},{9,8},{10,11... | collective-permute-start | bytes 786440 | tf_op jit(solution)/shard_map/ppermute | solution.py:472
  14.2 1.5 %collective-permute-start.6 = (bf16[16,2048]{1,0:T(8,128)(2,1)S(1)}, bf16[16,2048]{1,0:T(8,128)(2,1)S(1)}, u32[]{:S(2)}, u32[]{:S(2)}) collective-permute-start(bf16[16,2048]{1,0:T(8,128)(2,1)S(1)} %outermost_rows.1.refs_8_), channel_id=1, source_target_pairs={{0,1},{1,0},{2,3},{3,2},{4,5},{5,4},{6,7},{7,6},{8,9},{9,8},{10,11... | collective-permute-start | bytes 196616 | tf_op jit(solution)/shard_map/ppermute | solution.py:481
